TPU v7x, 32 devices: a whole 2x2x4 slice. The times are simulated.
32 devices in a mesh: ctx: 8 (over z, core), exp: 4 (over y, x).
Axes of the slice: x: 2, y: 2, z: 4, core: 2. Of those that a mesh axis runs over, the one named last changes fastest.
Arguments:
- query_input: bfloat16 [1024, 8192], P('ctx', 'exp'), may hold values from -6 to 6
- key_input: bfloat16 [1024, 8192], P('ctx', 'exp'), may hold values from -6 to 6
- value_input: bfloat16 [1024, 8192], P('ctx', 'exp'), may hold values from -6 to 6
- gate_logits: float32 [2, 1024, 64], P(None, 'ctx', 'exp'), may hold values from -6 to 6
- comp_weight: float32 [2, 32, 64], P(None, None, 'exp'), may hold values from -6 to 6
- out_proj: bfloat16 [8192, 7168], P('exp', 'ctx'), may hold values from -0.0625 to 0.0625
- residual_in: bfloat16 [1024, 7168], P(('ctx', 'exp')), may hold values from -3 to 3
- ffn_gain: float32 [7168], replicated, may hold values from 0.25 to 1.75
- expert_ids: int32 [1024, 2], P(('ctx', 'exp')), may hold values from 0 to 3, all different within a row; in each aligned block of 32 rows (0 to 31, 32 to 63, ...) at most 32 rows name the same one
- route_gates: float32 [1024, 2], P(('ctx', 'exp')), may hold values from 0.2 to 1
- expert_gate: bfloat16 [4, 7168, 2048], P('exp', None, 'ctx'), may hold values from -0.0625 to 0.0625
- expert_up: bfloat16 [4, 7168, 2048], P('exp', None, 'ctx'), may hold values from -0.0625 to 0.0625
- expert_down: bfloat16 [4, 2048, 7168], P('exp', 'ctx'), may hold values from -0.125 to 0.125
Outputs:
- layer_out: bfloat16 [1024, 7168], P(('ctx', 'exp'))
Inputs may be any that keep to these rules, and one draw needn't show every extreme that they name: `expert_ids`: each token names 2 different experts. In every aligned block of 32 consecutive tokens no expert is named more than 32 times, a bound that some block reaches.
All inputs are finite; a program needn't handle non-finite values.
Results may differ from a plain program's by a relative error of at most 0.0085.
Values may be sent and summed in bfloat16 or wider, within the bound.
No kernel may reach another device: no remote copies, remote signals or barrier semaphores. Data moves between devices by JAX's collectives and lax.ppermute only.
A program may use at most 128 MiB of HBM per device.

v0:
```python
import math

import jax
import jax.numpy as jnp
from jax import lax
from jax.sharding import PartitionSpec as P

WINDOW = 512


score_gain = 2.0
norm_eps = 1e-06


def passed_along(block, axis, distance):
    devices = range(lax.axis_size(axis))
    route = [(i - distance, i) for i in devices if i - distance in devices]
    return lax.ppermute(block, axis, route)


def head_norm(matrix, head_width):
    row_count = matrix.shape[0]
    shaped = matrix.reshape(row_count, -1, head_width).astype(jnp.float32)
    scaled = shaped * lax.rsqrt(jnp.mean(shaped * shaped, axis=2, keepdims=True) + norm_eps)
    return scaled.reshape(row_count, -1)


def compress(extended, position_weights, head_width):
    stride_len = position_weights.shape[0] // 2
    head_count = position_weights.shape[1]
    blocks = extended.reshape(-1, stride_len, head_count, head_width).astype(jnp.float32)
    first_half = jnp.einsum(
        "nshd,sh->nhd", blocks[:-1], position_weights[:stride_len], precision=lax.Precision.HIGHEST
    )
    second_half = jnp.einsum(
        "nshd,sh->nhd", blocks[1:], position_weights[stride_len:], precision=lax.Precision.HIGHEST
    )
    return (first_half + second_half).reshape(blocks.shape[0] - 1, head_count * head_width)


def local(
    query_input,
    key_input,
    value_input,
    gate_logits,
    comp_weight,
    out_proj,
    residual_in,
    ffn_gain,
    expert_ids,
    route_gates,
    expert_gate,
    expert_up,
    expert_down,
):
    row_count = query_input.shape[0]
    head_count = comp_weight.shape[2]
    head_width = query_input.shape[1] // head_count
    block_len = comp_weight.shape[1]
    stride_len = block_len // 2
    exp_count = lax.axis_size("exp")
    ctx_index = lax.axis_index("ctx")
    scale = score_gain / math.sqrt(head_width)
    query_norm = head_norm(query_input, head_width).astype(jnp.bfloat16)
    key_norm = head_norm(key_input, head_width).astype(jnp.bfloat16)
    next_keys, next_values = passed_along(
        (key_input[:stride_len], value_input[:stride_len]), "ctx", -1
    )
    comp_keys = head_norm(
        compress(jnp.concatenate([key_input, next_keys], 0), comp_weight[0], head_width), head_width
    ).astype(jnp.bfloat16)
    comp_values = compress(
        jnp.concatenate([value_input, next_values], 0), comp_weight[1], head_width
    ).astype(jnp.bfloat16)
    query_pos = ctx_index * row_count + jnp.arange(row_count, dtype=jnp.int32)
    query_heads = query_norm.reshape(row_count, head_count, head_width)
    part_keys = lax.all_gather(comp_keys, "ctx", axis=0, tiled=True)
    part_values = lax.all_gather(comp_values, "ctx", axis=0, tiled=True)
    part_count = part_keys.shape[0]
    scores = jnp.einsum(
        "thd,nhd->htn",
        query_heads,
        part_keys.reshape(part_count, head_count, head_width),
        preferred_element_type=jnp.float32,
    )
    block_end = jnp.arange(part_count, dtype=jnp.int32) * stride_len + block_len - 1
    visible = block_end[None, :] <= query_pos[:, None]
    weights = jnp.where(visible[None], jnp.exp(scale * scores), 0.0)
    running_total = jnp.sum(weights, axis=2).T
    collected = jnp.einsum(
        "htn,nhd->thd",
        weights.astype(jnp.bfloat16),
        part_values.reshape(part_count, head_count, head_width),
        preferred_element_type=jnp.float32,
    )
    cmp_sum = collected.reshape(row_count, -1)
    no_block = (query_pos < block_len - 1).astype(jnp.float32)
    cmp_out = (
        cmp_sum.reshape(row_count, head_count, head_width)
        / (running_total + no_block[:, None])[:, :, None]
    )
    shift_count = max(1, WINDOW // row_count)
    earlier_keys = []
    earlier_values = []
    for distance in range(shift_count, 0, -1):
        moved_keys, moved_values = passed_along((key_norm, value_input), "ctx", distance)
        earlier_keys.append(moved_keys)
        earlier_values.append(moved_values)
    near_keys = jnp.concatenate(earlier_keys + [key_norm], 0)
    near_values = jnp.concatenate(earlier_values + [value_input], 0)
    key_pos = ctx_index * row_count - WINDOW + jnp.arange(near_keys.shape[0], dtype=jnp.int32)
    near_scores = jnp.einsum(
        "thd,shd->hts",
        query_heads,
        near_keys.reshape(-1, head_count, head_width),
        preferred_element_type=jnp.float32,
    )
    inside = (
        (key_pos[None, :] <= query_pos[:, None])
        & (key_pos[None, :] > query_pos[:, None] - WINDOW)
        & (key_pos[None, :] >= 0)
    )
    near_weights = jnp.where(inside[None], jnp.exp(scale * near_scores), 0.0)
    win_total = jnp.sum(near_weights, axis=2).T
    win_sum = jnp.einsum(
        "hts,shd->thd",
        near_weights.astype(jnp.bfloat16),
        near_values.reshape(-1, head_count, head_width),
        preferred_element_type=jnp.float32,
    )
    win_out = win_sum / win_total[:, :, None]
    branch_gates = jax.nn.sigmoid(gate_logits)
    attended = (
        (branch_gates[0][:, :, None] * cmp_out + branch_gates[1][:, :, None] * win_out)
        .reshape(row_count, -1)
        .astype(jnp.bfloat16)
    )
    token_share = row_count // exp_count
    spread = jnp.einsum(
        "cerh,hd->ecrd",
        lax.all_gather(attended.reshape(1, exp_count, token_share, -1), "ctx", axis=0, tiled=True),
        out_proj,
        preferred_element_type=jnp.float32,
    )
    owned = lax.psum_scatter(spread, "exp", scatter_dimension=0, tiled=True)
    joined = lax.all_to_all(owned, "ctx", split_axis=1, concat_axis=3, tiled=True)
    projected = joined.reshape(token_share, -1)
    hidden_state = residual_in.astype(jnp.float32) + projected
    mean_square = jnp.mean(hidden_state * hidden_state, axis=1, keepdims=True)
    normed = (hidden_state * lax.rsqrt(mean_square + norm_eps) * ffn_gain).astype(jnp.bfloat16)
    model_width = normed.shape[1]
    top_count = expert_ids.shape[1]
    capacity = max(2, 2 * token_share * top_count // exp_count)
    flat_ids = expert_ids.reshape(-1)
    chosen = (flat_ids[:, None] == jnp.arange(exp_count, dtype=jnp.int32)[None, :]).astype(
        jnp.int32
    )
    slots = jnp.sum((jnp.cumsum(chosen, axis=0) - chosen) * chosen, axis=1)
    targets = (flat_ids * capacity + slots).reshape(token_share, top_count)
    slot_range = jnp.arange(exp_count * capacity, dtype=jnp.int32)
    dispatch_map = jnp.sum(
        (slot_range[:, None, None] == targets[None, :, :]).astype(jnp.float32), axis=2
    ).astype(jnp.bfloat16)
    outgoing = (
        jnp.dot(dispatch_map, normed, preferred_element_type=jnp.float32)
        .astype(jnp.bfloat16)
        .reshape(exp_count, capacity, model_width)
    )
    arrived = lax.all_to_all(outgoing, "exp", split_axis=0, concat_axis=0, tiled=True)
    gate_cols = expert_gate[0]
    up_cols = expert_up[0]
    down_rows = expert_down[0]
    portion = lax.all_gather(arrived, "ctx", axis=0, tiled=True)
    flat_rows = portion.reshape(-1, model_width)
    gate_part = jnp.dot(flat_rows, gate_cols, preferred_element_type=jnp.float32)
    up_part = jnp.dot(flat_rows, up_cols, preferred_element_type=jnp.float32)
    activated = (jax.nn.silu(gate_part) * up_part).astype(jnp.bfloat16)
    partial_out = jnp.dot(activated, down_rows, preferred_element_type=jnp.float32).reshape(
        portion.shape
    )
    finished = lax.psum_scatter(
        partial_out.astype(jnp.bfloat16), "ctx", scatter_dimension=0, tiled=True
    )
    returned = lax.all_to_all(finished, "exp", split_axis=0, concat_axis=0, tiled=True).reshape(
        -1, model_width
    )
    combine_map = jnp.sum(
        jnp.where(slot_range[None, None, :] == targets[:, :, None], route_gates[:, :, None], 0.0),
        axis=1,
    )
    moe_out = jnp.dot(combine_map, returned.astype(jnp.float32), precision=lax.Precision.HIGHEST)
    return (hidden_state + moe_out).astype(jnp.bfloat16)


def solution(mesh):
    in_specs = (
        P("ctx", "exp"),
        P("ctx", "exp"),
        P("ctx", "exp"),
        P(None, "ctx", "exp"),
        P(None, None, "exp"),
        P("exp", "ctx"),
        P(("ctx", "exp"), None),
        P(),
        P(("ctx", "exp"), None),
        P(("ctx", "exp"), None),
        P("exp", None, "ctx"),
        P("exp", None, "ctx"),
        P("exp", "ctx", None),
    )
    out_specs = P(("ctx", "exp"), None)
    return jax.shard_map(local, mesh=mesh, in_specs=in_specs, out_specs=out_specs, check_vma=False)
```

profile of v0, /device:TPU:0, one launch (start us, length us, event | category | flops | bytes accessed | tf_op | source)
XLA Modules:
  0.0 712.8 jit_solution(15557337336287658790)
XLA Ops:
  8.9 6.0 collective-permute-start.6
  14.9 3.4 collective-permute-start.7
  18.3 2.9 collective-permute-start.8
  32.6 70.1 %all_gather.13 = bf16[64,2048]{1,0:T(8,128)(2,1)S(1)} all-gather(bf16[8,2048]{1,0:T(8,128)(2,1)S(1)} %fusion.62), channel_id=1, replica_groups=mesh['ctx'=8,'exp'=4] {'ctx'}, dimensions={0}, use_global_device_ids=true | all-gather | bytes 294912 | tf_op jit(solution)/shard_map/all_gather | solution.py:77
  107.6 3.0 collective-permute-start.4
  111.8 2.2 collective-permute-start.5
  120.6 9.3 %collective-permute-done.4 = bf16[128,2048]{1,0:T(8,128)(2,1)S(1)} collective-permute-done((bf16[128,2048]{1,0:T(8,128)(2,1)S(1)}, bf16[128,2048]{1,0:T(8,128)(2,1)S(1)}, u32[]{:S(2)}, u32[]{:S(2)}) %collective-permute-start.4) | collective-permute-done | bytes 524320 | tf_op jit(solution)/shard_map/ppermute | solution.py:18
  132.7 4.5 copy.86
  137.7 25.2 %all_gather.12 = bf16[64,2048]{1,0:T(8,128)(2,1)S(1)} all-gather(bf16[8,2048]{1,0:T(8,128)(2,1)S(1)} %fusion.61), channel_id=1, replica_groups=mesh['ctx'=8,'exp'=4] {'ctx'}, dimensions={0}, use_global_device_ids=true | all-gather | bytes 294912 | tf_op jit(solution)/shard_map/all_gather | solution.py:78
  162.9 2.7 fusion.1
  168.9 45.4 %all-gather.3.cloned.1.call-done = bf16[8,4,32,2048]{3,2,1,0:T(8,128)(2,1)} async-done(((bf16[1,4,32,2048]{3,2,1,0:T(8,128)(2,1)}), bf16[8,4,32,2048]{3,2,1,0:T(8,128)(2,1)}) %all-gather.3.cloned.1.call-update) | async-done | bytes 4194320 | tf_op jit(solution)/shard_map/all_gather | solution.py:141
  214.3 9.6 %fusion.15 = f32[4,8,32,896]{3,2,0,1:T(8,128)} fusion(bf16[8,4,32,2048]{3,2,1,0:T(8,128)(2,1)} %all-gather.3.cloned.1.call-done, bf16[2048,896]{1,0:T(8,128)(2,1)} %param.18), kind=kOutput, calls=%fused_computation.18 | convolution fusion | flops 3758096384 | bytes 11534336 | tf_op jit(solution)/shard_map/cerh,hd->ecrd/dot_general | solution.py:139
  225.1 93.6 %all-reduce.3.cloned.1.call-done = f32[4,8,32,896]{3,2,0,1:T(8,128)} async-done(((f32[4,8,32,896]{3,2,0,1:T(8,128)}), f32[4,8,32,896]{3,2,0,1:T(8,128)}) %all-reduce.3.cloned.1.call-update) | async-done | bytes 3670032
  318.8 2.8 constant_dynamic-slice_fusion
  321.6 4.6 all-to-all-start
  327.1 22.9 %all-to-all-done = f32[1,8,32,896]{3,2,0,1:T(8,128)S(1)} async-done(((f32[1,8,32,896]{3,2,0,1:T(8,128)}), f32[1,8,32,896]{3,2,0,1:T(8,128)S(1)}, u32[]{:S(2)}, u32[]{:S(2)}) %all-to-all-start) | async-done | bytes 917536 | tf_op jit(solution)/shard_map/all_to_all | solution.py:146
  351.0 25.9 %all_to_all.25 = bf16[4,32,7168]{2,1,0:T(8,128)(2,1)} all-to-all(bf16[4,32,7168]{2,1,0:T(8,128)(2,1)S(1)} %bitcast.177), channel_id=1, replica_groups=mesh['ctx'=8,'exp'=4] {'exp'}, dimensions={0} | all-to-all | bytes 3670016 | tf_op jit(solution)/shard_map/all_to_all | solution.py:169
  376.9 131.8 %all-gather.5.cloned.1.call-done = bf16[32,32,7168]{2,1,0:T(8,128)(2,1)} async-done(((bf16[4,32,7168]{2,1,0:T(8,128)(2,1)}), bf16[32,32,7168]{2,1,0:T(8,128)(2,1)}) %all-gather.5.cloned.1.call-update) | async-done | bytes 14680080 | tf_op jit(solution)/shard_map/all_gather | solution.py:173
  508.8 8.9 %fusion.8 = f32[1024,256]{1,0:T(8,128)S(1)} fusion(bf16[1024,7168]{1,0:T(8,128)(2,1)} %bitcast.201, bf16[1,7168,256]{2,1,0:T(8,128)(2,1)} %param.23), kind=kOutput, calls=%fused_computation.12 | convolution fusion | flops 3758096384 | bytes 19398656 | tf_op jit(solution)/shard_map/dot_general | solution.py:175
  520.2 4.0 fusion.27
  524.2 9.3 %convolution_convert_fusion = bf16[32,32,7168]{2,1,0:T(8,128)(2,1)} fusion(bf16[32,32,256]{2,1,0:T(8,128)(2,1)S(1)} %bitcast.185, bf16[1,256,7168]{2,1,0:T(8,128)(2,1)} %param.25), kind=kOutput, calls=%fused_computation | convolution fusion | flops 3765436416 | bytes 18874368 | tf_op jit(solution)/shard_map/dot_general | solution.py:178
  533.6 147.4 %reduce-scatter.5.cloned.1.call-done = bf16[4,32,7168]{2,1,0:T(8,128)(2,1)} async-done(((bf16[32,32,7168]{2,1,0:T(8,128)(2,1)}), bf16[4,32,7168]{2,1,0:T(8,128)(2,1)}) %reduce-scatter.5.cloned.1.call-update) | async-done | bytes 1835024 | tf_op jit(solution)/shard_map/reduce_scatter | solution.py:181
  681.0 3.7 all-to-all-start.2
  684.7 20.0 %all-to-all-done.2 = bf16[4,32,7168]{2,1,0:T(8,128)(2,1)S(1)} async-done(((bf16[4,32,7168]{2,1,0:T(8,128)(2,1)}), bf16[4,32,7168]{2,1,0:T(8,128)(2,1)S(1)}, u32[]{:S(2)}, u32[]{:S(2)}) %all-to-all-start.2) | async-done | bytes 1835040 | tf_op jit(solution)/shard_map/all_to_all | solution.py:184
  (126 shorter events, 40.0 us)
Async XLA Ops:
  6.5 207.7 %all-gather.3.cloned.1.call-start = ((), (), s32[]{:S(2)}) async-start(), calls=%async_computation.4 | async-start | bytes 4718592 | tf_op jit(solution)/shard_map/all_gather | solution.py:141
  8.0 19.9 %copy-start.5 = (bf16[128,2048]{1,0:T(8,128)(2,1)S(1)}, bf16[128,2048]{1,0:T(8,128)(2,1)}, u32[]{:S(2)}) copy-start(bf16[128,2048]{1,0:T(8,128)(2,1)} %param.13) | copy-start | bytes 1572868
  8.9 94.9 %collective-permute-start.6 = (bf16[128,2048]{0,1:T(8,128)(2,1)}, bf16[128,2048]{0,1:T(8,128)(2,1)S(1)}, u32[]{:S(2)}, u32[]{:S(2)}) collective-permute-start(bf16[128,2048]{0,1:T(8,128)(2,1)} %fusion.35), channel_id=1, source_target_pairs={{0,16},{4,20},{8,24},{12,28},{1,17},{5,21},{9,25},{13,29},{2,18},{... | collective-permute-start | bytes 1572872 | tf_op jit(solution)/shard_map/ppermute | solution.py:18
  14.9 92.8 %collective-permute-start.7 = (bf16[128,2048]{0,1:T(8,128)(2,1)}, bf16[128,2048]{0,1:T(8,128)(2,1)}, u32[]{:S(2)}, u32[]{:S(2)}) collective-permute-start(bf16[128,2048]{0,1:T(8,128)(2,1)} %fusion.35), channel_id=1, source_target_pairs={{0,12},{4,16},{8,20},{12,24},{16,28},{1,13},{5,17},{9,21},{13,25},... | collective-permute-start | bytes 1572872 | tf_op jit(solution)/shard_map/ppermute | solution.py:18
  18.3 93.5 %collective-permute-start.8 = (bf16[128,2048]{0,1:T(8,128)(2,1)}, bf16[128,2048]{0,1:T(8,128)(2,1)}, u32[]{:S(2)}, u32[]{:S(2)}) collective-permute-start(bf16[128,2048]{0,1:T(8,128)(2,1)} %fusion.35), channel_id=1, source_target_pairs={{0,8},{4,12},{8,16},{12,20},{16,24},{20,28},{1,9},{5,13},{9,17},{1... | collective-permute-start | bytes 1572872 | tf_op jit(solution)/shard_map/ppermute | solution.py:18
  21.3 93.9 %collective-permute-start.9 = (bf16[128,2048]{0,1:T(8,128)(2,1)}, bf16[128,2048]{0,1:T(8,128)(2,1)}, u32[]{:S(2)}, u32[]{:S(2)}) collective-permute-start(bf16[128,2048]{0,1:T(8,128)(2,1)} %fusion.35), channel_id=1, source_target_pairs={{0,4},{4,8},{8,12},{12,16},{16,20},{20,24},{24,28},{1,5},{5,9},{9,... | collective-permute-start | bytes 1572872 | tf_op jit(solution)/shard_map/ppermute | solution.py:18
  24.2 5.5 collective-permute-start.1
  28.3 74.4 %copy-start.6 = (bf16[16,16,8,128]{3,2,1,0:T(8,128)(2,1)}, bf16[16,16,8,128]{3,2,1,0:T(8,128)(2,1)S(1)}, u32[]{:S(2)}) copy-start(bf16[16,16,8,128]{3,2,1,0:T(8,128)(2,1)S(1)} %fusion.36) | copy-start | bytes 1572868
  29.8 89.1 %collective-permute-start.2 = (bf16[128,2048]{1,0:T(8,128)(2,1)S(1)}, bf16[128,2048]{1,0:T(8,128)(2,1)S(1)}, u32[]{:S(2)}, u32[]{:S(2)}) collective-permute-start(bf16[128,2048]{1,0:T(8,128)(2,1)S(1)} %copy-done.3), channel_id=1, source_target_pairs={{0,16},{4,20},{8,24},{12,28},{1,17},{5,21},{9,25},{13,29},{2,18},{... | collective-permute-start | bytes 1572872 | tf_op jit(solution)/shard_map/ppermute | solution.py:18
  104.7 15.1 %collective-permute-start.3 = (bf16[128,2048]{1,0:T(8,128)(2,1)S(1)}, bf16[128,2048]{1,0:T(8,128)(2,1)S(1)}, u32[]{:S(2)}, u32[]{:S(2)}) collective-permute-start(bf16[128,2048]{1,0:T(8,128)(2,1)S(1)} %copy-done.3), channel_id=1, source_target_pairs={{0,12},{4,16},{8,20},{12,24},{16,28},{1,13},{5,17},{9,21},{13,25},... | collective-permute-start | bytes 1572872 | tf_op jit(solution)/shard_map/ppermute | solution.py:18
  107.6 22.2 %collective-permute-start.4 = (bf16[128,2048]{1,0:T(8,128)(2,1)S(1)}, bf16[128,2048]{1,0:T(8,128)(2,1)S(1)}, u32[]{:S(2)}, u32[]{:S(2)}) collective-permute-start(bf16[128,2048]{1,0:T(8,128)(2,1)S(1)} %copy-done.3), channel_id=1, source_target_pairs={{0,8},{4,12},{8,16},{12,20},{16,24},{20,28},{1,9},{5,13},{9,17},{1... | collective-permute-start | bytes 1572872 | tf_op jit(solution)/shard_map/ppermute | solution.py:18
  111.8 18.9 %collective-permute-start.5 = (bf16[128,2048]{1,0:T(8,128)(2,1)S(1)}, bf16[128,2048]{1,0:T(8,128)(2,1)S(1)}, u32[]{:S(2)}, u32[]{:S(2)}) collective-permute-start(bf16[128,2048]{1,0:T(8,128)(2,1)S(1)} %copy-done.3), channel_id=1, source_target_pairs={{0,4},{4,8},{8,12},{12,16},{16,20},{20,24},{24,28},{1,5},{5,9},{9,... | collective-permute-start | bytes 1572872 | tf_op jit(solution)/shard_map/ppermute | solution.py:18
  115.2 16.3 %collective-permute-start = (bf16[16,2048]{1,0:T(8,128)(2,1)S(1)}, bf16[16,2048]{1,0:T(8,128)(2,1)S(1)}, u32[]{:S(2)}, u32[]{:S(2)}) collective-permute-start(bf16[16,2048]{1,0:T(8,128)(2,1)S(1)} %slice.66), channel_id=1, source_target_pairs={{4,0},{8,4},{12,8},{16,12},{20,16},{24,20},{28,24},{5,1},{9,5},{13... | collective-permute-start | bytes 196616 | tf_op jit(solution)/shard_map/ppermute | solution.py:18
  168.7 150.1 %all-reduce.3.cloned.1.call-start = ((), (), s32[]{:S(2)}) async-start(), calls=%async_computation.7 | async-start | bytes 7340032
  223.9 102.4 %copy-start.11 = (s32[32,2]{0,1:T(2,128)S(1)}, s32[32,2]{0,1:T(2,128)}, u32[]{:S(2)}) copy-start(s32[32,2]{0,1:T(2,128)} %param.21) | copy-start | bytes 772
  223.9 126.1 %copy-start.1 = (bf16[32,7168]{1,0:T(8,128)(2,1)S(1)}, bf16[32,7168]{1,0:T(8,128)(2,1)}, u32[]{:S(2)}) copy-start(bf16[32,7168]{1,0:T(8,128)(2,1)} %param.19) | copy-start | bytes 1376260
  223.9 126.4 %copy-start.9 = (f32[7168]{0:T(1024)S(1)}, f32[7168]{0:T(1024)}, u32[]{:S(2)}) copy-start(f32[7168]{0:T(1024)} %param.20) | copy-start | bytes 86020
  321.6 28.4 %all-to-all-start = ((f32[1,8,32,896]{3,2,0,1:T(8,128)}), f32[1,8,32,896]{3,2,0,1:T(8,128)S(1)}, u32[]{:S(2)}, u32[]{:S(2)}) async-start(f32[1,8,32,896]{3,2,0,1:T(8,128)} %constant_dynamic-slice_fusion), calls=%async_computation | async-start | bytes 1835008 | tf_op jit(solution)/shard_map/all_to_all | solution.py:146
  326.2 182.6 %all-gather.5.cloned.1.call-start = ((), (), s32[]{:S(2)}) async-start(), calls=%async_computation.5 | async-start | bytes 16515072 | tf_op jit(solution)/shard_map/all_gather | solution.py:173
  376.9 304.1 %reduce-scatter.5.cloned.1.call-start = ((), (), s32[]{:S(2)}) async-start(), calls=%async_computation.6 | async-start | bytes 16515072 | tf_op jit(solution)/shard_map/reduce_scatter | solution.py:181
  508.8 10.4 %copy-start.13 = (bf16[32,32,7168]{2,1,0:T(8,128)(2,1)S(1)}, bf16[32,32,7168]{2,1,0:T(8,128)(2,1)}, u32[]{:S(2)}) copy-start(bf16[32,32,7168]{2,1,0:T(8,128)(2,1)} %all-gather.5.cloned.1.call-done) | copy-start | bytes 44040196
  508.8 11.4 %copy-start.14 = (bf16[1,7168,256]{2,1,0:T(8,128)(2,1)S(1)}, bf16[1,7168,256]{2,1,0:T(8,128)(2,1)}, u32[]{:S(2)}) copy-start(bf16[1,7168,256]{2,1,0:T(8,128)(2,1)} %param.24) | copy-start | bytes 11010052
  533.6 151.1 %copy-start.12 = (f32[32,2]{0,1:T(2,128)S(1)}, f32[32,2]{0,1:T(2,128)}, u32[]{:S(2)}) copy-start(f32[32,2]{0,1:T(2,128)} %param.22) | copy-start | bytes 772
  681.0 23.7 %all-to-all-start.2 = ((bf16[4,32,7168]{2,1,0:T(8,128)(2,1)}), bf16[4,32,7168]{2,1,0:T(8,128)(2,1)S(1)}, u32[]{:S(2)}, u32[]{:S(2)}) async-start(bf16[4,32,7168]{2,1,0:T(8,128)(2,1)} %reduce-scatter.5.cloned.1.call-done), calls=%async_computation.3 | async-start | bytes 3670016 | tf_op jit(solution)/shard_map/all_to_all | solution.py:184
  (9 other events, 16.4 us)
Sparse Core Ops, SparseCore 0:
  168.8 45.4 all-gather.2
  224.0 94.6 all-reduce.2
  377.0 131.7 all-gather.4
  533.7 147.2 reduce-scatter.4
where the time goes:
time: 714 us; the launch traced here: 713 us
  waiting for transfers between devices  471 us (66%)
  blocking collectives  121 us (17%)
  matrix products  41.1 us (6%)
  starting transfers between devices  34.7 us (5%)
  local copies, waits for them, and re-layouts  26.3 us (4%)
  between operations  13.7 us (2%)
    reduce_scatter x1, waiting for transfers between devices, local(): lax.psum_scatter(partial_out.astype(jnp.bfloat16), 'ctx', scatter_dimensi...  147 us
    all_gather x1, waiting for transfers between devices, local(): portion = lax.all_gather(arrived, 'ctx', axis=0, tiled=True)  132 us
    unnamed x5, waiting for transfers between devices  93.7 us
    all_gather x1, blocking collectives, local(): part_keys = lax.all_gather(comp_keys, 'ctx', axis=0, tiled=True)  70.1 us
    all_gather x1, waiting for transfers between devices, local(): lax.all_gather(attended.reshape(1, exp_count, token_share, -1), 'ctx', ax...  45.4 us
    ppermute x10, starting transfers between devices, passed_along(): return lax.ppermute(block, axis, route)  26.1 us
    all_to_all x1, blocking collectives, local(): lax.all_to_all(outgoing, 'exp', split_axis=0, concat_axis=0, tiled=True)  25.9 us
    all_gather x1, blocking collectives, local(): part_values = lax.all_gather(comp_values, 'ctx', axis=0, tiled=True)  25.2 us
  transfers between devices with their start and end apart: 16, of which 7 were waited for; matrix products, arithmetic and copies ran while one was open for 2% of the time, Pallas kernels for 0%

commit v1 on v0

v1 whole, which is shorter than its diff:
```python
import math

import jax
import jax.numpy as jnp
from jax import lax
from jax.sharding import PartitionSpec as P

WINDOW = 512


score_gain = 2.0
norm_eps = 1e-06


def passed_along(block, axis, distance):
    devices = range(lax.axis_size(axis))
    route = [(i - distance, i) for i in devices if i - distance in devices]
    return lax.ppermute(block, axis, route)


def head_norm(matrix, head_width):
    row_count = matrix.shape[0]
    shaped = matrix.reshape(row_count, -1, head_width).astype(jnp.float32)
    scaled = shaped * lax.rsqrt(jnp.mean(shaped * shaped, axis=2, keepdims=True) + norm_eps)
    return scaled.reshape(row_count, -1)


def compress(extended, position_weights, head_width):
    stride_len = position_weights.shape[0] // 2
    head_count = position_weights.shape[1]
    blocks = extended.reshape(-1, stride_len, head_count, head_width).astype(jnp.float32)
    first_half = jnp.einsum(
        "nshd,sh->nhd", blocks[:-1], position_weights[:stride_len], precision=lax.Precision.HIGHEST
    )
    second_half = jnp.einsum(
        "nshd,sh->nhd", blocks[1:], position_weights[stride_len:], precision=lax.Precision.HIGHEST
    )
    return (first_half + second_half).reshape(blocks.shape[0] - 1, head_count * head_width)


def window_attention(query_input, key_input, value_input, gate_logits, comp_weight):
    row_count = query_input.shape[0]
    head_count = comp_weight.shape[2]
    head_width = query_input.shape[1] // head_count
    block_len = comp_weight.shape[1]
    stride_len = block_len // 2
    exp_count = lax.axis_size("exp")
    ctx_index = lax.axis_index("ctx")
    scale = score_gain / math.sqrt(head_width)
    query_norm = head_norm(query_input, head_width).astype(jnp.bfloat16)
    key_norm = head_norm(key_input, head_width).astype(jnp.bfloat16)
    next_keys, next_values = passed_along(
        (key_input[:stride_len], value_input[:stride_len]), "ctx", -1
    )
    comp_keys = head_norm(
        compress(jnp.concatenate([key_input, next_keys], 0), comp_weight[0], head_width), head_width
    ).astype(jnp.bfloat16)
    comp_values = compress(
        jnp.concatenate([value_input, next_values], 0), comp_weight[1], head_width
    ).astype(jnp.bfloat16)
    query_pos = ctx_index * row_count + jnp.arange(row_count, dtype=jnp.int32)
    query_heads = query_norm.reshape(row_count, head_count, head_width)
    part_keys = lax.all_gather(comp_keys, "ctx", axis=0, tiled=True)
    part_values = lax.all_gather(comp_values, "ctx", axis=0, tiled=True)
    part_count = part_keys.shape[0]
    scores = jnp.einsum(
        "thd,nhd->htn",
        query_heads,
        part_keys.reshape(part_count, head_count, head_width),
        preferred_element_type=jnp.float32,
    )
    block_end = jnp.arange(part_count, dtype=jnp.int32) * stride_len + block_len - 1
    visible = block_end[None, :] <= query_pos[:, None]
    weights = jnp.where(visible[None], jnp.exp(scale * scores), 0.0)
    running_total = jnp.sum(weights, axis=2).T
    collected = jnp.einsum(
        "htn,nhd->thd",
        weights.astype(jnp.bfloat16),
        part_values.reshape(part_count, head_count, head_width),
        preferred_element_type=jnp.float32,
    )
    cmp_sum = collected.reshape(row_count, -1)
    no_block = (query_pos < block_len - 1).astype(jnp.float32)
    cmp_out = (
        cmp_sum.reshape(row_count, head_count, head_width)
        / (running_total + no_block[:, None])[:, :, None]
    )
    shift_count = max(1, WINDOW // row_count)
    earlier_keys = []
    earlier_values = []
    for distance in range(shift_count, 0, -1):
        moved_keys, moved_values = passed_along((key_norm, value_input), "ctx", distance)
        earlier_keys.append(moved_keys)
        earlier_values.append(moved_values)
    near_keys = jnp.concatenate(earlier_keys + [key_norm], 0)
    near_values = jnp.concatenate(earlier_values + [value_input], 0)
    key_pos = ctx_index * row_count - WINDOW + jnp.arange(near_keys.shape[0], dtype=jnp.int32)
    near_scores = jnp.einsum(
        "thd,shd->hts",
        query_heads,
        near_keys.reshape(-1, head_count, head_width),
        preferred_element_type=jnp.float32,
    )
    inside = (
        (key_pos[None, :] <= query_pos[:, None])
        & (key_pos[None, :] > query_pos[:, None] - WINDOW)
        & (key_pos[None, :] >= 0)
    )
    near_weights = jnp.where(inside[None], jnp.exp(scale * near_scores), 0.0)
    win_total = jnp.sum(near_weights, axis=2).T
    win_sum = jnp.einsum(
        "hts,shd->thd",
        near_weights.astype(jnp.bfloat16),
        near_values.reshape(-1, head_count, head_width),
        preferred_element_type=jnp.float32,
    )
    win_out = win_sum / win_total[:, :, None]
    branch_gates = jax.nn.sigmoid(gate_logits)
    attended = (
        (branch_gates[0][:, :, None] * cmp_out + branch_gates[1][:, :, None] * win_out)
        .reshape(row_count, -1)
        .astype(jnp.bfloat16)
    )
    return attended


def head_attention(query_input, key_input, value_input, gate_logits, comp_weight):
    row_count = query_input.shape[0]
    head_count = comp_weight.shape[2]
    head_width = query_input.shape[1] // head_count
    block_len = comp_weight.shape[1]
    stride_len = block_len // 2
    ctx_count = lax.axis_size("ctx")
    ctx_index = lax.axis_index("ctx")
    own = head_count // ctx_count
    width = own * head_width
    seq_len = ctx_count * row_count
    scale = score_gain / math.sqrt(head_width)
    packed = jnp.stack([query_input, key_input, value_input], 0).reshape(
        3, row_count, ctx_count, width
    )
    packed = jnp.transpose(packed, (2, 0, 1, 3))
    moved = lax.all_to_all(packed, "ctx", split_axis=0, concat_axis=0, tiled=True)
    moved = jnp.transpose(moved, (1, 0, 2, 3)).reshape(3, seq_len, width)
    logits = lax.all_gather(gate_logits, "ctx", axis=1, tiled=True)
    logits = lax.dynamic_slice_in_dim(logits, ctx_index * own, own, 2)
    weights_own = lax.dynamic_slice_in_dim(comp_weight, ctx_index * own, own, 2)
    queries = head_norm(moved[0], head_width).astype(jnp.bfloat16)
    keys = head_norm(moved[1], head_width).astype(jnp.bfloat16)
    values = moved[2]
    tail_rows = jnp.zeros((stride_len, width), jnp.bfloat16)
    comp_keys = head_norm(
        compress(jnp.concatenate([moved[1], tail_rows], 0), weights_own[0], head_width), head_width
    ).astype(jnp.bfloat16)
    comp_values = compress(
        jnp.concatenate([values, tail_rows], 0), weights_own[1], head_width
    ).astype(jnp.bfloat16)
    query_heads = queries.reshape(seq_len, own, head_width)
    part_count = comp_keys.shape[0]
    query_pos = jnp.arange(seq_len, dtype=jnp.int32)
    scores = jnp.einsum(
        "thd,nhd->htn",
        query_heads,
        comp_keys.reshape(part_count, own, head_width),
        preferred_element_type=jnp.float32,
    )
    block_end = jnp.arange(part_count, dtype=jnp.int32) * stride_len + block_len - 1
    visible = block_end[None, :] <= query_pos[:, None]
    weights = jnp.where(visible[None], jnp.exp(scale * scores), 0.0)
    total = jnp.sum(weights, axis=2).T
    cmp_sum = jnp.einsum(
        "htn,nhd->thd",
        weights.astype(jnp.bfloat16),
        comp_values.reshape(part_count, own, head_width),
        preferred_element_type=jnp.float32,
    )
    no_block = (query_pos < block_len - 1).astype(jnp.float32)
    cmp_out = cmp_sum / (total + no_block[:, None])[:, :, None]
    reach = WINDOW + row_count
    pad = jnp.zeros((WINDOW, width), jnp.bfloat16)
    key_pad = jnp.concatenate([pad, keys], 0)
    value_pad = jnp.concatenate([pad, values], 0)
    near_keys = jnp.stack(
        [key_pad[i * row_count : i * row_count + reach] for i in range(ctx_count)]
    ).reshape(ctx_count, reach, own, head_width)
    near_values = jnp.stack(
        [value_pad[i * row_count : i * row_count + reach] for i in range(ctx_count)]
    ).reshape(ctx_count, reach, own, head_width)
    near_scores = jnp.einsum(
        "bthd,bshd->bhts",
        query_heads.reshape(ctx_count, row_count, own, head_width),
        near_keys,
        preferred_element_type=jnp.float32,
    )
    rows = jnp.arange(row_count, dtype=jnp.int32)[None, :, None]
    cols = jnp.arange(reach, dtype=jnp.int32)[None, None, :] - WINDOW
    first = (jnp.arange(ctx_count, dtype=jnp.int32) * row_count)[:, None, None]
    inside = (cols <= rows) & (cols > rows - WINDOW) & (cols + first >= 0)
    near_weights = jnp.where(inside[:, None], jnp.exp(scale * near_scores), 0.0)
    win_total = jnp.transpose(jnp.sum(near_weights, axis=3), (0, 2, 1)).reshape(seq_len, own)
    win_sum = jnp.einsum(
        "bhts,bshd->bthd",
        near_weights.astype(jnp.bfloat16),
        near_values,
        preferred_element_type=jnp.float32,
    ).reshape(seq_len, own, head_width)
    win_out = win_sum / win_total[:, :, None]
    gates = jax.nn.sigmoid(logits)
    return (
        (gates[0][:, :, None] * cmp_out + gates[1][:, :, None] * win_out)
        .reshape(seq_len, width)
        .astype(jnp.bfloat16)
    )


def local(
    query_input,
    key_input,
    value_input,
    gate_logits,
    comp_weight,
    out_proj,
    residual_in,
    ffn_gain,
    expert_ids,
    route_gates,
    expert_gate,
    expert_up,
    expert_down,
):
    row_count = query_input.shape[0]
    ctx_count = lax.axis_size("ctx")
    exp_count = lax.axis_size("exp")
    ctx_index = lax.axis_index("ctx")
    exp_index = lax.axis_index("exp")
    share = row_count // exp_count
    seq_len = row_count * ctx_count
    cols = out_proj.shape[1]
    model_width = cols * ctx_count
    hidden_units = expert_gate.shape[2]
    own_tokens = ctx_count * share

    experts = jnp.arange(exp_count, dtype=jnp.int32)
    route_table = jnp.sum(
        jnp.where(expert_ids[:, :, None] == experts, route_gates[:, :, None], 0.0), axis=1
    )
    route_all = lax.all_gather(route_table, ("ctx", "exp"), axis=0, tiled=True)
    route_own = lax.dynamic_slice_in_dim(route_all, exp_index, 1, 1)
    residual = lax.all_to_all(residual_in, "ctx", split_axis=1, concat_axis=0, tiled=True)

    attention_args = (query_input, key_input, value_input, gate_logits, comp_weight)
    if comp_weight.shape[2] % ctx_count == 0:
        attended = head_attention(*attention_args)
        width = attended.shape[1]
        attended = jnp.transpose(
            attended.reshape(ctx_count, exp_count, share, width), (1, 0, 2, 3)
        ).reshape(seq_len, width)
        spread_heads = lax.all_gather(attended, "ctx", axis=0)
        partial = jnp.einsum(
            "csk,ckd->sd",
            spread_heads,
            out_proj.reshape(ctx_count, width, cols),
            preferred_element_type=jnp.float32,
        )
    else:
        attended = window_attention(*attention_args)
        spread_rows = lax.all_gather(
            attended.reshape(1, exp_count, share, -1), "ctx", axis=0, tiled=True
        )
        partial = jnp.einsum(
            "cerh,hd->ecrd", spread_rows, out_proj, preferred_element_type=jnp.float32
        )
    pieces = lax.all_to_all(
        partial.astype(jnp.bfloat16).reshape(exp_count, own_tokens, cols),
        "exp",
        split_axis=0,
        concat_axis=0,
        tiled=True,
    )
    hidden_state = residual.reshape(own_tokens, cols).astype(jnp.float32) + jnp.sum(
        pieces.astype(jnp.float32), axis=0
    )
    gain = lax.dynamic_slice_in_dim(ffn_gain, ctx_index * cols, cols, 0)
    scaled = (hidden_state * gain).astype(jnp.bfloat16)
    squares = jnp.sum(hidden_state * hidden_state, axis=1)
    rows = lax.all_gather(scaled, ("ctx", "exp"), axis=0, tiled=True)
    rows = rows.reshape(ctx_count, seq_len, cols)
    squares = lax.all_gather(squares, ("ctx", "exp"), axis=0, tiled=True)
    mean_square = jnp.sum(squares.reshape(ctx_count, seq_len), axis=0) / model_width
    inverse = lax.rsqrt(mean_square + norm_eps)[:, None]

    gate_part = inverse * jnp.einsum(
        "ctk,ckf->tf",
        rows,
        expert_gate.reshape(ctx_count, cols, hidden_units),
        preferred_element_type=jnp.float32,
    )
    up_part = inverse * jnp.einsum(
        "ctk,ckf->tf",
        rows,
        expert_up.reshape(ctx_count, cols, hidden_units),
        preferred_element_type=jnp.float32,
    )
    activated = (jax.nn.silu(gate_part) * up_part).astype(jnp.bfloat16)
    activated = jnp.transpose(
        activated.reshape(exp_count, ctx_count, share, hidden_units), (1, 0, 2, 3)
    ).reshape(seq_len, hidden_units)
    outs = jnp.dot(activated, expert_down[0], preferred_element_type=jnp.float32)
    outs = (outs * route_own).astype(jnp.bfloat16)
    outs = outs.reshape(ctx_count, exp_count, share, model_width)
    place = (0, exp_index, 0, ctx_index * cols)
    mine = lax.dynamic_slice(outs, place, (ctx_count, 1, share, cols))
    mine = mine.astype(jnp.float32) + hidden_state.reshape(ctx_count, 1, share, cols)
    outs = lax.dynamic_update_slice(outs, mine.astype(jnp.bfloat16), place)
    return lax.psum_scatter(
        outs.reshape(seq_len, model_width), ("ctx", "exp"), scatter_dimension=0, tiled=True
    )


def solution(mesh):
    in_specs = (
        P("ctx", "exp"),
        P("ctx", "exp"),
        P("ctx", "exp"),
        P(None, "ctx", "exp"),
        P(None, None, "exp"),
        P("exp", "ctx"),
        P(("ctx", "exp"), None),
        P(),
        P(("ctx", "exp"), None),
        P(("ctx", "exp"), None),
        P("exp", None, "ctx"),
        P("exp", None, "ctx"),
        P("exp", "ctx", None),
    )
    out_specs = P(("ctx", "exp"), None)
    return jax.shard_map(local, mesh=mesh, in_specs=in_specs, out_specs=out_specs, check_vma=False)
```

time: 714 us -> 717 us (level)
  waiting for transfers between devices: 471 us -> 394 us
  blocking collectives: 121 us -> 175 us
  local copies, waits for them, and re-layouts: 26.3 us -> 69.7 us
  starting transfers between devices: 34.7 us -> 13.7 us
    reduce_scatter x1, waiting for transfers between devices: 147 us -> 312 us  [local(): lax.psum_scatter(outs.reshape(seq_len, model_width), ('ctx', 'exp'), scat...]
    all_gather x2, waiting for transfers between devices: 177 us -> 47.6 us  [the longest x1 47.6 us: local(): spread_heads = lax.all_gather(attended, 'ctx', axis=0)]
    unnamed x5 -> x3, waiting for transfers between devices: 93.7 us -> 0.05 us
    all_gather x2 -> x3, blocking collectives: 95.3 us -> 175 us  [the longest x1 66.8 us: local(): route_all = lax.all_gather(route_table, ('ctx', 'exp'), axis=0, tiled=True)]
    ppermute x10 -> x0, starting transfers between devices: 26.1 us -> none  [passed_along(): return lax.ppermute(block, axis, route)]
    all_to_all x1 -> x0, blocking collectives: 25.9 us -> none  [local(): lax.all_to_all(outgoing, 'exp', split_axis=0, concat_axis=0, tiled=True)]
    another operation x0 -> x18, local copies, waits for them, and re-layouts: none -> 24.3 us  [the longest x9 14.5 us: head_attention(): jnp.stack([key_pad[i * row_count:i * row_count + reach] for i in range(ct...]
    slice x2 -> x21, local copies, waits for them, and re-layouts: 0.85 us -> 18.3 us  [the longest x9 11.4 us: head_attention(): key_pad[i * row_count:i * row_count + reach]]
  transfers between devices with their start and end apart: 16 -> 6, of which waited for: 7 -> 4; matrix products, arithmetic and copies ran while one was open for 2% -> 1% of each run, Pallas kernels for 0% -> 0%
where the time goes in v1:
time: 717 us; the launch traced here: 716 us
  waiting for transfers between devices  394 us (55%)
  blocking collectives  175 us (24%)
  local copies, waits for them, and re-layouts  69.7 us (10%)
  matrix products  39.6 us (6%)
  between operations  13.9 us (2%)
  starting transfers between devices  13.7 us (2%)
  other arithmetic  9.92 us (1%)
    reduce_scatter x1, waiting for transfers between devices, local(): lax.psum_scatter(outs.reshape(seq_len, model_width), ('ctx', 'exp'), scat...  312 us
    all_gather x1, blocking collectives, local(): route_all = lax.all_gather(route_table, ('ctx', 'exp'), axis=0, tiled=True)  66.8 us
    all_gather x1, blocking collectives, local(): squares = lax.all_gather(squares, ('ctx', 'exp'), axis=0, tiled=True)  64.1 us
    all_gather x1, waiting for transfers between devices, local(): spread_heads = lax.all_gather(attended, 'ctx', axis=0)  47.6 us
    all_gather x1, blocking collectives, head_attention(): logits = lax.all_gather(gate_logits, 'ctx', axis=1, tiled=True)  44.1 us
    all_to_all x1, waiting for transfers between devices, local(): lax.all_to_all(partial.astype(jnp.bfloat16).reshape(exp_count, own_tokens...  21.8 us
    another operation x9, local copies, waits for them, and re-layouts, head_attention(): jnp.stack([key_pad[i * row_count:i * row_count + reach] for i in range(ct...  14.5 us
  transfers between devices with their start and end apart: 6, of which 4 were waited for; matrix products, arithmetic and copies ran while one was open for 1% of the time, Pallas kernels for 0%

profile of v1, /device:TPU:0, one launch (start us, length us, event | category | flops | bytes accessed | tf_op | source)
XLA Modules:
  0.0 715.9 jit_solution(7682381504439019602)
XLA Ops:
  12.0 6.3 all-to-all-start.1
  18.4 44.1 %all_gather.15 = f32[2,1024,16]{1,2,0:T(8,128)S(1)} all-gather(f32[2,128,16]{1,2,0:T(8,128)S(1)} %copy-done.28), channel_id=1, replica_groups=mesh['ctx'=8,'exp'=4] {'ctx'}, dimensions={1}, use_global_device_ids=true | all-gather | bytes 147456 | tf_op jit(solution)/shard_map/all_gather | solution.py:145
  97.2 1.9 copy.242
  99.1 1.9 copy.250
  106.6 1.9 copy.245
  114.3 1.9 copy.248
  117.1 1.9 copy.247
  120.0 1.9 copy.243
  126.0 2.4 fusion
  128.4 2.3 fusion.8
  137.9 47.6 %all-gather.5.cloned.1.call-done = bf16[8,1024,256]{2,1,0:T(8,128)(2,1)} async-done(((bf16[1,1024,256]{2,1,0:T(8,128)(2,1)}), bf16[8,1024,256]{2,1,0:T(8,128)(2,1)}) %all-gather.5.cloned.1.call-update) | async-done | bytes 4194320 | tf_op jit(solution)/shard_map/all_gather | solution.py:258
  185.5 9.0 %bitcast_convert_fusion = bf16[1024,896]{1,0:T(8,128)(2,1)} fusion(bf16[8,1024,256]{2,1,0:T(8,128)(2,1)} %all-gather.5.cloned.1.call-done, bf16[8,256,896]{2,1,0:T(8,128)(2,1)} %bitcast.231), kind=kOutput, calls=%fused_computation.5 | convolution fusion | flops 3759013888 | bytes 9699328 | tf_op jit(solution)/shard_map/csk,ckd->sd/dot_general | solution.py:259
  194.5 3.8 all-to-all-start.2
  199.1 21.8 %all-to-all-done.2 = bf16[4,256,896]{2,1,0:T(8,128)(2,1)S(1)} async-done(((bf16[4,256,896]{2,1,0:T(8,128)(2,1)}), bf16[4,256,896]{2,1,0:T(8,128)(2,1)S(1)}, u32[]{:S(2)}, u32[]{:S(2)}) %all-to-all-start.2) | async-done | bytes 1835040 | tf_op jit(solution)/shard_map/all_to_all | solution.py:273
  220.9 3.5 all-to-all-start
  225.5 12.8 %all-to-all-done = bf16[32,8,896]{2,0,1:T(8,128)(2,1)S(1)} async-done(((bf16[32,8,896]{2,0,1:T(8,128)(2,1)}), bf16[32,8,896]{2,0,1:T(8,128)(2,1)S(1)}, u32[]{:S(2)}, u32[]{:S(2)}) %all-to-all-start) | async-done | bytes 458784 | tf_op jit(solution)/shard_map/all_to_all | solution.py:249
  239.3 66.8 %all-gather.1 = f32[32,32,4]{1,2,0:T(4,128)S(1)} all-gather(f32[1,32,4]{1,2,0:T(4,128)S(1)} %bitcast.223), channel_id=1, replica_groups=mesh['ctx'=8,'exp'=4] {'ctx','exp'}, dimensions={0}, use_global_device_ids=true | all-gather | bytes 16896 | tf_op jit(solution)/shard_map/all_gather | solution.py:247
  306.4 64.1 %all-gather = f32[32,1,256]{2,1,0:T(1,128)S(1)} all-gather(f32[1,1,256]{2,1,0:T(1,128)S(1)} %reshape.330), channel_id=1, replica_groups=mesh['ctx'=8,'exp'=4] {'ctx','exp'}, dimensions={0}, use_global_device_ids=true | all-gather | bytes 33792 | tf_op jit(solution)/shard_map/all_gather | solution.py:288
  370.7 8.5 %fusion.15 = f32[1024,256]{1,0:T(8,128)S(1)} fusion(bf16[8,1024,896]{2,1,0:T(8,128)(2,1)} %bitcast.229, bf16[8,896,256]{2,1,0:T(8,128)(2,1)} %bitcast.232, f32[1024]{0:T(1024)S(1)} %add_rsqrt_fusion.2), kind=kOutput, calls=%fused_computation.20 | convolution fusion | flops 3758358528 | bytes 19402752 | tf_op jit(solution)/shard_map/ctk,ckf->tf/dot_general | solution.py:292
  379.1 1.9 copy-done.35
  382.1 4.0 fusion.18
  386.1 9.3 %multiply_convert_fusion = bf16[1024,7168]{1,0:T(8,128)(2,1)} fusion(f32[1024]{0:T(1024)S(1)} %bitcast.228, bf16[1024,256]{1,0:T(8,128)(2,1)S(1)} %bitcast.218, bf16[1,256,7168]{2,1,0:T(8,128)(2,1)} %param.25), kind=kOutput, calls=%fused_computation | convolution fusion | flops 3772776448 | bytes 18878464 | tf_op jit(solution)/shard_map/dot_general | solution.py:308
  395.5 2.0 fusion.36
  397.5 311.9 %reduce-scatter.2.cloned.1.call-done = bf16[32,7168]{1,0:T(8,128)(2,1)} async-done(((bf16[1024,7168]{1,0:T(8,128)(2,1)}), bf16[32,7168]{1,0:T(8,128)(2,1)}) %reduce-scatter.2.cloned.1.call-update) | async-done | bytes 458768 | tf_op jit(solution)/shard_map/reduce_scatter | solution.py:315
  (187 shorter events, 68.6 us)
Async XLA Ops:
  10.7 7.7 %copy-start.28 = (f32[2,128,16]{1,2,0:T(8,128)S(1)}, f32[2,128,16]{1,2,0:T(8,128)}, u32[]{:S(2)}) copy-start(f32[2,128,16]{1,2,0:T(8,128)} %param.16) | copy-start | bytes 49156
  12.0 54.7 %all-to-all-start.1 = ((bf16[8,3,128,256]{2,3,1,0:T(8,128)(2,1)}), bf16[8,3,128,256]{2,3,1,0:T(8,128)(2,1)S(1)}, u32[]{:S(2)}, u32[]{:S(2)}) async-start(bf16[8,3,128,256]{2,3,1,0:T(8,128)(2,1)} %copy.215), calls=%async_computation.1 | async-start | bytes 3145728 | tf_op jit(solution)/shard_map/all_to_all | solution.py:143
  18.3 167.2 %all-gather.5.cloned.1.call-start = ((), (), s32[]{:S(2)}) async-start(), calls=%async_computation.4 | async-start | bytes 4718592 | tf_op jit(solution)/shard_map/all_gather | solution.py:258
  71.9 4.3 copy-start.3
  76.7 6.6 copy-start.10
  76.7 7.4 %copy-start = (bf16[1,8,128,256]{3,2,1,0:T(8,128)(2,1)S(1)}, bf16[1,8,128,256]{3,2,1,0:T(8,128)(2,1)}, u32[]{:S(2)}) copy-start(bf16[1,8,128,256]{3,2,1,0:T(8,128)(2,1)} %get-tuple-element.6) | copy-start | bytes 1572868
  86.5 3.3 copy-start.2
  90.5 3.4 copy-start.8
  97.2 11.3 %copy-start.7 = (bf16[640,256]{1,0:T(8,128)(2,1)S(1)}, bf16[640,256]{1,0:T(8,128)(2,1)}, u32[]{:S(2)}) copy-start(bf16[640,256]{1,0:T(8,128)(2,1)} %get-tuple-element.15) | copy-start | bytes 983044
  112.1 10.8 %copy-start.19 = (bf16[1,640,2,128]{3,1,2,0:T(8,128)(2,1)S(1)}, bf16[1,640,2,128]{3,1,2,0:T(8,128)(2,1)}, u32[]{:S(2)}) copy-start(bf16[1,640,2,128]{3,1,2,0:T(8,128)(2,1)} %copy.223) | copy-start | bytes 983044
  114.3 8.7 %copy-start.20 = (bf16[1,640,2,128]{3,1,2,0:T(8,128)(2,1)S(1)}, bf16[1,640,2,128]{3,1,2,0:T(8,128)(2,1)}, u32[]{:S(2)}) copy-start(bf16[1,640,2,128]{3,1,2,0:T(8,128)(2,1)} %copy.244) | copy-start | bytes 983044
  117.1 7.0 copy-start.21
  120.0 4.3 copy-start.22
  130.7 3.3 copy-start.5
  130.7 3.6 copy-start.26
  194.5 3.8 copy-start.27
  194.5 26.4 %all-to-all-start.2 = ((bf16[4,256,896]{2,1,0:T(8,128)(2,1)}), bf16[4,256,896]{2,1,0:T(8,128)(2,1)S(1)}, u32[]{:S(2)}, u32[]{:S(2)}) async-start(bf16[4,256,896]{2,1,0:T(8,128)(2,1)} %bitcast.200), calls=%async_computation.2 | async-start | bytes 3670016 | tf_op jit(solution)/shard_map/all_to_all | solution.py:273
  220.9 17.4 %all-to-all-start = ((bf16[32,8,896]{2,0,1:T(8,128)(2,1)}), bf16[32,8,896]{2,0,1:T(8,128)(2,1)S(1)}, u32[]{:S(2)}, u32[]{:S(2)}) async-start(bf16[32,8,896]{2,0,1:T(8,128)(2,1)} %bitcast.183), calls=%async_computation | async-start | bytes 917504 | tf_op jit(solution)/shard_map/all_to_all | solution.py:249
  224.4 14.8 %copy-start.33 = (f32[32,2]{0,1:T(2,128)S(1)}, f32[32,2]{0,1:T(2,128)}, u32[]{:S(2)}) copy-start(f32[32,2]{0,1:T(2,128)} %param.22) | copy-start | bytes 772
  224.4 14.8 %copy-start.34 = (s32[32,2]{0,1:T(2,128)S(1)}, s32[32,2]{0,1:T(2,128)}, u32[]{:S(2)}) copy-start(s32[32,2]{0,1:T(2,128)} %param.21) | copy-start | bytes 772
  224.5 146.2 %all-gather.7.cloned.1.call-start = ((), (), s32[]{:S(2)}) async-start(), calls=%async_computation.5 | async-start | bytes 15138816 | tf_op jit(solution)/shard_map/all_gather | solution.py:286
  239.2 470.2 %reduce-scatter.2.cloned.1.call-start = ((), (), s32[]{:S(2)}) async-start(), calls=%async_computation.6 | async-start | bytes 15138816 | tf_op jit(solution)/shard_map/reduce_scatter | solution.py:315
  370.7 10.4 %copy-start.35 = (bf16[8192,896]{1,0:T(8,128)(2,1)S(1)}, bf16[8192,896]{1,0:T(8,128)(2,1)}, u32[]{:S(2)}) copy-start(bf16[8192,896]{1,0:T(8,128)(2,1)} %all-gather.7.cloned.1.call-done) | copy-start | bytes 44040196
  370.7 11.4 %copy-start.36 = (bf16[1,7168,256]{2,1,0:T(8,128)(2,1)S(1)}, bf16[1,7168,256]{2,1,0:T(8,128)(2,1)}, u32[]{:S(2)}) copy-start(bf16[1,7168,256]{2,1,0:T(8,128)(2,1)} %param.24) | copy-start | bytes 11010052
  (19 other events, 32.3 us)
Sparse Core Ops, SparseCore 0:
  138.0 47.4 all-gather.4
  239.3 104.2 all-gather.6
  397.6 311.7 reduce-scatter.1

commit v2 on v1

--- a/solution.py
+++ b/solution.py
@@ -1,8 +1,11 @@
+import functools
 import math
 
 import jax
 import jax.numpy as jnp
 from jax import lax
+from jax.experimental import pallas as pl
+from jax.experimental.pallas import tpu as pltpu
 from jax.sharding import PartitionSpec as P
 
 WINDOW = 512
@@ -124,96 +127,7 @@
     return attended
 
 
-def head_attention(query_input, key_input, value_input, gate_logits, comp_weight):
-    row_count = query_input.shape[0]
-    head_count = comp_weight.shape[2]
-    head_width = query_input.shape[1] // head_count
-    block_len = comp_weight.shape[1]
-    stride_len = block_len // 2
-    ctx_count = lax.axis_size("ctx")
-    ctx_index = lax.axis_index("ctx")
-    own = head_count // ctx_count
-    width = own * head_width
-    seq_len = ctx_count * row_count
-    scale = score_gain / math.sqrt(head_width)
-    packed = jnp.stack([query_input, key_input, value_input], 0).reshape(
-        3, row_count, ctx_count, width
-    )
-    packed = jnp.transpose(packed, (2, 0, 1, 3))
-    moved = lax.all_to_all(packed, "ctx", split_axis=0, concat_axis=0, tiled=True)
-    moved = jnp.transpose(moved, (1, 0, 2, 3)).reshape(3, seq_len, width)
-    logits = lax.all_gather(gate_logits, "ctx", axis=1, tiled=True)
-    logits = lax.dynamic_slice_in_dim(logits, ctx_index * own, own, 2)
-    weights_own = lax.dynamic_slice_in_dim(comp_weight, ctx_index * own, own, 2)
-    queries = head_norm(moved[0], head_width).astype(jnp.bfloat16)
-    keys = head_norm(moved[1], head_width).astype(jnp.bfloat16)
-    values = moved[2]
-    tail_rows = jnp.zeros((stride_len, width), jnp.bfloat16)
-    comp_keys = head_norm(
-        compress(jnp.concatenate([moved[1], tail_rows], 0), weights_own[0], head_width), head_width
-    ).astype(jnp.bfloat16)
-    comp_values = compress(
-        jnp.concatenate([values, tail_rows], 0), weights_own[1], head_width
-    ).astype(jnp.bfloat16)
-    query_heads = queries.reshape(seq_len, own, head_width)
-    part_count = comp_keys.shape[0]
-    query_pos = jnp.arange(seq_len, dtype=jnp.int32)
-    scores = jnp.einsum(
-        "thd,nhd->htn",
-        query_heads,
-        comp_keys.reshape(part_count, own, head_width),
-        preferred_element_type=jnp.float32,
-    )
-    block_end = jnp.arange(part_count, dtype=jnp.int32) * stride_len + block_len - 1
-    visible = block_end[None, :] <= query_pos[:, None]
-    weights = jnp.where(visible[None], jnp.exp(scale * scores), 0.0)
-    total = jnp.sum(weights, axis=2).T
-    cmp_sum = jnp.einsum(
-        "htn,nhd->thd",
-        weights.astype(jnp.bfloat16),
-        comp_values.reshape(part_count, own, head_width),
-        preferred_element_type=jnp.float32,
-    )
-    no_block = (query_pos < block_len - 1).astype(jnp.float32)
-    cmp_out = cmp_sum / (total + no_block[:, None])[:, :, None]
-    reach = WINDOW + row_count
-    pad = jnp.zeros((WINDOW, width), jnp.bfloat16)
-    key_pad = jnp.concatenate([pad, keys], 0)
-    value_pad = jnp.concatenate([pad, values], 0)
-    near_keys = jnp.stack(
-        [key_pad[i * row_count : i * row_count + reach] for i in range(ctx_count)]
-    ).reshape(ctx_count, reach, own, head_width)
-    near_values = jnp.stack(
-        [value_pad[i * row_count : i * row_count + reach] for i in range(ctx_count)]
-    ).reshape(ctx_count, reach, own, head_width)
-    near_scores = jnp.einsum(
-        "bthd,bshd->bhts",
-        query_heads.reshape(ctx_count, row_count, own, head_width),
-        near_keys,
-        preferred_element_type=jnp.float32,
-    )
-    rows = jnp.arange(row_count, dtype=jnp.int32)[None, :, None]
-    cols = jnp.arange(reach, dtype=jnp.int32)[None, None, :] - WINDOW
-    first = (jnp.arange(ctx_count, dtype=jnp.int32) * row_count)[:, None, None]
-    inside = (cols <= rows) & (cols > rows - WINDOW) & (cols + first >= 0)
-    near_weights = jnp.where(inside[:, None], jnp.exp(scale * near_scores), 0.0)
-    win_total = jnp.transpose(jnp.sum(near_weights, axis=3), (0, 2, 1)).reshape(seq_len, own)
-    win_sum = jnp.einsum(
-        "bhts,bshd->bthd",
-        near_weights.astype(jnp.bfloat16),
-        near_values,
-        preferred_element_type=jnp.float32,
-    ).reshape(seq_len, own, head_width)
-    win_out = win_sum / win_total[:, :, None]
-    gates = jax.nn.sigmoid(logits)
-    return (
-        (gates[0][:, :, None] * cmp_out + gates[1][:, :, None] * win_out)
-        .reshape(seq_len, width)
-        .astype(jnp.bfloat16)
-    )
-
-
-def local(
+def general(
     query_input,
     key_input,
     value_input,
@@ -249,27 +163,13 @@
     residual = lax.all_to_all(residual_in, "ctx", split_axis=1, concat_axis=0, tiled=True)
 
     attention_args = (query_input, key_input, value_input, gate_logits, comp_weight)
-    if comp_weight.shape[2] % ctx_count == 0:
-        attended = head_attention(*attention_args)
-        width = attended.shape[1]
-        attended = jnp.transpose(
-            attended.reshape(ctx_count, exp_count, share, width), (1, 0, 2, 3)
-        ).reshape(seq_len, width)
-        spread_heads = lax.all_gather(attended, "ctx", axis=0)
-        partial = jnp.einsum(
-            "csk,ckd->sd",
-            spread_heads,
-            out_proj.reshape(ctx_count, width, cols),
-            preferred_element_type=jnp.float32,
-        )
-    else:
-        attended = window_attention(*attention_args)
-        spread_rows = lax.all_gather(
-            attended.reshape(1, exp_count, share, -1), "ctx", axis=0, tiled=True
-        )
-        partial = jnp.einsum(
-            "cerh,hd->ecrd", spread_rows, out_proj, preferred_element_type=jnp.float32
-        )
+    attended = window_attention(*attention_args)
+    spread_rows = lax.all_gather(
+        attended.reshape(1, exp_count, share, -1), "ctx", axis=0, tiled=True
+    )
+    partial = jnp.einsum(
+        "cerh,hd->ecrd", spread_rows, out_proj, preferred_element_type=jnp.float32
+    )
     pieces = lax.all_to_all(
         partial.astype(jnp.bfloat16).reshape(exp_count, own_tokens, cols),
         "exp",
@@ -315,6 +215,313 @@
     return lax.psum_scatter(
         outs.reshape(seq_len, model_width), ("ctx", "exp"), scatter_dimension=0, tiled=True
     )
+
+
+def high_low(values):
+    high = lax.reduce_precision(values, 8, 7)
+    return jnp.stack([high, values - high], 0).astype(jnp.bfloat16)
+
+
+def unit_rows(block):
+    return block * lax.rsqrt(jnp.mean(block * block, axis=1, keepdims=True) + norm_eps)
+
+
+def attend_kernel(row_count, share, block_len, head_width, moved, taps, gates, out, keys, values):
+    ctx_count = moved.shape[0]
+    own = moved.shape[2] // head_width
+    seq_len = row_count * ctx_count
+    stride_len = block_len // 2
+    part_count = seq_len // stride_len
+    scale = score_gain / math.sqrt(head_width)
+
+    def dot(left, right):
+        return jnp.dot(left, right, preferred_element_type=jnp.float32)
+
+    def dot_rows(left, right):
+        return lax.dot_general(
+            left, right, (((1,), (1,)), ((), ())), preferred_element_type=jnp.float32
+        )
+
+    def compressed(row, block):
+        group = lax.broadcasted_iota(jnp.int32, (part_count, seq_len), 0)
+        token_group = lax.broadcasted_iota(jnp.int32, (part_count, seq_len), 1) // stride_len
+        band = jnp.where(token_group == group, taps[row : row + 1, :], 0.0)
+        band = jnp.where(token_group == group + 1, taps[row + 1 : row + 2, :], band)
+        high = band.astype(jnp.bfloat16)
+        low = (band - high.astype(jnp.float32)).astype(jnp.bfloat16)
+        return dot(high, block) + dot(low, block)
+
+    for head in range(own):
+        lanes = slice(head * head_width, (head + 1) * head_width)
+        raw_keys = moved[:, row_count : 2 * row_count, lanes].reshape(seq_len, head_width)
+        keys[...] = unit_rows(raw_keys.astype(jnp.float32)).astype(jnp.bfloat16)
+        raw_values = moved[:, 2 * row_count : 3 * row_count, lanes].reshape(seq_len, head_width)
+        values[...] = raw_values
+        comp_keys = unit_rows(compressed(2 * head, raw_keys)).astype(jnp.bfloat16)
+        comp_values = compressed(2 * (own + head), raw_values).astype(jnp.bfloat16)
+        for block in range(ctx_count):
+            query = moved[block, 0:row_count, lanes].astype(jnp.float32)
+            query = unit_rows(query).astype(jnp.bfloat16)
+            base = block * row_count
+            rows = slice(base, base + row_count)
+            spot = base + lax.broadcasted_iota(jnp.int32, (row_count, part_count), 0)
+            ends = lax.broadcasted_iota(jnp.int32, (row_count, part_count), 1) * stride_len
+            seen = ends + (block_len - 1) <= spot
+            weight = jnp.where(seen, jnp.exp(scale * dot_rows(query, comp_keys)), 0.0)
+            total = jnp.sum(weight, axis=1, keepdims=True)
+            total = total + jnp.where(spot[:, :1] < block_len - 1, 1.0, 0.0)
+            far = dot(weight.astype(jnp.bfloat16), comp_values) / total
+            start = max(0, base - WINDOW)
+            reach = base + row_count - start
+            spot = base + lax.broadcasted_iota(jnp.int32, (row_count, reach), 0)
+            key_spot = start + lax.broadcasted_iota(jnp.int32, (row_count, reach), 1)
+            seen = (key_spot <= spot) & (key_spot > spot - WINDOW)
+            score = dot_rows(query, keys[start : start + reach, :])
+            weight = jnp.where(seen, jnp.exp(scale * score), 0.0)
+            total = jnp.sum(weight, axis=1, keepdims=True)
+            near = dot(weight.astype(jnp.bfloat16), values[start : start + reach, :]) / total
+            mixed = (
+                gates[rows, head : head + 1] * far
+                + gates[rows, own + head : own + head + 1] * near
+            ).astype(jnp.bfloat16)
+            for part in range(row_count // share):
+                target = (part * ctx_count + block) * share
+                out[target : target + share, lanes] = mixed[part * share : (part + 1) * share]
+
+
+def attend(moved, taps, gates, row_count, share, block_len, head_width):
+    seq_len = moved.shape[0] * row_count
+    width = moved.shape[2]
+    return pl.pallas_call(
+        functools.partial(attend_kernel, row_count, share, block_len, head_width),
+        out_shape=jax.ShapeDtypeStruct((seq_len, width), jnp.bfloat16),
+        scratch_shapes=[
+            pltpu.VMEM((seq_len, head_width), jnp.bfloat16),
+            pltpu.VMEM((seq_len, head_width), jnp.bfloat16),
+        ],
+        compiler_params=pltpu.CompilerParams(vmem_limit_bytes=48 * 2**20),
+        name="attend",
+    )(moved, taps, gates)
+
+
+def expert_kernel(ctx_count, exp_count, share, rows, gain, gate_w, up_w, route, out, gate_acc, up_acc, squares):
+    step = pl.program_id(0)
+
+    @pl.when(step == 0)
+    def _():
+        gate_acc[...] = jnp.zeros_like(gate_acc)
+        up_acc[...] = jnp.zeros_like(up_acc)
+        squares[...] = jnp.zeros_like(squares)
+
+    block = rows[0]
+    gate_acc[...] += jnp.dot(block, gate_w[...], preferred_element_type=jnp.float32)
+    up_acc[...] += jnp.dot(block, up_w[...], preferred_element_type=jnp.float32)
+    lane = squares.shape[1]
+    total = squares[...]
+    for part in range(block.shape[1] // lane):
+        lanes = slice(part * lane, (part + 1) * lane)
+        plain = block[:, lanes].astype(jnp.float32) * (1.0 / gain[0, :, lanes])
+        total = total + plain * plain
+    squares[...] = total
+
+    @pl.when(step == pl.num_programs(0) - 1)
+    def _():
+        model_width = ctx_count * rows.shape[2]
+        mean_square = jnp.sum(squares[...], axis=1, keepdims=True) / model_width
+        inverse = lax.rsqrt(mean_square + norm_eps)
+        gate_part = gate_acc[...] * inverse
+        up_part = up_acc[...] * inverse
+        active = gate_part / (1.0 + jnp.exp(-gate_part)) * up_part * route[...]
+        active = active.astype(jnp.bfloat16)
+        half = share // 2
+        for exp_spot in range(exp_count):
+            for ctx_spot in range(ctx_count):
+                base = (exp_spot * ctx_count + ctx_spot) * share
+                target = (ctx_spot * exp_count + exp_spot) * half
+                out[0, target : target + half, :] = active[base : base + half]
+                target = (exp_spot * ctx_count + ctx_spot) * half
+                out[1, target : target + half, :] = active[base + half : base + share]
+
+
+def run_expert(rows, gain, gate_w, up_w, route, exp_count, share):
+    ctx_count, seq_len, cols = rows.shape
+    units = gate_w.shape[1]
+    lane = math.gcd(128, cols)
+    return pl.pallas_call(
+        functools.partial(expert_kernel, ctx_count, exp_count, share),
+        grid=(ctx_count,),
+        in_specs=[
+            pl.BlockSpec((1, seq_len, cols), lambda i: (i, 0, 0)),
+            pl.BlockSpec((1, 1, cols), lambda i: (i, 0, 0)),
+            pl.BlockSpec((cols, units), lambda i: (i, 0)),
+            pl.BlockSpec((cols, units), lambda i: (i, 0)),
+            pl.BlockSpec((seq_len, 1), lambda i: (0, 0)),
+        ],
+        out_specs=pl.BlockSpec((2, seq_len // 2, units), lambda i: (0, 0, 0)),
+        out_shape=jax.ShapeDtypeStruct((2, seq_len // 2, units), jnp.bfloat16),
+        scratch_shapes=[
+            pltpu.VMEM((seq_len, units), jnp.float32),
+            pltpu.VMEM((seq_len, units), jnp.float32),
+            pltpu.VMEM((seq_len, lane), jnp.float32),
+        ],
+        compiler_params=pltpu.CompilerParams(vmem_limit_bytes=48 * 2**20),
+        cost_estimate=pl.CostEstimate(
+            flops=4 * seq_len * units * ctx_count * cols,
+            bytes_accessed=2 * ctx_count * cols * (seq_len + 2 * units),
+            transcendentals=seq_len * units,
+        ),
+        name="expert",
+    )(rows, gain.reshape(ctx_count, 1, cols), gate_w, up_w, route)
+
+
+def by_heads(
+    query_input,
+    key_input,
+    value_input,
+    gate_logits,
+    comp_weight,
+    out_proj,
+    residual_in,
+    ffn_gain,
+    expert_ids,
+    route_gates,
+    expert_gate,
+    expert_up,
+    expert_down,
+):
+    row_count = query_input.shape[0]
+    head_count = comp_weight.shape[2]
+    head_width = query_input.shape[1] // head_count
+    block_len = comp_weight.shape[1]
+    stride_len = block_len // 2
+    ctx_count = lax.axis_size("ctx")
+    exp_count = lax.axis_size("exp")
+    ctx_index = lax.axis_index("ctx")
+    exp_index = lax.axis_index("exp")
+    own = head_count // ctx_count
+    width = own * head_width
+    share = row_count // exp_count
+    half = share // 2
+    seq_len = row_count * ctx_count
+    cols = out_proj.shape[1]
+    model_width = cols * ctx_count
+    own_tokens = ctx_count * share
+
+    experts = jnp.arange(exp_count, dtype=jnp.int32)
+    table = jnp.sum(
+        jnp.where(expert_ids[:, :, None] == experts, route_gates[:, :, None], 0.0), axis=1
+    )
+    table = jnp.broadcast_to(high_low(table).reshape(1, -1), (ctx_count, 2 * share * exp_count))
+    gates = high_low(jax.nn.sigmoid(gate_logits)).reshape(2, 2, row_count, ctx_count, own)
+    gates = jnp.transpose(gates, (3, 0, 1, 2, 4)).reshape(ctx_count, -1)
+    side = jnp.concatenate([gates, table], 1)
+    side_rows = -(-side.shape[1] // width)
+    residual_rows = -(-share * cols // width)
+    side_rows += -(3 * row_count + residual_rows + side_rows) % 16
+    side = jnp.pad(side, ((0, 0), (0, side_rows * width - side.shape[1])))
+    residual = jnp.transpose(residual_in.reshape(share, ctx_count, cols), (1, 0, 2))
+    residual = residual.reshape(ctx_count, share * cols)
+    residual = jnp.pad(residual, ((0, 0), (0, residual_rows * width - share * cols)))
+    heads = [
+        jnp.transpose(block.reshape(row_count, ctx_count, width), (1, 0, 2))
+        for block in (query_input, key_input, value_input)
+    ]
+    packed = jnp.concatenate(
+        heads
+        + [
+            residual.reshape(ctx_count, residual_rows, width),
+            side.reshape(ctx_count, side_rows, width),
+        ],
+        1,
+    )
+    moved = lax.all_to_all(packed, "ctx", split_axis=0, concat_axis=0, tiled=True)
+    residual = moved[:, 3 * row_count : 3 * row_count + residual_rows].reshape(ctx_count, -1)
+    residual = residual[:, : share * cols].reshape(own_tokens, cols)
+    side = moved[:, 3 * row_count + residual_rows :].reshape(ctx_count, -1).astype(jnp.float32)
+    gate_size = 4 * row_count * own
+    gates = side[:, :gate_size].reshape(ctx_count, 2, 2, row_count, own)
+    gates = jnp.transpose(gates[:, 0] + gates[:, 1], (0, 2, 1, 3)).reshape(seq_len, 2 * own)
+    table = side[:, gate_size : gate_size + 2 * share * exp_count]
+    table = table.reshape(ctx_count, 2, share, exp_count)
+
+    taps = lax.dynamic_slice_in_dim(comp_weight, ctx_index * own, own, 2)
+    taps = jnp.transpose(taps.reshape(2, 2, stride_len, own), (0, 3, 1, 2))
+    taps = jnp.tile(taps.reshape(4 * own, stride_len), (1, seq_len // stride_len))
+    attended = attend(moved, taps, gates, row_count, share, block_len, head_width)
+
+    spread_heads = lax.all_gather(attended, "ctx", axis=0)
+    partial = jnp.einsum(
+        "csk,ckd->sd",
+        spread_heads,
+        out_proj.reshape(ctx_count, width, cols),
+        preferred_element_type=jnp.float32,
+    ).astype(jnp.bfloat16)
+    table = jnp.transpose(table, (3, 1, 0, 2)).reshape(exp_count, -1).astype(jnp.bfloat16)
+    table_rows = -(-table.shape[1] // cols)
+    table_rows += -table_rows % 16
+    table = jnp.pad(table, ((0, 0), (0, table_rows * cols - table.shape[1])))
+    pieces = jnp.concatenate(
+        [
+            partial.reshape(exp_count, own_tokens, cols),
+            table.reshape(exp_count, table_rows, cols),
+        ],
+        1,
+    )
+    pieces = lax.all_to_all(pieces, "exp", split_axis=0, concat_axis=0, tiled=True)
+    route = pieces[:, own_tokens:].reshape(exp_count, -1)[:, : 2 * own_tokens]
+    route = jnp.sum(route.reshape(exp_count, 2, own_tokens).astype(jnp.float32), axis=1)
+    hidden_state = residual.astype(jnp.float32) + jnp.sum(
+        pieces[:, :own_tokens].astype(jnp.float32), axis=0
+    )
+    gain = lax.dynamic_slice_in_dim(ffn_gain, ctx_index * cols, cols, 0)
+    scaled = (hidden_state * gain).astype(jnp.bfloat16)
+    rows = lax.all_gather(scaled, ("ctx", "exp"), axis=0, tiled=True)
+    active = run_expert(
+        rows.reshape(ctx_count, seq_len, cols),
+        ffn_gain,
+        expert_gate[0],
+        expert_up[0],
+        route.reshape(seq_len, 1),
+        exp_count,
+        share,
+    )
+    hidden_state = hidden_state.reshape(ctx_count, share, cols)
+
+    outs = jnp.dot(active[0], expert_down[0], preferred_element_type=jnp.float32)
+    outs = outs.astype(jnp.bfloat16).reshape(ctx_count, exp_count, half, model_width)
+    place = (0, exp_index, 0, ctx_index * cols)
+    mine = lax.dynamic_slice(outs, place, (ctx_count, 1, half, cols)).astype(jnp.float32)
+    mine = mine + hidden_state[:, None, :half]
+    outs = lax.dynamic_update_slice(outs, mine.astype(jnp.bfloat16), place)
+    first = lax.psum_scatter(
+        outs.reshape(ctx_count, exp_count * half, model_width),
+        "ctx",
+        scatter_dimension=0,
+        tiled=True,
+    )
+    first = lax.all_to_all(
+        first.reshape(exp_count, half, model_width), "exp", split_axis=0, concat_axis=0, tiled=True
+    )
+    first = jnp.sum(first.astype(jnp.float32), axis=0).astype(jnp.bfloat16)
+
+    outs = jnp.dot(active[1], expert_down[0], preferred_element_type=jnp.float32)
+    outs = outs.astype(jnp.bfloat16).reshape(exp_count, ctx_count, half, model_width)
+    place = (exp_index, 0, 0, ctx_index * cols)
+    mine = lax.dynamic_slice(outs, place, (1, ctx_count, half, cols)).astype(jnp.float32)
+    mine = mine + hidden_state[None, :, half:]
+    outs = lax.dynamic_update_slice(outs, mine.astype(jnp.bfloat16), place)
+    outs = lax.all_to_all(outs, "exp", split_axis=0, concat_axis=0, tiled=True)
+    outs = jnp.sum(outs.astype(jnp.float32), axis=0).astype(jnp.bfloat16)
+    second = lax.psum_scatter(outs, "ctx", scatter_dimension=0, tiled=True)
+    return jnp.concatenate([first, second.reshape(half, model_width)], 0)
+
+
+def local(*args):
+    head_count = args[4].shape[2]
+    share = args[0].shape[0] // lax.axis_size("exp")
+    if head_count % lax.axis_size("ctx") == 0 and share % 32 == 0:
+        return by_heads(*args)
+    return general(*args)
 
 
 def solution(mesh):

time: 717 us -> 431 us (0.60)
  waiting for transfers between devices: 394 us -> 234 us
  blocking collectives: 175 us -> 102 us
  local copies, waits for them, and re-layouts: 69.7 us -> 17 us
  matrix products: 39.6 us -> 17 us
  Pallas kernels: 0 us -> 19.8 us
    reduce_scatter x1 -> x2, waiting for transfers between devices: 312 us -> 16.9 us  [the longest x1 16.9 us: by_heads(): second = lax.psum_scatter(outs, 'ctx', scatter_dimension=0, tiled=True)]
    all_gather x3 -> x0, blocking collectives: 175 us -> none  [the longest x1 66.8 us: local(): route_all = lax.all_gather(route_table, ('ctx', 'exp'), axis=0, tiled=True)]
    all_to_all x0 -> x2, blocking collectives: none -> 102 us  [the longest x1 85.9 us: by_heads(): outs = lax.all_to_all(outs, 'exp', split_axis=0, concat_axis=0, tiled=True)]
    all_gather x2, waiting for transfers between devices: 47.6 us -> 144 us  [the longest x1 99.4 us: by_heads(): rows = lax.all_gather(scaled, ('ctx', 'exp'), axis=0, tiled=True)]
    all_to_all x3 -> x2, waiting for transfers between devices: 34.6 us -> 72.2 us  [the longest x1 48.7 us: by_heads(): lax.all_to_all(packed, 'ctx', split_axis=0, concat_axis=0, tiled=True)]
    another operation x18 -> x5, local copies, waits for them, and re-layouts: 24.3 us -> 0.3 us  [the longest x2 0.18 us: by_heads(): jnp.tile(taps.reshape(4 * own, stride_len), (1, seq_len // stride_len))]
    dot_general x12 -> x3, matrix products: 39.6 us -> 17 us  [the longest x1 7.79 us: by_heads(): jnp.einsum('csk,ckd->sd', spread_heads, out_proj.reshape(ctx_count, width...]
    pallas_call x0 -> x2, Pallas kernels: none -> 19.8 us  [the longest x1 13.7 us: run_expert(): pl.pallas_call(functools.partial(expert_kernel, ctx_count, exp_count, sha...]
  transfers between devices with their start and end apart: 6 -> 6, of which waited for: 4 -> 5; matrix products, arithmetic and copies ran while one was open for 1% -> 4% of each run, Pallas kernels for 0% -> 0%
where the time goes in v2:
time: 431 us; the launch traced here: 430 us
  waiting for transfers between devices  234 us (54%)
  blocking collectives  102 us (24%)
  Pallas kernels  19.8 us (5%)
  local copies, waits for them, and re-layouts  17 us (4%)
  matrix products  17 us (4%)
  other arithmetic  16.4 us (4%)
  between operations  13.5 us (3%)
  starting transfers between devices  11.1 us (3%)
    all_gather x1, waiting for transfers between devices, by_heads(): rows = lax.all_gather(scaled, ('ctx', 'exp'), axis=0, tiled=True)  99.4 us
    all_to_all x1, blocking collectives, by_heads(): outs = lax.all_to_all(outs, 'exp', split_axis=0, concat_axis=0, tiled=True)  85.9 us
    all_to_all x1, waiting for transfers between devices, by_heads(): lax.all_to_all(packed, 'ctx', split_axis=0, concat_axis=0, tiled=True)  48.7 us
    all_gather x1, waiting for transfers between devices, by_heads(): spread_heads = lax.all_gather(attended, 'ctx', axis=0)  45.1 us
    all_to_all x1, waiting for transfers between devices, by_heads(): lax.all_to_all(pieces, 'exp', split_axis=0, concat_axis=0, tiled=True)  23.5 us
    reduce_scatter x1, waiting for transfers between devices, by_heads(): second = lax.psum_scatter(outs, 'ctx', scatter_dimension=0, tiled=True)  16.9 us
    all_to_all x1, blocking collectives, by_heads(): lax.all_to_all(first.reshape(exp_count, half, model_width), 'exp', split_...  15.7 us
    pallas_call x1, Pallas kernels, run_expert(): pl.pallas_call(functools.partial(expert_kernel, ctx_count, exp_count, sha...  13.7 us
  transfers between devices with their start and end apart: 6, of which 5 were waited for; matrix products, arithmetic and copies ran while one was open for 4% of the time, Pallas kernels for 0%

profile of v2, /device:TPU:0, one launch (start us, length us, event | category | flops | bytes accessed | tf_op | source)
XLA Modules:
  0.0 430.1 jit_solution(4684666644790474725)
XLA Ops:
  8.6 1.1 copy.116
  10.2 1.3 copy.83
  16.8 6.3 %all-to-all-start = ((bf16[8,512,256]{2,1,0:T(8,128)(2,1)}), bf16[8,512,256]{2,1,0:T(8,128)(2,1)S(1)}, u32[]{:S(2)}, u32[]{:S(2)}) async-start(bf16[8,512,256]{2,1,0:T(8,128)(2,1)} %bitcast_dynamic-update-slice_fusion.3), calls=%async_computation | async-start | bytes 4194304 | tf_op jit(solution)/shard_map/all_to_all | solution.py:437
  23.4 48.7 %all-to-all-done.moved = bf16[8,512,256]{2,1,0:T(8,128)(2,1)S(1)} async-done(((bf16[8,512,256]{2,1,0:T(8,128)(2,1)}), bf16[8,512,256]{2,1,0:T(8,128)(2,1)S(1)}, u32[]{:S(2)}, u32[]{:S(2)}) %all-to-all-start) | async-done | bytes 2097184 | tf_op jit(solution)/shard_map/all_to_all | solution.py:437
  73.9 6.1 %attend.1 = bf16[1024,256]{1,0:T(8,128)(2,1)} custom-call(bf16[8,512,256]{2,1,0:T(8,128)(2,1)S(1)} %all-to-all-done.moved, f32[8,1024]{1,0:T(8,128)S(1)} %tile.12.taps, f32[1024,4]{1,0:T(8,128)S(1)} %copy.97.gates), custom_call_target="tpu_custom_call" | custom-call | tf_op jit(solution)/shard_map/attend/pallas_call | solution.py:295
  81.1 45.1 %all-gather.6.cloned.1.call-done = bf16[8192,256]{1,0:T(8,128)(2,1)} async-done(((bf16[1024,256]{1,0:T(8,128)(2,1)}), bf16[8192,256]{1,0:T(8,128)(2,1)}) %all-gather.6.cloned.1.call-update) | async-done | bytes 4194320 | tf_op jit(solution)/shard_map/all_gather | solution.py:452
  126.2 7.8 %bitcast_convert_fusion = bf16[1024,896]{1,0:T(8,128)(2,1)S(1)} fusion(bf16[8,1024,256]{2,1,0:T(8,128)(2,1)} %bitcast.144, bf16[8,256,896]{2,1,0:T(8,128)(2,1)} %bitcast.145), kind=kOutput, calls=%fused_computation.4 | convolution fusion | flops 3759013888 | bytes 9699328 | tf_op jit(solution)/shard_map/csk,ckd->sd/dot_general | solution.py:453
  134.0 1.4 pad_maximum_fusion
  135.4 4.4 %all-to-all-start.1 = ((bf16[4,272,896]{2,1,0:T(8,128)(2,1)}), bf16[4,272,896]{2,1,0:T(8,128)(2,1)}, u32[]{:S(2)}, u32[]{:S(2)}) async-start(bf16[4,272,896]{2,1,0:T(8,128)(2,1)} %pad_maximum_fusion), calls=%async_computation.1 | async-start | bytes 3899392 | tf_op jit(solution)/shard_map/all_to_all | solution.py:470
  140.4 23.5 %all-to-all-done.1 = bf16[4,272,896]{2,1,0:T(8,128)(2,1)} async-done(((bf16[4,272,896]{2,1,0:T(8,128)(2,1)}), bf16[4,272,896]{2,1,0:T(8,128)(2,1)}, u32[]{:S(2)}, u32[]{:S(2)}) %all-to-all-start.1) | async-done | bytes 1949728 | tf_op jit(solution)/shard_map/all_to_all | solution.py:470
  163.9 1.8 convert_reduce_fusion
  166.9 1.2 reshape.151
  169.3 1.3 add.52
  170.6 99.4 %all-gather.4.cloned.1.call-done = bf16[8192,896]{1,0:T(8,128)(2,1)} async-done(((bf16[256,896]{1,0:T(8,128)(2,1)}), bf16[8192,896]{1,0:T(8,128)(2,1)}) %all-gather.4.cloned.1.call-update) | async-done | bytes 14680080 | tf_op jit(solution)/shard_map/all_gather | solution.py:478
  270.0 2.0 copy-done.3
  272.0 13.7 %expert.1 = bf16[2,512,256]{2,1,0:T(8,128)(2,1)S(1)} custom-call(bf16[8,1024,896]{2,1,0:T(8,128)(2,1)} %bitcast.143, f32[8,1,896]{2,1,0:T(1,128)S(1)} %bitcast.115, bf16[7168,256]{1,0:T(8,128)(2,1)S(1)} %bitcast.116, bf16[7168,256]{1,0:T(8,128)(2,1)} %bitcast.146, f32[1024,1]{1,0:T(8,128)S(1)} %bitcast.114), custom_call_target="tpu_custom_call" | custom-call | flops 7516192768 | bytes 22020096 | tf_op jit(solution)/shard_map/expert/pallas_call | solution.py:350
  285.8 5.1 %convolution_convert_fusion.1 = bf16[512,7168]{1,0:T(8,128)(2,1)} fusion(bf16[1,256,7168]{2,1,0:T(8,128)(2,1)S(1)} %copy-done.4, bf16[2,512,256]{2,1,0:T(8,128)(2,1)S(1)} %expert.1), kind=kOutput, calls=%fused_computation.1 | convolution fusion | flops 1882718208 | bytes 11272192 | tf_op jit(solution)/shard_map/dot_general | solution.py:490
  290.9 1.0 constant_dynamic-slice_fusion
  292.7 4.1 convolution_convert_fusion
  296.9 85.9 %all_to_all.20 = bf16[4,8,16,7168]{3,2,1,0:T(8,128)(2,1)} all-to-all(bf16[4,8,16,7168]{3,2,1,0:T(8,128)(2,1)S(1)} %fusion.9), channel_id=1, replica_groups=mesh['ctx'=8,'exp'=4] {'exp'}, dimensions={0} | all-to-all | bytes 14680064 | tf_op jit(solution)/shard_map/all_to_all | solution.py:513
  382.8 6.2 %reduce_sum.61 = bf16[8,16,7168]{2,1,0:T(8,128)(2,1)} reduce(bf16[4,8,16,7168]{3,2,1,0:T(8,128)(2,1)} %all_to_all.20, bf16[]{:T(256)} %constant.8.clone.1), dimensions={0}, to_apply=%region_5.6 | reduce | flops 2752512 | bytes 9175042 | tf_op jit(solution)/shard_map/reduce_sum | solution.py:514
  389.1 15.7 %all_to_all.21 = bf16[4,16,7168]{2,1,0:T(8,128)(2,1)S(1)} all-to-all(bf16[4,16,7168]{2,1,0:T(8,128)(2,1)} %bitcast.128), channel_id=1, replica_groups=mesh['ctx'=8,'exp'=4] {'exp'}, dimensions={0} | all-to-all | bytes 1835008 | tf_op jit(solution)/shard_map/all_to_all | solution.py:502
  405.0 16.9 %reduce-scatter.5.cloned.1.call-done = bf16[1,16,7168]{2,1,0:T(8,128)(2,1)} async-done(((bf16[8,16,7168]{2,1,0:T(8,128)(2,1)}), bf16[1,16,7168]{2,1,0:T(8,128)(2,1)}) %reduce-scatter.5.cloned.1.call-update) | async-done | bytes 229392 | tf_op jit(solution)/shard_map/reduce_scatter | solution.py:515
  421.8 1.7 pad_maximum_fusion.1
  (80 shorter events, 14.8 us)
Async XLA Ops:
  6.5 16.6 %copy-start = (f32[2,32,16]{1,2,0:T(8,128)S(1)}, f32[2,32,16]{1,2,0:T(8,128)}, u32[]{:S(2)}) copy-start(f32[2,32,16]{1,2,0:T(8,128)} %param.17) | copy-start | bytes 12292
  6.5 5.2 %copy-start.6 = (bf16[128,2048]{1,0:T(8,128)(2,1)S(1)}, bf16[128,2048]{1,0:T(8,128)(2,1)}, u32[]{:S(2)}) copy-start(bf16[128,2048]{1,0:T(8,128)(2,1)} %param.14) | copy-start | bytes 1572868
  6.5 5.7 %copy-start.7 = (bf16[128,2048]{1,0:T(8,128)(2,1)S(1)}, bf16[128,2048]{1,0:T(8,128)(2,1)}, u32[]{:S(2)}) copy-start(bf16[128,2048]{1,0:T(8,128)(2,1)} %param.15) | copy-start | bytes 1572868
  16.8 55.4 %all-to-all-start = ((bf16[8,512,256]{2,1,0:T(8,128)(2,1)}), bf16[8,512,256]{2,1,0:T(8,128)(2,1)S(1)}, u32[]{:S(2)}, u32[]{:S(2)}) async-start(bf16[8,512,256]{2,1,0:T(8,128)(2,1)} %bitcast_dynamic-update-slice_fusion.3), calls=%async_computation | async-start | bytes 4194304 | tf_op jit(solution)/shard_map/all_to_all | solution.py:437
  23.1 103.1 %all-gather.6.cloned.1.call-start = ((), (), s32[]{:S(2)}) async-start(), calls=%async_computation.9 | async-start | bytes 4718592 | tf_op jit(solution)/shard_map/all_gather | solution.py:452
  72.6 1.0 copy-start.5
  134.0 6.0 %copy-start.2 = (f32[7168]{0:T(1024)S(1)}, f32[7168]{0:T(1024)}, u32[]{:S(2)}) copy-start(f32[7168]{0:T(1024)} %param.20) | copy-start | bytes 86020
  135.4 28.5 %all-to-all-start.1 = ((bf16[4,272,896]{2,1,0:T(8,128)(2,1)}), bf16[4,272,896]{2,1,0:T(8,128)(2,1)}, u32[]{:S(2)}, u32[]{:S(2)}) async-start(bf16[4,272,896]{2,1,0:T(8,128)(2,1)} %pad_maximum_fusion), calls=%async_computation.1 | async-start | bytes 3899392 | tf_op jit(solution)/shard_map/all_to_all | solution.py:470
  139.9 130.1 %all-gather.4.cloned.1.call-start = ((), (), s32[]{:S(2)}) async-start(), calls=%async_computation.6 | async-start | bytes 15138816 | tf_op jit(solution)/shard_map/all_gather | solution.py:478
  166.6 222.4 %reduce-scatter.3.cloned.1.call-start = ((), (), s32[]{:S(2)}) async-start(), calls=%async_computation.7 | async-start | bytes 8257536 | tf_op jit(solution)/shard_map/reduce_scatter | solution.py:496
  270.0 2.0 copy-start.3
  272.0 13.7 %copy-start.4 = (bf16[1,256,7168]{2,1,0:T(8,128)(2,1)S(1)}, bf16[1,256,7168]{2,1,0:T(8,128)(2,1)}, u32[]{:S(2)}) copy-start(bf16[1,256,7168]{2,1,0:T(8,128)(2,1)} %param.25) | copy-start | bytes 11010052
  292.6 129.2 %reduce-scatter.5.cloned.1.call-start = ((), (), s32[]{:S(2)}) async-start(), calls=%async_computation.8 | async-start | bytes 2064384 | tf_op jit(solution)/shard_map/reduce_scatter | solution.py:515
  382.8 40.7 %copy-start.1 = (f32[2,32,16]{1,2,0:T(8,128)S(1)}, f32[2,32,16]{1,2,0:T(8,128)}, u32[]{:S(2)}) copy-start(f32[2,32,16]{1,2,0:T(8,128)} %param.17) | copy-start | bytes 12292
Sparse Core Ops, SparseCore 0:
  80.1 46.0 all-gather.5
  166.7 103.1 all-gather.3
  292.8 77.8 reduce-scatter.2
  389.1 32.6 reduce-scatter.4

commit v3 on v2

--- a/solution.py
+++ b/solution.py
@@ -304,74 +304,128 @@
     )(moved, taps, gates)
 
 
-def expert_kernel(ctx_count, exp_count, share, rows, gain, gate_w, up_w, route, out, gate_acc, up_acc, squares):
+def expert_kernel(exp_count, share, rows, gain, gate_w, up_w, gate_v, up_v, route, out, total, squares):
     step = pl.program_id(0)
 
     @pl.when(step == 0)
     def _():
-        gate_acc[...] = jnp.zeros_like(gate_acc)
-        up_acc[...] = jnp.zeros_like(up_acc)
+        total[...] = jnp.zeros_like(total)
         squares[...] = jnp.zeros_like(squares)
 
     block = rows[0]
-    gate_acc[...] += jnp.dot(block, gate_w[...], preferred_element_type=jnp.float32)
-    up_acc[...] += jnp.dot(block, up_w[...], preferred_element_type=jnp.float32)
+    for spot, weight in enumerate((gate_w, up_w, gate_v, up_v)):
+        total[spot] += jnp.dot(block, weight[...], preferred_element_type=jnp.float32)
     lane = squares.shape[1]
-    total = squares[...]
+    collected = squares[...]
     for part in range(block.shape[1] // lane):
         lanes = slice(part * lane, (part + 1) * lane)
         plain = block[:, lanes].astype(jnp.float32) * (1.0 / gain[0, :, lanes])
-        total = total + plain * plain
-    squares[...] = total
+        collected = collected + plain * plain
+    squares[...] = collected
 
     @pl.when(step == pl.num_programs(0) - 1)
     def _():
-        model_width = ctx_count * rows.shape[2]
+        model_width = pl.num_programs(0) * block.shape[1]
         mean_square = jnp.sum(squares[...], axis=1, keepdims=True) / model_width
         inverse = lax.rsqrt(mean_square + norm_eps)
-        gate_part = gate_acc[...] * inverse
-        up_part = up_acc[...] * inverse
-        active = gate_part / (1.0 + jnp.exp(-gate_part)) * up_part * route[...]
-        active = active.astype(jnp.bfloat16)
         half = share // 2
-        for exp_spot in range(exp_count):
-            for ctx_spot in range(ctx_count):
-                base = (exp_spot * ctx_count + ctx_spot) * share
-                target = (ctx_spot * exp_count + exp_spot) * half
-                out[0, target : target + half, :] = active[base : base + half]
-                target = (exp_spot * ctx_count + ctx_spot) * half
-                out[1, target : target + half, :] = active[base + half : base + share]
-
-
-def run_expert(rows, gain, gate_w, up_w, route, exp_count, share):
-    ctx_count, seq_len, cols = rows.shape
-    units = gate_w.shape[1]
+        chip_count = block.shape[0] // (exp_count * share)
+        for core in range(2):
+            gate_part = total[2 * core] * inverse
+            up_part = total[2 * core + 1] * inverse
+            active = gate_part / (1.0 + jnp.exp(-gate_part)) * up_part * route[...]
+            active = active.astype(jnp.bfloat16)
+            for exp_spot in range(exp_count):
+                for chip in range(chip_count):
+                    base = (exp_spot * chip_count + chip) * share
+                    target = (chip * exp_count + exp_spot) * half
+                    out[0, core, target : target + half, :] = active[base : base + half]
+                    target = (exp_spot * chip_count + chip) * half
+                    out[1, core, target : target + half, :] = active[base + half : base + share]
+
+
+def run_expert(rows, gain, weights, route, exp_count, share):
+    chip_count, row_total, wide = rows.shape
+    cols = wide // 2
+    steps = 2 * chip_count
+    units = weights[0].shape[1]
     lane = math.gcd(128, cols)
+    by_cols = pl.BlockSpec((cols, units), lambda i: (i, 0))
     return pl.pallas_call(
-        functools.partial(expert_kernel, ctx_count, exp_count, share),
-        grid=(ctx_count,),
+        functools.partial(expert_kernel, exp_count, share),
+        grid=(steps,),
         in_specs=[
-            pl.BlockSpec((1, seq_len, cols), lambda i: (i, 0, 0)),
+            pl.BlockSpec((1, row_total, cols), lambda i: (i // 2, 0, i % 2)),
             pl.BlockSpec((1, 1, cols), lambda i: (i, 0, 0)),
-            pl.BlockSpec((cols, units), lambda i: (i, 0)),
-            pl.BlockSpec((cols, units), lambda i: (i, 0)),
-            pl.BlockSpec((seq_len, 1), lambda i: (0, 0)),
+            by_cols,
+            by_cols,
+            by_cols,
+            by_cols,
+            pl.BlockSpec((row_total, 1), lambda i: (0, 0)),
         ],
-        out_specs=pl.BlockSpec((2, seq_len // 2, units), lambda i: (0, 0, 0)),
-        out_shape=jax.ShapeDtypeStruct((2, seq_len // 2, units), jnp.bfloat16),
+        out_specs=pl.BlockSpec((2, 2, row_total // 2, units), lambda i: (0, 0, 0, 0)),
+        out_shape=jax.ShapeDtypeStruct((2, 2, row_total // 2, units), jnp.bfloat16),
         scratch_shapes=[
-            pltpu.VMEM((seq_len, units), jnp.float32),
-            pltpu.VMEM((seq_len, units), jnp.float32),
-            pltpu.VMEM((seq_len, lane), jnp.float32),
+            pltpu.VMEM((4, row_total, units), jnp.float32),
+            pltpu.VMEM((row_total, lane), jnp.float32),
         ],
         compiler_params=pltpu.CompilerParams(vmem_limit_bytes=48 * 2**20),
         cost_estimate=pl.CostEstimate(
-            flops=4 * seq_len * units * ctx_count * cols,
-            bytes_accessed=2 * ctx_count * cols * (seq_len + 2 * units),
-            transcendentals=seq_len * units,
+            flops=8 * row_total * units * steps * cols,
+            bytes_accessed=2 * steps * cols * (row_total + 4 * units),
+            transcendentals=2 * row_total * units,
         ),
         name="expert",
-    )(rows, gain.reshape(ctx_count, 1, cols), gate_w, up_w, route)
+    )(rows, gain.reshape(steps, 1, cols), *weights, route)
+
+
+def down_kernel(exp_dim, spots, active, down_w, down_v, hidden, out):
+    step = pl.program_id(0)
+    sums = jnp.dot(active[0], down_w[...], preferred_element_type=jnp.float32)
+    sums += jnp.dot(active[1], down_v[...], preferred_element_type=jnp.float32)
+    out[...] = sums.astype(out.dtype).reshape(out.shape)
+
+    @pl.when(step // 2 == spots[0])
+    def _():
+        spot = pl.ds(spots[1], 1)
+        place = (spot,) if exp_dim == 0 else (slice(None), spot)
+        piece = out[place].astype(jnp.float32)
+        out[place] = (piece + hidden[...].reshape(piece.shape)).astype(out.dtype)
+
+
+def run_down(spots, active, down_w, down_v, hidden, exp_count, exp_dim):
+    units, model_width = down_w.shape
+    chip_count, half, wide = hidden.shape
+    cols = wide // 2
+    lead = (exp_count, chip_count) if exp_dim == 0 else (chip_count, exp_count)
+    by_cols = pl.BlockSpec((units, cols), lambda i, _: (0, i))
+    rows = active.shape[1]
+    return pl.pallas_call(
+        functools.partial(down_kernel, exp_dim),
+        grid_spec=pltpu.PrefetchScalarGridSpec(
+            num_scalar_prefetch=1,
+            grid=(model_width // cols,),
+            in_specs=[
+                pl.BlockSpec((2, rows, units), lambda i, _: (0, 0, 0)),
+                by_cols,
+                by_cols,
+                pl.BlockSpec((chip_count, half, cols), lambda i, _: (0, 0, i % 2)),
+            ],
+            out_specs=pl.BlockSpec(lead + (half, cols), lambda i, _: (0, 0, 0, i)),
+        ),
+        out_shape=jax.ShapeDtypeStruct(lead + (half, model_width), jnp.bfloat16),
+        compiler_params=pltpu.CompilerParams(vmem_limit_bytes=48 * 2**20),
+        cost_estimate=pl.CostEstimate(
+            flops=4 * rows * units * model_width,
+            bytes_accessed=2 * model_width * (rows + 2 * units),
+            transcendentals=0,
+        ),
+        name="down",
+    )(spots, active, down_w, down_v, hidden)
+
+
+def sibling(block):
+    return lax.ppermute(block, "core", [(0, 1), (1, 0)])
 
 
 def by_heads(
@@ -394,9 +448,13 @@
     head_width = query_input.shape[1] // head_count
     block_len = comp_weight.shape[1]
     stride_len = block_len // 2
-    ctx_count = lax.axis_size("ctx")
+    ctx = ("z", "core")
+    chip_count = lax.axis_size("z")
+    ctx_count = chip_count * lax.axis_size("core")
     exp_count = lax.axis_size("exp")
-    ctx_index = lax.axis_index("ctx")
+    chip_index = lax.axis_index("z")
+    core_index = lax.axis_index("core")
+    ctx_index = 2 * chip_index + core_index
     exp_index = lax.axis_index("exp")
     own = head_count // ctx_count
     width = own * head_width
@@ -406,6 +464,10 @@
     cols = out_proj.shape[1]
     model_width = cols * ctx_count
     own_tokens = ctx_count * share
+
+    other_gate = sibling(expert_gate[0])
+    other_up = sibling(expert_up[0])
+    other_down = sibling(expert_down[0])
 
     experts = jnp.arange(exp_count, dtype=jnp.int32)
     table = jnp.sum(
@@ -434,7 +496,7 @@
         ],
         1,
     )
-    moved = lax.all_to_all(packed, "ctx", split_axis=0, concat_axis=0, tiled=True)
+    moved = lax.all_to_all(packed, ctx, split_axis=0, concat_axis=0, tiled=True)
     residual = moved[:, 3 * row_count : 3 * row_count + residual_rows].reshape(ctx_count, -1)
     residual = residual[:, : share * cols].reshape(own_tokens, cols)
     side = moved[:, 3 * row_count + residual_rows :].reshape(ctx_count, -1).astype(jnp.float32)
@@ -442,14 +504,15 @@
     gates = side[:, :gate_size].reshape(ctx_count, 2, 2, row_count, own)
     gates = jnp.transpose(gates[:, 0] + gates[:, 1], (0, 2, 1, 3)).reshape(seq_len, 2 * own)
     table = side[:, gate_size : gate_size + 2 * share * exp_count]
-    table = table.reshape(ctx_count, 2, share, exp_count)
+    table = table.reshape(chip_count, 2, 2, share, exp_count)
+    table = lax.dynamic_index_in_dim(table, core_index, 1, keepdims=False)
 
     taps = lax.dynamic_slice_in_dim(comp_weight, ctx_index * own, own, 2)
     taps = jnp.transpose(taps.reshape(2, 2, stride_len, own), (0, 3, 1, 2))
     taps = jnp.tile(taps.reshape(4 * own, stride_len), (1, seq_len // stride_len))
     attended = attend(moved, taps, gates, row_count, share, block_len, head_width)
 
-    spread_heads = lax.all_gather(attended, "ctx", axis=0)
+    spread_heads = lax.all_gather(attended, ctx, axis=0)
     partial = jnp.einsum(
         "csk,ckd->sd",
         spread_heads,
@@ -468,34 +531,38 @@
         1,
     )
     pieces = lax.all_to_all(pieces, "exp", split_axis=0, concat_axis=0, tiled=True)
-    route = pieces[:, own_tokens:].reshape(exp_count, -1)[:, : 2 * own_tokens]
-    route = jnp.sum(route.reshape(exp_count, 2, own_tokens).astype(jnp.float32), axis=1)
+    chip_tokens = chip_count * share
+    route = pieces[:, own_tokens:].reshape(exp_count, -1)[:, : 2 * chip_tokens]
+    route = jnp.sum(route.reshape(exp_count, 2, chip_tokens).astype(jnp.float32), axis=1)
     hidden_state = residual.astype(jnp.float32) + jnp.sum(
         pieces[:, :own_tokens].astype(jnp.float32), axis=0
     )
-    gain = lax.dynamic_slice_in_dim(ffn_gain, ctx_index * cols, cols, 0)
-    scaled = (hidden_state * gain).astype(jnp.bfloat16)
-    rows = lax.all_gather(scaled, ("ctx", "exp"), axis=0, tiled=True)
+    hidden_state = hidden_state.reshape(chip_count, 2, share, cols)
+    kept = lax.dynamic_index_in_dim(hidden_state, core_index, 1, keepdims=False)
+    given = lax.dynamic_index_in_dim(hidden_state, 1 - core_index, 1, keepdims=False)
+    given = sibling(given)
+    hidden_state = jnp.concatenate(
+        [jnp.where(core_index == 0, kept, given), jnp.where(core_index == 0, given, kept)], 2
+    )
+    gain = lax.dynamic_slice_in_dim(ffn_gain, chip_index * 2 * cols, 2 * cols, 0)
+    scaled = (hidden_state * gain).astype(jnp.bfloat16).reshape(chip_tokens, 2 * cols)
+    rows = lax.all_gather(scaled, ("z", "exp"), axis=0, tiled=True)
     active = run_expert(
-        rows.reshape(ctx_count, seq_len, cols),
+        rows.reshape(chip_count, exp_count * chip_tokens, 2 * cols),
         ffn_gain,
-        expert_gate[0],
-        expert_up[0],
-        route.reshape(seq_len, 1),
+        (expert_gate[0], expert_up[0], other_gate, other_up),
+        route.reshape(exp_count * chip_tokens, 1),
         exp_count,
         share,
     )
-    hidden_state = hidden_state.reshape(ctx_count, share, cols)
-
-    outs = jnp.dot(active[0], expert_down[0], preferred_element_type=jnp.float32)
-    outs = outs.astype(jnp.bfloat16).reshape(ctx_count, exp_count, half, model_width)
-    place = (0, exp_index, 0, ctx_index * cols)
-    mine = lax.dynamic_slice(outs, place, (ctx_count, 1, half, cols)).astype(jnp.float32)
-    mine = mine + hidden_state[:, None, :half]
-    outs = lax.dynamic_update_slice(outs, mine.astype(jnp.bfloat16), place)
+    spots = jnp.stack([chip_index, exp_index]).astype(jnp.int32)
+
+    outs = run_down(
+        spots, active[0], expert_down[0], other_down, hidden_state[:, :half], exp_count, 1
+    )
     first = lax.psum_scatter(
-        outs.reshape(ctx_count, exp_count * half, model_width),
-        "ctx",
+        outs.reshape(chip_count, exp_count * half, model_width),
+        "z",
         scatter_dimension=0,
         tiled=True,
     )
@@ -504,41 +571,48 @@
     )
     first = jnp.sum(first.astype(jnp.float32), axis=0).astype(jnp.bfloat16)
 
-    outs = jnp.dot(active[1], expert_down[0], preferred_element_type=jnp.float32)
-    outs = outs.astype(jnp.bfloat16).reshape(exp_count, ctx_count, half, model_width)
-    place = (exp_index, 0, 0, ctx_index * cols)
-    mine = lax.dynamic_slice(outs, place, (1, ctx_count, half, cols)).astype(jnp.float32)
-    mine = mine + hidden_state[None, :, half:]
-    outs = lax.dynamic_update_slice(outs, mine.astype(jnp.bfloat16), place)
+    outs = run_down(
+        spots, active[1], expert_down[0], other_down, hidden_state[:, half:], exp_count, 0
+    )
     outs = lax.all_to_all(outs, "exp", split_axis=0, concat_axis=0, tiled=True)
     outs = jnp.sum(outs.astype(jnp.float32), axis=0).astype(jnp.bfloat16)
-    second = lax.psum_scatter(outs, "ctx", scatter_dimension=0, tiled=True)
+    second = lax.psum_scatter(outs, "z", scatter_dimension=0, tiled=True)
     return jnp.concatenate([first, second.reshape(half, model_width)], 0)
 
 
-def local(*args):
-    head_count = args[4].shape[2]
-    share = args[0].shape[0] // lax.axis_size("exp")
-    if head_count % lax.axis_size("ctx") == 0 and share % 32 == 0:
-        return by_heads(*args)
-    return general(*args)
+def specs(ctx):
+    in_specs = (
+        P(ctx, "exp"),
+        P(ctx, "exp"),
+        P(ctx, "exp"),
+        P(None, ctx, "exp"),
+        P(None, None, "exp"),
+        P("exp", ctx),
+        P((*ctx, "exp"), None),
+        P(),
+        P((*ctx, "exp"), None),
+        P((*ctx, "exp"), None),
+        P("exp", None, ctx),
+        P("exp", None, ctx),
+        P("exp", ctx, None),
+    )
+    return in_specs, P((*ctx, "exp"), None)
 
 
 def solution(mesh):
-    in_specs = (
-        P("ctx", "exp"),
-        P("ctx", "exp"),
-        P("ctx", "exp"),
-        P(None, "ctx", "exp"),
-        P(None, None, "exp"),
-        P("exp", "ctx"),
-        P(("ctx", "exp"), None),
-        P(),
-        P(("ctx", "exp"), None),
-        P(("ctx", "exp"), None),
-        P("exp", None, "ctx"),
-        P("exp", None, "ctx"),
-        P("exp", "ctx", None),
-    )
-    out_specs = P(("ctx", "exp"), None)
-    return jax.shard_map(local, mesh=mesh, in_specs=in_specs, out_specs=out_specs, check_vma=False)
+    ctx_count, exp_count = mesh.shape["ctx"], mesh.shape["exp"]
+
+    def run(*args):
+        head_count = args[4].shape[2] // exp_count
+        share = args[0].shape[0] // (ctx_count * exp_count)
+        body, axes, where = general, ("ctx",), mesh
+        if head_count % ctx_count == 0 and share % 32 == 0 and ctx_count % 2 == 0:
+            split = mesh.devices.reshape(ctx_count // 2, 2, exp_count)
+            where = jax.sharding.Mesh(split, ("z", "core", "exp"))
+            body, axes = by_heads, ("z", "core")
+        in_specs, out_specs = specs(axes)
+        return jax.shard_map(
+            body, mesh=where, in_specs=in_specs, out_specs=out_specs, check_vma=False
+        )(*args)
+
+    return run

time: 431 us -> 398 us (0.923)
  blocking collectives: 102 us -> 61.2 us
  Pallas kernels: 19.8 us -> 35.7 us
  matrix products: 17 us -> 7.79 us
  waiting for transfers between devices: 234 us -> 239 us
    all_to_all x1, blocking collectives: 85.9 us -> 44.9 us  [by_heads(): outs = lax.all_to_all(outs, 'exp', split_axis=0, concat_axis=0, tiled=True)]
    pallas_call x1 -> x3, Pallas kernels: 13.7 us -> 29.6 us  [the longest x2 16.1 us: run_down(): pl.pallas_call(functools.partial(down_kernel, exp_dim), grid_spec=pltpu.P...]
    ppermute x0 -> x4, waiting for transfers between devices: none -> 11.3 us  [sibling(): return lax.ppermute(block, 'core', [(0, 1), (1, 0)])]
    all_gather x2, waiting for transfers between devices: 144 us -> 135 us  [the longest x1 89.1 us: by_heads(): rows = lax.all_gather(scaled, ('z', 'exp'), axis=0, tiled=True)]
    dot_general x2 -> x0, matrix products: 9.22 us -> none  [the longest x1 5.1 us: by_heads(): jnp.dot(active[0], expert_down[0], preferred_element_type=jnp.float32)]
    unnamed x29 -> x28, local copies, waits for them, and re-layouts: 8.97 us -> 9.62 us
  transfers between devices with their start and end apart: 6 -> 10, of which waited for: 5 -> 9; matrix products, arithmetic and copies ran while one was open for 4% -> 2% of each run, Pallas kernels for 0% -> 5%
where the time goes in v3:
time: 398 us; the launch traced here: 396 us
  waiting for transfers between devices  239 us (60%)
  blocking collectives  61.2 us (15%)
  Pallas kernels  35.7 us (9%)
  local copies, waits for them, and re-layouts  15 us (4%)
  between operations  13.6 us (3%)
  other arithmetic  12.1 us (3%)
  starting transfers between devices  11.9 us (3%)
  matrix products  7.79 us (2%)
    all_gather x1, waiting for transfers between devices, by_heads(): rows = lax.all_gather(scaled, ('z', 'exp'), axis=0, tiled=True)  89.1 us
    all_to_all x1, waiting for transfers between devices, by_heads(): moved = lax.all_to_all(packed, ctx, split_axis=0, concat_axis=0, tiled=True)  48.7 us
    all_gather x1, waiting for transfers between devices, by_heads(): spread_heads = lax.all_gather(attended, ctx, axis=0)  45.6 us
    all_to_all x1, blocking collectives, by_heads(): outs = lax.all_to_all(outs, 'exp', split_axis=0, concat_axis=0, tiled=True)  44.9 us
    all_to_all x1, waiting for transfers between devices, by_heads(): lax.all_to_all(pieces, 'exp', split_axis=0, concat_axis=0, tiled=True)  23.6 us
    all_to_all x1, blocking collectives, by_heads(): lax.all_to_all(first.reshape(exp_count, half, model_width), 'exp', split_...  16.3 us
    pallas_call x2, Pallas kernels, run_down(): pl.pallas_call(functools.partial(down_kernel, exp_dim), grid_spec=pltpu.P...  16.1 us
    pallas_call x1, Pallas kernels, run_expert(): pl.pallas_call(functools.partial(expert_kernel, exp_count, share), grid=(...  13.5 us
  transfers between devices with their start and end apart: 10, of which 9 were waited for; matrix products, arithmetic and copies ran while one was open for 2% of the time, Pallas kernels for 5%

profile of v3, /device:TPU:0, one launch (start us, length us, event | category | flops | bytes accessed | tf_op | source)
XLA Modules:
  0.0 396.5 jit_solution(394603565266430394)
XLA Ops:
  15.8 6.3 %all-to-all-start = ((bf16[8,512,256]{2,1,0:T(8,128)(2,1)}), bf16[8,512,256]{2,1,0:T(8,128)(2,1)S(1)}, u32[]{:S(2)}, u32[]{:S(2)}) async-start(bf16[8,512,256]{2,1,0:T(8,128)(2,1)} %bitcast_dynamic-update-slice_fusion.3), calls=%async_computation | async-start | bytes 4194304 | tf_op jit(solution)/shard_map/all_to_all | solution.py:499
  22.5 48.7 %all-to-all-done.moved = bf16[8,512,256]{2,1,0:T(8,128)(2,1)S(1)} async-done(((bf16[8,512,256]{2,1,0:T(8,128)(2,1)}), bf16[8,512,256]{2,1,0:T(8,128)(2,1)S(1)}, u32[]{:S(2)}, u32[]{:S(2)}) %all-to-all-start) | async-done | bytes 2097184 | tf_op jit(solution)/shard_map/all_to_all | solution.py:499
  72.0 6.1 %attend.1 = bf16[1024,256]{1,0:T(8,128)(2,1)} custom-call(bf16[8,512,256]{2,1,0:T(8,128)(2,1)S(1)} %all-to-all-done.moved, f32[8,1024]{1,0:T(8,128)S(1)} %tile.12.taps, f32[1024,4]{1,0:T(8,128)S(1)} %copy.87.gates), custom_call_target="tpu_custom_call" | custom-call | tf_op jit(solution)/shard_map/attend/pallas_call | solution.py:295
  78.7 45.6 %all-gather.6.cloned.1.call-done = bf16[8192,256]{1,0:T(8,128)(2,1)} async-done(((bf16[1024,256]{1,0:T(8,128)(2,1)}), bf16[8192,256]{1,0:T(8,128)(2,1)}) %all-gather.6.cloned.1.call-update) | async-done | bytes 4194320 | tf_op jit(solution)/shard_map/all_gather | solution.py:515
  124.3 7.8 %bitcast_convert_fusion = bf16[1024,896]{1,0:T(8,128)(2,1)S(1)} fusion(bf16[8,1024,256]{2,1,0:T(8,128)(2,1)} %bitcast.121, bf16[8,256,896]{2,1,0:T(8,128)(2,1)} %bitcast.122), kind=kOutput, calls=%fused_computation | convolution fusion | flops 3759013888 | bytes 9699328 | tf_op jit(solution)/shard_map/csk,ckd->sd/dot_general | solution.py:516
  132.1 1.4 pad_maximum_fusion
  133.6 4.4 %all-to-all-start.1 = ((bf16[4,272,896]{2,1,0:T(8,128)(2,1)}), bf16[4,272,896]{2,1,0:T(8,128)(2,1)}, u32[]{:S(2)}, u32[]{:S(2)}) async-start(bf16[4,272,896]{2,1,0:T(8,128)(2,1)} %pad_maximum_fusion), calls=%async_computation.1 | async-start | bytes 3899392 | tf_op jit(solution)/shard_map/all_to_all | solution.py:533
  138.4 23.6 %all-to-all-done.1 = bf16[4,272,896]{2,1,0:T(8,128)(2,1)} async-done(((bf16[4,272,896]{2,1,0:T(8,128)(2,1)}), bf16[4,272,896]{2,1,0:T(8,128)(2,1)}, u32[]{:S(2)}, u32[]{:S(2)}) %all-to-all-start.1) | async-done | bytes 1949728 | tf_op jit(solution)/shard_map/all_to_all | solution.py:533
  162.0 1.9 convert_reduce_fusion
  164.8 1.2 collective-permute-done
  169.2 4.8 %collective-permute-done.1.gate_v = bf16[7168,256]{1,0:T(8,128)(2,1)} collective-permute-done((bf16[7168,256]{1,0:T(8,128)(2,1)}, bf16[7168,256]{1,0:T(8,128)(2,1)}, u32[]{:S(2)}, u32[]{:S(2)}) %collective-permute-start.1) | collective-permute-done | bytes 3670048 | tf_op jit(solution)/shard_map/ppermute | solution.py:428
  174.0 5.2 %collective-permute-done.2.up_v = bf16[7168,256]{1,0:T(8,128)(2,1)} collective-permute-done((bf16[7168,256]{1,0:T(8,128)(2,1)}, bf16[7168,256]{1,0:T(8,128)(2,1)}, u32[]{:S(2)}, u32[]{:S(2)}) %collective-permute-start.2) | collective-permute-done | bytes 3670048 | tf_op jit(solution)/shard_map/ppermute | solution.py:428
  179.2 89.1 %all-gather.4.cloned.1.call-done = bf16[2048,1792]{1,0:T(8,128)(2,1)} async-done(((bf16[128,1792]{1,0:T(8,128)(2,1)}), bf16[2048,1792]{1,0:T(8,128)(2,1)}) %all-gather.4.cloned.1.call-update) | async-done | bytes 7340048 | tf_op jit(solution)/shard_map/all_gather | solution.py:549
  268.3 2.0 copy-done.4
  270.4 13.5 %expert.1 = bf16[2,2,256,256]{3,2,1,0:T(8,128)(2,1)S(1)} custom-call(bf16[4,512,1792]{2,1,0:T(8,128)(2,1)} %bitcast.120, f32[8,1,896]{2,1,0:T(1,128)S(1)} %bitcast.89, bf16[7168,256]{1,0:T(8,128)(2,1)S(1)} %bitcast.91, bf16[7168,256]{1,0:T(8,128)(2,1)} %bitcast.124, bf16[7168,256]{1,0:T(8,128)(2,1)} %collective-permute-done.1.gate_v, ...), custom_call_target="tpu_custom_call" | custom-call | flops 7516192768 | bytes 22020096 | tf_op jit(solution)/shard_map/expert/pallas_call | solution.py:354
  283.9 8.0 %down.2 = bf16[4,4,16,7168]{3,2,1,0:T(8,128)(2,1)S(1)} custom-call(s32[2]{0:T(128)S(1)} %pad_add_fusion.spots, bf16[2,256,256]{2,1,0:T(8,128)(2,1)S(1)} %get-tuple-element.9.active, bf16[256,7168]{1,0:T(8,128)(2,1)} %bitcast.93, bf16[256,7168]{1,0:T(8,128)(2,1)} %collective-permute-done.3.down_v, f32[4,16,1792]{2,1,0:T(8,128)S(1)} %get-tuple-element.7.hidden), custom_call_target="tpu_custom_call" | custom-call | flops 1879048192 | bytes 11010048 | tf_op jit(solution)/shard_map/down/pallas_call | solution.py:403
  292.0 1.8 copy-done.2
  293.8 8.1 %down.3 = bf16[4,4,16,7168]{3,2,1,0:T(8,128)(2,1)S(1)} custom-call(s32[2]{0:T(128)S(1)} %pad_add_fusion.spots, bf16[2,256,256]{2,1,0:T(8,128)(2,1)S(1)} %get-tuple-element.10.active, bf16[256,7168]{1,0:T(8,128)(2,1)} %bitcast.94, bf16[256,7168]{1,0:T(8,128)(2,1)} %collective-permute-done.3.down_v, f32[4,16,1792]{2,1,0:T(8,128)S(1)} %get-tuple-element.8.hidden), custom_call_target="tpu_custom_call" | custom-call | flops 1879048192 | bytes 11010048 | tf_op jit(solution)/shard_map/down/pallas_call | solution.py:403
  302.0 44.9 %all_to_all.20 = bf16[4,4,16,7168]{3,2,1,0:T(8,128)(2,1)} all-to-all(bf16[4,4,16,7168]{3,2,1,0:T(8,128)(2,1)S(1)} %down.3), channel_id=1, replica_groups=mesh['z'=4,'core'=2,'exp'=4] {'exp'}, dimensions={0} | all-to-all | bytes 7340032 | tf_op jit(solution)/shard_map/all_to_all | solution.py:577
  346.8 3.9 reduce_sum.61
  350.7 9.8 %reduce-scatter.3.cloned.1.call-done = bf16[1,64,7168]{2,1,0:T(8,128)(2,1)} async-done(((bf16[4,64,7168]{2,1,0:T(8,128)(2,1)}), bf16[1,64,7168]{2,1,0:T(8,128)(2,1)}) %reduce-scatter.3.cloned.1.call-update) | async-done | bytes 917520 | tf_op jit(solution)/shard_map/reduce_scatter | solution.py:563
  360.5 16.3 %all_to_all.21 = bf16[4,16,7168]{2,1,0:T(8,128)(2,1)S(1)} all-to-all(bf16[4,16,7168]{2,1,0:T(8,128)(2,1)} %bitcast.105), channel_id=1, replica_groups=mesh['z'=4,'core'=2,'exp'=4] {'exp'}, dimensions={0} | all-to-all | bytes 1835008 | tf_op jit(solution)/shard_map/all_to_all | solution.py:569
  377.1 11.1 %reduce-scatter.5.cloned.1.call-done = bf16[1,16,7168]{2,1,0:T(8,128)(2,1)} async-done(((bf16[4,16,7168]{2,1,0:T(8,128)(2,1)}), bf16[1,16,7168]{2,1,0:T(8,128)(2,1)}) %reduce-scatter.5.cloned.1.call-update) | async-done | bytes 229392 | tf_op jit(solution)/shard_map/reduce_scatter | solution.py:579
  388.2 1.7 pad_maximum_fusion.2
  (90 shorter events, 15.5 us)
Async XLA Ops:
  6.5 15.7 %copy-start = (f32[2,32,16]{1,2,0:T(8,128)S(1)}, f32[2,32,16]{1,2,0:T(8,128)}, u32[]{:S(2)}) copy-start(f32[2,32,16]{1,2,0:T(8,128)} %param.17) | copy-start | bytes 12292
  6.5 3.7 copy-start.5
  8.5 2.2 copy-start.6
  10.2 1.0 copy-start.7
  15.8 55.4 %all-to-all-start = ((bf16[8,512,256]{2,1,0:T(8,128)(2,1)}), bf16[8,512,256]{2,1,0:T(8,128)(2,1)S(1)}, u32[]{:S(2)}, u32[]{:S(2)}) async-start(bf16[8,512,256]{2,1,0:T(8,128)(2,1)} %bitcast_dynamic-update-slice_fusion.3), calls=%async_computation | async-start | bytes 4194304 | tf_op jit(solution)/shard_map/all_to_all | solution.py:499
  22.2 102.2 %all-gather.6.cloned.1.call-start = ((), (), s32[]{:S(2)}) async-start(), calls=%async_computation.9 | async-start | bytes 4718592 | tf_op jit(solution)/shard_map/all_gather | solution.py:515
  133.6 28.5 %all-to-all-start.1 = ((bf16[4,272,896]{2,1,0:T(8,128)(2,1)}), bf16[4,272,896]{2,1,0:T(8,128)(2,1)}, u32[]{:S(2)}, u32[]{:S(2)}) async-start(bf16[4,272,896]{2,1,0:T(8,128)(2,1)} %pad_maximum_fusion), calls=%async_computation.1 | async-start | bytes 3899392 | tf_op jit(solution)/shard_map/all_to_all | solution.py:533
  138.0 130.3 %all-gather.4.cloned.1.call-start = ((), (), s32[]{:S(2)}) async-start(), calls=%async_computation.6 | async-start | bytes 7798784 | tf_op jit(solution)/shard_map/all_gather | solution.py:549
  163.9 0.8 copy-start.3
  164.1 1.9 collective-permute-start
  166.9 193.6 %reduce-scatter.3.cloned.1.call-start = ((), (), s32[]{:S(2)}) async-start(), calls=%async_computation.7 | async-start | bytes 4587520 | tf_op jit(solution)/shard_map/reduce_scatter | solution.py:563
  167.1 6.8 %collective-permute-start.1 = (bf16[7168,256]{1,0:T(8,128)(2,1)}, bf16[7168,256]{1,0:T(8,128)(2,1)}, u32[]{:S(2)}, u32[]{:S(2)}) collective-permute-start(bf16[7168,256]{1,0:T(8,128)(2,1)} %bitcast.90), channel_id=1, source_target_pairs={{0,4},{4,0},{1,5},{5,1},{2,6},{6,2},{3,7},{7,3},{8,12},{12,8},{9,1... | collective-permute-start | bytes 11010056 | tf_op jit(solution)/shard_map/ppermute | solution.py:428
  167.3 11.9 %collective-permute-start.2 = (bf16[7168,256]{1,0:T(8,128)(2,1)}, bf16[7168,256]{1,0:T(8,128)(2,1)}, u32[]{:S(2)}, u32[]{:S(2)}) collective-permute-start(bf16[7168,256]{1,0:T(8,128)(2,1)} %bitcast.123), channel_id=1, source_target_pairs={{0,4},{4,0},{1,5},{5,1},{2,6},{6,2},{3,7},{7,3},{8,12},{12,8},{9,1... | collective-permute-start | bytes 11010056 | tf_op jit(solution)/shard_map/ppermute | solution.py:428
  167.7 116.2 %collective-permute-start.3 = (bf16[256,7168]{1,0:T(8,128)(2,1)}, bf16[256,7168]{1,0:T(8,128)(2,1)}, u32[]{:S(2)}, u32[]{:S(2)}) collective-permute-start(bf16[256,7168]{1,0:T(8,128)(2,1)} %bitcast.92), channel_id=1, source_target_pairs={{0,4},{4,0},{1,5},{5,1},{2,6},{6,2},{3,7},{7,3},{8,12},{12,8},{9,1... | collective-permute-start | bytes 11010056 | tf_op jit(solution)/shard_map/ppermute | solution.py:428
  268.3 2.0 copy-start.4
  291.9 1.8 copy-start.2
  293.8 94.4 %reduce-scatter.5.cloned.1.call-start = ((), (), s32[]{:S(2)}) async-start(), calls=%async_computation.8 | async-start | bytes 1146880 | tf_op jit(solution)/shard_map/reduce_scatter | solution.py:579
  350.7 39.2 %copy-start.1 = (f32[2,32,16]{1,2,0:T(8,128)S(1)}, f32[2,32,16]{1,2,0:T(8,128)}, u32[]{:S(2)}) copy-start(f32[2,32,16]{1,2,0:T(8,128)} %param.17) | copy-start | bytes 12292
Sparse Core Ops, SparseCore 0:
  78.2 46.0 all-gather.5
  167.0 101.2 all-gather.3
  293.9 66.5 reduce-scatter.2
  362.7 25.4 reduce-scatter.4

commit v4 on v3

--- a/solution.py
+++ b/solution.py
@@ -284,9 +284,12 @@
                 gates[rows, head : head + 1] * far
                 + gates[rows, own + head : own + head + 1] * near
             ).astype(jnp.bfloat16)
+            half = share // 2
             for part in range(row_count // share):
-                target = (part * ctx_count + block) * share
-                out[target : target + share, lanes] = mixed[part * share : (part + 1) * share]
+                for group in range(2):
+                    target = (part * ctx_count + block) * half
+                    base = part * share + group * half
+                    out[group, target : target + half, lanes] = mixed[base : base + half]
 
 
 def attend(moved, taps, gates, row_count, share, block_len, head_width):
@@ -294,7 +297,7 @@
     width = moved.shape[2]
     return pl.pallas_call(
         functools.partial(attend_kernel, row_count, share, block_len, head_width),
-        out_shape=jax.ShapeDtypeStruct((seq_len, width), jnp.bfloat16),
+        out_shape=jax.ShapeDtypeStruct((2, seq_len // 2, width), jnp.bfloat16),
         scratch_shapes=[
             pltpu.VMEM((seq_len, head_width), jnp.bfloat16),
             pltpu.VMEM((seq_len, head_width), jnp.bfloat16),
@@ -304,7 +307,7 @@
     )(moved, taps, gates)
 
 
-def expert_kernel(exp_count, share, rows, gain, gate_w, up_w, gate_v, up_v, route, out, total, squares):
+def expert_kernel(exp_dim, spots, own, along, across, far_a, far_b, gain, gate_w, up_w, gate_v, up_v, route, out, total, squares):
     step = pl.program_id(0)
 
     @pl.when(step == 0)
@@ -312,7 +315,8 @@
         total[...] = jnp.zeros_like(total)
         squares[...] = jnp.zeros_like(squares)
 
-    block = rows[0]
+    far = jnp.where(step < pl.num_programs(0) // 2, far_a[0], far_b[0])
+    block = jnp.concatenate([own[0], along[0], across[0], far], 0)
     for spot, weight in enumerate((gate_w, up_w, gate_v, up_v)):
         total[spot] += jnp.dot(block, weight[...], preferred_element_type=jnp.float32)
     lane = squares.shape[1]
@@ -328,64 +332,79 @@
         model_width = pl.num_programs(0) * block.shape[1]
         mean_square = jnp.sum(squares[...], axis=1, keepdims=True) / model_width
         inverse = lax.rsqrt(mean_square + norm_eps)
-        half = share // 2
-        chip_count = block.shape[0] // (exp_count * share)
+        tokens = own.shape[1]
         for core in range(2):
             gate_part = total[2 * core] * inverse
             up_part = total[2 * core + 1] * inverse
-            active = gate_part / (1.0 + jnp.exp(-gate_part)) * up_part * route[...]
-            active = active.astype(jnp.bfloat16)
-            for exp_spot in range(exp_count):
-                for chip in range(chip_count):
-                    base = (exp_spot * chip_count + chip) * share
-                    target = (chip * exp_count + exp_spot) * half
-                    out[0, core, target : target + half, :] = active[base : base + half]
-                    target = (exp_spot * chip_count + chip) * half
-                    out[1, core, target : target + half, :] = active[base + half : base + share]
-
-
-def run_expert(rows, gain, weights, route, exp_count, share):
-    chip_count, row_total, wide = rows.shape
+            active = gate_part / (1.0 + jnp.exp(-gate_part)) * up_part
+            for source in range(block.shape[0] // tokens):
+                spot = pl.ds(jnp.bitwise_xor(spots[1], source), 1)
+                piece = active[source * tokens : (source + 1) * tokens] * route[spot][0]
+                piece = piece.astype(jnp.bfloat16)
+                if exp_dim == 0:
+                    out[core, spot] = piece.reshape((1,) + out.shape[2:])
+                else:
+                    out[core, :, spot] = piece.reshape(out.shape[1], 1, *out.shape[3:])
+
+
+def run_expert(spots, blocks, gain, weights, route, half, exp_dim):
+    chip_count, tokens, wide = blocks[0].shape
     cols = wide // 2
+    middle = chip_count // 2
     steps = 2 * chip_count
     units = weights[0].shape[1]
+    exp_count = route.shape[0]
+    row_total = exp_count * tokens
     lane = math.gcd(128, cols)
-    by_cols = pl.BlockSpec((cols, units), lambda i: (i, 0))
-    return pl.pallas_call(
-        functools.partial(expert_kernel, exp_count, share),
-        grid=(steps,),
-        in_specs=[
-            pl.BlockSpec((1, row_total, cols), lambda i: (i // 2, 0, i % 2)),
-            pl.BlockSpec((1, 1, cols), lambda i: (i, 0, 0)),
-            by_cols,
-            by_cols,
-            by_cols,
-            by_cols,
-            pl.BlockSpec((row_total, 1), lambda i: (0, 0)),
-        ],
-        out_specs=pl.BlockSpec((2, 2, row_total // 2, units), lambda i: (0, 0, 0, 0)),
-        out_shape=jax.ShapeDtypeStruct((2, 2, row_total // 2, units), jnp.bfloat16),
-        scratch_shapes=[
-            pltpu.VMEM((4, row_total, units), jnp.float32),
-            pltpu.VMEM((row_total, lane), jnp.float32),
-        ],
-        compiler_params=pltpu.CompilerParams(vmem_limit_bytes=48 * 2**20),
+    lead = (exp_count, tokens // half) if exp_dim == 0 else (tokens // half, exp_count)
+    by_chip = pl.BlockSpec((1, tokens, cols), lambda i, _: (i // 2, 0, i % 2))
+    by_cols = pl.BlockSpec((cols, units), lambda i, _: (i, 0))
+    out = pl.pallas_call(
+        functools.partial(expert_kernel, exp_dim),
+        grid_spec=pltpu.PrefetchScalarGridSpec(
+            num_scalar_prefetch=1,
+            grid=(steps,),
+            in_specs=[
+                by_chip,
+                by_chip,
+                by_chip,
+                pl.BlockSpec(
+                    (1, tokens, cols), lambda i, _: (jnp.minimum(i // 2, middle - 1), 0, i % 2)
+                ),
+                pl.BlockSpec(
+                    (1, tokens, cols), lambda i, _: (jnp.maximum(i // 2 - middle, 0), 0, i % 2)
+                ),
+                pl.BlockSpec((1, 1, cols), lambda i, _: (i, 0, 0)),
+                by_cols,
+                by_cols,
+                by_cols,
+                by_cols,
+                pl.BlockSpec((exp_count, tokens, 1), lambda i, _: (0, 0, 0)),
+            ],
+            out_specs=pl.BlockSpec((2,) + lead + (half, units), lambda i, _: (0, 0, 0, 0, 0)),
+            scratch_shapes=[
+                pltpu.VMEM((4, row_total, units), jnp.float32),
+                pltpu.VMEM((row_total, lane), jnp.float32),
+            ],
+        ),
+        out_shape=jax.ShapeDtypeStruct((2,) + lead + (half, units), jnp.bfloat16),
+        compiler_params=pltpu.CompilerParams(vmem_limit_bytes=40 * 2**20),
         cost_estimate=pl.CostEstimate(
             flops=8 * row_total * units * steps * cols,
             bytes_accessed=2 * steps * cols * (row_total + 4 * units),
             transcendentals=2 * row_total * units,
         ),
         name="expert",
-    )(rows, gain.reshape(steps, 1, cols), *weights, route)
+    )(spots, *blocks, gain.reshape(steps, 1, cols), *weights, route)
+    return out.reshape(2, row_total, units)
 
 
 def down_kernel(exp_dim, spots, active, down_w, down_v, hidden, out):
-    step = pl.program_id(0)
     sums = jnp.dot(active[0], down_w[...], preferred_element_type=jnp.float32)
     sums += jnp.dot(active[1], down_v[...], preferred_element_type=jnp.float32)
     out[...] = sums.astype(out.dtype).reshape(out.shape)
 
-    @pl.when(step // 2 == spots[0])
+    @pl.when(pl.program_id(0) == spots[0])
     def _():
         spot = pl.ds(spots[1], 1)
         place = (spot,) if exp_dim == 0 else (slice(None), spot)
@@ -396,7 +415,7 @@
 def run_down(spots, active, down_w, down_v, hidden, exp_count, exp_dim):
     units, model_width = down_w.shape
     chip_count, half, wide = hidden.shape
-    cols = wide // 2
+    cols = wide
     lead = (exp_count, chip_count) if exp_dim == 0 else (chip_count, exp_count)
     by_cols = pl.BlockSpec((units, cols), lambda i, _: (0, i))
     rows = active.shape[1]
@@ -409,12 +428,12 @@
                 pl.BlockSpec((2, rows, units), lambda i, _: (0, 0, 0)),
                 by_cols,
                 by_cols,
-                pl.BlockSpec((chip_count, half, cols), lambda i, _: (0, 0, i % 2)),
+                pl.BlockSpec((chip_count, half, cols), lambda i, _: (0, 0, 0)),
             ],
             out_specs=pl.BlockSpec(lead + (half, cols), lambda i, _: (0, 0, 0, i)),
         ),
         out_shape=jax.ShapeDtypeStruct(lead + (half, model_width), jnp.bfloat16),
-        compiler_params=pltpu.CompilerParams(vmem_limit_bytes=48 * 2**20),
+        compiler_params=pltpu.CompilerParams(vmem_limit_bytes=40 * 2**20),
         cost_estimate=pl.CostEstimate(
             flops=4 * rows * units * model_width,
             bytes_accessed=2 * model_width * (rows + 2 * units),
@@ -426,6 +445,11 @@
 
 def sibling(block):
     return lax.ppermute(block, "core", [(0, 1), (1, 0)])
+
+
+def plane_step(block, step):
+    count = lax.axis_size("exp")
+    return lax.ppermute(block, "exp", [(i, i ^ step) for i in range(count)])
 
 
 def by_heads(
@@ -512,56 +536,66 @@
     taps = jnp.tile(taps.reshape(4 * own, stride_len), (1, seq_len // stride_len))
     attended = attend(moved, taps, gates, row_count, share, block_len, head_width)
 
-    spread_heads = lax.all_gather(attended, ctx, axis=0)
-    partial = jnp.einsum(
-        "csk,ckd->sd",
-        spread_heads,
-        out_proj.reshape(ctx_count, width, cols),
-        preferred_element_type=jnp.float32,
-    ).astype(jnp.bfloat16)
     table = jnp.transpose(table, (3, 1, 0, 2)).reshape(exp_count, -1).astype(jnp.bfloat16)
     table_rows = -(-table.shape[1] // cols)
     table_rows += -table_rows % 16
     table = jnp.pad(table, ((0, 0), (0, table_rows * cols - table.shape[1])))
-    pieces = jnp.concatenate(
-        [
-            partial.reshape(exp_count, own_tokens, cols),
-            table.reshape(exp_count, table_rows, cols),
-        ],
-        1,
-    )
-    pieces = lax.all_to_all(pieces, "exp", split_axis=0, concat_axis=0, tiled=True)
-    chip_tokens = chip_count * share
-    route = pieces[:, own_tokens:].reshape(exp_count, -1)[:, : 2 * chip_tokens]
-    route = jnp.sum(route.reshape(exp_count, 2, chip_tokens).astype(jnp.float32), axis=1)
-    hidden_state = residual.astype(jnp.float32) + jnp.sum(
-        pieces[:, :own_tokens].astype(jnp.float32), axis=0
-    )
-    hidden_state = hidden_state.reshape(chip_count, 2, share, cols)
-    kept = lax.dynamic_index_in_dim(hidden_state, core_index, 1, keepdims=False)
-    given = lax.dynamic_index_in_dim(hidden_state, 1 - core_index, 1, keepdims=False)
-    given = sibling(given)
-    hidden_state = jnp.concatenate(
-        [jnp.where(core_index == 0, kept, given), jnp.where(core_index == 0, given, kept)], 2
-    )
+    table = table.reshape(exp_count, table_rows, cols)
     gain = lax.dynamic_slice_in_dim(ffn_gain, chip_index * 2 * cols, 2 * cols, 0)
-    scaled = (hidden_state * gain).astype(jnp.bfloat16).reshape(chip_tokens, 2 * cols)
-    rows = lax.all_gather(scaled, ("z", "exp"), axis=0, tiled=True)
-    active = run_expert(
-        rows.reshape(chip_count, exp_count * chip_tokens, 2 * cols),
-        ffn_gain,
-        (expert_gate[0], expert_up[0], other_gate, other_up),
-        route.reshape(exp_count * chip_tokens, 1),
-        exp_count,
-        share,
-    )
     spots = jnp.stack([chip_index, exp_index]).astype(jnp.int32)
-
-    outs = run_down(
-        spots, active[0], expert_down[0], other_down, hidden_state[:, :half], exp_count, 1
-    )
+    group_tokens = ctx_count * half
+    hidden, blocks = [], []
+    for group in range(2):
+        spread_heads = lax.all_gather(attended[group], ctx, axis=0)
+        pieces = jnp.einsum(
+            "csk,ckd->sd",
+            spread_heads,
+            out_proj.reshape(ctx_count, width, cols),
+            preferred_element_type=jnp.float32,
+        ).astype(jnp.bfloat16)
+        pieces = pieces.reshape(exp_count, group_tokens, cols)
+        if group == 0:
+            pieces = jnp.concatenate([pieces, table], 1)
+        else:
+            pieces, _ = lax.optimization_barrier((pieces, scaled))
+        pieces = lax.all_to_all(pieces, "exp", split_axis=0, concat_axis=0, tiled=True)
+        if group == 0:
+            route = pieces[:, group_tokens:].reshape(exp_count, -1)[:, : 2 * chip_count * share]
+            route = jnp.sum(
+                route.reshape(exp_count, 2, chip_count, 2, half).astype(jnp.float32), axis=1
+            )
+        sums = jnp.sum(pieces[:, :group_tokens].astype(jnp.float32), axis=0)
+        own_rows = residual.reshape(ctx_count, 2, half, cols)[:, group]
+        sums = sums.reshape(ctx_count, half, cols) + own_rows.astype(jnp.float32)
+        sums = sums.reshape(chip_count, 2, half, cols)
+        kept = lax.dynamic_index_in_dim(sums, core_index, 1, keepdims=False)
+        given = sibling(lax.dynamic_index_in_dim(sums, 1 - core_index, 1, keepdims=False))
+        sums = jnp.concatenate(
+            [jnp.where(core_index == 0, kept, given), jnp.where(core_index == 0, given, kept)], 2
+        )
+        scaled = (sums * gain).astype(jnp.bfloat16).reshape(chip_count * half, 2 * cols)
+        plane = lax.all_gather(scaled, "z", axis=0)
+        along, across = plane_step(plane, 1), plane_step(plane, 2)
+        far_a = plane_step(along[: chip_count // 2], 2)
+        far_b = plane_step(across[chip_count // 2 :], 1)
+        hidden.append(sums)
+        blocks.append((plane, along, across, far_a, far_b))
+
+    weights = (expert_gate[0], expert_up[0], other_gate, other_up)
+    outs = []
+    for group in range(2):
+        route_rows = route[:, :, group].reshape(exp_count, chip_count * half, 1)
+        active = run_expert(
+            spots, blocks[group], ffn_gain, weights, route_rows, half, 1 - group
+        )
+        outs.append(
+            run_down(
+                spots, active, expert_down[0], other_down, hidden[group], exp_count, 1 - group
+            )
+        )
+
     first = lax.psum_scatter(
-        outs.reshape(chip_count, exp_count * half, model_width),
+        outs[0].reshape(chip_count, exp_count * half, model_width),
         "z",
         scatter_dimension=0,
         tiled=True,
@@ -571,12 +605,9 @@
     )
     first = jnp.sum(first.astype(jnp.float32), axis=0).astype(jnp.bfloat16)
 
-    outs = run_down(
-        spots, active[1], expert_down[0], other_down, hidden_state[:, half:], exp_count, 0
-    )
-    outs = lax.all_to_all(outs, "exp", split_axis=0, concat_axis=0, tiled=True)
-    outs = jnp.sum(outs.astype(jnp.float32), axis=0).astype(jnp.bfloat16)
-    second = lax.psum_scatter(outs, "z", scatter_dimension=0, tiled=True)
+    second = lax.all_to_all(outs[1], "exp", split_axis=0, concat_axis=0, tiled=True)
+    second = jnp.sum(second.astype(jnp.float32), axis=0).astype(jnp.bfloat16)
+    second = lax.psum_scatter(second, "z", scatter_dimension=0, tiled=True)
     return jnp.concatenate([first, second.reshape(half, model_width)], 0)
 
 
@@ -606,7 +637,8 @@
         head_count = args[4].shape[2] // exp_count
         share = args[0].shape[0] // (ctx_count * exp_count)
         body, axes, where = general, ("ctx",), mesh
-        if head_count % ctx_count == 0 and share % 32 == 0 and ctx_count % 2 == 0:
+        whole = head_count % ctx_count == 0 and share % 32 == 0 and ctx_count % 4 == 0
+        if whole and exp_count.bit_length() == 3 and exp_count.bit_count() == 1:
             split = mesh.devices.reshape(ctx_count // 2, 2, exp_count)
             where = jax.sharding.Mesh(split, ("z", "core", "exp"))
             body, axes = by_heads, ("z", "core")

time: 398 us -> 398 us (level)
  waiting for transfers between devices: 239 us -> 173 us
  blocking collectives: 61.2 us -> 98.7 us
  local copies, waits for them, and re-layouts: 15 us -> 29.1 us
  starting transfers between devices: 11.9 us -> 23.3 us
    all_gather x2, waiting for transfers between devices: 135 us -> 47.4 us  [by_heads(): spread_heads = lax.all_gather(attended[group], ctx, axis=0)]
    ppermute x0 -> x8, waiting for transfers between devices: none -> 50.3 us  [plane_step(): return lax.ppermute(block, 'exp', [(i, i ^ step) for i in range(count)])]
    all_gather x0 -> x2, blocking collectives: none -> 49.9 us  [by_heads(): plane = lax.all_gather(scaled, 'z', axis=0)]
    all_to_all x1 -> x2, waiting for transfers between devices: 23.6 us -> 9.97 us  [by_heads(): lax.all_to_all(pieces, 'exp', split_axis=0, concat_axis=0, tiled=True)]
    all_to_all x1, blocking collectives: 44.9 us -> 36.1 us  [by_heads(): lax.all_to_all(outs[1], 'exp', split_axis=0, concat_axis=0, tiled=True)]
    reduce_scatter x2, waiting for transfers between devices: 20.9 us -> 12.3 us  [the longest x1 12.3 us: by_heads(): second = lax.psum_scatter(second, 'z', scatter_dimension=0, tiled=True)]
    ppermute x0 -> x8, starting transfers between devices: none -> 8.2 us  [plane_step(): return lax.ppermute(block, 'exp', [(i, i ^ step) for i in range(count)])]
    ppermute x4 -> x5, waiting for transfers between devices: 11.3 us -> 3.4 us  [sibling(): return lax.ppermute(block, 'core', [(0, 1), (1, 0)])]
  transfers between devices with their start and end apart: 10 -> 20, of which waited for: 9 -> 13; matrix products, arithmetic and copies ran while one was open for 2% -> 7% of each run, Pallas kernels for 5% -> 7%
where the time goes in v4:
time: 398 us; the launch traced here: 397 us
  waiting for transfers between devices  173 us (43%)
  blocking collectives  98.7 us (25%)
  Pallas kernels  36.5 us (9%)
  local copies, waits for them, and re-layouts  29.1 us (7%)
  starting transfers between devices  23.3 us (6%)
  between operations  13.7 us (3%)
  other arithmetic  12.1 us (3%)
  matrix products  10.9 us (3%)
    ppermute x8, waiting for transfers between devices, plane_step(): return lax.ppermute(block, 'exp', [(i, i ^ step) for i in range(count)])  50.3 us
    all_gather x2, blocking collectives, by_heads(): plane = lax.all_gather(scaled, 'z', axis=0)  49.9 us
    all_to_all x1, waiting for transfers between devices, by_heads(): moved = lax.all_to_all(packed, ctx, split_axis=0, concat_axis=0, tiled=True)  48.7 us
    all_gather x2, waiting for transfers between devices, by_heads(): spread_heads = lax.all_gather(attended[group], ctx, axis=0)  47.4 us
    all_to_all x1, blocking collectives, by_heads(): lax.all_to_all(outs[1], 'exp', split_axis=0, concat_axis=0, tiled=True)  36.1 us
    pallas_call x2, Pallas kernels, run_expert(): pl.pallas_call(functools.partial(expert_kernel, exp_dim), grid_spec=pltpu...  20.6 us
    unnamed x54, local copies, waits for them, and re-layouts  17.3 us
    all_to_all x1, blocking collectives, by_heads(): lax.all_to_all(first.reshape(exp_count, half, model_width), 'exp', split_...  12.7 us
  transfers between devices with their start and end apart: 20, of which 13 were waited for; matrix products, arithmetic and copies ran while one was open for 7% of the time, Pallas kernels for 7%

profile of v4, /device:TPU:0, one launch (start us, length us, event | category | flops | bytes accessed | tf_op | source)
XLA Modules:
  0.0 397.2 jit_solution(5930172840074059394)
XLA Ops:
  15.9 6.3 %all-to-all-start = ((bf16[8,512,256]{2,1,0:T(8,128)(2,1)}), bf16[8,512,256]{2,1,0:T(8,128)(2,1)S(1)}, u32[]{:S(2)}, u32[]{:S(2)}) async-start(bf16[8,512,256]{2,1,0:T(8,128)(2,1)} %bitcast_dynamic-update-slice_fusion.3), calls=%async_computation | async-start | bytes 4194304 | tf_op jit(solution)/shard_map/all_to_all | solution.py:523
  22.6 48.7 %all-to-all-done.moved = bf16[8,512,256]{2,1,0:T(8,128)(2,1)S(1)} async-done(((bf16[8,512,256]{2,1,0:T(8,128)(2,1)}), bf16[8,512,256]{2,1,0:T(8,128)(2,1)S(1)}, u32[]{:S(2)}, u32[]{:S(2)}) %all-to-all-start) | async-done | bytes 2097184 | tf_op jit(solution)/shard_map/all_to_all | solution.py:523
  72.1 5.3 %attend.1 = bf16[2,512,256]{2,1,0:T(8,128)(2,1)S(1)} custom-call(bf16[8,512,256]{2,1,0:T(8,128)(2,1)S(1)} %all-to-all-done.moved, f32[8,1024]{1,0:T(8,128)S(1)} %tile.12.taps, f32[1024,4]{1,0:T(8,128)S(1)} %copy.95.gates), custom_call_target="tpu_custom_call" | custom-call | tf_op jit(solution)/shard_map/attend/pallas_call | solution.py:298
  79.6 26.8 %all-gather.5.cloned.1.call-done = bf16[8,512,256]{2,1,0:T(8,128)(2,1)} async-done(((bf16[1,512,256]{2,1,0:T(8,128)(2,1)}), bf16[8,512,256]{2,1,0:T(8,128)(2,1)}) %all-gather.5.cloned.1.call-update) | async-done | bytes 2097168 | tf_op jit(solution)/shard_map/all_gather | solution.py:549
  106.4 5.9 %bitcast_convert_fusion = bf16[512,896]{1,0:T(8,128)(2,1)} fusion(bf16[8,512,256]{2,1,0:T(8,128)(2,1)} %all-gather.5.cloned.1.call-done, bf16[8,256,896]{2,1,0:T(8,128)(2,1)} %bitcast.152), kind=kOutput, calls=%fused_computation | convolution fusion | flops 1879506944 | bytes 6684672 | tf_op jit(solution)/shard_map/csk,ckd->sd/dot_general | solution.py:550
  112.4 3.6 all-to-all-start.3
  116.0 20.6 %all-gather.3.cloned.1.call-done = bf16[8,512,256]{2,1,0:T(8,128)(2,1)} async-done(((bf16[1,512,256]{2,1,0:T(8,128)(2,1)}), bf16[8,512,256]{2,1,0:T(8,128)(2,1)}) %all-gather.3.cloned.1.call-update) | async-done | bytes 2097168 | tf_op jit(solution)/shard_map/all_gather | solution.py:549
  136.6 5.0 %bitcast_convert_fusion.1 = bf16[512,896]{1,0:T(8,128)(2,1)S(1)} fusion(bf16[8,512,256]{2,1,0:T(8,128)(2,1)} %all-gather.3.cloned.1.call-done, bf16[8,256,896]{2,1,0:T(8,128)(2,1)} %bitcast.153), kind=kOutput, calls=%fused_computation.1 | convolution fusion | flops 1879506944 | bytes 6684672 | tf_op jit(solution)/shard_map/csk,ckd->sd/dot_general | solution.py:550
  143.7 3.6 all-to-all-start.1
  151.4 10.0 %all-to-all-done.1 = bf16[4,144,896]{2,1,0:T(8,128)(2,1)S(1)} async-done(((bf16[4,144,896]{2,1,0:T(8,128)(2,1)}), bf16[4,144,896]{2,1,0:T(8,128)(2,1)S(1)}, u32[]{:S(2)}, u32[]{:S(2)}) %all-to-all-start.1) | async-done | bytes 1032224 | tf_op jit(solution)/shard_map/all_to_all | solution.py:561
  166.0 19.7 %all_gather.13.own = bf16[4,64,1792]{2,1,0:T(8,128)(2,1)S(1)} all-gather(bf16[1,64,1792]{2,1,0:T(8,128)(2,1)S(1)} %get-tuple-element.17), channel_id=1, replica_groups=mesh['z'=4,'core'=2,'exp'=4] {'z'}, dimensions={0}, use_global_device_ids=true | all-gather | bytes 1146880 | tf_op jit(solution)/shard_map/all_gather | solution.py:577
  190.0 17.0 %collective-permute-done.2.across = bf16[4,64,1792]{2,1,0:T(8,128)(2,1)S(1)} collective-permute-done((bf16[4,64,1792]{2,1,0:T(8,128)(2,1)S(1)}, bf16[4,64,1792]{2,1,0:T(8,128)(2,1)S(1)}, u32[]{:S(2)}, u32[]{:S(2)}) %collective-permute-start.2) | collective-permute-done | bytes 917536 | tf_op jit(solution)/shard_map/ppermute | solution.py:452
  213.2 5.5 %collective-permute-done.4.far_b = bf16[2,64,1792]{2,1,0:T(8,128)(2,1)S(1)} collective-permute-done((bf16[2,64,1792]{2,1,0:T(8,128)(2,1)}, bf16[2,64,1792]{2,1,0:T(8,128)(2,1)S(1)}, u32[]{:S(2)}, u32[]{:S(2)}) %collective-permute-start.4) | collective-permute-done | bytes 458784 | tf_op jit(solution)/shard_map/ppermute | solution.py:452
  224.9 10.3 %expert.2 = bf16[2,4,4,16,256]{4,3,2,1,0:T(8,128)(2,1)S(1)} custom-call(s32[2]{0:T(128)S(1)} %pad_add_fusion.spots, bf16[4,64,1792]{2,1,0:T(8,128)(2,1)S(1)} %all_gather.13.own, bf16[4,64,1792]{2,1,0:T(8,128)(2,1)S(1)} %collective-permute-done.1.along, bf16[4,64,1792]{2,1,0:T(8,128)(2,1)S(1)} %collective-permute-done.2.across, ...), custom_call_target="tpu_custom_call" | custom-call | flops 3758096384 | bytes 18350080 | tf_op jit(solution)/shard_map/expert/pallas_call | solution.py:362
  235.2 5.4 %down.2 = bf16[4,4,16,7168]{3,2,1,0:T(8,128)(2,1)S(1)} custom-call(s32[2]{0:T(128)S(1)} %pad_add_fusion.spots, bf16[2,256,256]{2,1,0:T(8,128)(2,1)S(1)} %bitcast.119, bf16[256,7168]{1,0:T(8,128)(2,1)S(1)} %bitcast.116, bf16[256,7168]{1,0:T(8,128)(2,1)} %collective-permute-done.7.down_v, f32[4,16,1792]{2,1,0:T(8,128)S(1)} %pad_maximum_fusion.1.hidden), custom_call_target="tpu_custom_call" | custom-call | flops 1879048192 | bytes 11010048 | tf_op jit(solution)/shard_map/down/pallas_call | solution.py:422
  243.4 30.2 %all_gather.15.own = bf16[4,64,1792]{2,1,0:T(8,128)(2,1)S(1)} all-gather(bf16[1,64,1792]{2,1,0:T(8,128)(2,1)S(1)} %copy-done.17), channel_id=1, replica_groups=mesh['z'=4,'core'=2,'exp'=4] {'z'}, dimensions={0}, use_global_device_ids=true | all-gather | bytes 1146880 | tf_op jit(solution)/shard_map/all_gather | solution.py:577
  274.9 17.0 %collective-permute-done.10.across = bf16[4,64,1792]{2,1,0:T(8,128)(2,1)S(1)} collective-permute-done((bf16[4,64,1792]{2,1,0:T(8,128)(2,1)S(1)}, bf16[4,64,1792]{2,1,0:T(8,128)(2,1)S(1)}, u32[]{:S(2)}, u32[]{:S(2)}) %collective-permute-start.10) | collective-permute-done | bytes 917536 | tf_op jit(solution)/shard_map/ppermute | solution.py:452
  296.8 4.6 %collective-permute-done.12.far_b = bf16[2,64,1792]{2,1,0:T(8,128)(2,1)S(1)} collective-permute-done((bf16[2,64,1792]{2,1,0:T(8,128)(2,1)}, bf16[2,64,1792]{2,1,0:T(8,128)(2,1)S(1)}, u32[]{:S(2)}, u32[]{:S(2)}) %collective-permute-start.12) | collective-permute-done | bytes 458784 | tf_op jit(solution)/shard_map/ppermute | solution.py:452
  308.0 10.3 %expert.3 = bf16[2,4,4,16,256]{4,3,2,1,0:T(8,128)(2,1)S(1)} custom-call(s32[2]{0:T(128)S(1)} %pad_add_fusion.spots, bf16[4,64,1792]{2,1,0:T(8,128)(2,1)S(1)} %all_gather.15.own, bf16[4,64,1792]{2,1,0:T(8,128)(2,1)S(1)} %collective-permute-done.9.along, bf16[4,64,1792]{2,1,0:T(8,128)(2,1)S(1)} %collective-permute-done.10.across, ...), custom_call_target="tpu_custom_call" | custom-call | flops 3758096384 | bytes 18350080 | tf_op jit(solution)/shard_map/expert/pallas_call | solution.py:362
  318.3 5.4 %down.3 = bf16[4,4,16,7168]{3,2,1,0:T(8,128)(2,1)S(1)} custom-call(s32[2]{0:T(128)S(1)} %pad_add_fusion.spots, bf16[2,256,256]{2,1,0:T(8,128)(2,1)S(1)} %bitcast.118, bf16[256,7168]{1,0:T(8,128)(2,1)S(1)} %bitcast.117, bf16[256,7168]{1,0:T(8,128)(2,1)} %collective-permute-done.7.down_v, f32[4,16,1792]{2,1,0:T(8,128)S(1)} %pad_maximum_fusion.2.hidden), custom_call_target="tpu_custom_call" | custom-call | flops 1879048192 | bytes 11010048 | tf_op jit(solution)/shard_map/down/pallas_call | solution.py:422
  323.7 36.1 %all_to_all.25 = bf16[4,4,16,7168]{3,2,1,0:T(8,128)(2,1)} all-to-all(bf16[4,4,16,7168]{3,2,1,0:T(8,128)(2,1)S(1)} %down.3), channel_id=1, replica_groups=mesh['z'=4,'core'=2,'exp'=4] {'exp'}, dimensions={0} | all-to-all | bytes 7340032 | tf_op jit(solution)/shard_map/all_to_all | solution.py:608
  359.8 3.8 reduce_sum.68
  363.7 12.7 %all_to_all.26 = bf16[4,16,7168]{2,1,0:T(8,128)(2,1)S(1)} all-to-all(bf16[4,16,7168]{2,1,0:T(8,128)(2,1)} %bitcast.134), channel_id=1, replica_groups=mesh['z'=4,'core'=2,'exp'=4] {'exp'}, dimensions={0} | all-to-all | bytes 1835008 | tf_op jit(solution)/shard_map/all_to_all | solution.py:603
  376.6 12.3 %reduce-scatter.5.cloned.1.call-done = bf16[1,16,7168]{2,1,0:T(8,128)(2,1)} async-done(((bf16[4,16,7168]{2,1,0:T(8,128)(2,1)}), bf16[1,16,7168]{2,1,0:T(8,128)(2,1)}) %reduce-scatter.5.cloned.1.call-update) | async-done | bytes 229392 | tf_op jit(solution)/shard_map/reduce_scatter | solution.py:610
  (152 shorter events, 57.4 us)
Async XLA Ops:
  15.9 55.4 %all-to-all-start = ((bf16[8,512,256]{2,1,0:T(8,128)(2,1)}), bf16[8,512,256]{2,1,0:T(8,128)(2,1)S(1)}, u32[]{:S(2)}, u32[]{:S(2)}) async-start(bf16[8,512,256]{2,1,0:T(8,128)(2,1)} %bitcast_dynamic-update-slice_fusion.3), calls=%async_computation | async-start | bytes 4194304 | tf_op jit(solution)/shard_map/all_to_all | solution.py:523
  22.2 84.2 %all-gather.5.cloned.1.call-start = ((), (), s32[]{:S(2)}) async-start(), calls=%async_computation.9 | async-start | bytes 2359296 | tf_op jit(solution)/shard_map/all_gather | solution.py:549
  78.2 58.4 %all-gather.3.cloned.1.call-start = ((), (), s32[]{:S(2)}) async-start(), calls=%async_computation.7 | async-start | bytes 2359296 | tf_op jit(solution)/shard_map/all_gather | solution.py:549
  112.4 30.4 %all-to-all-start.3 = ((bf16[4,128,896]{2,1,0:T(8,128)(2,1)}), bf16[4,128,896]{2,1,0:T(8,128)(2,1)S(1)}, u32[]{:S(2)}, u32[]{:S(2)}) async-start(bf16[4,128,896]{2,1,0:T(8,128)(2,1)} %bitcast.135), calls=%async_computation.4 | async-start | bytes 1835008 | tf_op jit(solution)/shard_map/all_to_all | solution.py:561
  143.7 17.6 %all-to-all-start.1 = ((bf16[4,144,896]{2,1,0:T(8,128)(2,1)}), bf16[4,144,896]{2,1,0:T(8,128)(2,1)S(1)}, u32[]{:S(2)}, u32[]{:S(2)}) async-start(bf16[4,144,896]{2,1,0:T(8,128)(2,1)} %pad_maximum_fusion), calls=%async_computation.1 | async-start | bytes 2064384 | tf_op jit(solution)/shard_map/all_to_all | solution.py:561
  147.3 216.3 %reduce-scatter.3.cloned.1.call-start = ((), (), s32[]{:S(2)}) async-start(), calls=%async_computation.8 | async-start | bytes 4587520 | tf_op jit(solution)/shard_map/reduce_scatter | solution.py:597
  147.5 65.7 %collective-permute-start.5 = (bf16[7168,256]{1,0:T(8,128)(2,1)}, bf16[7168,256]{1,0:T(8,128)(2,1)}, u32[]{:S(2)}, u32[]{:S(2)}) collective-permute-start(bf16[7168,256]{1,0:T(8,128)(2,1)} %bitcast.108), channel_id=1, source_target_pairs={{0,4},{4,0},{1,5},{5,1},{2,6},{6,2},{3,7},{7,3},{8,12},{12,8},{9,1... | collective-permute-start | bytes 11010056 | tf_op jit(solution)/shard_map/ppermute | solution.py:447
  147.7 65.4 %collective-permute-start.6 = (bf16[7168,256]{1,0:T(8,128)(2,1)}, bf16[7168,256]{1,0:T(8,128)(2,1)}, u32[]{:S(2)}, u32[]{:S(2)}) collective-permute-start(bf16[7168,256]{1,0:T(8,128)(2,1)} %bitcast.111), channel_id=1, source_target_pairs={{0,4},{4,0},{1,5},{5,1},{2,6},{6,2},{3,7},{7,3},{8,12},{12,8},{9,1... | collective-permute-start | bytes 11010056 | tf_op jit(solution)/shard_map/ppermute | solution.py:447
  148.0 87.2 %collective-permute-start.7 = (bf16[256,7168]{1,0:T(8,128)(2,1)}, bf16[256,7168]{1,0:T(8,128)(2,1)}, u32[]{:S(2)}, u32[]{:S(2)}) collective-permute-start(bf16[256,7168]{1,0:T(8,128)(2,1)} %bitcast.115), channel_id=1, source_target_pairs={{0,4},{4,0},{1,5},{5,1},{2,6},{6,2},{3,7},{7,3},{8,12},{12,8},{9,1... | collective-permute-start | bytes 11010056 | tf_op jit(solution)/shard_map/ppermute | solution.py:447
  151.0 10.6 %collective-permute-start.8 = (f32[4,16,896]{2,1,0:T(8,128)S(1)}, f32[4,16,896]{2,1,0:T(8,128)S(1)}, u32[]{:S(2)}, u32[]{:S(2)}) collective-permute-start(f32[4,16,896]{2,1,0:T(8,128)S(1)} %dynamic-slice_bitcast_fusion), channel_id=1, source_target_pairs={{0,4},{4,0},{1,5},{5,1},{2,6},{6,2},{3,7},{7,3},{8,12},{12,8},{9,1... | collective-permute-start | bytes 688136 | tf_op jit(solution)/shard_map/ppermute | solution.py:447
  161.5 3.6 collective-permute-start
  161.7 24.0 %copy-start.13 = (f32[4,16,896]{2,1,0:T(8,128)}, f32[4,16,896]{2,1,0:T(8,128)S(1)}, u32[]{:S(2)}) copy-start(f32[4,16,896]{2,1,0:T(8,128)S(1)} %get-tuple-element.9) | copy-start | bytes 688132
  161.7 25.8 %copy-start.14 = (f32[4,16,896]{2,1,0:T(8,128)}, f32[4,16,896]{2,1,0:T(8,128)S(1)}, u32[]{:S(2)}) copy-start(f32[4,16,896]{2,1,0:T(8,128)S(1)} %get-tuple-element.10) | copy-start | bytes 688132
  165.1 22.3 %copy-start.15 = (f32[4,16,896]{2,1,0:T(8,128)}, f32[4,16,896]{2,1,0:T(8,128)S(1)}, u32[]{:S(2)}) copy-start(f32[4,16,896]{2,1,0:T(8,128)S(1)} %get-tuple-element.7) | copy-start | bytes 688132
  185.7 21.4 %collective-permute-start.2 = (bf16[4,64,1792]{2,1,0:T(8,128)(2,1)S(1)}, bf16[4,64,1792]{2,1,0:T(8,128)(2,1)S(1)}, u32[]{:S(2)}, u32[]{:S(2)}) collective-permute-start(bf16[4,64,1792]{2,1,0:T(8,128)(2,1)S(1)} %all_gather.13.own), channel_id=1, source_target_pairs={{0,2},{1,3},{2,0},{3,1},{4,6},{5,7},{6,4},{7,5},{8,10},{9,11},{10,... | collective-permute-start | bytes 2752520 | tf_op jit(solution)/shard_map/ppermute | solution.py:452
  187.5 22.0 %collective-permute-start.1 = (bf16[4,64,1792]{2,1,0:T(8,128)(2,1)S(1)}, bf16[4,64,1792]{2,1,0:T(8,128)(2,1)S(1)}, u32[]{:S(2)}, u32[]{:S(2)}) collective-permute-start(bf16[4,64,1792]{2,1,0:T(8,128)(2,1)S(1)} %all_gather.13.own), channel_id=1, source_target_pairs={{0,1},{1,0},{2,3},{3,2},{4,5},{5,4},{6,7},{7,6},{8,9},{9,8},{10,11... | collective-permute-start | bytes 2752520 | tf_op jit(solution)/shard_map/ppermute | solution.py:452
  207.9 10.8 %collective-permute-start.4 = (bf16[2,64,1792]{2,1,0:T(8,128)(2,1)}, bf16[2,64,1792]{2,1,0:T(8,128)(2,1)S(1)}, u32[]{:S(2)}, u32[]{:S(2)}) collective-permute-start(bf16[2,64,1792]{2,1,0:T(8,128)(2,1)} %slice.86), channel_id=1, source_target_pairs={{0,1},{1,0},{2,3},{3,2},{4,5},{5,4},{6,7},{7,6},{8,9},{9,8},{10,11... | collective-permute-start | bytes 1376264 | tf_op jit(solution)/shard_map/ppermute | solution.py:452
  210.3 10.5 %collective-permute-start.3 = (bf16[2,64,1792]{2,1,0:T(8,128)(2,1)}, bf16[2,64,1792]{2,1,0:T(8,128)(2,1)}, u32[]{:S(2)}, u32[]{:S(2)}) collective-permute-start(bf16[2,64,1792]{2,1,0:T(8,128)(2,1)} %slice.85), channel_id=1, source_target_pairs={{0,2},{1,3},{2,0},{3,1},{4,6},{5,7},{6,4},{7,5},{8,10},{9,11},{10,... | collective-permute-start | bytes 1376264 | tf_op jit(solution)/shard_map/ppermute | solution.py:452
  242.5 146.4 %reduce-scatter.5.cloned.1.call-start = ((), (), s32[]{:S(2)}) async-start(), calls=%async_computation.10 | async-start | bytes 1146880 | tf_op jit(solution)/shard_map/reduce_scatter | solution.py:610
  273.6 18.3 %collective-permute-start.10 = (bf16[4,64,1792]{2,1,0:T(8,128)(2,1)S(1)}, bf16[4,64,1792]{2,1,0:T(8,128)(2,1)S(1)}, u32[]{:S(2)}, u32[]{:S(2)}) collective-permute-start(bf16[4,64,1792]{2,1,0:T(8,128)(2,1)S(1)} %all_gather.15.own), channel_id=1, source_target_pairs={{0,2},{1,3},{2,0},{3,1},{4,6},{5,7},{6,4},{7,5},{8,10},{9,11},{10,... | collective-permute-start | bytes 2752520 | tf_op jit(solution)/shard_map/ppermute | solution.py:452
  274.9 19.4 %collective-permute-start.9 = (bf16[4,64,1792]{2,1,0:T(8,128)(2,1)S(1)}, bf16[4,64,1792]{2,1,0:T(8,128)(2,1)S(1)}, u32[]{:S(2)}, u32[]{:S(2)}) collective-permute-start(bf16[4,64,1792]{2,1,0:T(8,128)(2,1)S(1)} %all_gather.15.own), channel_id=1, source_target_pairs={{0,1},{1,0},{2,3},{3,2},{4,5},{5,4},{6,7},{7,6},{8,9},{9,8},{10,11... | collective-permute-start | bytes 2752520 | tf_op jit(solution)/shard_map/ppermute | solution.py:452
  292.7 8.7 %collective-permute-start.12 = (bf16[2,64,1792]{2,1,0:T(8,128)(2,1)}, bf16[2,64,1792]{2,1,0:T(8,128)(2,1)S(1)}, u32[]{:S(2)}, u32[]{:S(2)}) collective-permute-start(bf16[2,64,1792]{2,1,0:T(8,128)(2,1)} %slice.93), channel_id=1, source_target_pairs={{0,1},{1,0},{2,3},{3,2},{4,5},{5,4},{6,7},{7,6},{8,9},{9,8},{10,11... | collective-permute-start | bytes 1376264 | tf_op jit(solution)/shard_map/ppermute | solution.py:452
  295.1 8.8 %collective-permute-start.11 = (bf16[2,64,1792]{2,1,0:T(8,128)(2,1)}, bf16[2,64,1792]{2,1,0:T(8,128)(2,1)}, u32[]{:S(2)}, u32[]{:S(2)}) collective-permute-start(bf16[2,64,1792]{2,1,0:T(8,128)(2,1)} %slice.92), channel_id=1, source_target_pairs={{0,2},{1,3},{2,0},{3,1},{4,6},{5,7},{6,4},{7,5},{8,10},{9,11},{10,... | collective-permute-start | bytes 1376264 | tf_op jit(solution)/shard_map/ppermute | solution.py:452
  363.6 27.0 %copy-start.1 = (f32[2,32,16]{1,2,0:T(8,128)S(1)}, f32[2,32,16]{1,2,0:T(8,128)}, u32[]{:S(2)}) copy-start(f32[2,32,16]{1,2,0:T(8,128)} %param.17) | copy-start | bytes 12292
  (17 other events, 89.7 us)
Sparse Core Ops, SparseCore 0:
  78.4 28.0 all-gather.4
  108.0 28.5 all-gather.2
  242.6 77.5 reduce-scatter.2
  363.8 25.0 reduce-scatter.4

commit v5 on v4

--- a/solution.py
+++ b/solution.py
@@ -544,26 +544,19 @@
     gain = lax.dynamic_slice_in_dim(ffn_gain, chip_index * 2 * cols, 2 * cols, 0)
     spots = jnp.stack([chip_index, exp_index]).astype(jnp.int32)
     group_tokens = ctx_count * half
-    hidden, blocks = [], []
-    for group in range(2):
-        spread_heads = lax.all_gather(attended[group], ctx, axis=0)
+    def project(spread_heads):
         pieces = jnp.einsum(
             "csk,ckd->sd",
             spread_heads,
             out_proj.reshape(ctx_count, width, cols),
             preferred_element_type=jnp.float32,
         ).astype(jnp.bfloat16)
-        pieces = pieces.reshape(exp_count, group_tokens, cols)
-        if group == 0:
-            pieces = jnp.concatenate([pieces, table], 1)
-        else:
-            pieces, _ = lax.optimization_barrier((pieces, scaled))
-        pieces = lax.all_to_all(pieces, "exp", split_axis=0, concat_axis=0, tiled=True)
-        if group == 0:
-            route = pieces[:, group_tokens:].reshape(exp_count, -1)[:, : 2 * chip_count * share]
-            route = jnp.sum(
-                route.reshape(exp_count, 2, chip_count, 2, half).astype(jnp.float32), axis=1
-            )
+        return pieces.reshape(exp_count, group_tokens, cols)
+
+    def exchange(pieces):
+        return lax.all_to_all(pieces, "exp", split_axis=0, concat_axis=0, tiled=True)
+
+    def settle(pieces, group):
         sums = jnp.sum(pieces[:, :group_tokens].astype(jnp.float32), axis=0)
         own_rows = residual.reshape(ctx_count, 2, half, cols)[:, group]
         sums = sums.reshape(ctx_count, half, cols) + own_rows.astype(jnp.float32)
@@ -574,12 +567,32 @@
             [jnp.where(core_index == 0, kept, given), jnp.where(core_index == 0, given, kept)], 2
         )
         scaled = (sums * gain).astype(jnp.bfloat16).reshape(chip_count * half, 2 * cols)
-        plane = lax.all_gather(scaled, "z", axis=0)
-        along, across = plane_step(plane, 1), plane_step(plane, 2)
-        far_a = plane_step(along[: chip_count // 2], 2)
-        far_b = plane_step(across[chip_count // 2 :], 1)
-        hidden.append(sums)
-        blocks.append((plane, along, across, far_a, far_b))
+        return sums, scaled
+
+    middle = chip_count // 2
+    spread_first = lax.all_gather(attended[0], ctx, axis=0)
+    spread_first, later = lax.optimization_barrier((spread_first, attended[1]))
+    spread_second = lax.all_gather(later, ctx, axis=0)
+    pieces = exchange(jnp.concatenate([project(spread_first), table], 1))
+    route = pieces[:, group_tokens:].reshape(exp_count, -1)[:, : 2 * chip_count * share]
+    route = jnp.sum(
+        route.reshape(exp_count, 2, chip_count, 2, half).astype(jnp.float32), axis=1
+    )
+    sums_first, scaled_first = settle(pieces, 0)
+    pieces = project(spread_second)
+    pieces, scaled_first = lax.optimization_barrier((pieces, scaled_first))
+    sums_second, scaled_second = settle(exchange(pieces), 1)
+    plane_first = lax.all_gather(scaled_first, "z", axis=0)
+    along, across = plane_step(plane_first, 1), plane_step(plane_first, 2)
+    plane_second = lax.all_gather(scaled_second, "z", axis=0)
+    along, across, plane_second = lax.optimization_barrier((along, across, plane_second))
+    far_a, far_b = plane_step(along[:middle], 2), plane_step(across[middle:], 1)
+    far_a, far_b, plane_second = lax.optimization_barrier((far_a, far_b, plane_second))
+    blocks = [(plane_first, along, across, far_a, far_b)]
+    along, across = plane_step(plane_second, 1), plane_step(plane_second, 2)
+    far_a, far_b = plane_step(along[:middle], 2), plane_step(across[middle:], 1)
+    blocks.append((plane_second, along, across, far_a, far_b))
+    hidden = [sums_first, sums_second]
 
     weights = (expert_gate[0], expert_up[0], other_gate, other_up)
     outs = []

time: 398 us -> 371 us (0.932)
  waiting for transfers between devices: 173 us -> 151 us
  blocking collectives: 98.7 us -> 93.8 us
    ppermute x8, waiting for transfers between devices: 50.3 us -> 31.6 us  [plane_step(): return lax.ppermute(block, 'exp', [(i, i ^ step) for i in range(count)])]
    all_to_all x2, waiting for transfers between devices: 9.97 us -> 24.4 us  [exchange(): lax.all_to_all(pieces, 'exp', split_axis=0, concat_axis=0, tiled=True)]
    all_gather x2, waiting for transfers between devices: 47.4 us -> 33.9 us  [the longest x1 28.1 us: by_heads(): spread_first = lax.all_gather(attended[0], ctx, axis=0)]
    all_gather x2, blocking collectives: 49.9 us -> 39.9 us  [the longest x1 20 us: by_heads(): plane_second = lax.all_gather(scaled_second, 'z', axis=0)]
    all_to_all x1, blocking collectives: 36.1 us -> 41.2 us  [by_heads(): lax.all_to_all(outs[1], 'exp', split_axis=0, concat_axis=0, tiled=True)]
    unnamed x54 -> x50, local copies, waits for them, and re-layouts: 17.3 us -> 17.3 us
where the time goes in v5:
time: 371 us; the launch traced here: 369 us
  waiting for transfers between devices  151 us (41%)
  blocking collectives  93.8 us (25%)
  Pallas kernels  36.6 us (10%)
  local copies, waits for them, and re-layouts  29 us (8%)
  starting transfers between devices  22.9 us (6%)
  between operations  13.7 us (4%)
  other arithmetic  11.3 us (3%)
  matrix products  10.9 us (3%)
    all_to_all x1, waiting for transfers between devices, by_heads(): moved = lax.all_to_all(packed, ctx, split_axis=0, concat_axis=0, tiled=True)  48.7 us
    all_to_all x1, blocking collectives, by_heads(): lax.all_to_all(outs[1], 'exp', split_axis=0, concat_axis=0, tiled=True)  41.2 us
    ppermute x8, waiting for transfers between devices, plane_step(): return lax.ppermute(block, 'exp', [(i, i ^ step) for i in range(count)])  31.6 us
    all_gather x1, waiting for transfers between devices, by_heads(): spread_first = lax.all_gather(attended[0], ctx, axis=0)  28.1 us
    all_to_all x2, waiting for transfers between devices, exchange(): lax.all_to_all(pieces, 'exp', split_axis=0, concat_axis=0, tiled=True)  24.4 us
    pallas_call x2, Pallas kernels, run_expert(): pl.pallas_call(functools.partial(expert_kernel, exp_dim), grid_spec=pltpu...  20.7 us
    all_gather x1, blocking collectives, by_heads(): plane_second = lax.all_gather(scaled_second, 'z', axis=0)  20 us
    all_gather x1, blocking collectives, by_heads(): plane_first = lax.all_gather(scaled_first, 'z', axis=0)  20 us
  transfers between devices with their start and end apart: 20, of which 13 were waited for; matrix products, arithmetic and copies ran while one was open for 7% of the time, Pallas kernels for 7%

profile of v5, /device:TPU:0, one launch (start us, length us, event | category | flops | bytes accessed | tf_op | source)
XLA Modules:
  0.0 369.3 jit_solution(4597557568953280198)
XLA Ops:
  15.8 6.3 %all-to-all-start = ((bf16[8,512,256]{2,1,0:T(8,128)(2,1)}), bf16[8,512,256]{2,1,0:T(8,128)(2,1)S(1)}, u32[]{:S(2)}, u32[]{:S(2)}) async-start(bf16[8,512,256]{2,1,0:T(8,128)(2,1)} %bitcast_dynamic-update-slice_fusion.3), calls=%async_computation | async-start | bytes 4194304 | tf_op jit(solution)/shard_map/all_to_all | solution.py:523
  22.5 48.7 %all-to-all-done.moved = bf16[8,512,256]{2,1,0:T(8,128)(2,1)S(1)} async-done(((bf16[8,512,256]{2,1,0:T(8,128)(2,1)}), bf16[8,512,256]{2,1,0:T(8,128)(2,1)S(1)}, u32[]{:S(2)}, u32[]{:S(2)}) %all-to-all-start) | async-done | bytes 2097184 | tf_op jit(solution)/shard_map/all_to_all | solution.py:523
  72.0 5.3 %attend.1 = bf16[2,512,256]{2,1,0:T(8,128)(2,1)S(1)} custom-call(bf16[8,512,256]{2,1,0:T(8,128)(2,1)S(1)} %all-to-all-done.moved, f32[8,1024]{1,0:T(8,128)S(1)} %tile.12.taps, f32[1024,4]{1,0:T(8,128)S(1)} %copy.95.gates), custom_call_target="tpu_custom_call" | custom-call | tf_op jit(solution)/shard_map/attend/pallas_call | solution.py:298
  78.2 28.1 %all-gather.5.cloned.1.call-done = bf16[8,512,256]{2,1,0:T(8,128)(2,1)} async-done(((bf16[1,512,256]{2,1,0:T(8,128)(2,1)}), bf16[8,512,256]{2,1,0:T(8,128)(2,1)}) %all-gather.5.cloned.1.call-update) | async-done | bytes 2097168 | tf_op jit(solution)/shard_map/all_gather | solution.py:573
  107.0 5.0 %bitcast_convert_fusion = bf16[512,896]{1,0:T(8,128)(2,1)S(1)} fusion(bf16[8,512,256]{2,1,0:T(8,128)(2,1)} %all-gather.5.cloned.1.call-done, bf16[8,256,896]{2,1,0:T(8,128)(2,1)} %bitcast.158), kind=kOutput, calls=%fused_computation | convolution fusion | flops 1879506944 | bytes 6684672 | tf_op jit(solution)/shard_map/csk,ckd->sd/dot_general | solution.py:548
  113.1 3.6 all-to-all-start.1
  119.1 11.7 %all-to-all-done.1 = bf16[4,144,896]{2,1,0:T(8,128)(2,1)S(1)} async-done(((bf16[4,144,896]{2,1,0:T(8,128)(2,1)}), bf16[4,144,896]{2,1,0:T(8,128)(2,1)S(1)}, u32[]{:S(2)}, u32[]{:S(2)}) %all-to-all-start.1) | async-done | bytes 1032224 | tf_op jit(solution)/shard_map/all_to_all | solution.py:557
  132.6 5.8 %all-gather.7.cloned.1.call-done = bf16[4096,256]{1,0:T(8,128)(2,1)} async-done(((bf16[512,256]{1,0:T(8,128)(2,1)}), bf16[4096,256]{1,0:T(8,128)(2,1)}) %all-gather.7.cloned.1.call-update) | async-done | bytes 2097168 | tf_op jit(solution)/shard_map/all_gather | solution.py:575
  138.4 5.9 %bitcast_convert_fusion.1 = bf16[512,896]{1,0:T(8,128)(2,1)} fusion(bf16[8,512,256]{2,1,0:T(8,128)(2,1)} %bitcast.160, bf16[8,256,896]{2,1,0:T(8,128)(2,1)} %bitcast.159), kind=kOutput, calls=%fused_computation.1 | convolution fusion | flops 1879506944 | bytes 6684672 | tf_op jit(solution)/shard_map/csk,ckd->sd/dot_general | solution.py:548
  144.4 3.7 all-to-all-start.2
  148.2 12.7 %all-to-all-done.2 = bf16[4,128,896]{2,1,0:T(8,128)(2,1)S(1)} async-done(((bf16[4,128,896]{2,1,0:T(8,128)(2,1)}), bf16[4,128,896]{2,1,0:T(8,128)(2,1)S(1)}, u32[]{:S(2)}, u32[]{:S(2)}) %all-to-all-start.2) | async-done | bytes 917536 | tf_op jit(solution)/shard_map/all_to_all | solution.py:557
  161.2 20.0 %all-gather.1 = bf16[256,1792]{1,0:T(8,128)(2,1)S(1)} all-gather(bf16[64,1792]{1,0:T(8,128)(2,1)S(1)} %fusion), channel_id=3, replica_groups=mesh['z'=4,'core'=2,'exp'=4] {'z'}, dimensions={0}, use_global_device_ids=true | all-gather | bytes 1146880 | tf_op jit(solution)/shard_map/all_gather | solution.py:585
  184.0 20.0 %all_gather.23.own = bf16[4,64,1792]{2,1,0:T(8,128)(2,1)S(1)} all-gather(bf16[1,64,1792]{2,1,0:T(8,128)(2,1)S(1)} %fusion.1), channel_id=1, replica_groups=mesh['z'=4,'core'=2,'exp'=4] {'z'}, dimensions={0}, use_global_device_ids=true | all-gather | bytes 1146880 | tf_op jit(solution)/shard_map/all_gather | solution.py:587
  210.0 6.8 %collective-permute-done.5.far_b = bf16[2,64,1792]{2,1,0:T(8,128)(2,1)S(1)} collective-permute-done((bf16[2,64,1792]{2,1,0:T(8,128)(2,1)}, bf16[2,64,1792]{2,1,0:T(8,128)(2,1)S(1)}, u32[]{:S(2)}, u32[]{:S(2)}) %collective-permute-start.5) | collective-permute-done | bytes 458784 | tf_op jit(solution)/shard_map/ppermute | solution.py:452
  222.4 10.3 %expert.2 = bf16[2,4,4,16,256]{4,3,2,1,0:T(8,128)(2,1)S(1)} custom-call(s32[2]{0:T(128)S(1)} %pad_add_fusion.spots, bf16[4,64,1792]{2,1,0:T(8,128)(2,1)S(1)} %bitcast.124, bf16[4,64,1792]{2,1,0:T(8,128)(2,1)S(1)} %copy-done.10, bf16[4,64,1792]{2,1,0:T(8,128)(2,1)S(1)} %collective-permute-done.2.across, bf16[2,64,1792]{2,1,0:T(8,128)(2,1)} %collective-permute-done.4.far_a, ...), custom_call_target="tpu_custom_call" | custom-call | flops 3758096384 | bytes 18350080 | tf_op jit(solution)/shard_map/expert/pallas_call | solution.py:362
  232.7 5.4 %down.2 = bf16[4,4,16,7168]{3,2,1,0:T(8,128)(2,1)S(1)} custom-call(s32[2]{0:T(128)S(1)} %pad_add_fusion.spots, bf16[2,256,256]{2,1,0:T(8,128)(2,1)S(1)} %bitcast.126, bf16[256,7168]{1,0:T(8,128)(2,1)S(1)} %bitcast.120, bf16[256,7168]{1,0:T(8,128)(2,1)} %collective-permute-done.8.down_v, f32[4,16,1792]{2,1,0:T(8,128)S(1)} %pad_maximum_fusion.1.hidden), custom_call_target="tpu_custom_call" | custom-call | flops 1879048192 | bytes 11010048 | tf_op jit(solution)/shard_map/down/pallas_call | solution.py:422
  242.2 16.6 %collective-permute-done.10.across = bf16[4,64,1792]{2,1,0:T(8,128)(2,1)S(1)} collective-permute-done((bf16[4,64,1792]{2,1,0:T(8,128)(2,1)S(1)}, bf16[4,64,1792]{2,1,0:T(8,128)(2,1)S(1)}, u32[]{:S(2)}, u32[]{:S(2)}) %collective-permute-start.10) | collective-permute-done | bytes 917536 | tf_op jit(solution)/shard_map/ppermute | solution.py:452
  263.8 5.9 %collective-permute-done.12.far_b = bf16[2,64,1792]{2,1,0:T(8,128)(2,1)S(1)} collective-permute-done((bf16[2,64,1792]{2,1,0:T(8,128)(2,1)}, bf16[2,64,1792]{2,1,0:T(8,128)(2,1)S(1)}, u32[]{:S(2)}, u32[]{:S(2)}) %collective-permute-start.12) | collective-permute-done | bytes 458784 | tf_op jit(solution)/shard_map/ppermute | solution.py:452
  275.3 10.4 %expert.3 = bf16[2,4,4,16,256]{4,3,2,1,0:T(8,128)(2,1)S(1)} custom-call(s32[2]{0:T(128)S(1)} %pad_add_fusion.spots, bf16[4,64,1792]{2,1,0:T(8,128)(2,1)S(1)} %all_gather.23.own, bf16[4,64,1792]{2,1,0:T(8,128)(2,1)S(1)} %collective-permute-done.9.along, bf16[4,64,1792]{2,1,0:T(8,128)(2,1)S(1)} %collective-permute-done.10.across, ...), custom_call_target="tpu_custom_call" | custom-call | flops 3758096384 | bytes 18350080 | tf_op jit(solution)/shard_map/expert/pallas_call | solution.py:362
  285.7 5.4 %down.3 = bf16[4,4,16,7168]{3,2,1,0:T(8,128)(2,1)S(1)} custom-call(s32[2]{0:T(128)S(1)} %pad_add_fusion.spots, bf16[2,256,256]{2,1,0:T(8,128)(2,1)S(1)} %bitcast.125, bf16[256,7168]{1,0:T(8,128)(2,1)S(1)} %bitcast.121, bf16[256,7168]{1,0:T(8,128)(2,1)} %collective-permute-done.8.down_v, f32[4,16,1792]{2,1,0:T(8,128)S(1)} %pad_maximum_fusion.2.hidden), custom_call_target="tpu_custom_call" | custom-call | flops 1879048192 | bytes 11010048 | tf_op jit(solution)/shard_map/down/pallas_call | solution.py:422
  291.0 41.2 %all_to_all.25 = bf16[4,4,16,7168]{3,2,1,0:T(8,128)(2,1)} all-to-all(bf16[4,4,16,7168]{3,2,1,0:T(8,128)(2,1)S(1)} %down.3), channel_id=1, replica_groups=mesh['z'=4,'core'=2,'exp'=4] {'exp'}, dimensions={0} | all-to-all | bytes 7340032 | tf_op jit(solution)/shard_map/all_to_all | solution.py:621
  332.2 3.8 %reduce_sum.68 = bf16[4,16,7168]{2,1,0:T(8,128)(2,1)} reduce(bf16[4,4,16,7168]{3,2,1,0:T(8,128)(2,1)} %all_to_all.25, bf16[]{:T(256)} %constant.39.clone.1), dimensions={0}, to_apply=%region_6.7 | reduce | flops 1376256 | bytes 4587522 | tf_op jit(solution)/shard_map/reduce_sum | solution.py:622
  336.1 12.7 %all_to_all.26 = bf16[4,16,7168]{2,1,0:T(8,128)(2,1)S(1)} all-to-all(bf16[4,16,7168]{2,1,0:T(8,128)(2,1)} %bitcast.141), channel_id=1, replica_groups=mesh['z'=4,'core'=2,'exp'=4] {'exp'}, dimensions={0} | all-to-all | bytes 1835008 | tf_op jit(solution)/shard_map/all_to_all | solution.py:616
  349.1 12.0 %reduce-scatter.5.cloned.1.call-done = bf16[1,16,7168]{2,1,0:T(8,128)(2,1)} async-done(((bf16[4,16,7168]{2,1,0:T(8,128)(2,1)}), bf16[1,16,7168]{2,1,0:T(8,128)(2,1)}) %reduce-scatter.5.cloned.1.call-update) | async-done | bytes 229392 | tf_op jit(solution)/shard_map/reduce_scatter | solution.py:623
  (149 shorter events, 48.4 us)
Async XLA Ops:
  6.5 15.7 %copy-start = (f32[2,32,16]{1,2,0:T(8,128)S(1)}, f32[2,32,16]{1,2,0:T(8,128)}, u32[]{:S(2)}) copy-start(f32[2,32,16]{1,2,0:T(8,128)} %param.17) | copy-start | bytes 12292
  15.8 55.4 %all-to-all-start = ((bf16[8,512,256]{2,1,0:T(8,128)(2,1)}), bf16[8,512,256]{2,1,0:T(8,128)(2,1)S(1)}, u32[]{:S(2)}, u32[]{:S(2)}) async-start(bf16[8,512,256]{2,1,0:T(8,128)(2,1)} %bitcast_dynamic-update-slice_fusion.3), calls=%async_computation | async-start | bytes 4194304 | tf_op jit(solution)/shard_map/all_to_all | solution.py:523
  22.1 84.2 %all-gather.5.cloned.1.call-start = ((), (), s32[]{:S(2)}) async-start(), calls=%async_computation.7 | async-start | bytes 2359296 | tf_op jit(solution)/shard_map/all_gather | solution.py:573
  78.1 60.3 %all-gather.7.cloned.1.call-start = ((), (), s32[]{:S(2)}) async-start(), calls=%async_computation.10 | async-start | bytes 2359296 | tf_op jit(solution)/shard_map/all_gather | solution.py:575
  113.1 17.7 %all-to-all-start.1 = ((bf16[4,144,896]{2,1,0:T(8,128)(2,1)}), bf16[4,144,896]{2,1,0:T(8,128)(2,1)S(1)}, u32[]{:S(2)}, u32[]{:S(2)}) async-start(bf16[4,144,896]{2,1,0:T(8,128)(2,1)} %pad_maximum_fusion), calls=%async_computation.1 | async-start | bytes 2064384 | tf_op jit(solution)/shard_map/all_to_all | solution.py:557
  119.0 13.1 %copy-start.11 = (f32[7168]{0:T(1024)S(1)}, f32[7168]{0:T(1024)}, u32[]{:S(2)}) copy-start(f32[7168]{0:T(1024)} %param.20) | copy-start | bytes 86020
  131.0 1.6 collective-permute-start
  131.1 86.1 %collective-permute-start.6 = (bf16[7168,256]{1,0:T(8,128)(2,1)}, bf16[7168,256]{1,0:T(8,128)(2,1)}, u32[]{:S(2)}, u32[]{:S(2)}) collective-permute-start(bf16[7168,256]{1,0:T(8,128)(2,1)} %bitcast.112), channel_id=1, source_target_pairs={{0,4},{4,0},{1,5},{5,1},{2,6},{6,2},{3,7},{7,3},{8,12},{12,8},{9,1... | collective-permute-start | bytes 11010056 | tf_op jit(solution)/shard_map/ppermute | solution.py:447
  131.6 85.6 %collective-permute-start.7 = (bf16[7168,256]{1,0:T(8,128)(2,1)}, bf16[7168,256]{1,0:T(8,128)(2,1)}, u32[]{:S(2)}, u32[]{:S(2)}) collective-permute-start(bf16[7168,256]{1,0:T(8,128)(2,1)} %bitcast.115), channel_id=1, source_target_pairs={{0,4},{4,0},{1,5},{5,1},{2,6},{6,2},{3,7},{7,3},{8,12},{12,8},{9,1... | collective-permute-start | bytes 11010056 | tf_op jit(solution)/shard_map/ppermute | solution.py:447
  131.6 101.1 %collective-permute-start.8 = (bf16[256,7168]{1,0:T(8,128)(2,1)}, bf16[256,7168]{1,0:T(8,128)(2,1)}, u32[]{:S(2)}, u32[]{:S(2)}) collective-permute-start(bf16[256,7168]{1,0:T(8,128)(2,1)} %bitcast.119), channel_id=1, source_target_pairs={{0,4},{4,0},{1,5},{5,1},{2,6},{6,2},{3,7},{7,3},{8,12},{12,8},{9,1... | collective-permute-start | bytes 11010056 | tf_op jit(solution)/shard_map/ppermute | solution.py:447
  132.6 11.8 %copy-start.14 = (f32[4,16,896]{2,1,0:T(8,128)}, f32[4,16,896]{2,1,0:T(8,128)S(1)}, u32[]{:S(2)}) copy-start(f32[4,16,896]{2,1,0:T(8,128)S(1)} %get-tuple-element.29) | copy-start | bytes 688132
  144.4 16.6 %all-to-all-start.2 = ((bf16[4,128,896]{2,1,0:T(8,128)(2,1)}), bf16[4,128,896]{2,1,0:T(8,128)(2,1)S(1)}, u32[]{:S(2)}, u32[]{:S(2)}) async-start(bf16[4,128,896]{2,1,0:T(8,128)(2,1)} %bitcast.23), calls=%async_computation.2 | async-start | bytes 1835008 | tf_op jit(solution)/shard_map/all_to_all | solution.py:557
  148.1 188.1 %reduce-scatter.3.cloned.1.call-start = ((), (), s32[]{:S(2)}) async-start(), calls=%async_computation.8 | async-start | bytes 4587520 | tf_op jit(solution)/shard_map/reduce_scatter | solution.py:610
  161.1 21.5 %collective-permute-start.3 = (f32[4,16,896]{2,1,0:T(8,128)S(1)}, f32[4,16,896]{2,1,0:T(8,128)S(1)}, u32[]{:S(2)}, u32[]{:S(2)}) collective-permute-start(f32[4,16,896]{2,1,0:T(8,128)S(1)} %dynamic-slice_bitcast_fusion), channel_id=1, source_target_pairs={{0,4},{4,0},{1,5},{5,1},{2,6},{6,2},{3,7},{7,3},{8,12},{12,8},{9,1... | collective-permute-start | bytes 688136 | tf_op jit(solution)/shard_map/ppermute | solution.py:447
  181.2 22.8 %collective-permute-start.2 = (bf16[4,64,1792]{2,1,0:T(8,128)(2,1)S(1)}, bf16[4,64,1792]{2,1,0:T(8,128)(2,1)S(1)}, u32[]{:S(2)}, u32[]{:S(2)}) collective-permute-start(bf16[4,64,1792]{2,1,0:T(8,128)(2,1)S(1)} %bitcast.122), channel_id=1, source_target_pairs={{0,2},{1,3},{2,0},{3,1},{4,6},{5,7},{6,4},{7,5},{8,10},{9,11},{10,... | collective-permute-start | bytes 2752520 | tf_op jit(solution)/shard_map/ppermute | solution.py:452
  182.7 21.4 %collective-permute-start.1 = (bf16[4,64,1792]{2,1,0:T(8,128)(2,1)S(1)}, bf16[4,64,1792]{2,1,0:T(8,128)(2,1)S(1)}, u32[]{:S(2)}, u32[]{:S(2)}) collective-permute-start(bf16[4,64,1792]{2,1,0:T(8,128)(2,1)S(1)} %bitcast.123), channel_id=1, source_target_pairs={{0,1},{1,0},{2,3},{3,2},{4,5},{5,4},{6,7},{7,6},{8,9},{9,8},{10,11... | collective-permute-start | bytes 2752520 | tf_op jit(solution)/shard_map/ppermute | solution.py:452
  206.6 10.3 %collective-permute-start.5 = (bf16[2,64,1792]{2,1,0:T(8,128)(2,1)}, bf16[2,64,1792]{2,1,0:T(8,128)(2,1)S(1)}, u32[]{:S(2)}, u32[]{:S(2)}) collective-permute-start(bf16[2,64,1792]{2,1,0:T(8,128)(2,1)} %slice.69), channel_id=1, source_target_pairs={{0,1},{1,0},{2,3},{3,2},{4,5},{5,4},{6,7},{7,6},{8,9},{9,8},{10,11... | collective-permute-start | bytes 1376264 | tf_op jit(solution)/shard_map/ppermute | solution.py:452
  208.1 9.1 %collective-permute-start.4 = (bf16[2,64,1792]{2,1,0:T(8,128)(2,1)}, bf16[2,64,1792]{2,1,0:T(8,128)(2,1)}, u32[]{:S(2)}, u32[]{:S(2)}) collective-permute-start(bf16[2,64,1792]{2,1,0:T(8,128)(2,1)} %slice.68), channel_id=1, source_target_pairs={{0,2},{1,3},{2,0},{3,1},{4,6},{5,7},{6,4},{7,5},{8,10},{9,11},{10,... | collective-permute-start | bytes 1376264 | tf_op jit(solution)/shard_map/ppermute | solution.py:452
  240.0 121.1 %reduce-scatter.5.cloned.1.call-start = ((), (), s32[]{:S(2)}) async-start(), calls=%async_computation.9 | async-start | bytes 1146880 | tf_op jit(solution)/shard_map/reduce_scatter | solution.py:623
  240.1 18.8 %collective-permute-start.10 = (bf16[4,64,1792]{2,1,0:T(8,128)(2,1)S(1)}, bf16[4,64,1792]{2,1,0:T(8,128)(2,1)S(1)}, u32[]{:S(2)}, u32[]{:S(2)}) collective-permute-start(bf16[4,64,1792]{2,1,0:T(8,128)(2,1)S(1)} %all_gather.23.own), channel_id=1, source_target_pairs={{0,2},{1,3},{2,0},{3,1},{4,6},{5,7},{6,4},{7,5},{8,10},{9,11},{10,... | collective-permute-start | bytes 2752520 | tf_op jit(solution)/shard_map/ppermute | solution.py:452
  241.6 20.0 %collective-permute-start.9 = (bf16[4,64,1792]{2,1,0:T(8,128)(2,1)S(1)}, bf16[4,64,1792]{2,1,0:T(8,128)(2,1)S(1)}, u32[]{:S(2)}, u32[]{:S(2)}) collective-permute-start(bf16[4,64,1792]{2,1,0:T(8,128)(2,1)S(1)} %all_gather.23.own), channel_id=1, source_target_pairs={{0,1},{1,0},{2,3},{3,2},{4,5},{5,4},{6,7},{7,6},{8,9},{9,8},{10,11... | collective-permute-start | bytes 2752520 | tf_op jit(solution)/shard_map/ppermute | solution.py:452
  259.7 10.1 %collective-permute-start.12 = (bf16[2,64,1792]{2,1,0:T(8,128)(2,1)}, bf16[2,64,1792]{2,1,0:T(8,128)(2,1)S(1)}, u32[]{:S(2)}, u32[]{:S(2)}) collective-permute-start(bf16[2,64,1792]{2,1,0:T(8,128)(2,1)} %slice.91), channel_id=1, source_target_pairs={{0,1},{1,0},{2,3},{3,2},{4,5},{5,4},{6,7},{7,6},{8,9},{9,8},{10,11... | collective-permute-start | bytes 1376264 | tf_op jit(solution)/shard_map/ppermute | solution.py:452
  262.4 8.8 %collective-permute-start.11 = (bf16[2,64,1792]{2,1,0:T(8,128)(2,1)}, bf16[2,64,1792]{2,1,0:T(8,128)(2,1)}, u32[]{:S(2)}, u32[]{:S(2)}) collective-permute-start(bf16[2,64,1792]{2,1,0:T(8,128)(2,1)} %slice.90), channel_id=1, source_target_pairs={{0,2},{1,3},{2,0},{3,1},{4,6},{5,7},{6,4},{7,5},{8,10},{9,11},{10,... | collective-permute-start | bytes 1376264 | tf_op jit(solution)/shard_map/ppermute | solution.py:452
  336.1 26.7 %copy-start.1 = (f32[2,32,16]{1,2,0:T(8,128)S(1)}, f32[2,32,16]{1,2,0:T(8,128)}, u32[]{:S(2)}) copy-start(f32[2,32,16]{1,2,0:T(8,128)} %param.17) | copy-start | bytes 12292
  (15 other events, 53.0 us)
Sparse Core Ops, SparseCore 0:
  78.3 27.9 all-gather.4
  107.9 30.4 all-gather.6
  240.1 67.9 reduce-scatter.2
  336.2 24.8 reduce-scatter.4

commit v6 on v5

--- a/solution.py
+++ b/solution.py
@@ -388,7 +388,7 @@
             ],
         ),
         out_shape=jax.ShapeDtypeStruct((2,) + lead + (half, units), jnp.bfloat16),
-        compiler_params=pltpu.CompilerParams(vmem_limit_bytes=40 * 2**20),
+        compiler_params=pltpu.CompilerParams(vmem_limit_bytes=56 * 2**20),
         cost_estimate=pl.CostEstimate(
             flops=8 * row_total * units * steps * cols,
             bytes_accessed=2 * steps * cols * (row_total + 4 * units),
@@ -433,7 +433,7 @@
             out_specs=pl.BlockSpec(lead + (half, cols), lambda i, _: (0, 0, 0, i)),
         ),
         out_shape=jax.ShapeDtypeStruct(lead + (half, model_width), jnp.bfloat16),
-        compiler_params=pltpu.CompilerParams(vmem_limit_bytes=40 * 2**20),
+        compiler_params=pltpu.CompilerParams(vmem_limit_bytes=56 * 2**20),
         cost_estimate=pl.CostEstimate(
             flops=4 * rows * units * model_width,
             bytes_accessed=2 * model_width * (rows + 2 * units),
@@ -581,34 +581,29 @@
     sums_first, scaled_first = settle(pieces, 0)
     pieces = project(spread_second)
     pieces, scaled_first = lax.optimization_barrier((pieces, scaled_first))
-    sums_second, scaled_second = settle(exchange(pieces), 1)
     plane_first = lax.all_gather(scaled_first, "z", axis=0)
+    pieces, plane_first = lax.optimization_barrier((exchange(pieces), plane_first))
+    sums_second, scaled_second = settle(pieces, 1)
     along, across = plane_step(plane_first, 1), plane_step(plane_first, 2)
     plane_second = lax.all_gather(scaled_second, "z", axis=0)
     along, across, plane_second = lax.optimization_barrier((along, across, plane_second))
     far_a, far_b = plane_step(along[:middle], 2), plane_step(across[middle:], 1)
     far_a, far_b, plane_second = lax.optimization_barrier((far_a, far_b, plane_second))
-    blocks = [(plane_first, along, across, far_a, far_b)]
+    weights = (expert_gate[0], expert_up[0], other_gate, other_up)
+
+    def run_group(blocks, sums, group):
+        route_rows = route[:, :, group].reshape(exp_count, chip_count * half, 1)
+        active = run_expert(spots, blocks, ffn_gain, weights, route_rows, half, 1 - group)
+        return run_down(spots, active, expert_down[0], other_down, sums, exp_count, 1 - group)
+
+    first = run_group((plane_first, along, across, far_a, far_b), sums_first, 0)
     along, across = plane_step(plane_second, 1), plane_step(plane_second, 2)
+    first, along, across = lax.optimization_barrier((first, along, across))
     far_a, far_b = plane_step(along[:middle], 2), plane_step(across[middle:], 1)
-    blocks.append((plane_second, along, across, far_a, far_b))
-    hidden = [sums_first, sums_second]
-
-    weights = (expert_gate[0], expert_up[0], other_gate, other_up)
-    outs = []
-    for group in range(2):
-        route_rows = route[:, :, group].reshape(exp_count, chip_count * half, 1)
-        active = run_expert(
-            spots, blocks[group], ffn_gain, weights, route_rows, half, 1 - group
-        )
-        outs.append(
-            run_down(
-                spots, active, expert_down[0], other_down, hidden[group], exp_count, 1 - group
-            )
-        )
+    second = run_group((plane_second, along, across, far_a, far_b), sums_second, 1)
 
     first = lax.psum_scatter(
-        outs[0].reshape(chip_count, exp_count * half, model_width),
+        first.reshape(chip_count, exp_count * half, model_width),
         "z",
         scatter_dimension=0,
         tiled=True,
@@ -618,7 +613,7 @@
     )
     first = jnp.sum(first.astype(jnp.float32), axis=0).astype(jnp.bfloat16)
 
-    second = lax.all_to_all(outs[1], "exp", split_axis=0, concat_axis=0, tiled=True)
+    second = lax.all_to_all(second, "exp", split_axis=0, concat_axis=0, tiled=True)
     second = jnp.sum(second.astype(jnp.float32), axis=0).astype(jnp.bfloat16)
     second = lax.psum_scatter(second, "z", scatter_dimension=0, tiled=True)
     return jnp.concatenate([first, second.reshape(half, model_width)], 0)

time: 371 us -> 347 us (0.935)
  waiting for transfers between devices: 151 us -> 122 us
  local copies, waits for them, and re-layouts: 29 us -> 17.8 us
  Pallas kernels: 36.6 us -> 46 us
  blocking collectives: 93.8 us -> 97.8 us
    ppermute x8, waiting for transfers between devices: 31.6 us -> 17.9 us  [plane_step(): return lax.ppermute(block, 'exp', [(i, i ^ step) for i in range(count)])]
    all_to_all x2, waiting for transfers between devices: 24.4 us -> 11 us  [exchange(): lax.all_to_all(pieces, 'exp', split_axis=0, concat_axis=0, tiled=True)]
    unnamed x50 -> x46, local copies, waits for them, and re-layouts: 17.3 us -> 6.58 us
    pallas_call x2, Pallas kernels: 20.7 us -> 25.9 us  [run_expert(): pl.pallas_call(functools.partial(expert_kernel, exp_dim), grid_spec=pltpu...]
    pallas_call x2, Pallas kernels: 10.7 us -> 14.9 us  [run_down(): pl.pallas_call(functools.partial(down_kernel, exp_dim), grid_spec=pltpu.P...]
    all_to_all x1, blocking collectives: 41.2 us -> 45.2 us  [by_heads(): lax.all_to_all(second, 'exp', split_axis=0, concat_axis=0, tiled=True)]
  transfers between devices with their start and end apart: 20 -> 20, of which waited for: 13 -> 11; matrix products, arithmetic and copies ran while one was open for 7% -> 8% of each run, Pallas kernels for 7% -> 12%
where the time goes in v6:
time: 347 us; the launch traced here: 346 us
  waiting for transfers between devices  122 us (35%)
  blocking collectives  97.8 us (28%)
  Pallas kernels  46 us (13%)
  starting transfers between devices  25.1 us (7%)
  local copies, waits for them, and re-layouts  17.8 us (5%)
  between operations  13.7 us (4%)
  other arithmetic  13.1 us (4%)
  matrix products  11 us (3%)
    all_to_all x1, waiting for transfers between devices, by_heads(): moved = lax.all_to_all(packed, ctx, split_axis=0, concat_axis=0, tiled=True)  48.7 us
    all_to_all x1, blocking collectives, by_heads(): lax.all_to_all(second, 'exp', split_axis=0, concat_axis=0, tiled=True)  45.2 us
    all_gather x1, waiting for transfers between devices, by_heads(): spread_first = lax.all_gather(attended[0], ctx, axis=0)  28.1 us
    pallas_call x2, Pallas kernels, run_expert(): pl.pallas_call(functools.partial(expert_kernel, exp_dim), grid_spec=pltpu...  25.9 us
    all_gather x1, blocking collectives, by_heads(): plane_second = lax.all_gather(scaled_second, 'z', axis=0)  19.9 us
    all_gather x1, blocking collectives, by_heads(): plane_first = lax.all_gather(scaled_first, 'z', axis=0)  19.9 us
    ppermute x8, waiting for transfers between devices, plane_step(): return lax.ppermute(block, 'exp', [(i, i ^ step) for i in range(count)])  17.9 us
    pallas_call x2, Pallas kernels, run_down(): pl.pallas_call(functools.partial(down_kernel, exp_dim), grid_spec=pltpu.P...  14.9 us
  transfers between devices with their start and end apart: 20, of which 11 were waited for; matrix products, arithmetic and copies ran while one was open for 8% of the time, Pallas kernels for 12%

profile of v6, /device:TPU:0, one launch (start us, length us, event | category | flops | bytes accessed | tf_op | source)
XLA Modules:
  0.0 346.2 jit_solution(12073045101561327782)
XLA Ops:
  15.8 6.3 %all-to-all-start = ((bf16[8,512,256]{2,1,0:T(8,128)(2,1)}), bf16[8,512,256]{2,1,0:T(8,128)(2,1)S(1)}, u32[]{:S(2)}, u32[]{:S(2)}) async-start(bf16[8,512,256]{2,1,0:T(8,128)(2,1)} %bitcast_dynamic-update-slice_fusion.3), calls=%async_computation | async-start | bytes 4194304 | tf_op jit(solution)/shard_map/all_to_all | solution.py:523
  22.5 48.7 %all-to-all-done.moved = bf16[8,512,256]{2,1,0:T(8,128)(2,1)S(1)} async-done(((bf16[8,512,256]{2,1,0:T(8,128)(2,1)}), bf16[8,512,256]{2,1,0:T(8,128)(2,1)S(1)}, u32[]{:S(2)}, u32[]{:S(2)}) %all-to-all-start) | async-done | bytes 2097184 | tf_op jit(solution)/shard_map/all_to_all | solution.py:523
  72.0 5.3 %attend.1 = bf16[2,512,256]{2,1,0:T(8,128)(2,1)S(1)} custom-call(bf16[8,512,256]{2,1,0:T(8,128)(2,1)S(1)} %all-to-all-done.moved, f32[8,1024]{1,0:T(8,128)S(1)} %tile.12.taps, f32[1024,4]{1,0:T(8,128)S(1)} %copy.95.gates), custom_call_target="tpu_custom_call" | custom-call | tf_op jit(solution)/shard_map/attend/pallas_call | solution.py:298
  78.2 28.1 %all-gather.5.cloned.1.call-done = bf16[8,512,256]{2,1,0:T(8,128)(2,1)} async-done(((bf16[1,512,256]{2,1,0:T(8,128)(2,1)}), bf16[8,512,256]{2,1,0:T(8,128)(2,1)}) %all-gather.5.cloned.1.call-update) | async-done | bytes 2097168 | tf_op jit(solution)/shard_map/all_gather | solution.py:573
  106.9 5.0 %bitcast_convert_fusion = bf16[512,896]{1,0:T(8,128)(2,1)S(1)} fusion(bf16[8,512,256]{2,1,0:T(8,128)(2,1)} %all-gather.5.cloned.1.call-done, bf16[8,256,896]{2,1,0:T(8,128)(2,1)} %bitcast.158), kind=kOutput, calls=%fused_computation | convolution fusion | flops 1879506944 | bytes 6684672 | tf_op jit(solution)/shard_map/csk,ckd->sd/dot_general | solution.py:548
  113.0 3.6 %all-to-all-start.1 = ((bf16[4,144,896]{2,1,0:T(8,128)(2,1)}), bf16[4,144,896]{2,1,0:T(8,128)(2,1)S(1)}, u32[]{:S(2)}, u32[]{:S(2)}) async-start(bf16[4,144,896]{2,1,0:T(8,128)(2,1)} %pad_maximum_fusion), calls=%async_computation.1 | async-start | bytes 2064384 | tf_op jit(solution)/shard_map/all_to_all | solution.py:557
  119.7 11.0 %all-to-all-done.1 = bf16[4,144,896]{2,1,0:T(8,128)(2,1)S(1)} async-done(((bf16[4,144,896]{2,1,0:T(8,128)(2,1)}), bf16[4,144,896]{2,1,0:T(8,128)(2,1)S(1)}, u32[]{:S(2)}, u32[]{:S(2)}) %all-to-all-start.1) | async-done | bytes 1032224 | tf_op jit(solution)/shard_map/all_to_all | solution.py:557
  133.2 5.1 %all-gather.7.cloned.1.call-done = bf16[4096,256]{1,0:T(8,128)(2,1)} async-done(((bf16[512,256]{1,0:T(8,128)(2,1)}), bf16[4096,256]{1,0:T(8,128)(2,1)}) %all-gather.7.cloned.1.call-update) | async-done | bytes 2097168 | tf_op jit(solution)/shard_map/all_gather | solution.py:575
  138.4 6.0 %bitcast_convert_fusion.1 = bf16[512,896]{1,0:T(8,128)(2,1)} fusion(bf16[8,512,256]{2,1,0:T(8,128)(2,1)} %bitcast.160, bf16[8,256,896]{2,1,0:T(8,128)(2,1)} %bitcast.159), kind=kOutput, calls=%fused_computation.1 | convolution fusion | flops 1879506944 | bytes 6684672 | tf_op jit(solution)/shard_map/csk,ckd->sd/dot_general | solution.py:548
  144.3 3.7 %all-to-all-start.2 = ((bf16[4,128,896]{2,1,0:T(8,128)(2,1)}), bf16[4,128,896]{2,1,0:T(8,128)(2,1)S(1)}, u32[]{:S(2)}, u32[]{:S(2)}) async-start(bf16[4,128,896]{2,1,0:T(8,128)(2,1)} %bitcast.23), calls=%async_computation.2 | async-start | bytes 1835008 | tf_op jit(solution)/shard_map/all_to_all | solution.py:557
  148.4 19.9 %all-gather.1 = bf16[256,1792]{1,0:T(8,128)(2,1)S(1)} all-gather(bf16[64,1792]{1,0:T(8,128)(2,1)} %fusion), channel_id=3, replica_groups=mesh['z'=4,'core'=2,'exp'=4] {'z'}, dimensions={0}, use_global_device_ids=true | all-gather | bytes 1146880 | tf_op jit(solution)/shard_map/all_gather | solution.py:584
  169.7 1.8 collective-permute-start.2
  173.1 19.9 %all_gather.23.own = bf16[4,64,1792]{2,1,0:T(8,128)(2,1)S(1)} all-gather(bf16[1,64,1792]{2,1,0:T(8,128)(2,1)S(1)} %fusion.1), channel_id=1, replica_groups=mesh['z'=4,'core'=2,'exp'=4] {'z'}, dimensions={0}, use_global_device_ids=true | all-gather | bytes 1146880 | tf_op jit(solution)/shard_map/all_gather | solution.py:588
  197.6 8.4 %collective-permute-done.5.far_b = bf16[2,64,1792]{2,1,0:T(8,128)(2,1)} collective-permute-done((bf16[2,64,1792]{2,1,0:T(8,128)(2,1)S(1)}, bf16[2,64,1792]{2,1,0:T(8,128)(2,1)}, u32[]{:S(2)}, u32[]{:S(2)}) %collective-permute-start.5) | collective-permute-done | bytes 458784 | tf_op jit(solution)/shard_map/ppermute | solution.py:452
  211.3 12.9 %expert.2 = bf16[2,4,4,16,256]{4,3,2,1,0:T(8,128)(2,1)} custom-call(s32[2]{0:T(128)} %pad_add_fusion.spots, bf16[4,64,1792]{2,1,0:T(8,128)(2,1)} %bitcast.124, bf16[4,64,1792]{2,1,0:T(8,128)(2,1)} %copy-done.10, bf16[4,64,1792]{2,1,0:T(8,128)(2,1)} %copy-done.8, bf16[2,64,1792]{2,1,0:T(8,128)(2,1)} %collective-permute-done.4.far_a, ...), custom_call_target="tpu_custom_call" | custom-call | flops 3758096384 | bytes 18350080 | tf_op jit(solution)/shard_map/expert/pallas_call | solution.py:362
  224.2 7.4 %down.2 = bf16[4,4,16,7168]{3,2,1,0:T(8,128)(2,1)} custom-call(s32[2]{0:T(128)} %pad_add_fusion.spots, bf16[2,256,256]{2,1,0:T(8,128)(2,1)} %bitcast.137, bf16[256,7168]{1,0:T(8,128)(2,1)} %bitcast.120, bf16[256,7168]{1,0:T(8,128)(2,1)} %collective-permute-done.8.down_v, f32[4,16,1792]{2,1,0:T(8,128)} %pad_maximum_fusion.1.hidden), custom_call_target="tpu_custom_call" | custom-call | flops 1879048192 | bytes 11010048 | tf_op jit(solution)/shard_map/down/pallas_call | solution.py:422
  236.2 7.0 %collective-permute-done.12.far_b = bf16[2,64,1792]{2,1,0:T(8,128)(2,1)S(1)} collective-permute-done((bf16[2,64,1792]{2,1,0:T(8,128)(2,1)S(1)}, bf16[2,64,1792]{2,1,0:T(8,128)(2,1)S(1)}, u32[]{:S(2)}, u32[]{:S(2)}) %collective-permute-start.12) | collective-permute-done | bytes 458784 | tf_op jit(solution)/shard_map/ppermute | solution.py:452
  244.8 13.0 %expert.3 = bf16[2,4,4,16,256]{4,3,2,1,0:T(8,128)(2,1)} custom-call(s32[2]{0:T(128)} %pad_add_fusion.spots, bf16[4,64,1792]{2,1,0:T(8,128)(2,1)} %copy-done.2, bf16[4,64,1792]{2,1,0:T(8,128)(2,1)} %copy-done.11, bf16[4,64,1792]{2,1,0:T(8,128)(2,1)} %copy-done.9, bf16[2,64,1792]{2,1,0:T(8,128)(2,1)} %copy-done.16, bf16[2,64,1792]{2,1,0:T(8,128)(2,1)} %copy-done.15, ...), custom_call_target="tpu_custom_call" | custom-call | flops 3758096384 | bytes 18350080 | tf_op jit(solution)/shard_map/expert/pallas_call | solution.py:362
  257.8 7.4 %down.3 = bf16[4,4,16,7168]{3,2,1,0:T(8,128)(2,1)} custom-call(s32[2]{0:T(128)} %pad_add_fusion.spots, bf16[2,256,256]{2,1,0:T(8,128)(2,1)} %bitcast.136, bf16[256,7168]{1,0:T(8,128)(2,1)} %bitcast.121, bf16[256,7168]{1,0:T(8,128)(2,1)} %collective-permute-done.8.down_v, f32[4,16,1792]{2,1,0:T(8,128)} %pad_maximum_fusion.2.hidden), custom_call_target="tpu_custom_call" | custom-call | flops 1879048192 | bytes 11010048 | tf_op jit(solution)/shard_map/down/pallas_call | solution.py:422
  265.2 45.2 %all_to_all.25 = bf16[4,4,16,7168]{3,2,1,0:T(8,128)(2,1)} all-to-all(bf16[4,4,16,7168]{3,2,1,0:T(8,128)(2,1)} %down.3), channel_id=1, replica_groups=mesh['z'=4,'core'=2,'exp'=4] {'exp'}, dimensions={0} | all-to-all | bytes 7340032 | tf_op jit(solution)/shard_map/all_to_all | solution.py:616
  310.4 3.9 %reduce_sum.68 = bf16[4,16,7168]{2,1,0:T(8,128)(2,1)} reduce(bf16[4,4,16,7168]{3,2,1,0:T(8,128)(2,1)} %all_to_all.25, bf16[]{:T(256)} %constant.39.clone.1), dimensions={0}, to_apply=%region_6.7 | reduce | flops 1376256 | bytes 4587522 | tf_op jit(solution)/shard_map/reduce_sum | solution.py:617
  314.3 12.7 %all_to_all.26 = bf16[4,16,7168]{2,1,0:T(8,128)(2,1)S(1)} all-to-all(bf16[4,16,7168]{2,1,0:T(8,128)(2,1)} %bitcast.139), channel_id=1, replica_groups=mesh['z'=4,'core'=2,'exp'=4] {'exp'}, dimensions={0} | all-to-all | bytes 1835008 | tf_op jit(solution)/shard_map/all_to_all | solution.py:611
  327.3 10.7 %reduce-scatter.5.cloned.1.call-done = bf16[1,16,7168]{2,1,0:T(8,128)(2,1)} async-done(((bf16[4,16,7168]{2,1,0:T(8,128)(2,1)}), bf16[1,16,7168]{2,1,0:T(8,128)(2,1)}) %reduce-scatter.5.cloned.1.call-update) | async-done | bytes 229392 | tf_op jit(solution)/shard_map/reduce_scatter | solution.py:618
  337.9 1.7 pad_maximum_fusion.3
  (145 shorter events, 37.8 us)
Async XLA Ops:
  15.8 55.4 %all-to-all-start = ((bf16[8,512,256]{2,1,0:T(8,128)(2,1)}), bf16[8,512,256]{2,1,0:T(8,128)(2,1)S(1)}, u32[]{:S(2)}, u32[]{:S(2)}) async-start(bf16[8,512,256]{2,1,0:T(8,128)(2,1)} %bitcast_dynamic-update-slice_fusion.3), calls=%async_computation | async-start | bytes 4194304 | tf_op jit(solution)/shard_map/all_to_all | solution.py:523
  22.1 84.2 %all-gather.5.cloned.1.call-start = ((), (), s32[]{:S(2)}) async-start(), calls=%async_computation.7 | async-start | bytes 2359296 | tf_op jit(solution)/shard_map/all_gather | solution.py:573
  78.1 60.2 %all-gather.7.cloned.1.call-start = ((), (), s32[]{:S(2)}) async-start(), calls=%async_computation.10 | async-start | bytes 2359296 | tf_op jit(solution)/shard_map/all_gather | solution.py:575
  113.0 17.7 %all-to-all-start.1 = ((bf16[4,144,896]{2,1,0:T(8,128)(2,1)}), bf16[4,144,896]{2,1,0:T(8,128)(2,1)S(1)}, u32[]{:S(2)}, u32[]{:S(2)}) async-start(bf16[4,144,896]{2,1,0:T(8,128)(2,1)} %pad_maximum_fusion), calls=%async_computation.1 | async-start | bytes 2064384 | tf_op jit(solution)/shard_map/all_to_all | solution.py:557
  130.9 1.6 collective-permute-start
  131.0 80.3 %collective-permute-start.6 = (bf16[7168,256]{1,0:T(8,128)(2,1)}, bf16[7168,256]{1,0:T(8,128)(2,1)}, u32[]{:S(2)}, u32[]{:S(2)}) collective-permute-start(bf16[7168,256]{1,0:T(8,128)(2,1)} %bitcast.112), channel_id=1, source_target_pairs={{0,4},{4,0},{1,5},{5,1},{2,6},{6,2},{3,7},{7,3},{8,12},{12,8},{9,1... | collective-permute-start | bytes 11010056 | tf_op jit(solution)/shard_map/ppermute | solution.py:447
  131.5 79.8 %collective-permute-start.7 = (bf16[7168,256]{1,0:T(8,128)(2,1)}, bf16[7168,256]{1,0:T(8,128)(2,1)}, u32[]{:S(2)}, u32[]{:S(2)}) collective-permute-start(bf16[7168,256]{1,0:T(8,128)(2,1)} %bitcast.115), channel_id=1, source_target_pairs={{0,4},{4,0},{1,5},{5,1},{2,6},{6,2},{3,7},{7,3},{8,12},{12,8},{9,1... | collective-permute-start | bytes 11010056 | tf_op jit(solution)/shard_map/ppermute | solution.py:447
  144.3 24.0 %all-to-all-start.2 = ((bf16[4,128,896]{2,1,0:T(8,128)(2,1)}), bf16[4,128,896]{2,1,0:T(8,128)(2,1)S(1)}, u32[]{:S(2)}, u32[]{:S(2)}) async-start(bf16[4,128,896]{2,1,0:T(8,128)(2,1)} %bitcast.23), calls=%async_computation.2 | async-start | bytes 1835008 | tf_op jit(solution)/shard_map/all_to_all | solution.py:557
  148.0 166.3 %reduce-scatter.3.cloned.1.call-start = ((), (), s32[]{:S(2)}) async-start(), calls=%async_computation.8 | async-start | bytes 4587520 | tf_op jit(solution)/shard_map/reduce_scatter | solution.py:605
  148.1 76.2 %collective-permute-start.8 = (bf16[256,7168]{1,0:T(8,128)(2,1)}, bf16[256,7168]{1,0:T(8,128)(2,1)}, u32[]{:S(2)}, u32[]{:S(2)}) collective-permute-start(bf16[256,7168]{1,0:T(8,128)(2,1)} %bitcast.119), channel_id=1, source_target_pairs={{0,4},{4,0},{1,5},{5,1},{2,6},{6,2},{3,7},{7,3},{8,12},{12,8},{9,1... | collective-permute-start | bytes 11010056 | tf_op jit(solution)/shard_map/ppermute | solution.py:447
  169.7 1.8 collective-permute-start.3
  169.7 23.3 %collective-permute-start.2 = (bf16[4,64,1792]{2,1,0:T(8,128)(2,1)S(1)}, bf16[4,64,1792]{2,1,0:T(8,128)(2,1)S(1)}, u32[]{:S(2)}, u32[]{:S(2)}) collective-permute-start(bf16[4,64,1792]{2,1,0:T(8,128)(2,1)S(1)} %bitcast.122), channel_id=1, source_target_pairs={{0,2},{1,3},{2,0},{3,1},{4,6},{5,7},{6,4},{7,5},{8,10},{9,11},{10,... | collective-permute-start | bytes 2752520 | tf_op jit(solution)/shard_map/ppermute | solution.py:452
  171.5 22.4 %collective-permute-start.1 = (bf16[4,64,1792]{2,1,0:T(8,128)(2,1)S(1)}, bf16[4,64,1792]{2,1,0:T(8,128)(2,1)S(1)}, u32[]{:S(2)}, u32[]{:S(2)}) collective-permute-start(bf16[4,64,1792]{2,1,0:T(8,128)(2,1)S(1)} %bitcast.123), channel_id=1, source_target_pairs={{0,1},{1,0},{2,3},{3,2},{4,5},{5,4},{6,7},{7,6},{8,9},{9,8},{10,11... | collective-permute-start | bytes 2752520 | tf_op jit(solution)/shard_map/ppermute | solution.py:452
  173.0 20.9 %copy-start.4 = (f32[4,16,896]{2,1,0:T(8,128)}, f32[4,16,896]{2,1,0:T(8,128)S(1)}, u32[]{:S(2)}) copy-start(f32[4,16,896]{2,1,0:T(8,128)S(1)} %get-tuple-element.37) | copy-start | bytes 688132
  173.0 20.9 %copy-start.6 = (f32[4,16,896]{2,1,0:T(8,128)}, f32[4,16,896]{2,1,0:T(8,128)S(1)}, u32[]{:S(2)}) copy-start(f32[4,16,896]{2,1,0:T(8,128)S(1)} %get-tuple-element.38) | copy-start | bytes 688132
  193.0 31.2 %copy-start.2 = (bf16[4,64,1792]{2,1,0:T(8,128)(2,1)}, bf16[4,64,1792]{2,1,0:T(8,128)(2,1)S(1)}, u32[]{:S(2)}) copy-start(bf16[4,64,1792]{2,1,0:T(8,128)(2,1)S(1)} %all_gather.23.own) | copy-start | bytes 2752516
  194.0 11.9 %collective-permute-start.5 = (bf16[2,64,1792]{2,1,0:T(8,128)(2,1)S(1)}, bf16[2,64,1792]{2,1,0:T(8,128)(2,1)}, u32[]{:S(2)}, u32[]{:S(2)}) collective-permute-start(bf16[2,64,1792]{2,1,0:T(8,128)(2,1)S(1)} %slice.69), channel_id=1, source_target_pairs={{0,1},{1,0},{2,3},{3,2},{4,5},{5,4},{6,7},{7,6},{8,9},{9,8},{10,11... | collective-permute-start | bytes 1376264 | tf_op jit(solution)/shard_map/ppermute | solution.py:452
  195.6 11.6 %collective-permute-start.4 = (bf16[2,64,1792]{2,1,0:T(8,128)(2,1)S(1)}, bf16[2,64,1792]{2,1,0:T(8,128)(2,1)}, u32[]{:S(2)}, u32[]{:S(2)}) collective-permute-start(bf16[2,64,1792]{2,1,0:T(8,128)(2,1)S(1)} %slice.68), channel_id=1, source_target_pairs={{0,2},{1,3},{2,0},{3,1},{4,6},{5,7},{6,4},{7,5},{8,10},{9,11},{10,... | collective-permute-start | bytes 1376264 | tf_op jit(solution)/shard_map/ppermute | solution.py:452
  207.1 24.5 %collective-permute-start.10 = (bf16[4,64,1792]{2,1,0:T(8,128)(2,1)S(1)}, bf16[4,64,1792]{2,1,0:T(8,128)(2,1)S(1)}, u32[]{:S(2)}, u32[]{:S(2)}) collective-permute-start(bf16[4,64,1792]{2,1,0:T(8,128)(2,1)S(1)} %all_gather.23.own), channel_id=1, source_target_pairs={{0,2},{1,3},{2,0},{3,1},{4,6},{5,7},{6,4},{7,5},{8,10},{9,11},{10,... | collective-permute-start | bytes 2752520 | tf_op jit(solution)/shard_map/ppermute | solution.py:452
  208.5 23.1 %collective-permute-start.9 = (bf16[4,64,1792]{2,1,0:T(8,128)(2,1)S(1)}, bf16[4,64,1792]{2,1,0:T(8,128)(2,1)S(1)}, u32[]{:S(2)}, u32[]{:S(2)}) collective-permute-start(bf16[4,64,1792]{2,1,0:T(8,128)(2,1)S(1)} %all_gather.23.own), channel_id=1, source_target_pairs={{0,1},{1,0},{2,3},{3,2},{4,5},{5,4},{6,7},{7,6},{8,9},{9,8},{10,11... | collective-permute-start | bytes 2752520 | tf_op jit(solution)/shard_map/ppermute | solution.py:452
  231.7 106.2 %reduce-scatter.5.cloned.1.call-start = ((), (), s32[]{:S(2)}) async-start(), calls=%async_computation.9 | async-start | bytes 1146880 | tf_op jit(solution)/shard_map/reduce_scatter | solution.py:618
  232.9 10.3 %collective-permute-start.12 = (bf16[2,64,1792]{2,1,0:T(8,128)(2,1)S(1)}, bf16[2,64,1792]{2,1,0:T(8,128)(2,1)S(1)}, u32[]{:S(2)}, u32[]{:S(2)}) collective-permute-start(bf16[2,64,1792]{2,1,0:T(8,128)(2,1)S(1)} %slice.74), channel_id=1, source_target_pairs={{0,1},{1,0},{2,3},{3,2},{4,5},{5,4},{6,7},{7,6},{8,9},{9,8},{10,11... | collective-permute-start | bytes 1376264 | tf_op jit(solution)/shard_map/ppermute | solution.py:452
  234.0 9.7 %collective-permute-start.11 = (bf16[2,64,1792]{2,1,0:T(8,128)(2,1)S(1)}, bf16[2,64,1792]{2,1,0:T(8,128)(2,1)S(1)}, u32[]{:S(2)}, u32[]{:S(2)}) collective-permute-start(bf16[2,64,1792]{2,1,0:T(8,128)(2,1)S(1)} %slice.73), channel_id=1, source_target_pairs={{0,2},{1,3},{2,0},{3,1},{4,6},{5,7},{6,4},{7,5},{8,10},{9,11},{10,... | collective-permute-start | bytes 1376264 | tf_op jit(solution)/shard_map/ppermute | solution.py:452
  314.3 25.4 %copy-start.1 = (f32[2,32,16]{1,2,0:T(8,128)S(1)}, f32[2,32,16]{1,2,0:T(8,128)}, u32[]{:S(2)}) copy-start(f32[2,32,16]{1,2,0:T(8,128)} %param.17) | copy-start | bytes 12292
  (13 other events, 41.1 us)
Sparse Core Ops, SparseCore 0:
  78.2 27.9 all-gather.4
  107.9 30.4 all-gather.6
  231.8 66.9 reduce-scatter.2
  314.4 23.4 reduce-scatter.4

commit v7 on v6

--- a/solution.py
+++ b/solution.py
@@ -226,7 +226,7 @@
     return block * lax.rsqrt(jnp.mean(block * block, axis=1, keepdims=True) + norm_eps)
 
 
-def attend_kernel(row_count, share, block_len, head_width, moved, taps, gates, out, keys, values):
+def attend_kernel(row_count, share, block_len, head_width, moved, taps, gates, out_a, out_b, keys, values):
     ctx_count = moved.shape[0]
     own = moved.shape[2] // head_width
     seq_len = row_count * ctx_count
@@ -289,7 +289,7 @@
                 for group in range(2):
                     target = (part * ctx_count + block) * half
                     base = part * share + group * half
-                    out[group, target : target + half, lanes] = mixed[base : base + half]
+                    (out_a, out_b)[group][target : target + half, lanes] = mixed[base : base + half]
 
 
 def attend(moved, taps, gates, row_count, share, block_len, head_width):
@@ -297,7 +297,7 @@
     width = moved.shape[2]
     return pl.pallas_call(
         functools.partial(attend_kernel, row_count, share, block_len, head_width),
-        out_shape=jax.ShapeDtypeStruct((2, seq_len // 2, width), jnp.bfloat16),
+        out_shape=[jax.ShapeDtypeStruct((seq_len // 2, width), jnp.bfloat16)] * 2,
         scratch_shapes=[
             pltpu.VMEM((seq_len, head_width), jnp.bfloat16),
             pltpu.VMEM((seq_len, head_width), jnp.bfloat16),
@@ -305,6 +305,66 @@
         compiler_params=pltpu.CompilerParams(vmem_limit_bytes=48 * 2**20),
         name="attend",
     )(moved, taps, gates)
+
+
+def project_kernel(spots, left_a, left_b, proj_a, proj_b, table, out, total):
+    step = pl.program_id(0)
+    sums = jnp.dot(left_a[0], proj_a[0], preferred_element_type=jnp.float32)
+    sums += jnp.dot(left_b[0], proj_b[0], preferred_element_type=jnp.float32)
+
+    @pl.when(step == 0)
+    def _():
+        total[...] = sums
+
+    @pl.when(step > 0)
+    def _():
+        total[...] += sums
+
+    @pl.when(step == pl.num_programs(0) - 1)
+    def _():
+        exp_count = out.shape[0]
+        tokens = total.shape[0] // exp_count
+        for spot in range(exp_count):
+            rows = total[spot * tokens : (spot + 1) * tokens]
+            out[spot, :tokens] = rows.astype(jnp.bfloat16)
+            if out.shape[1] > tokens:
+                out[spot, tokens:] = table[spot]
+
+
+def run_project(spots, left_a, left_b, paired, proj, table, exp_count, extra):
+    tokens, width = left_a.shape[1:]
+    cols = proj.shape[2]
+    steps = proj.shape[0] // 2
+    rows = tokens // exp_count + (table.shape[1] if extra else 0)
+    if paired:
+        maps = [lambda i, s: (2 * i, 0, 0), lambda i, s: (2 * i + 1, 0, 0)] * 2
+    else:
+        maps = [lambda i, s: (i, 0, 0)] * 2
+        maps += [lambda i, s: (2 * i + s[0], 0, 0), lambda i, s: (2 * i + 1 - s[0], 0, 0)]
+    return pl.pallas_call(
+        project_kernel,
+        grid_spec=pltpu.PrefetchScalarGridSpec(
+            num_scalar_prefetch=1,
+            grid=(steps,),
+            in_specs=[
+                pl.BlockSpec((1, tokens, width), maps[0]),
+                pl.BlockSpec((1, tokens, width), maps[1]),
+                pl.BlockSpec((1, width, cols), maps[2]),
+                pl.BlockSpec((1, width, cols), maps[3]),
+                pl.BlockSpec(table.shape, lambda i, s: (0, 0, 0)),
+            ],
+            out_specs=pl.BlockSpec((exp_count, rows, cols), lambda i, s: (0, 0, 0)),
+            scratch_shapes=[pltpu.VMEM((tokens, cols), jnp.float32)],
+        ),
+        out_shape=jax.ShapeDtypeStruct((exp_count, rows, cols), jnp.bfloat16),
+        compiler_params=pltpu.CompilerParams(vmem_limit_bytes=40 * 2**20),
+        cost_estimate=pl.CostEstimate(
+            flops=4 * tokens * width * cols * steps,
+            bytes_accessed=4 * steps * width * (tokens + cols) + 2 * exp_count * rows * cols,
+            transcendentals=0,
+        ),
+        name="project",
+    )(spots, left_a, left_b, proj, proj, table)
 
 
 def expert_kernel(exp_dim, spots, own, along, across, far_a, far_b, gain, gate_w, up_w, gate_v, up_v, route, out, total, squares):
@@ -342,22 +402,22 @@
                 piece = active[source * tokens : (source + 1) * tokens] * route[spot][0]
                 piece = piece.astype(jnp.bfloat16)
                 if exp_dim == 0:
-                    out[core, spot] = piece.reshape((1,) + out.shape[2:])
+                    out[core, source] = piece.reshape(out.shape[2:])
                 else:
                     out[core, :, spot] = piece.reshape(out.shape[1], 1, *out.shape[3:])
 
 
 def run_expert(spots, blocks, gain, weights, route, half, exp_dim):
     chip_count, tokens, wide = blocks[0].shape
-    cols = wide // 2
+    cols = wide
     middle = chip_count // 2
-    steps = 2 * chip_count
+    steps = chip_count
     units = weights[0].shape[1]
     exp_count = route.shape[0]
     row_total = exp_count * tokens
     lane = math.gcd(128, cols)
     lead = (exp_count, tokens // half) if exp_dim == 0 else (tokens // half, exp_count)
-    by_chip = pl.BlockSpec((1, tokens, cols), lambda i, _: (i // 2, 0, i % 2))
+    by_chip = pl.BlockSpec((1, tokens, cols), lambda i, _: (i, 0, 0))
     by_cols = pl.BlockSpec((cols, units), lambda i, _: (i, 0))
     out = pl.pallas_call(
         functools.partial(expert_kernel, exp_dim),
@@ -369,10 +429,10 @@
                 by_chip,
                 by_chip,
                 pl.BlockSpec(
-                    (1, tokens, cols), lambda i, _: (jnp.minimum(i // 2, middle - 1), 0, i % 2)
+                    (1, tokens, cols), lambda i, _: (jnp.minimum(i, middle - 1), 0, 0)
                 ),
                 pl.BlockSpec(
-                    (1, tokens, cols), lambda i, _: (jnp.maximum(i // 2 - middle, 0), 0, i % 2)
+                    (1, tokens, cols), lambda i, _: (jnp.maximum(i - middle, 0), 0, 0)
                 ),
                 pl.BlockSpec((1, 1, cols), lambda i, _: (i, 0, 0)),
                 by_cols,
@@ -399,44 +459,53 @@
     return out.reshape(2, row_total, units)
 
 
-def down_kernel(exp_dim, spots, active, down_w, down_v, hidden, out):
+def down_kernel(start, spots, active, down_w, down_v, hidden, *outs):
     sums = jnp.dot(active[0], down_w[...], preferred_element_type=jnp.float32)
     sums += jnp.dot(active[1], down_v[...], preferred_element_type=jnp.float32)
-    out[...] = sums.astype(out.dtype).reshape(out.shape)
-
-    @pl.when(pl.program_id(0) == spots[0])
+    sums = sums.astype(jnp.bfloat16)
+    kept = outs[0]
+    if len(outs) == 1:
+        kept[...] = sums.reshape(kept.shape)
+    else:
+        tokens = sums.shape[0] // len(outs)
+        for source, out in enumerate(outs):
+            out[...] = sums[source * tokens : (source + 1) * tokens].reshape(out.shape)
+
+    @pl.when(pl.program_id(0) + start == spots[0])
     def _():
-        spot = pl.ds(spots[1], 1)
-        place = (spot,) if exp_dim == 0 else (slice(None), spot)
-        piece = out[place].astype(jnp.float32)
-        out[place] = (piece + hidden[...].reshape(piece.shape)).astype(out.dtype)
-
-
-def run_down(spots, active, down_w, down_v, hidden, exp_count, exp_dim):
-    units, model_width = down_w.shape
-    chip_count, half, wide = hidden.shape
-    cols = wide
-    lead = (exp_count, chip_count) if exp_dim == 0 else (chip_count, exp_count)
-    by_cols = pl.BlockSpec((units, cols), lambda i, _: (0, i))
+        place = (slice(None), pl.ds(spots[1], 1)) if len(outs) == 1 else ...
+        piece = kept[place].astype(jnp.float32)
+        kept[place] = (piece + hidden[...].reshape(piece.shape)).astype(kept.dtype)
+
+
+def run_down(spots, active, down_w, down_v, hidden, exp_count, start, stop):
+    units = down_w.shape[0]
+    chip_count, half, cols = hidden.shape
     rows = active.shape[1]
+    whole = stop - start == chip_count
+    lead = (chip_count, exp_count) if whole else (chip_count,)
+    zeros = (0,) * len(lead + (half,))
+    by_cols = pl.BlockSpec((units, cols), lambda i, _: (0, i + start))
+    count = 1 if whole else exp_count
+    shape = lead + (half, (stop - start) * cols)
     return pl.pallas_call(
-        functools.partial(down_kernel, exp_dim),
+        functools.partial(down_kernel, start),
         grid_spec=pltpu.PrefetchScalarGridSpec(
             num_scalar_prefetch=1,
-            grid=(model_width // cols,),
+            grid=(stop - start,),
             in_specs=[
                 pl.BlockSpec((2, rows, units), lambda i, _: (0, 0, 0)),
                 by_cols,
                 by_cols,
                 pl.BlockSpec((chip_count, half, cols), lambda i, _: (0, 0, 0)),
             ],
-            out_specs=pl.BlockSpec(lead + (half, cols), lambda i, _: (0, 0, 0, i)),
+            out_specs=[pl.BlockSpec(lead + (half, cols), lambda i, _: (*zeros, i))] * count,
         ),
-        out_shape=jax.ShapeDtypeStruct(lead + (half, model_width), jnp.bfloat16),
+        out_shape=[jax.ShapeDtypeStruct(shape, jnp.bfloat16)] * count,
         compiler_params=pltpu.CompilerParams(vmem_limit_bytes=56 * 2**20),
         cost_estimate=pl.CostEstimate(
-            flops=4 * rows * units * model_width,
-            bytes_accessed=2 * model_width * (rows + 2 * units),
+            flops=4 * rows * units * cols * (stop - start),
+            bytes_accessed=2 * cols * (stop - start) * (rows + 2 * units),
             transcendentals=0,
         ),
         name="down",
@@ -544,15 +613,6 @@
     gain = lax.dynamic_slice_in_dim(ffn_gain, chip_index * 2 * cols, 2 * cols, 0)
     spots = jnp.stack([chip_index, exp_index]).astype(jnp.int32)
     group_tokens = ctx_count * half
-    def project(spread_heads):
-        pieces = jnp.einsum(
-            "csk,ckd->sd",
-            spread_heads,
-            out_proj.reshape(ctx_count, width, cols),
-            preferred_element_type=jnp.float32,
-        ).astype(jnp.bfloat16)
-        return pieces.reshape(exp_count, group_tokens, cols)
-
     def exchange(pieces):
         return lax.all_to_all(pieces, "exp", split_axis=0, concat_axis=0, tiled=True)
 
@@ -570,16 +630,23 @@
         return sums, scaled
 
     middle = chip_count // 2
-    spread_first = lax.all_gather(attended[0], ctx, axis=0)
+    proj = out_proj.reshape(ctx_count, width, cols)
+    core_spot = core_index.astype(jnp.int32).reshape(1)
+    spread_first = lax.all_gather(attended[0], "z", axis=0)
+    spread_other = sibling(spread_first)
     spread_first, later = lax.optimization_barrier((spread_first, attended[1]))
     spread_second = lax.all_gather(later, ctx, axis=0)
-    pieces = exchange(jnp.concatenate([project(spread_first), table], 1))
+    pieces = exchange(
+        run_project(core_spot, spread_first, spread_other, False, proj, table, exp_count, True)
+    )
     route = pieces[:, group_tokens:].reshape(exp_count, -1)[:, : 2 * chip_count * share]
     route = jnp.sum(
         route.reshape(exp_count, 2, chip_count, 2, half).astype(jnp.float32), axis=1
     )
     sums_first, scaled_first = settle(pieces, 0)
-    pieces = project(spread_second)
+    pieces = run_project(
+        core_spot, spread_second, spread_second, True, proj, table, exp_count, False
+    )
     pieces, scaled_first = lax.optimization_barrier((pieces, scaled_first))
     plane_first = lax.all_gather(scaled_first, "z", axis=0)
     pieces, plane_first = lax.optimization_barrier((exchange(pieces), plane_first))
@@ -591,16 +658,20 @@
     far_a, far_b, plane_second = lax.optimization_barrier((far_a, far_b, plane_second))
     weights = (expert_gate[0], expert_up[0], other_gate, other_up)
 
-    def run_group(blocks, sums, group):
+    def run_active(blocks, group):
         route_rows = route[:, :, group].reshape(exp_count, chip_count * half, 1)
-        active = run_expert(spots, blocks, ffn_gain, weights, route_rows, half, 1 - group)
-        return run_down(spots, active, expert_down[0], other_down, sums, exp_count, 1 - group)
-
-    first = run_group((plane_first, along, across, far_a, far_b), sums_first, 0)
+        return run_expert(spots, blocks, ffn_gain, weights, route_rows, half, 1 - group)
+
+    def run_outs(active, sums, start, stop):
+        return run_down(
+            spots, active, expert_down[0], other_down, sums, exp_count, start, stop
+        )
+
+    active = run_active((plane_first, along, across, far_a, far_b), 0)
+    (first,) = run_outs(active, sums_first, 0, chip_count)
     along, across = plane_step(plane_second, 1), plane_step(plane_second, 2)
     first, along, across = lax.optimization_barrier((first, along, across))
     far_a, far_b = plane_step(along[:middle], 2), plane_step(across[middle:], 1)
-    second = run_group((plane_second, along, across, far_a, far_b), sums_second, 1)
 
     first = lax.psum_scatter(
         first.reshape(chip_count, exp_count * half, model_width),
@@ -608,14 +679,22 @@
         scatter_dimension=0,
         tiled=True,
     )
+    active = run_active((plane_second, along, across, far_a, far_b), 1)
+
+    sides = []
+    for start, stop in ((0, middle), (middle, chip_count)):
+        own, *given = run_outs(active, sums_second, start, stop)
+        total = own.astype(jnp.float32)
+        for step, block in enumerate(given, 1):
+            total = total + plane_step(block, step).astype(jnp.float32)
+        sides.append(total.astype(jnp.bfloat16))
+    second = jnp.concatenate(sides, 2)
+    second, first = lax.optimization_barrier((second, first))
+    second = lax.psum_scatter(second, "z", scatter_dimension=0, tiled=True)
     first = lax.all_to_all(
         first.reshape(exp_count, half, model_width), "exp", split_axis=0, concat_axis=0, tiled=True
     )
     first = jnp.sum(first.astype(jnp.float32), axis=0).astype(jnp.bfloat16)
-
-    second = lax.all_to_all(second, "exp", split_axis=0, concat_axis=0, tiled=True)
-    second = jnp.sum(second.astype(jnp.float32), axis=0).astype(jnp.bfloat16)
-    second = lax.psum_scatter(second, "z", scatter_dimension=0, tiled=True)
     return jnp.concatenate([first, second.reshape(half, model_width)], 0)
 
 

time: 347 us -> 338 us (0.974)
  blocking collectives: 97.8 us -> 54.9 us
  waiting for transfers between devices: 122 us -> 146 us
  matrix products: 11 us -> 0 us
  starting transfers between devices: 25.1 us -> 35.1 us
  Pallas kernels: 46 us -> 53.7 us
  local copies, waits for them, and re-layouts: 17.8 us -> 24.1 us
    all_to_all x1 -> x0, blocking collectives: 45.2 us -> none  [by_heads(): lax.all_to_all(second, 'exp', split_axis=0, concat_axis=0, tiled=True)]
    ppermute x8 -> x14, waiting for transfers between devices: 17.9 us -> 45.7 us  [plane_step(): return lax.ppermute(block, 'exp', [(i, i ^ step) for i in range(count)])]
    pallas_call x2 -> x5, Pallas kernels: 14.9 us -> 26 us  [the longest x3 16.8 us: run_down(): pl.pallas_call(functools.partial(down_kernel, start), grid_spec=pltpu.Pre...]
    dot_general x2 -> x0, matrix products: 11 us -> none  [project(): jnp.einsum('csk,ckd->sd', spread_heads, out_proj.reshape(ctx_count, width...]
    unnamed x46 -> x58, local copies, waits for them, and re-layouts: 6.58 us -> 13.7 us
    ppermute x8 -> x14, starting transfers between devices: 10.3 us -> 17 us  [plane_step(): return lax.ppermute(block, 'exp', [(i, i ^ step) for i in range(count)])]
    all_gather x1, waiting for transfers between devices: 5.11 us -> 0.01 us  [by_heads(): spread_second = lax.all_gather(later, ctx, axis=0)]
    pallas_call x2, Pallas kernels: 25.9 us -> 21.7 us  [run_expert(): pl.pallas_call(functools.partial(expert_kernel, exp_dim), grid_spec=pltpu...]
  transfers between devices with their start and end apart: 20 -> 27, of which waited for: 11 -> 16; matrix products, arithmetic and copies ran while one was open for 8% -> 4% of each run, Pallas kernels for 12% -> 14%
where the time goes in v7:
time: 338 us; the launch traced here: 337 us
  waiting for transfers between devices  146 us (43%)
  blocking collectives  54.9 us (16%)
  Pallas kernels  53.7 us (16%)
  starting transfers between devices  35.1 us (10%)
  local copies, waits for them, and re-layouts  24.1 us (7%)
  between operations  13.6 us (4%)
  other arithmetic  9.65 us (3%)
    all_to_all x1, waiting for transfers between devices, by_heads(): moved = lax.all_to_all(packed, ctx, split_axis=0, concat_axis=0, tiled=True)  48.7 us
    ppermute x14, waiting for transfers between devices, plane_step(): return lax.ppermute(block, 'exp', [(i, i ^ step) for i in range(count)])  45.7 us
    all_gather x1, waiting for transfers between devices, by_heads(): spread_first = lax.all_gather(attended[0], 'z', axis=0)  26.9 us
    pallas_call x2, Pallas kernels, run_expert(): pl.pallas_call(functools.partial(expert_kernel, exp_dim), grid_spec=pltpu...  21.7 us
    all_gather x1, blocking collectives, by_heads(): plane_first = lax.all_gather(scaled_first, 'z', axis=0)  20.4 us
    all_gather x1, blocking collectives, by_heads(): plane_second = lax.all_gather(scaled_second, 'z', axis=0)  20.1 us
    ppermute x14, starting transfers between devices, plane_step(): return lax.ppermute(block, 'exp', [(i, i ^ step) for i in range(count)])  17 us
    pallas_call x3, Pallas kernels, run_down(): pl.pallas_call(functools.partial(down_kernel, start), grid_spec=pltpu.Pre...  16.8 us
  transfers between devices with their start and end apart: 27, of which 16 were waited for; matrix products, arithmetic and copies ran while one was open for 4% of the time, Pallas kernels for 14%

profile of v7, /device:TPU:0, one launch (start us, length us, event | category | flops | bytes accessed | tf_op | source)
XLA Modules:
  0.0 336.8 jit_solution(14406172385547546969)
XLA Ops:
  15.8 6.3 %all-to-all-start = ((bf16[8,512,256]{2,1,0:T(8,128)(2,1)}), bf16[8,512,256]{2,1,0:T(8,128)(2,1)S(1)}, u32[]{:S(2)}, u32[]{:S(2)}) async-start(bf16[8,512,256]{2,1,0:T(8,128)(2,1)} %bitcast_dynamic-update-slice_fusion.3), calls=%async_computation | async-start | bytes 4194304 | tf_op jit(solution)/shard_map/all_to_all | solution.py:592
  22.5 48.7 %all-to-all-done.moved = bf16[8,512,256]{2,1,0:T(8,128)(2,1)S(1)} async-done(((bf16[8,512,256]{2,1,0:T(8,128)(2,1)}), bf16[8,512,256]{2,1,0:T(8,128)(2,1)S(1)}, u32[]{:S(2)}, u32[]{:S(2)}) %all-to-all-start) | async-done | bytes 2097184 | tf_op jit(solution)/shard_map/all_to_all | solution.py:592
  72.0 6.1 %attend.1 = (bf16[512,256]{1,0:T(8,128)(2,1)}, bf16[512,256]{1,0:T(8,128)(2,1)}) custom-call(bf16[8,512,256]{2,1,0:T(8,128)(2,1)S(1)} %all-to-all-done.moved, f32[8,1024]{1,0:T(8,128)S(1)} %tile.12.taps, f32[1024,4]{1,0:T(8,128)S(1)} %copy.116.gates), custom_call_target="tpu_custom_call" | custom-call | tf_op jit(solution)/shard_map/attend/pallas_call | solution.py:298
  78.2 26.9 %all-gather.6.cloned.1.call-done = bf16[2048,256]{1,0:T(8,128)(2,1)} async-done(((bf16[512,256]{1,0:T(8,128)(2,1)}), bf16[2048,256]{1,0:T(8,128)(2,1)}) %all-gather.6.cloned.1.call-update) | async-done | bytes 1048592 | tf_op jit(solution)/shard_map/all_gather | solution.py:635
  111.3 4.6 %project.3 = bf16[4,144,896]{2,1,0:T(8,128)(2,1)} custom-call(s32[1]{0:T(128)} %bitcast.2.spots, bf16[4,512,256]{2,1,0:T(8,128)(2,1)S(1)} %bitcast.109, bf16[4,512,256]{2,1,0:T(8,128)(2,1)S(1)} %collective-permute-done.left_b, bf16[8,256,896]{2,1,0:T(8,128)(2,1)S(1)} %bitcast.102, bf16[8,256,896]{2,1,0:T(8,128)(2,1)S(1)} %bitcast.103, ...), custom_call_target="tpu_custom_call" | custom-call | flops 1879048192 | bytes 6799360 | tf_op jit(solution)/shard_map/project/pallas_call | solution.py:344
  116.0 3.6 %all-to-all-start.1 = ((bf16[4,144,896]{2,1,0:T(8,128)(2,1)}), bf16[4,144,896]{2,1,0:T(8,128)(2,1)S(1)}, u32[]{:S(2)}, u32[]{:S(2)}) async-start(bf16[4,144,896]{2,1,0:T(8,128)(2,1)} %project.3), calls=%async_computation.1 | async-start | bytes 2064384 | tf_op jit(solution)/shard_map/all_to_all | solution.py:617
  122.7 10.8 %all-to-all-done.1 = bf16[4,144,896]{2,1,0:T(8,128)(2,1)S(1)} async-done(((bf16[4,144,896]{2,1,0:T(8,128)(2,1)}), bf16[4,144,896]{2,1,0:T(8,128)(2,1)S(1)}, u32[]{:S(2)}, u32[]{:S(2)}) %all-to-all-start.1) | async-done | bytes 1032224 | tf_op jit(solution)/shard_map/all_to_all | solution.py:617
  139.6 4.6 %project.2 = bf16[4,128,896]{2,1,0:T(8,128)(2,1)} custom-call(s32[1]{0:T(128)} %bitcast.2.spots, bf16[8,512,256]{2,1,0:T(8,128)(2,1)S(1)} %bitcast.106, bf16[8,512,256]{2,1,0:T(8,128)(2,1)S(1)} %bitcast.107, bf16[8,256,896]{2,1,0:T(8,128)(2,1)S(1)} %bitcast.104, bf16[8,256,896]{2,1,0:T(8,128)(2,1)S(1)} %bitcast.105, bf16[4,16,896]{2,1,0:T(8,128)(2,1)S(1)} %bitcast.111), custom_call_target="tpu_custom_call" | custom-call | flops 1879048192 | bytes 6684672 | tf_op jit(solution)/shard_map/project/pallas_call | solution.py:344
  144.2 7.2 %all-to-all-start.2 = ((bf16[4,128,896]{2,1,0:T(8,128)(2,1)}), bf16[4,128,896]{2,1,0:T(8,128)(2,1)S(1)}, u32[]{:S(2)}, u32[]{:S(2)}) async-start(bf16[4,128,896]{2,1,0:T(8,128)(2,1)} %project.2), calls=%async_computation.2 | async-start | bytes 1835008 | tf_op jit(solution)/shard_map/all_to_all | solution.py:617
  151.5 20.4 %all-gather.2 = bf16[256,1792]{1,0:T(8,128)(2,1)S(1)} all-gather(bf16[64,1792]{1,0:T(8,128)(2,1)} %fusion), channel_id=4, replica_groups=mesh['z'=4,'core'=2,'exp'=4] {'z'}, dimensions={0}, use_global_device_ids=true | all-gather | bytes 1146880 | tf_op jit(solution)/shard_map/all_gather | solution.py:651
  176.9 20.1 %all_gather.27.own = bf16[4,64,1792]{2,1,0:T(8,128)(2,1)S(1)} all-gather(bf16[1,64,1792]{2,1,0:T(8,128)(2,1)S(1)} %fusion.1), channel_id=1, replica_groups=mesh['z'=4,'core'=2,'exp'=4] {'z'}, dimensions={0}, use_global_device_ids=true | all-gather | bytes 1146880 | tf_op jit(solution)/shard_map/all_gather | solution.py:655
  201.5 8.3 %collective-permute-done.6.far_b = bf16[2,64,1792]{2,1,0:T(8,128)(2,1)} collective-permute-done((bf16[2,64,1792]{2,1,0:T(8,128)(2,1)S(1)}, bf16[2,64,1792]{2,1,0:T(8,128)(2,1)}, u32[]{:S(2)}, u32[]{:S(2)}) %collective-permute-start.6) | collective-permute-done | bytes 458784 | tf_op jit(solution)/shard_map/ppermute | solution.py:521
  215.2 10.8 %expert.2 = bf16[2,4,4,16,256]{4,3,2,1,0:T(8,128)(2,1)} custom-call(s32[2]{0:T(128)} %pad_add_fusion.spots, bf16[4,64,1792]{2,1,0:T(8,128)(2,1)} %bitcast.125, bf16[4,64,1792]{2,1,0:T(8,128)(2,1)} %copy-done.14, bf16[4,64,1792]{2,1,0:T(8,128)(2,1)} %copy-done.12, bf16[2,64,1792]{2,1,0:T(8,128)(2,1)} %collective-permute-done.5.far_a, ...), custom_call_target="tpu_custom_call" | custom-call | flops 3758096384 | bytes 18350080 | tf_op jit(solution)/shard_map/expert/pallas_call | solution.py:422
  226.1 7.5 %down.3 = bf16[4,4,16,7168]{3,2,1,0:T(8,128)(2,1)} custom-call(s32[2]{0:T(128)} %pad_add_fusion.spots, bf16[2,256,256]{2,1,0:T(8,128)(2,1)} %bitcast.139, bf16[256,7168]{1,0:T(8,128)(2,1)} %bitcast.113, bf16[256,7168]{1,0:T(8,128)(2,1)} %collective-permute-done.9.down_v, f32[4,16,1792]{2,1,0:T(8,128)} %pad_maximum_fusion.1.hidden), custom_call_target="tpu_custom_call" | custom-call | flops 1879048192 | bytes 11010048 | tf_op jit(solution)/shard_map/down/pallas_call | solution.py:491
  238.0 7.0 %collective-permute-done.13.far_b = bf16[2,64,1792]{2,1,0:T(8,128)(2,1)S(1)} collective-permute-done((bf16[2,64,1792]{2,1,0:T(8,128)(2,1)S(1)}, bf16[2,64,1792]{2,1,0:T(8,128)(2,1)S(1)}, u32[]{:S(2)}, u32[]{:S(2)}) %collective-permute-start.13) | collective-permute-done | bytes 458784 | tf_op jit(solution)/shard_map/ppermute | solution.py:521
  246.6 10.8 %expert.3 = bf16[2,4,4,16,256]{4,3,2,1,0:T(8,128)(2,1)} custom-call(s32[2]{0:T(128)} %pad_add_fusion.spots, bf16[4,64,1792]{2,1,0:T(8,128)(2,1)} %copy-done.6, bf16[4,64,1792]{2,1,0:T(8,128)(2,1)} %copy-done.15, bf16[4,64,1792]{2,1,0:T(8,128)(2,1)} %copy-done.13, bf16[2,64,1792]{2,1,0:T(8,128)(2,1)} %copy-done.22, bf16[2,64,1792]{2,1,0:T(8,128)(2,1)} %copy-done.21, ...), custom_call_target="tpu_custom_call" | custom-call | flops 3758096384 | bytes 18350080 | tf_op jit(solution)/shard_map/expert/pallas_call | solution.py:422
  257.5 4.6 %down.5 = (bf16[4,16,3584]{2,1,0:T(8,128)(2,1)}, bf16[4,16,3584]{2,1,0:T(8,128)(2,1)}, bf16[4,16,3584]{2,1,0:T(8,128)(2,1)}, bf16[4,16,3584]{2,1,0:T(8,128)(2,1)}) custom-call(s32[2]{0:T(128)} %pad_add_fusion.spots, bf16[2,256,256]{2,1,0:T(8,128)(2,1)} %bitcast.126, bf16[256,7168]{1,0:T(8,128)(2,1)} %bitcast.114, ...), custom_call_target="tpu_custom_call" | custom-call | flops 939524096 | bytes 5505024 | tf_op jit(solution)/shard_map/down/pallas_call | solution.py:491
  265.6 4.7 %down.4 = (bf16[4,16,3584]{2,1,0:T(8,128)(2,1)}, bf16[4,16,3584]{2,1,0:T(8,128)(2,1)}, bf16[4,16,3584]{2,1,0:T(8,128)(2,1)}, bf16[4,16,3584]{2,1,0:T(8,128)(2,1)}) custom-call(s32[2]{0:T(128)} %pad_add_fusion.spots, bf16[2,256,256]{2,1,0:T(8,128)(2,1)} %bitcast.127, bf16[256,7168]{1,0:T(8,128)(2,1)} %bitcast.115, ...), custom_call_target="tpu_custom_call" | custom-call | flops 939524096 | bytes 5505024 | tf_op jit(solution)/shard_map/down/pallas_call | solution.py:491
  272.2 3.6 %collective-permute-done.17 = bf16[4,16,3584]{2,1,0:T(8,128)(2,1)S(1)} collective-permute-done((bf16[4,16,3584]{2,1,0:T(8,128)(2,1)}, bf16[4,16,3584]{2,1,0:T(8,128)(2,1)S(1)}, u32[]{:S(2)}, u32[]{:S(2)}) %collective-permute-start.17) | collective-permute-done | bytes 458784 | tf_op jit(solution)/shard_map/ppermute | solution.py:521
  277.0 7.5 %collective-permute-done.18 = bf16[4,16,3584]{2,1,0:T(8,128)(2,1)S(1)} collective-permute-done((bf16[4,16,3584]{2,1,0:T(8,128)(2,1)}, bf16[4,16,3584]{2,1,0:T(8,128)(2,1)S(1)}, u32[]{:S(2)}, u32[]{:S(2)}) %collective-permute-start.18) | collective-permute-done | bytes 458784 | tf_op jit(solution)/shard_map/ppermute | solution.py:521
  286.1 9.4 %collective-permute-done.14 = bf16[4,16,3584]{2,1,0:T(8,128)(2,1)S(1)} collective-permute-done((bf16[4,16,3584]{2,1,0:T(8,128)(2,1)}, bf16[4,16,3584]{2,1,0:T(8,128)(2,1)S(1)}, u32[]{:S(2)}, u32[]{:S(2)}) %collective-permute-start.14) | collective-permute-done | bytes 458784 | tf_op jit(solution)/shard_map/ppermute | solution.py:521
  295.5 6.1 %collective-permute-done.15 = bf16[4,16,3584]{2,1,0:T(8,128)(2,1)S(1)} collective-permute-done((bf16[4,16,3584]{2,1,0:T(8,128)(2,1)}, bf16[4,16,3584]{2,1,0:T(8,128)(2,1)S(1)}, u32[]{:S(2)}, u32[]{:S(2)}) %collective-permute-start.15) | collective-permute-done | bytes 458784 | tf_op jit(solution)/shard_map/ppermute | solution.py:521
  302.9 14.4 %all_to_all.20 = bf16[4,16,7168]{2,1,0:T(8,128)(2,1)S(1)} all-to-all(bf16[4,16,7168]{2,1,0:T(8,128)(2,1)} %bitcast.141), channel_id=1, replica_groups=mesh['z'=4,'core'=2,'exp'=4] {'exp'}, dimensions={0} | all-to-all | bytes 1835008 | tf_op jit(solution)/shard_map/all_to_all | solution.py:694
  317.5 11.1 %reduce-scatter.5.cloned.1.call-done = bf16[1,16,7168]{2,1,0:T(8,128)(2,1)} async-done(((bf16[4,16,7168]{2,1,0:T(8,128)(2,1)}), bf16[1,16,7168]{2,1,0:T(8,128)(2,1)}) %reduce-scatter.5.cloned.1.call-update) | async-done | bytes 229392 | tf_op jit(solution)/shard_map/reduce_scatter | solution.py:693
  (171 shorter events, 57.8 us)
Async XLA Ops:
  15.8 55.4 %all-to-all-start = ((bf16[8,512,256]{2,1,0:T(8,128)(2,1)}), bf16[8,512,256]{2,1,0:T(8,128)(2,1)S(1)}, u32[]{:S(2)}, u32[]{:S(2)}) async-start(bf16[8,512,256]{2,1,0:T(8,128)(2,1)} %bitcast_dynamic-update-slice_fusion.3), calls=%async_computation | async-start | bytes 4194304 | tf_op jit(solution)/shard_map/all_to_all | solution.py:592
  22.2 82.9 %all-gather.6.cloned.1.call-start = ((), (), s32[]{:S(2)}) async-start(), calls=%async_computation.8 | async-start | bytes 1310720 | tf_op jit(solution)/shard_map/all_gather | solution.py:635
  78.1 57.9 %all-gather.8.cloned.1.call-start = ((), (), s32[]{:S(2)}) async-start(), calls=%async_computation.9 | async-start | bytes 2359296 | tf_op jit(solution)/shard_map/all_gather | solution.py:638
  116.0 17.5 %all-to-all-start.1 = ((bf16[4,144,896]{2,1,0:T(8,128)(2,1)}), bf16[4,144,896]{2,1,0:T(8,128)(2,1)S(1)}, u32[]{:S(2)}, u32[]{:S(2)}) async-start(bf16[4,144,896]{2,1,0:T(8,128)(2,1)} %project.3), calls=%async_computation.1 | async-start | bytes 2064384 | tf_op jit(solution)/shard_map/all_to_all | solution.py:617
  133.8 81.4 %collective-permute-start.7 = (bf16[7168,256]{1,0:T(8,128)(2,1)}, bf16[7168,256]{1,0:T(8,128)(2,1)}, u32[]{:S(2)}, u32[]{:S(2)}) collective-permute-start(bf16[7168,256]{1,0:T(8,128)(2,1)} %bitcast.116), channel_id=1, source_target_pairs={{0,4},{4,0},{1,5},{5,1},{2,6},{6,2},{3,7},{7,3},{8,12},{12,8},{9,1... | collective-permute-start | bytes 11010056 | tf_op jit(solution)/shard_map/ppermute | solution.py:516
  134.3 80.9 %collective-permute-start.8 = (bf16[7168,256]{1,0:T(8,128)(2,1)}, bf16[7168,256]{1,0:T(8,128)(2,1)}, u32[]{:S(2)}, u32[]{:S(2)}) collective-permute-start(bf16[7168,256]{1,0:T(8,128)(2,1)} %bitcast.119), channel_id=1, source_target_pairs={{0,4},{4,0},{1,5},{5,1},{2,6},{6,2},{3,7},{7,3},{8,12},{12,8},{9,1... | collective-permute-start | bytes 11010056 | tf_op jit(solution)/shard_map/ppermute | solution.py:516
  144.2 27.6 %all-to-all-start.2 = ((bf16[4,128,896]{2,1,0:T(8,128)(2,1)}), bf16[4,128,896]{2,1,0:T(8,128)(2,1)S(1)}, u32[]{:S(2)}, u32[]{:S(2)}) async-start(bf16[4,128,896]{2,1,0:T(8,128)(2,1)} %project.2), calls=%async_computation.2 | async-start | bytes 1835008 | tf_op jit(solution)/shard_map/all_to_all | solution.py:617
  151.4 151.4 %reduce-scatter.3.cloned.1.call-start = ((), (), s32[]{:S(2)}) async-start(), calls=%async_computation.6 | async-start | bytes 4587520 | tf_op jit(solution)/shard_map/reduce_scatter | solution.py:676
  151.4 74.6 %collective-permute-start.9 = (bf16[256,7168]{1,0:T(8,128)(2,1)}, bf16[256,7168]{1,0:T(8,128)(2,1)}, u32[]{:S(2)}, u32[]{:S(2)}) collective-permute-start(bf16[256,7168]{1,0:T(8,128)(2,1)} %bitcast.112), channel_id=1, source_target_pairs={{0,4},{4,0},{1,5},{5,1},{2,6},{6,2},{3,7},{7,3},{8,12},{12,8},{9,1... | collective-permute-start | bytes 11010056 | tf_op jit(solution)/shard_map/ppermute | solution.py:516
  173.3 23.8 %collective-permute-start.3 = (bf16[4,64,1792]{2,1,0:T(8,128)(2,1)S(1)}, bf16[4,64,1792]{2,1,0:T(8,128)(2,1)S(1)}, u32[]{:S(2)}, u32[]{:S(2)}) collective-permute-start(bf16[4,64,1792]{2,1,0:T(8,128)(2,1)S(1)} %bitcast.123), channel_id=1, source_target_pairs={{0,2},{1,3},{2,0},{3,1},{4,6},{5,7},{6,4},{7,5},{8,10},{9,11},{10,... | collective-permute-start | bytes 2752520 | tf_op jit(solution)/shard_map/ppermute | solution.py:521
  175.3 22.4 %collective-permute-start.2 = (bf16[4,64,1792]{2,1,0:T(8,128)(2,1)S(1)}, bf16[4,64,1792]{2,1,0:T(8,128)(2,1)S(1)}, u32[]{:S(2)}, u32[]{:S(2)}) collective-permute-start(bf16[4,64,1792]{2,1,0:T(8,128)(2,1)S(1)} %bitcast.124), channel_id=1, source_target_pairs={{0,1},{1,0},{2,3},{3,2},{4,5},{5,4},{6,7},{7,6},{8,9},{9,8},{10,11... | collective-permute-start | bytes 2752520 | tf_op jit(solution)/shard_map/ppermute | solution.py:521
  198.0 11.8 %collective-permute-start.6 = (bf16[2,64,1792]{2,1,0:T(8,128)(2,1)S(1)}, bf16[2,64,1792]{2,1,0:T(8,128)(2,1)}, u32[]{:S(2)}, u32[]{:S(2)}) collective-permute-start(bf16[2,64,1792]{2,1,0:T(8,128)(2,1)S(1)} %slice.61), channel_id=1, source_target_pairs={{0,1},{1,0},{2,3},{3,2},{4,5},{5,4},{6,7},{7,6},{8,9},{9,8},{10,11... | collective-permute-start | bytes 1376264 | tf_op jit(solution)/shard_map/ppermute | solution.py:521
  199.4 11.6 %collective-permute-start.5 = (bf16[2,64,1792]{2,1,0:T(8,128)(2,1)S(1)}, bf16[2,64,1792]{2,1,0:T(8,128)(2,1)}, u32[]{:S(2)}, u32[]{:S(2)}) collective-permute-start(bf16[2,64,1792]{2,1,0:T(8,128)(2,1)S(1)} %slice.60), channel_id=1, source_target_pairs={{0,2},{1,3},{2,0},{3,1},{4,6},{5,7},{6,4},{7,5},{8,10},{9,11},{10,... | collective-permute-start | bytes 1376264 | tf_op jit(solution)/shard_map/ppermute | solution.py:521
  211.0 22.5 %collective-permute-start.11 = (bf16[4,64,1792]{2,1,0:T(8,128)(2,1)S(1)}, bf16[4,64,1792]{2,1,0:T(8,128)(2,1)S(1)}, u32[]{:S(2)}, u32[]{:S(2)}) collective-permute-start(bf16[4,64,1792]{2,1,0:T(8,128)(2,1)S(1)} %all_gather.27.own), channel_id=1, source_target_pairs={{0,2},{1,3},{2,0},{3,1},{4,6},{5,7},{6,4},{7,5},{8,10},{9,11},{10,... | collective-permute-start | bytes 2752520 | tf_op jit(solution)/shard_map/ppermute | solution.py:521
  212.4 21.2 %collective-permute-start.10 = (bf16[4,64,1792]{2,1,0:T(8,128)(2,1)S(1)}, bf16[4,64,1792]{2,1,0:T(8,128)(2,1)S(1)}, u32[]{:S(2)}, u32[]{:S(2)}) collective-permute-start(bf16[4,64,1792]{2,1,0:T(8,128)(2,1)S(1)} %all_gather.27.own), channel_id=1, source_target_pairs={{0,1},{1,0},{2,3},{3,2},{4,5},{5,4},{6,7},{7,6},{8,9},{9,8},{10,11... | collective-permute-start | bytes 2752520 | tf_op jit(solution)/shard_map/ppermute | solution.py:521
  233.6 94.9 %reduce-scatter.5.cloned.1.call-start = ((), (), s32[]{:S(2)}) async-start(), calls=%async_computation.7 | async-start | bytes 1146880 | tf_op jit(solution)/shard_map/reduce_scatter | solution.py:693
  234.8 10.3 %collective-permute-start.13 = (bf16[2,64,1792]{2,1,0:T(8,128)(2,1)S(1)}, bf16[2,64,1792]{2,1,0:T(8,128)(2,1)S(1)}, u32[]{:S(2)}, u32[]{:S(2)}) collective-permute-start(bf16[2,64,1792]{2,1,0:T(8,128)(2,1)S(1)} %slice.66), channel_id=1, source_target_pairs={{0,1},{1,0},{2,3},{3,2},{4,5},{5,4},{6,7},{7,6},{8,9},{9,8},{10,11... | collective-permute-start | bytes 1376264 | tf_op jit(solution)/shard_map/ppermute | solution.py:521
  235.8 9.7 %collective-permute-start.12 = (bf16[2,64,1792]{2,1,0:T(8,128)(2,1)S(1)}, bf16[2,64,1792]{2,1,0:T(8,128)(2,1)S(1)}, u32[]{:S(2)}, u32[]{:S(2)}) collective-permute-start(bf16[2,64,1792]{2,1,0:T(8,128)(2,1)S(1)} %slice.65), channel_id=1, source_target_pairs={{0,2},{1,3},{2,0},{3,1},{4,6},{5,7},{6,4},{7,5},{8,10},{9,11},{10,... | collective-permute-start | bytes 1376264 | tf_op jit(solution)/shard_map/ppermute | solution.py:521
  262.1 13.7 %collective-permute-start.17 = (bf16[4,16,3584]{2,1,0:T(8,128)(2,1)}, bf16[4,16,3584]{2,1,0:T(8,128)(2,1)S(1)}, u32[]{:S(2)}, u32[]{:S(2)}) collective-permute-start(bf16[4,16,3584]{2,1,0:T(8,128)(2,1)} %get-tuple-element.53), channel_id=1, source_target_pairs={{0,1},{1,0},{2,3},{3,2},{4,5},{5,4},{6,7},{7,6},{8,9},{9,8},{10,11... | collective-permute-start | bytes 1376264 | tf_op jit(solution)/shard_map/ppermute | solution.py:521
  263.1 21.4 %collective-permute-start.18 = (bf16[4,16,3584]{2,1,0:T(8,128)(2,1)}, bf16[4,16,3584]{2,1,0:T(8,128)(2,1)S(1)}, u32[]{:S(2)}, u32[]{:S(2)}) collective-permute-start(bf16[4,16,3584]{2,1,0:T(8,128)(2,1)} %get-tuple-element.54), channel_id=1, source_target_pairs={{0,2},{1,3},{2,0},{3,1},{4,6},{5,7},{6,4},{7,5},{8,10},{9,11},{10,... | collective-permute-start | bytes 1376264 | tf_op jit(solution)/shard_map/ppermute | solution.py:521
  263.9 22.0 %collective-permute-start.19 = (bf16[4,16,3584]{2,1,0:T(8,128)(2,1)}, bf16[4,16,3584]{2,1,0:T(8,128)(2,1)S(1)}, u32[]{:S(2)}, u32[]{:S(2)}) collective-permute-start(bf16[4,16,3584]{2,1,0:T(8,128)(2,1)} %get-tuple-element.55), channel_id=1, source_target_pairs={{0,3},{1,2},{2,1},{3,0},{4,7},{5,6},{6,5},{7,4},{8,11},{9,10},{10,... | collective-permute-start | bytes 1376264 | tf_op jit(solution)/shard_map/ppermute | solution.py:521
  270.3 25.2 %collective-permute-start.14 = (bf16[4,16,3584]{2,1,0:T(8,128)(2,1)}, bf16[4,16,3584]{2,1,0:T(8,128)(2,1)S(1)}, u32[]{:S(2)}, u32[]{:S(2)}) collective-permute-start(bf16[4,16,3584]{2,1,0:T(8,128)(2,1)} %get-tuple-element.49), channel_id=1, source_target_pairs={{0,1},{1,0},{2,3},{3,2},{4,5},{5,4},{6,7},{7,6},{8,9},{9,8},{10,11... | collective-permute-start | bytes 1376264 | tf_op jit(solution)/shard_map/ppermute | solution.py:521
  271.4 30.2 %collective-permute-start.15 = (bf16[4,16,3584]{2,1,0:T(8,128)(2,1)}, bf16[4,16,3584]{2,1,0:T(8,128)(2,1)S(1)}, u32[]{:S(2)}, u32[]{:S(2)}) collective-permute-start(bf16[4,16,3584]{2,1,0:T(8,128)(2,1)} %get-tuple-element.50), channel_id=1, source_target_pairs={{0,2},{1,3},{2,0},{3,1},{4,6},{5,7},{6,4},{7,5},{8,10},{9,11},{10,... | collective-permute-start | bytes 1376264 | tf_op jit(solution)/shard_map/ppermute | solution.py:521
  275.8 25.8 %collective-permute-start.16 = (bf16[4,16,3584]{2,1,0:T(8,128)(2,1)}, bf16[4,16,3584]{2,1,0:T(8,128)(2,1)S(1)}, u32[]{:S(2)}, u32[]{:S(2)}) collective-permute-start(bf16[4,16,3584]{2,1,0:T(8,128)(2,1)} %get-tuple-element.51), channel_id=1, source_target_pairs={{0,3},{1,2},{2,1},{3,0},{4,7},{5,6},{6,5},{7,4},{8,11},{9,10},{10,... | collective-permute-start | bytes 1376264 | tf_op jit(solution)/shard_map/ppermute | solution.py:521
  (26 other events, 206.5 us)
Sparse Core Ops, SparseCore 0:
  78.2 26.8 all-gather.5
  106.7 28.5 all-gather.7
  233.7 67.0 reduce-scatter.2
  303.0 25.4 reduce-scatter.4

commit v8 on v7

--- a/solution.py
+++ b/solution.py
@@ -357,7 +357,7 @@
             scratch_shapes=[pltpu.VMEM((tokens, cols), jnp.float32)],
         ),
         out_shape=jax.ShapeDtypeStruct((exp_count, rows, cols), jnp.bfloat16),
-        compiler_params=pltpu.CompilerParams(vmem_limit_bytes=40 * 2**20),
+        compiler_params=pltpu.CompilerParams(vmem_limit_bytes=56 * 2**20),
         cost_estimate=pl.CostEstimate(
             flops=4 * tokens * width * cols * steps,
             bytes_accessed=4 * steps * width * (tokens + cols) + 2 * exp_count * rows * cols,
@@ -633,6 +633,9 @@
     proj = out_proj.reshape(ctx_count, width, cols)
     core_spot = core_index.astype(jnp.int32).reshape(1)
     spread_first = lax.all_gather(attended[0], "z", axis=0)
+    spread_first, other_gate, other_up, other_down = lax.optimization_barrier(
+        (spread_first, other_gate, other_up, other_down)
+    )
     spread_other = sibling(spread_first)
     spread_first, later = lax.optimization_barrier((spread_first, attended[1]))
     spread_second = lax.all_gather(later, ctx, axis=0)
@@ -647,8 +650,10 @@
     pieces = run_project(
         core_spot, spread_second, spread_second, True, proj, table, exp_count, False
     )
-    pieces, scaled_first = lax.optimization_barrier((pieces, scaled_first))
-    plane_first = lax.all_gather(scaled_first, "z", axis=0)
+    pieces, sums_first = lax.optimization_barrier((pieces, sums_first))
+    wide = 1 << (2 * cols - 1).bit_length()
+    padded = jnp.pad(scaled_first, ((0, 0), (0, wide - 2 * cols)))
+    plane_first = lax.all_gather(padded, "z", axis=0)[:, :, : 2 * cols]
     pieces, plane_first = lax.optimization_barrier((exchange(pieces), plane_first))
     sums_second, scaled_second = settle(pieces, 1)
     along, across = plane_step(plane_first, 1), plane_step(plane_first, 2)

time: 338 us -> 330 us (0.976)
  blocking collectives: 54.9 us -> 33.1 us
  waiting for transfers between devices: 146 us -> 165 us
  starting transfers between devices: 35.1 us -> 30.8 us
  Pallas kernels: 53.7 us -> 57.7 us
  local copies, waits for them, and re-layouts: 24.1 us -> 20.6 us
    all_gather x1 -> x0, blocking collectives: 20.4 us -> none  [by_heads(): plane_first = lax.all_gather(scaled_first, 'z', axis=0)]
    all_gather x0 -> x1, waiting for transfers between devices: none -> 17.5 us  [by_heads(): plane_first = lax.all_gather(padded, 'z', axis=0)[:, :, :2 * cols]]
    unnamed x58 -> x42, local copies, waits for them, and re-layouts: 13.7 us -> 7.78 us
    pallas_call x2, Pallas kernels: 9.22 us -> 13.2 us  [run_project(): pl.pallas_call(project_kernel, grid_spec=pltpu.PrefetchScalarGridSpec(num...]
    all_to_all x2, starting transfers between devices: 10.9 us -> 7.14 us  [exchange(): lax.all_to_all(pieces, 'exp', split_axis=0, concat_axis=0, tiled=True)]
  transfers between devices with their start and end apart: 27 -> 28, of which waited for: 16 -> 17; matrix products, arithmetic and copies ran while one was open for 4% -> 4% of each run, Pallas kernels for 14% -> 18%
where the time goes in v8:
time: 330 us; the launch traced here: 329 us
  waiting for transfers between devices  165 us (50%)
  Pallas kernels  57.7 us (17%)
  blocking collectives  33.1 us (10%)
  starting transfers between devices  30.8 us (9%)
  local copies, waits for them, and re-layouts  20.6 us (6%)
  between operations  13.6 us (4%)
  other arithmetic  7.81 us (2%)
    ppermute x14, waiting for transfers between devices, plane_step(): return lax.ppermute(block, 'exp', [(i, i ^ step) for i in range(count)])  47.9 us
    all_to_all x1, waiting for transfers between devices, by_heads(): moved = lax.all_to_all(packed, ctx, split_axis=0, concat_axis=0, tiled=True)  47.8 us
    all_gather x1, waiting for transfers between devices, by_heads(): spread_first = lax.all_gather(attended[0], 'z', axis=0)  26.9 us
    pallas_call x2, Pallas kernels, run_expert(): pl.pallas_call(functools.partial(expert_kernel, exp_dim), grid_spec=pltpu...  21.7 us
    all_gather x1, blocking collectives, by_heads(): plane_second = lax.all_gather(scaled_second, 'z', axis=0)  19.6 us
    all_gather x1, waiting for transfers between devices, by_heads(): plane_first = lax.all_gather(padded, 'z', axis=0)[:, :, :2 * cols]  17.5 us
    pallas_call x3, Pallas kernels, run_down(): pl.pallas_call(functools.partial(down_kernel, start), grid_spec=pltpu.Pre...  16.8 us
    ppermute x14, starting transfers between devices, plane_step(): return lax.ppermute(block, 'exp', [(i, i ^ step) for i in range(count)])  15.8 us
  transfers between devices with their start and end apart: 28, of which 17 were waited for; matrix products, arithmetic and copies ran while one was open for 4% of the time, Pallas kernels for 18%

profile of v8, /device:TPU:0, one launch (start us, length us, event | category | flops | bytes accessed | tf_op | source)
XLA Modules:
  0.0 328.5 jit_solution(6917231944955758023)
XLA Ops:
  15.9 6.3 %all-to-all-start = ((bf16[8,512,256]{2,1,0:T(8,128)(2,1)}), bf16[8,512,256]{2,1,0:T(8,128)(2,1)S(1)}, u32[]{:S(2)}, u32[]{:S(2)}) async-start(bf16[8,512,256]{2,1,0:T(8,128)(2,1)} %bitcast_dynamic-update-slice_fusion.3), calls=%async_computation | async-start | bytes 4194304 | tf_op jit(solution)/shard_map/all_to_all | solution.py:592
  23.5 47.8 %all-to-all-done.moved = bf16[8,512,256]{2,1,0:T(8,128)(2,1)S(1)} async-done(((bf16[8,512,256]{2,1,0:T(8,128)(2,1)}), bf16[8,512,256]{2,1,0:T(8,128)(2,1)S(1)}, u32[]{:S(2)}, u32[]{:S(2)}) %all-to-all-start) | async-done | bytes 2097184 | tf_op jit(solution)/shard_map/all_to_all | solution.py:592
  72.1 6.0 %attend.1 = (bf16[512,256]{1,0:T(8,128)(2,1)}, bf16[512,256]{1,0:T(8,128)(2,1)}) custom-call(bf16[8,512,256]{2,1,0:T(8,128)(2,1)S(1)} %all-to-all-done.moved, f32[8,1024]{1,0:T(8,128)S(1)} %tile.12.taps, f32[1024,4]{1,0:T(8,128)S(1)} %copy.116.gates), custom_call_target="tpu_custom_call" | custom-call | tf_op jit(solution)/shard_map/attend/pallas_call | solution.py:298
  78.2 26.9 %all-gather.7.cloned.1.call-done = bf16[2048,256]{1,0:T(8,128)(2,1)} async-done(((bf16[512,256]{1,0:T(8,128)(2,1)}), bf16[2048,256]{1,0:T(8,128)(2,1)}) %all-gather.7.cloned.1.call-update) | async-done | bytes 1048592 | tf_op jit(solution)/shard_map/all_gather | solution.py:635
  109.1 6.7 %project.3 = bf16[4,144,896]{2,1,0:T(8,128)(2,1)} custom-call(s32[1]{0:T(128)} %bitcast.2.spots, bf16[4,512,256]{2,1,0:T(8,128)(2,1)} %bitcast.135, bf16[4,512,256]{2,1,0:T(8,128)(2,1)} %copy-done.7, bf16[8,256,896]{2,1,0:T(8,128)(2,1)} %bitcast.102, bf16[8,256,896]{2,1,0:T(8,128)(2,1)} %bitcast.103, bf16[4,16,896]{2,1,0:T(8,128)(2,1)} %bitcast.136), custom_call_target="tpu_custom_call" | custom-call | flops 1879048192 | bytes 6799360 | tf_op jit(solution)/shard_map/project/pallas_call | solution.py:344
  115.8 3.6 %all-to-all-start.1 = ((bf16[4,144,896]{2,1,0:T(8,128)(2,1)}), bf16[4,144,896]{2,1,0:T(8,128)(2,1)S(1)}, u32[]{:S(2)}, u32[]{:S(2)}) async-start(bf16[4,144,896]{2,1,0:T(8,128)(2,1)} %project.3), calls=%async_computation.1 | async-start | bytes 2064384 | tf_op jit(solution)/shard_map/all_to_all | solution.py:617
  121.8 11.5 %all-to-all-done.1 = bf16[4,144,896]{2,1,0:T(8,128)(2,1)S(1)} async-done(((bf16[4,144,896]{2,1,0:T(8,128)(2,1)}), bf16[4,144,896]{2,1,0:T(8,128)(2,1)S(1)}, u32[]{:S(2)}, u32[]{:S(2)}) %all-to-all-start.1) | async-done | bytes 1032224 | tf_op jit(solution)/shard_map/all_to_all | solution.py:617
  136.7 6.5 %project.2 = bf16[4,128,896]{2,1,0:T(8,128)(2,1)} custom-call(s32[1]{0:T(128)} %bitcast.2.spots, bf16[8,512,256]{2,1,0:T(8,128)(2,1)} %bitcast.117, bf16[8,512,256]{2,1,0:T(8,128)(2,1)} %bitcast.118, bf16[8,256,896]{2,1,0:T(8,128)(2,1)} %bitcast.104, bf16[8,256,896]{2,1,0:T(8,128)(2,1)} %bitcast.105, bf16[4,16,896]{2,1,0:T(8,128)(2,1)} %bitcast.137), custom_call_target="tpu_custom_call" | custom-call | flops 1879048192 | bytes 6684672 | tf_op jit(solution)/shard_map/project/pallas_call | solution.py:344
  143.2 3.5 %all-to-all-start.2 = ((bf16[4,128,896]{2,1,0:T(8,128)(2,1)}), bf16[4,128,896]{2,1,0:T(8,128)(2,1)S(1)}, u32[]{:S(2)}, u32[]{:S(2)}) async-start(bf16[4,128,896]{2,1,0:T(8,128)(2,1)} %project.2), calls=%async_computation.2 | async-start | bytes 1835008 | tf_op jit(solution)/shard_map/all_to_all | solution.py:617
  146.9 17.5 %all-gather.11.cloned.1.call-done = bf16[256,2048]{1,0:T(8,128)(2,1)} async-done(((bf16[64,2048]{1,0:T(8,128)(2,1)}), bf16[256,2048]{1,0:T(8,128)(2,1)}) %all-gather.11.cloned.1.call-update) | async-done | bytes 1048592 | tf_op jit(solution)/shard_map/all_gather | solution.py:656
  169.1 19.6 %all_gather.27.own = bf16[4,64,1792]{2,1,0:T(8,128)(2,1)S(1)} all-gather(bf16[1,64,1792]{2,1,0:T(8,128)(2,1)S(1)} %fusion.1), channel_id=1, replica_groups=mesh['z'=4,'core'=2,'exp'=4] {'z'}, dimensions={0}, use_global_device_ids=true | all-gather | bytes 1146880 | tf_op jit(solution)/shard_map/all_gather | solution.py:660
  193.6 9.2 %collective-permute-done.9.far_b = bf16[2,64,1792]{2,1,0:T(8,128)(2,1)} collective-permute-done((bf16[2,64,1792]{2,1,0:T(8,128)(2,1)S(1)}, bf16[2,64,1792]{2,1,0:T(8,128)(2,1)}, u32[]{:S(2)}, u32[]{:S(2)}) %collective-permute-start.9) | collective-permute-done | bytes 458784 | tf_op jit(solution)/shard_map/ppermute | solution.py:521
  206.5 10.8 %expert.2 = bf16[2,4,4,16,256]{4,3,2,1,0:T(8,128)(2,1)} custom-call(s32[2]{0:T(128)} %pad_add_fusion.spots, bf16[4,64,1792]{2,1,0:T(8,128)(2,1)} %copy-done.2, bf16[4,64,1792]{2,1,0:T(8,128)(2,1)} %copy-done.5, bf16[4,64,1792]{2,1,0:T(8,128)(2,1)} %copy-done.4, bf16[2,64,1792]{2,1,0:T(8,128)(2,1)} %collective-permute-done.8.far_a, ...), custom_call_target="tpu_custom_call" | custom-call | flops 3758096384 | bytes 18350080 | tf_op jit(solution)/shard_map/expert/pallas_call | solution.py:422
  217.3 7.5 %down.3 = bf16[4,4,16,7168]{3,2,1,0:T(8,128)(2,1)} custom-call(s32[2]{0:T(128)} %pad_add_fusion.spots, bf16[2,256,256]{2,1,0:T(8,128)(2,1)} %bitcast.132, bf16[256,7168]{1,0:T(8,128)(2,1)} %bitcast.107, bf16[256,7168]{1,0:T(8,128)(2,1)} %collective-permute-done.2.down_v, f32[4,16,1792]{2,1,0:T(8,128)} %pad_maximum_fusion.1.hidden), custom_call_target="tpu_custom_call" | custom-call | flops 1879048192 | bytes 11010048 | tf_op jit(solution)/shard_map/down/pallas_call | solution.py:491
  230.5 6.2 %collective-permute-done.13.far_b = bf16[2,64,1792]{2,1,0:T(8,128)(2,1)S(1)} collective-permute-done((bf16[2,64,1792]{2,1,0:T(8,128)(2,1)S(1)}, bf16[2,64,1792]{2,1,0:T(8,128)(2,1)S(1)}, u32[]{:S(2)}, u32[]{:S(2)}) %collective-permute-start.13) | collective-permute-done | bytes 458784 | tf_op jit(solution)/shard_map/ppermute | solution.py:521
  238.6 10.8 %expert.3 = bf16[2,4,4,16,256]{4,3,2,1,0:T(8,128)(2,1)} custom-call(s32[2]{0:T(128)} %pad_add_fusion.spots, bf16[4,64,1792]{2,1,0:T(8,128)(2,1)} %copy-done.3, bf16[4,64,1792]{2,1,0:T(8,128)(2,1)} %collective-permute-done.10.along, bf16[4,64,1792]{2,1,0:T(8,128)(2,1)} %copy-done.6, bf16[2,64,1792]{2,1,0:T(8,128)(2,1)} %copy-done.14, ...), custom_call_target="tpu_custom_call" | custom-call | flops 3758096384 | bytes 18350080 | tf_op jit(solution)/shard_map/expert/pallas_call | solution.py:422
  249.4 4.6 %down.5 = (bf16[4,16,3584]{2,1,0:T(8,128)(2,1)}, bf16[4,16,3584]{2,1,0:T(8,128)(2,1)}, bf16[4,16,3584]{2,1,0:T(8,128)(2,1)}, bf16[4,16,3584]{2,1,0:T(8,128)(2,1)}) custom-call(s32[2]{0:T(128)} %pad_add_fusion.spots, bf16[2,256,256]{2,1,0:T(8,128)(2,1)} %bitcast.119, bf16[256,7168]{1,0:T(8,128)(2,1)} %bitcast.108, ...), custom_call_target="tpu_custom_call" | custom-call | flops 939524096 | bytes 5505024 | tf_op jit(solution)/shard_map/down/pallas_call | solution.py:491
  257.5 4.7 %down.4 = (bf16[4,16,3584]{2,1,0:T(8,128)(2,1)}, bf16[4,16,3584]{2,1,0:T(8,128)(2,1)}, bf16[4,16,3584]{2,1,0:T(8,128)(2,1)}, bf16[4,16,3584]{2,1,0:T(8,128)(2,1)}) custom-call(s32[2]{0:T(128)} %pad_add_fusion.spots, bf16[2,256,256]{2,1,0:T(8,128)(2,1)} %bitcast.120, bf16[256,7168]{1,0:T(8,128)(2,1)} %bitcast.109, ...), custom_call_target="tpu_custom_call" | custom-call | flops 939524096 | bytes 5505024 | tf_op jit(solution)/shard_map/down/pallas_call | solution.py:491
  264.2 3.5 %collective-permute-done.17 = bf16[4,16,3584]{2,1,0:T(8,128)(2,1)S(1)} collective-permute-done((bf16[4,16,3584]{2,1,0:T(8,128)(2,1)}, bf16[4,16,3584]{2,1,0:T(8,128)(2,1)S(1)}, u32[]{:S(2)}, u32[]{:S(2)}) %collective-permute-start.17) | collective-permute-done | bytes 458784 | tf_op jit(solution)/shard_map/ppermute | solution.py:521
  269.1 9.6 %collective-permute-done.18 = bf16[4,16,3584]{2,1,0:T(8,128)(2,1)S(1)} collective-permute-done((bf16[4,16,3584]{2,1,0:T(8,128)(2,1)}, bf16[4,16,3584]{2,1,0:T(8,128)(2,1)S(1)}, u32[]{:S(2)}, u32[]{:S(2)}) %collective-permute-start.18) | collective-permute-done | bytes 458784 | tf_op jit(solution)/shard_map/ppermute | solution.py:521
  278.9 8.5 %collective-permute-done.14 = bf16[4,16,3584]{2,1,0:T(8,128)(2,1)S(1)} collective-permute-done((bf16[4,16,3584]{2,1,0:T(8,128)(2,1)}, bf16[4,16,3584]{2,1,0:T(8,128)(2,1)S(1)}, u32[]{:S(2)}, u32[]{:S(2)}) %collective-permute-start.14) | collective-permute-done | bytes 458784 | tf_op jit(solution)/shard_map/ppermute | solution.py:521
  287.4 6.8 %collective-permute-done.15 = bf16[4,16,3584]{2,1,0:T(8,128)(2,1)S(1)} collective-permute-done((bf16[4,16,3584]{2,1,0:T(8,128)(2,1)}, bf16[4,16,3584]{2,1,0:T(8,128)(2,1)S(1)}, u32[]{:S(2)}, u32[]{:S(2)}) %collective-permute-start.15) | collective-permute-done | bytes 458784 | tf_op jit(solution)/shard_map/ppermute | solution.py:521
  295.4 13.5 %all_to_all.20 = bf16[4,16,7168]{2,1,0:T(8,128)(2,1)S(1)} all-to-all(bf16[4,16,7168]{2,1,0:T(8,128)(2,1)} %bitcast.138), channel_id=1, replica_groups=mesh['z'=4,'core'=2,'exp'=4] {'exp'}, dimensions={0} | all-to-all | bytes 1835008 | tf_op jit(solution)/shard_map/all_to_all | solution.py:699
  309.1 11.1 %reduce-scatter.5.cloned.1.call-done = bf16[1,16,7168]{2,1,0:T(8,128)(2,1)} async-done(((bf16[4,16,7168]{2,1,0:T(8,128)(2,1)}), bf16[1,16,7168]{2,1,0:T(8,128)(2,1)}) %reduce-scatter.5.cloned.1.call-update) | async-done | bytes 229392 | tf_op jit(solution)/shard_map/reduce_scatter | solution.py:698
  (159 shorter events, 52.2 us)
Async XLA Ops:
  15.9 55.4 %all-to-all-start = ((bf16[8,512,256]{2,1,0:T(8,128)(2,1)}), bf16[8,512,256]{2,1,0:T(8,128)(2,1)S(1)}, u32[]{:S(2)}, u32[]{:S(2)}) async-start(bf16[8,512,256]{2,1,0:T(8,128)(2,1)} %bitcast_dynamic-update-slice_fusion.3), calls=%async_computation | async-start | bytes 4194304 | tf_op jit(solution)/shard_map/all_to_all | solution.py:592
  22.2 82.9 %all-gather.7.cloned.1.call-start = ((), (), s32[]{:S(2)}) async-start(), calls=%async_computation.8 | async-start | bytes 1310720 | tf_op jit(solution)/shard_map/all_gather | solution.py:635
  22.2 56.0 %collective-permute-start = (bf16[7168,256]{1,0:T(8,128)(2,1)}, bf16[7168,256]{1,0:T(8,128)(2,1)}, u32[]{:S(2)}, u32[]{:S(2)}) collective-permute-start(bf16[7168,256]{1,0:T(8,128)(2,1)} %bitcast.110), channel_id=1, source_target_pairs={{0,4},{4,0},{1,5},{5,1},{2,6},{6,2},{3,7},{7,3},{8,12},{12,8},{9,1... | collective-permute-start | bytes 11010056 | tf_op jit(solution)/shard_map/ppermute | solution.py:516
  22.7 55.5 %collective-permute-start.1 = (bf16[7168,256]{1,0:T(8,128)(2,1)}, bf16[7168,256]{1,0:T(8,128)(2,1)}, u32[]{:S(2)}, u32[]{:S(2)}) collective-permute-start(bf16[7168,256]{1,0:T(8,128)(2,1)} %bitcast.113), channel_id=1, source_target_pairs={{0,4},{4,0},{1,5},{5,1},{2,6},{6,2},{3,7},{7,3},{8,12},{12,8},{9,1... | collective-permute-start | bytes 11010056 | tf_op jit(solution)/shard_map/ppermute | solution.py:516
  22.8 55.4 %collective-permute-start.2 = (bf16[256,7168]{1,0:T(8,128)(2,1)}, bf16[256,7168]{1,0:T(8,128)(2,1)}, u32[]{:S(2)}, u32[]{:S(2)}) collective-permute-start(bf16[256,7168]{1,0:T(8,128)(2,1)} %bitcast.106), channel_id=1, source_target_pairs={{0,4},{4,0},{1,5},{5,1},{2,6},{6,2},{3,7},{7,3},{8,12},{12,8},{9,1... | collective-permute-start | bytes 11010056 | tf_op jit(solution)/shard_map/ppermute | solution.py:516
  78.1 58.6 %all-gather.9.cloned.1.call-start = ((), (), s32[]{:S(2)}) async-start(), calls=%async_computation.9 | async-start | bytes 2359296 | tf_op jit(solution)/shard_map/all_gather | solution.py:641
  115.8 17.5 %all-to-all-start.1 = ((bf16[4,144,896]{2,1,0:T(8,128)(2,1)}), bf16[4,144,896]{2,1,0:T(8,128)(2,1)S(1)}, u32[]{:S(2)}, u32[]{:S(2)}) async-start(bf16[4,144,896]{2,1,0:T(8,128)(2,1)} %project.3), calls=%async_computation.1 | async-start | bytes 2064384 | tf_op jit(solution)/shard_map/all_to_all | solution.py:617
  119.4 45.0 %all-gather.11.cloned.1.call-start = ((), (), s32[]{:S(2)}) async-start(), calls=%async_computation.10 | async-start | bytes 1310720 | tf_op jit(solution)/shard_map/all_gather | solution.py:656
  143.2 22.4 %all-to-all-start.2 = ((bf16[4,128,896]{2,1,0:T(8,128)(2,1)}), bf16[4,128,896]{2,1,0:T(8,128)(2,1)S(1)}, u32[]{:S(2)}, u32[]{:S(2)}) async-start(bf16[4,128,896]{2,1,0:T(8,128)(2,1)} %project.2), calls=%async_computation.2 | async-start | bytes 1835008 | tf_op jit(solution)/shard_map/all_to_all | solution.py:617
  146.7 148.7 %reduce-scatter.3.cloned.1.call-start = ((), (), s32[]{:S(2)}) async-start(), calls=%async_computation.6 | async-start | bytes 4587520 | tf_op jit(solution)/shard_map/reduce_scatter | solution.py:681
  166.0 22.8 %collective-permute-start.6 = (bf16[4,64,1792]{2,1,0:T(8,128)(2,1)S(1)}, bf16[4,64,1792]{2,1,0:T(8,128)(2,1)S(1)}, u32[]{:S(2)}, u32[]{:S(2)}) collective-permute-start(bf16[4,64,1792]{2,1,0:T(8,128)(2,1)S(1)} %slice.80.own), channel_id=1, source_target_pairs={{0,2},{1,3},{2,0},{3,1},{4,6},{5,7},{6,4},{7,5},{8,10},{9,11},{10,... | collective-permute-start | bytes 2752520 | tf_op jit(solution)/shard_map/ppermute | solution.py:521
  167.5 22.4 %collective-permute-start.5 = (bf16[4,64,1792]{2,1,0:T(8,128)(2,1)S(1)}, bf16[4,64,1792]{2,1,0:T(8,128)(2,1)S(1)}, u32[]{:S(2)}, u32[]{:S(2)}) collective-permute-start(bf16[4,64,1792]{2,1,0:T(8,128)(2,1)S(1)} %slice.80.own), channel_id=1, source_target_pairs={{0,1},{1,0},{2,3},{3,2},{4,5},{5,4},{6,7},{7,6},{8,9},{9,8},{10,11... | collective-permute-start | bytes 2752520 | tf_op jit(solution)/shard_map/ppermute | solution.py:521
  190.9 11.9 %collective-permute-start.9 = (bf16[2,64,1792]{2,1,0:T(8,128)(2,1)S(1)}, bf16[2,64,1792]{2,1,0:T(8,128)(2,1)}, u32[]{:S(2)}, u32[]{:S(2)}) collective-permute-start(bf16[2,64,1792]{2,1,0:T(8,128)(2,1)S(1)} %slice.65), channel_id=1, source_target_pairs={{0,1},{1,0},{2,3},{3,2},{4,5},{5,4},{6,7},{7,6},{8,9},{9,8},{10,11... | collective-permute-start | bytes 1376264 | tf_op jit(solution)/shard_map/ppermute | solution.py:521
  192.4 11.6 %collective-permute-start.8 = (bf16[2,64,1792]{2,1,0:T(8,128)(2,1)S(1)}, bf16[2,64,1792]{2,1,0:T(8,128)(2,1)}, u32[]{:S(2)}, u32[]{:S(2)}) collective-permute-start(bf16[2,64,1792]{2,1,0:T(8,128)(2,1)S(1)} %slice.64), channel_id=1, source_target_pairs={{0,2},{1,3},{2,0},{3,1},{4,6},{5,7},{6,4},{7,5},{8,10},{9,11},{10,... | collective-permute-start | bytes 1376264 | tf_op jit(solution)/shard_map/ppermute | solution.py:521
  204.0 20.8 %collective-permute-start.11 = (bf16[4,64,1792]{2,1,0:T(8,128)(2,1)S(1)}, bf16[4,64,1792]{2,1,0:T(8,128)(2,1)S(1)}, u32[]{:S(2)}, u32[]{:S(2)}) collective-permute-start(bf16[4,64,1792]{2,1,0:T(8,128)(2,1)S(1)} %all_gather.27.own), channel_id=1, source_target_pairs={{0,2},{1,3},{2,0},{3,1},{4,6},{5,7},{6,4},{7,5},{8,10},{9,11},{10,... | collective-permute-start | bytes 2752520 | tf_op jit(solution)/shard_map/ppermute | solution.py:521
  204.9 20.5 %collective-permute-start.10 = (bf16[4,64,1792]{2,1,0:T(8,128)(2,1)S(1)}, bf16[4,64,1792]{2,1,0:T(8,128)(2,1)}, u32[]{:S(2)}, u32[]{:S(2)}) collective-permute-start(bf16[4,64,1792]{2,1,0:T(8,128)(2,1)S(1)} %all_gather.27.own), channel_id=1, source_target_pairs={{0,1},{1,0},{2,3},{3,2},{4,5},{5,4},{6,7},{7,6},{8,9},{9,8},{10,11... | collective-permute-start | bytes 2752520 | tf_op jit(solution)/shard_map/ppermute | solution.py:521
  225.4 94.8 %reduce-scatter.5.cloned.1.call-start = ((), (), s32[]{:S(2)}) async-start(), calls=%async_computation.7 | async-start | bytes 1146880 | tf_op jit(solution)/shard_map/reduce_scatter | solution.py:698
  226.6 10.1 %collective-permute-start.13 = (bf16[2,64,1792]{2,1,0:T(8,128)(2,1)S(1)}, bf16[2,64,1792]{2,1,0:T(8,128)(2,1)S(1)}, u32[]{:S(2)}, u32[]{:S(2)}) collective-permute-start(bf16[2,64,1792]{2,1,0:T(8,128)(2,1)S(1)} %slice.70), channel_id=1, source_target_pairs={{0,1},{1,0},{2,3},{3,2},{4,5},{5,4},{6,7},{7,6},{8,9},{9,8},{10,11... | collective-permute-start | bytes 1376264 | tf_op jit(solution)/shard_map/ppermute | solution.py:521
  254.0 13.7 %collective-permute-start.17 = (bf16[4,16,3584]{2,1,0:T(8,128)(2,1)}, bf16[4,16,3584]{2,1,0:T(8,128)(2,1)S(1)}, u32[]{:S(2)}, u32[]{:S(2)}) collective-permute-start(bf16[4,16,3584]{2,1,0:T(8,128)(2,1)} %get-tuple-element.61), channel_id=1, source_target_pairs={{0,1},{1,0},{2,3},{3,2},{4,5},{5,4},{6,7},{7,6},{8,9},{9,8},{10,11... | collective-permute-start | bytes 1376264 | tf_op jit(solution)/shard_map/ppermute | solution.py:521
  255.1 23.6 %collective-permute-start.18 = (bf16[4,16,3584]{2,1,0:T(8,128)(2,1)}, bf16[4,16,3584]{2,1,0:T(8,128)(2,1)S(1)}, u32[]{:S(2)}, u32[]{:S(2)}) collective-permute-start(bf16[4,16,3584]{2,1,0:T(8,128)(2,1)} %get-tuple-element.62), channel_id=1, source_target_pairs={{0,2},{1,3},{2,0},{3,1},{4,6},{5,7},{6,4},{7,5},{8,10},{9,11},{10,... | collective-permute-start | bytes 1376264 | tf_op jit(solution)/shard_map/ppermute | solution.py:521
  256.0 22.7 %collective-permute-start.19 = (bf16[4,16,3584]{2,1,0:T(8,128)(2,1)}, bf16[4,16,3584]{2,1,0:T(8,128)(2,1)S(1)}, u32[]{:S(2)}, u32[]{:S(2)}) collective-permute-start(bf16[4,16,3584]{2,1,0:T(8,128)(2,1)} %get-tuple-element.63), channel_id=1, source_target_pairs={{0,3},{1,2},{2,1},{3,0},{4,7},{5,6},{6,5},{7,4},{8,11},{9,10},{10,... | collective-permute-start | bytes 1376264 | tf_op jit(solution)/shard_map/ppermute | solution.py:521
  262.2 25.2 %collective-permute-start.14 = (bf16[4,16,3584]{2,1,0:T(8,128)(2,1)}, bf16[4,16,3584]{2,1,0:T(8,128)(2,1)S(1)}, u32[]{:S(2)}, u32[]{:S(2)}) collective-permute-start(bf16[4,16,3584]{2,1,0:T(8,128)(2,1)} %get-tuple-element.57), channel_id=1, source_target_pairs={{0,1},{1,0},{2,3},{3,2},{4,5},{5,4},{6,7},{7,6},{8,9},{9,8},{10,11... | collective-permute-start | bytes 1376264 | tf_op jit(solution)/shard_map/ppermute | solution.py:521
  263.4 30.8 %collective-permute-start.15 = (bf16[4,16,3584]{2,1,0:T(8,128)(2,1)}, bf16[4,16,3584]{2,1,0:T(8,128)(2,1)S(1)}, u32[]{:S(2)}, u32[]{:S(2)}) collective-permute-start(bf16[4,16,3584]{2,1,0:T(8,128)(2,1)} %get-tuple-element.58), channel_id=1, source_target_pairs={{0,2},{1,3},{2,0},{3,1},{4,6},{5,7},{6,4},{7,5},{8,10},{9,11},{10,... | collective-permute-start | bytes 1376264 | tf_op jit(solution)/shard_map/ppermute | solution.py:521
  267.7 26.5 %collective-permute-start.16 = (bf16[4,16,3584]{2,1,0:T(8,128)(2,1)}, bf16[4,16,3584]{2,1,0:T(8,128)(2,1)S(1)}, u32[]{:S(2)}, u32[]{:S(2)}) collective-permute-start(bf16[4,16,3584]{2,1,0:T(8,128)(2,1)} %get-tuple-element.59), channel_id=1, source_target_pairs={{0,3},{1,2},{2,1},{3,0},{4,7},{5,6},{6,5},{7,4},{8,11},{9,10},{10,... | collective-permute-start | bytes 1376264 | tf_op jit(solution)/shard_map/ppermute | solution.py:521
  (19 other events, 161.4 us)
Sparse Core Ops, SparseCore 0:
  78.2 26.8 all-gather.6
  106.7 28.5 all-gather.8
  136.9 27.4 all-gather.10
  225.5 66.9 reduce-scatter.2
  295.6 24.6 reduce-scatter.4

commit v9 on v8

--- a/solution.py
+++ b/solution.py
@@ -226,6 +226,51 @@
     return block * lax.rsqrt(jnp.mean(block * block, axis=1, keepdims=True) + norm_eps)
 
 
+def side_spots(count, own, row_count, share, head_width):
+    spots = []
+    for piece in range(count):
+        first = 3 * row_count + piece // own * share
+        lane = piece % own * head_width
+        spots.append((slice(first, first + share), slice(lane, lane + head_width)))
+    return spots
+
+
+def pack_kernel(query, key, value, residual, side, out):
+    row_count, width = query.shape
+    share, head_width = side.shape[1:]
+    for spot, block in enumerate((query, key, value)):
+        out[0, spot * row_count : (spot + 1) * row_count, :] = block[...]
+    count = residual.shape[1] // head_width
+    spots = side_spots(count + 1, width // head_width, row_count, share, head_width)
+    for piece, (rows, lanes) in enumerate(spots[:-1]):
+        out[0, rows, lanes] = residual[:, piece * head_width : (piece + 1) * head_width]
+    rows, lanes = spots[-1]
+    out[0, rows, lanes] = side[0]
+
+
+def pack(query, key, value, residual, side, width):
+    ctx_count, share, head_width = side.shape
+    row_count = query.shape[0]
+    cols = residual.shape[1] // ctx_count
+    rows = 3 * row_count + (cols // head_width + 1) * head_width // width * share
+    heads = pl.BlockSpec((row_count, width), lambda i: (0, i))
+    return pl.pallas_call(
+        pack_kernel,
+        grid=(ctx_count,),
+        in_specs=[
+            heads,
+            heads,
+            heads,
+            pl.BlockSpec((share, cols), lambda i: (0, i)),
+            pl.BlockSpec((1, share, head_width), lambda i: (i, 0, 0)),
+        ],
+        out_specs=pl.BlockSpec((1, rows, width), lambda i: (i, 0, 0)),
+        out_shape=jax.ShapeDtypeStruct((ctx_count, rows, width), jnp.bfloat16),
+        compiler_params=pltpu.CompilerParams(vmem_limit_bytes=32 * 2**20),
+        name="pack",
+    )(query, key, value, residual, side)
+
+
 def attend_kernel(row_count, share, block_len, head_width, moved, taps, gates, out_a, out_b, keys, values):
     ctx_count = moved.shape[0]
     own = moved.shape[2] // head_width
@@ -273,11 +318,20 @@
             far = dot(weight.astype(jnp.bfloat16), comp_values) / total
             start = max(0, base - WINDOW)
             reach = base + row_count - start
-            spot = base + lax.broadcasted_iota(jnp.int32, (row_count, reach), 0)
-            key_spot = start + lax.broadcasted_iota(jnp.int32, (row_count, reach), 1)
-            seen = (key_spot <= spot) & (key_spot > spot - WINDOW)
             score = dot_rows(query, keys[start : start + reach, :])
-            weight = jnp.where(seen, jnp.exp(scale * score), 0.0)
+            weight = jnp.exp(scale * score)
+            edges = []
+            for first in range(0, reach, row_count):
+                piece = weight[:, first : first + row_count]
+                offset = base - start - first
+                ahead = lax.broadcasted_iota(jnp.int32, (row_count, row_count), 1)
+                ahead = ahead - lax.broadcasted_iota(jnp.int32, (row_count, row_count), 0)
+                if offset < row_count:
+                    piece = jnp.where(ahead <= offset, piece, 0.0)
+                if offset + row_count > WINDOW:
+                    piece = jnp.where(ahead > offset - WINDOW, piece, 0.0)
+                edges.append(piece)
+            weight = jnp.concatenate(edges, 1)
             total = jnp.sum(weight, axis=1, keepdims=True)
             near = dot(weight.astype(jnp.bfloat16), values[start : start + reach, :]) / total
             mixed = (
@@ -307,64 +361,66 @@
     )(moved, taps, gates)
 
 
-def project_kernel(spots, left_a, left_b, proj_a, proj_b, table, out, total):
+def project_kernel(paired, spots, left_a, left_b, proj, table, out, total):
     step = pl.program_id(0)
-    sums = jnp.dot(left_a[0], proj_a[0], preferred_element_type=jnp.float32)
-    sums += jnp.dot(left_b[0], proj_b[0], preferred_element_type=jnp.float32)
+    first = jnp.logical_or(paired, spots[0] == 0)
+    parts = []
+    for chip in range(left_a.shape[0]):
+        if paired:
+            parts += [left_a[chip, 0], left_a[chip, 1]]
+        else:
+            parts.append(jnp.where(first, left_a[chip, 0], left_b[chip, 0]))
+            parts.append(jnp.where(first, left_b[chip, 0], left_a[chip, 0]))
+    sums = jnp.dot(jnp.concatenate(parts, 1), proj[...], preferred_element_type=jnp.float32)
 
     @pl.when(step == 0)
     def _():
         total[...] = sums
-
-    @pl.when(step > 0)
-    def _():
-        total[...] += sums
 
     @pl.when(step == pl.num_programs(0) - 1)
     def _():
         exp_count = out.shape[0]
         tokens = total.shape[0] // exp_count
         for spot in range(exp_count):
-            rows = total[spot * tokens : (spot + 1) * tokens]
-            out[spot, :tokens] = rows.astype(jnp.bfloat16)
+            rows = slice(spot * tokens, (spot + 1) * tokens)
+            out[spot, :tokens] = (total[rows] + sums[rows]).astype(jnp.bfloat16)
             if out.shape[1] > tokens:
                 out[spot, tokens:] = table[spot]
 
 
 def run_project(spots, left_a, left_b, paired, proj, table, exp_count, extra):
+    depth, cols = proj.shape
     tokens, width = left_a.shape[1:]
-    cols = proj.shape[2]
-    steps = proj.shape[0] // 2
+    cores = 2 if paired else 1
+    chips = depth // (2 * width)
+    left_a = left_a.reshape(chips, cores, tokens, width)
+    left_b = left_b.reshape(chips, cores, tokens, width)
+    left = pl.BlockSpec((chips // 2, cores, tokens, width), lambda i, _: (i, 0, 0, 0))
+    unused = pl.BlockSpec((1, 1, tokens, width), lambda i, _: (0, 0, 0, 0))
     rows = tokens // exp_count + (table.shape[1] if extra else 0)
-    if paired:
-        maps = [lambda i, s: (2 * i, 0, 0), lambda i, s: (2 * i + 1, 0, 0)] * 2
-    else:
-        maps = [lambda i, s: (i, 0, 0)] * 2
-        maps += [lambda i, s: (2 * i + s[0], 0, 0), lambda i, s: (2 * i + 1 - s[0], 0, 0)]
     return pl.pallas_call(
-        project_kernel,
+        functools.partial(project_kernel, paired),
         grid_spec=pltpu.PrefetchScalarGridSpec(
             num_scalar_prefetch=1,
-            grid=(steps,),
+            grid=(2,),
             in_specs=[
-                pl.BlockSpec((1, tokens, width), maps[0]),
-                pl.BlockSpec((1, tokens, width), maps[1]),
-                pl.BlockSpec((1, width, cols), maps[2]),
-                pl.BlockSpec((1, width, cols), maps[3]),
-                pl.BlockSpec(table.shape, lambda i, s: (0, 0, 0)),
+                left,
+                unused if paired else left,
+                pl.BlockSpec((depth // 2, cols), lambda i, _: (i, 0)),
+                pl.BlockSpec(table.shape, lambda i, _: (0, 0, 0)),
             ],
-            out_specs=pl.BlockSpec((exp_count, rows, cols), lambda i, s: (0, 0, 0)),
+            out_specs=pl.BlockSpec((exp_count, rows, cols), lambda i, _: (0, 0, 0)),
             scratch_shapes=[pltpu.VMEM((tokens, cols), jnp.float32)],
         ),
         out_shape=jax.ShapeDtypeStruct((exp_count, rows, cols), jnp.bfloat16),
         compiler_params=pltpu.CompilerParams(vmem_limit_bytes=56 * 2**20),
         cost_estimate=pl.CostEstimate(
-            flops=4 * tokens * width * cols * steps,
-            bytes_accessed=4 * steps * width * (tokens + cols) + 2 * exp_count * rows * cols,
+            flops=2 * tokens * depth * cols,
+            bytes_accessed=2 * depth * (tokens + cols) + 2 * exp_count * rows * cols,
             transcendentals=0,
         ),
         name="project",
-    )(spots, left_a, left_b, proj, proj, table)
+    )(spots, left_a, left_b, proj, table)
 
 
 def expert_kernel(exp_dim, spots, own, along, across, far_a, far_b, gain, gate_w, up_w, gate_v, up_v, route, out, total, squares):
@@ -460,9 +516,9 @@
 
 
 def down_kernel(start, spots, active, down_w, down_v, hidden, *outs):
-    sums = jnp.dot(active[0], down_w[...], preferred_element_type=jnp.float32)
-    sums += jnp.dot(active[1], down_v[...], preferred_element_type=jnp.float32)
-    sums = sums.astype(jnp.bfloat16)
+    left = jnp.concatenate([active[0], active[1]], 1)
+    right = jnp.concatenate([down_w[...], down_v[...]], 0)
+    sums = jnp.dot(left, right, preferred_element_type=jnp.float32).astype(jnp.bfloat16)
     kept = outs[0]
     if len(outs) == 1:
         kept[...] = sums.reshape(kept.shape)
@@ -570,29 +626,14 @@
     gates = high_low(jax.nn.sigmoid(gate_logits)).reshape(2, 2, row_count, ctx_count, own)
     gates = jnp.transpose(gates, (3, 0, 1, 2, 4)).reshape(ctx_count, -1)
     side = jnp.concatenate([gates, table], 1)
-    side_rows = -(-side.shape[1] // width)
-    residual_rows = -(-share * cols // width)
-    side_rows += -(3 * row_count + residual_rows + side_rows) % 16
-    side = jnp.pad(side, ((0, 0), (0, side_rows * width - side.shape[1])))
-    residual = jnp.transpose(residual_in.reshape(share, ctx_count, cols), (1, 0, 2))
-    residual = residual.reshape(ctx_count, share * cols)
-    residual = jnp.pad(residual, ((0, 0), (0, residual_rows * width - share * cols)))
-    heads = [
-        jnp.transpose(block.reshape(row_count, ctx_count, width), (1, 0, 2))
-        for block in (query_input, key_input, value_input)
-    ]
-    packed = jnp.concatenate(
-        heads
-        + [
-            residual.reshape(ctx_count, residual_rows, width),
-            side.reshape(ctx_count, side_rows, width),
-        ],
-        1,
-    )
+    side = jnp.pad(side, ((0, 0), (0, share * head_width - side.shape[1])))
+    side = side.reshape(ctx_count, share, head_width)
+    packed = pack(query_input, key_input, value_input, residual_in, side, width)
     moved = lax.all_to_all(packed, ctx, split_axis=0, concat_axis=0, tiled=True)
-    residual = moved[:, 3 * row_count : 3 * row_count + residual_rows].reshape(ctx_count, -1)
-    residual = residual[:, : share * cols].reshape(own_tokens, cols)
-    side = moved[:, 3 * row_count + residual_rows :].reshape(ctx_count, -1).astype(jnp.float32)
+    spots = side_spots(cols // head_width + 1, own, row_count, share, head_width)
+    parts = [moved[:, rows, lanes] for rows, lanes in spots]
+    residual = jnp.concatenate(parts[:-1], 2).reshape(own_tokens, cols)
+    side = parts[-1].reshape(ctx_count, -1).astype(jnp.float32)
     gate_size = 4 * row_count * own
     gates = side[:, :gate_size].reshape(ctx_count, 2, 2, row_count, own)
     gates = jnp.transpose(gates[:, 0] + gates[:, 1], (0, 2, 1, 3)).reshape(seq_len, 2 * own)
@@ -630,7 +671,6 @@
         return sums, scaled
 
     middle = chip_count // 2
-    proj = out_proj.reshape(ctx_count, width, cols)
     core_spot = core_index.astype(jnp.int32).reshape(1)
     spread_first = lax.all_gather(attended[0], "z", axis=0)
     spread_first, other_gate, other_up, other_down = lax.optimization_barrier(
@@ -640,7 +680,9 @@
     spread_first, later = lax.optimization_barrier((spread_first, attended[1]))
     spread_second = lax.all_gather(later, ctx, axis=0)
     pieces = exchange(
-        run_project(core_spot, spread_first, spread_other, False, proj, table, exp_count, True)
+        run_project(
+            core_spot, spread_first, spread_other, False, out_proj, table, exp_count, True
+        )
     )
     route = pieces[:, group_tokens:].reshape(exp_count, -1)[:, : 2 * chip_count * share]
     route = jnp.sum(
@@ -648,7 +690,7 @@
     )
     sums_first, scaled_first = settle(pieces, 0)
     pieces = run_project(
-        core_spot, spread_second, spread_second, True, proj, table, exp_count, False
+        core_spot, spread_second, spread_second, True, out_proj, table, exp_count, False
     )
     pieces, sums_first = lax.optimization_barrier((pieces, sums_first))
     wide = 1 << (2 * cols - 1).bit_length()
@@ -729,8 +771,13 @@
         head_count = args[4].shape[2] // exp_count
         share = args[0].shape[0] // (ctx_count * exp_count)
         body, axes, where = general, ("ctx",), mesh
-        whole = head_count % ctx_count == 0 and share % 32 == 0 and ctx_count % 4 == 0
-        if whole and exp_count.bit_length() == 3 and exp_count.bit_count() == 1:
+        own = head_count // ctx_count
+        head_width = args[0].shape[1] // args[4].shape[2]
+        pieces = args[5].shape[1] // (ctx_count * head_width) + 1
+        fits = head_count % ctx_count == 0 and share % 32 == 0 and ctx_count % 8 == 0
+        fits = fits and exp_count.bit_length() == 3 and exp_count.bit_count() == 1
+        fits = fits and args[5].shape[1] % (ctx_count * head_width) == 0
+        if fits and pieces % own == 0:
             split = mesh.devices.reshape(ctx_count // 2, 2, exp_count)
             where = jax.sharding.Mesh(split, ("z", "core", "exp"))
             body, axes = by_heads, ("z", "core")

time: 330 us -> 328 us (level)
  local copies, waits for them, and re-layouts: 20.6 us -> 15.7 us
  waiting for transfers between devices: 165 us -> 169 us
    pallas_call x2 -> x3, Pallas kernels: 13.2 us -> 12.6 us  [the longest x2 12 us: run_project(): pl.pallas_call(functools.partial(project_kernel, paired), grid_spec=pltpu...]
    unnamed x42 -> x39, local copies, waits for them, and re-layouts: 7.78 us -> 8.08 us
  transfers between devices with their start and end apart: 28 -> 28, of which waited for: 17 -> 18; matrix products, arithmetic and copies ran while one was open for 4% -> 4% of each run, Pallas kernels for 18% -> 17%
where the time goes in v9:
time: 328 us; the launch traced here: 327 us
  waiting for transfers between devices  169 us (52%)
  Pallas kernels  57.1 us (17%)
  blocking collectives  33.2 us (10%)
  starting transfers between devices  30.6 us (9%)
  local copies, waits for them, and re-layouts  15.7 us (5%)
  between operations  13.6 us (4%)
  other arithmetic  7.78 us (2%)
    ppermute x14, waiting for transfers between devices, plane_step(): return lax.ppermute(block, 'exp', [(i, i ^ step) for i in range(count)])  47.8 us
    all_to_all x1, waiting for transfers between devices, by_heads(): moved = lax.all_to_all(packed, ctx, split_axis=0, concat_axis=0, tiled=True)  47.8 us
    all_gather x1, waiting for transfers between devices, by_heads(): spread_first = lax.all_gather(attended[0], 'z', axis=0)  26.9 us
    pallas_call x2, Pallas kernels, run_expert(): pl.pallas_call(functools.partial(expert_kernel, exp_dim), grid_spec=pltpu...  21.7 us
    all_gather x1, blocking collectives, by_heads(): plane_second = lax.all_gather(scaled_second, 'z', axis=0)  19.8 us
    all_gather x1, waiting for transfers between devices, by_heads(): plane_first = lax.all_gather(padded, 'z', axis=0)[:, :, :2 * cols]  19.1 us
    pallas_call x3, Pallas kernels, run_down(): pl.pallas_call(functools.partial(down_kernel, start), grid_spec=pltpu.Pre...  16.8 us
    ppermute x14, starting transfers between devices, plane_step(): return lax.ppermute(block, 'exp', [(i, i ^ step) for i in range(count)])  15.7 us
  transfers between devices with their start and end apart: 28, of which 18 were waited for; matrix products, arithmetic and copies ran while one was open for 4% of the time, Pallas kernels for 17%

profile of v9, /device:TPU:0, one launch (start us, length us, event | category | flops | bytes accessed | tf_op | source)
XLA Modules:
  0.0 327.4 jit_solution(10646522702110192814)
XLA Ops:
  14.8 6.3 %all-to-all-start = ((bf16[8,512,256]{2,1,0:T(8,128)(2,1)}), bf16[8,512,256]{2,1,0:T(8,128)(2,1)S(1)}, u32[]{:S(2)}, u32[]{:S(2)}) async-start(bf16[8,512,256]{2,1,0:T(8,128)(2,1)} %copy-done.2), calls=%async_computation | async-start | bytes 4194304 | tf_op jit(solution)/shard_map/all_to_all | solution.py:632
  22.4 47.8 %all-to-all-done.moved = bf16[8,512,256]{2,1,0:T(8,128)(2,1)S(1)} async-done(((bf16[8,512,256]{2,1,0:T(8,128)(2,1)}), bf16[8,512,256]{2,1,0:T(8,128)(2,1)S(1)}, u32[]{:S(2)}, u32[]{:S(2)}) %all-to-all-start) | async-done | bytes 2097184 | tf_op jit(solution)/shard_map/all_to_all | solution.py:632
  71.0 6.0 %attend.1 = (bf16[512,256]{1,0:T(8,128)(2,1)}, bf16[512,256]{1,0:T(8,128)(2,1)}) custom-call(bf16[8,512,256]{2,1,0:T(8,128)(2,1)S(1)} %all-to-all-done.moved, f32[8,1024]{1,0:T(8,128)S(1)} %tile.12.taps, f32[1024,4]{1,0:T(8,128)S(1)} %copy.85.gates), custom_call_target="tpu_custom_call" | custom-call | tf_op jit(solution)/shard_map/attend/pallas_call | solution.py:352
  77.2 26.9 %all-gather.7.cloned.1.call-done = bf16[2048,256]{1,0:T(8,128)(2,1)} async-done(((bf16[512,256]{1,0:T(8,128)(2,1)}), bf16[2048,256]{1,0:T(8,128)(2,1)}) %all-gather.7.cloned.1.call-update) | async-done | bytes 1048592 | tf_op jit(solution)/shard_map/all_gather | solution.py:675
  107.2 5.7 %project.3 = bf16[4,144,896]{2,1,0:T(8,128)(2,1)} custom-call(s32[1]{0:T(128)} %bitcast.2.spots, bf16[4,1,512,256]{3,2,1,0:T(8,128)(2,1)} %bitcast.139, bf16[4,1,512,256]{3,2,1,0:T(8,128)(2,1)} %bitcast.22.left_b, bf16[2048,896]{1,0:T(8,128)(2,1)} %proj.3, bf16[4,16,896]{2,1,0:T(8,128)(2,1)} %bitcast.124), custom_call_target="tpu_custom_call" | custom-call | flops 1879048192 | bytes 6799360 | tf_op jit(solution)/shard_map/project/pallas_call | solution.py:401
  112.9 3.6 %all-to-all-start.1 = ((bf16[4,144,896]{2,1,0:T(8,128)(2,1)}), bf16[4,144,896]{2,1,0:T(8,128)(2,1)S(1)}, u32[]{:S(2)}, u32[]{:S(2)}) async-start(bf16[4,144,896]{2,1,0:T(8,128)(2,1)} %project.3), calls=%async_computation.1 | async-start | bytes 2064384 | tf_op jit(solution)/shard_map/all_to_all | solution.py:658
  116.6 13.8 %all-to-all-done.1 = bf16[4,144,896]{2,1,0:T(8,128)(2,1)S(1)} async-done(((bf16[4,144,896]{2,1,0:T(8,128)(2,1)}), bf16[4,144,896]{2,1,0:T(8,128)(2,1)S(1)}, u32[]{:S(2)}, u32[]{:S(2)}) %all-to-all-start.1) | async-done | bytes 1032224 | tf_op jit(solution)/shard_map/all_to_all | solution.py:658
  134.3 6.3 %project.2 = bf16[4,128,896]{2,1,0:T(8,128)(2,1)} custom-call(s32[1]{0:T(128)} %bitcast.2.spots, bf16[4,2,512,256]{3,2,1,0:T(8,128)(2,1)} %bitcast.106, bf16[4,2,512,256]{3,2,1,0:T(8,128)(2,1)} %bitcast.107, bf16[2048,896]{1,0:T(8,128)(2,1)} %proj.3, bf16[4,16,896]{2,1,0:T(8,128)(2,1)} %bitcast.125), custom_call_target="tpu_custom_call" | custom-call | flops 1879048192 | bytes 6684672 | tf_op jit(solution)/shard_map/project/pallas_call | solution.py:401
  140.6 3.6 %all-to-all-start.2 = ((bf16[4,128,896]{2,1,0:T(8,128)(2,1)}), bf16[4,128,896]{2,1,0:T(8,128)(2,1)S(1)}, u32[]{:S(2)}, u32[]{:S(2)}) async-start(bf16[4,128,896]{2,1,0:T(8,128)(2,1)} %project.2), calls=%async_computation.2 | async-start | bytes 1835008 | tf_op jit(solution)/shard_map/all_to_all | solution.py:658
  144.2 19.1 %all-gather.11.cloned.1.call-done = bf16[256,2048]{1,0:T(8,128)(2,1)} async-done(((bf16[64,2048]{1,0:T(8,128)(2,1)}), bf16[256,2048]{1,0:T(8,128)(2,1)}) %all-gather.11.cloned.1.call-update) | async-done | bytes 1048592 | tf_op jit(solution)/shard_map/all_gather | solution.py:698
  168.0 19.8 %all_gather.27.own = bf16[4,64,1792]{2,1,0:T(8,128)(2,1)S(1)} all-gather(bf16[1,64,1792]{2,1,0:T(8,128)(2,1)S(1)} %fusion.1), channel_id=1, replica_groups=mesh['z'=4,'core'=2,'exp'=4] {'z'}, dimensions={0}, use_global_device_ids=true | all-gather | bytes 1146880 | tf_op jit(solution)/shard_map/all_gather | solution.py:702
  192.5 9.2 %collective-permute-done.9.far_b = bf16[2,64,1792]{2,1,0:T(8,128)(2,1)} collective-permute-done((bf16[2,64,1792]{2,1,0:T(8,128)(2,1)S(1)}, bf16[2,64,1792]{2,1,0:T(8,128)(2,1)}, u32[]{:S(2)}, u32[]{:S(2)}) %collective-permute-start.9) | collective-permute-done | bytes 458784 | tf_op jit(solution)/shard_map/ppermute | solution.py:577
  205.4 10.8 %expert.2 = bf16[2,4,4,16,256]{4,3,2,1,0:T(8,128)(2,1)} custom-call(s32[2]{0:T(128)} %pad_add_fusion.spots, bf16[4,64,1792]{2,1,0:T(8,128)(2,1)} %copy-done.7, bf16[4,64,1792]{2,1,0:T(8,128)(2,1)} %copy-done.10, bf16[4,64,1792]{2,1,0:T(8,128)(2,1)} %copy-done.9, bf16[2,64,1792]{2,1,0:T(8,128)(2,1)} %collective-permute-done.8.far_a, ...), custom_call_target="tpu_custom_call" | custom-call | flops 3758096384 | bytes 18350080 | tf_op jit(solution)/shard_map/expert/pallas_call | solution.py:478
  216.3 7.5 %down.3 = bf16[4,4,16,7168]{3,2,1,0:T(8,128)(2,1)} custom-call(s32[2]{0:T(128)} %pad_add_fusion.spots, bf16[2,256,256]{2,1,0:T(8,128)(2,1)} %bitcast.118, bf16[256,7168]{1,0:T(8,128)(2,1)} %bitcast.96, bf16[256,7168]{1,0:T(8,128)(2,1)} %collective-permute-done.2.down_v, f32[4,16,1792]{2,1,0:T(8,128)} %pad_maximum_fusion.2.hidden), custom_call_target="tpu_custom_call" | custom-call | flops 1879048192 | bytes 11010048 | tf_op jit(solution)/shard_map/down/pallas_call | solution.py:547
  229.4 6.2 %collective-permute-done.13.far_b = bf16[2,64,1792]{2,1,0:T(8,128)(2,1)S(1)} collective-permute-done((bf16[2,64,1792]{2,1,0:T(8,128)(2,1)S(1)}, bf16[2,64,1792]{2,1,0:T(8,128)(2,1)S(1)}, u32[]{:S(2)}, u32[]{:S(2)}) %collective-permute-start.13) | collective-permute-done | bytes 458784 | tf_op jit(solution)/shard_map/ppermute | solution.py:577
  237.5 10.8 %expert.3 = bf16[2,4,4,16,256]{4,3,2,1,0:T(8,128)(2,1)} custom-call(s32[2]{0:T(128)} %pad_add_fusion.spots, bf16[4,64,1792]{2,1,0:T(8,128)(2,1)} %copy-done.8, bf16[4,64,1792]{2,1,0:T(8,128)(2,1)} %collective-permute-done.10.along, bf16[4,64,1792]{2,1,0:T(8,128)(2,1)} %copy-done.11, bf16[2,64,1792]{2,1,0:T(8,128)(2,1)} %copy-done.15, ...), custom_call_target="tpu_custom_call" | custom-call | flops 3758096384 | bytes 18350080 | tf_op jit(solution)/shard_map/expert/pallas_call | solution.py:478
  248.4 4.6 %down.5 = (bf16[4,16,3584]{2,1,0:T(8,128)(2,1)}, bf16[4,16,3584]{2,1,0:T(8,128)(2,1)}, bf16[4,16,3584]{2,1,0:T(8,128)(2,1)}, bf16[4,16,3584]{2,1,0:T(8,128)(2,1)}) custom-call(s32[2]{0:T(128)} %pad_add_fusion.spots, bf16[2,256,256]{2,1,0:T(8,128)(2,1)} %bitcast.108, bf16[256,7168]{1,0:T(8,128)(2,1)} %bitcast.97, ...), custom_call_target="tpu_custom_call" | custom-call | flops 939524096 | bytes 5505024 | tf_op jit(solution)/shard_map/down/pallas_call | solution.py:547
  256.5 4.7 %down.4 = (bf16[4,16,3584]{2,1,0:T(8,128)(2,1)}, bf16[4,16,3584]{2,1,0:T(8,128)(2,1)}, bf16[4,16,3584]{2,1,0:T(8,128)(2,1)}, bf16[4,16,3584]{2,1,0:T(8,128)(2,1)}) custom-call(s32[2]{0:T(128)} %pad_add_fusion.spots, bf16[2,256,256]{2,1,0:T(8,128)(2,1)} %bitcast.109, bf16[256,7168]{1,0:T(8,128)(2,1)} %bitcast.98, ...), custom_call_target="tpu_custom_call" | custom-call | flops 939524096 | bytes 5505024 | tf_op jit(solution)/shard_map/down/pallas_call | solution.py:547
  263.2 3.5 %collective-permute-done.17 = bf16[4,16,3584]{2,1,0:T(8,128)(2,1)S(1)} collective-permute-done((bf16[4,16,3584]{2,1,0:T(8,128)(2,1)}, bf16[4,16,3584]{2,1,0:T(8,128)(2,1)S(1)}, u32[]{:S(2)}, u32[]{:S(2)}) %collective-permute-start.17) | collective-permute-done | bytes 458784 | tf_op jit(solution)/shard_map/ppermute | solution.py:577
  268.1 9.6 %collective-permute-done.18 = bf16[4,16,3584]{2,1,0:T(8,128)(2,1)S(1)} collective-permute-done((bf16[4,16,3584]{2,1,0:T(8,128)(2,1)}, bf16[4,16,3584]{2,1,0:T(8,128)(2,1)S(1)}, u32[]{:S(2)}, u32[]{:S(2)}) %collective-permute-start.18) | collective-permute-done | bytes 458784 | tf_op jit(solution)/shard_map/ppermute | solution.py:577
  277.9 8.5 %collective-permute-done.14 = bf16[4,16,3584]{2,1,0:T(8,128)(2,1)S(1)} collective-permute-done((bf16[4,16,3584]{2,1,0:T(8,128)(2,1)}, bf16[4,16,3584]{2,1,0:T(8,128)(2,1)S(1)}, u32[]{:S(2)}, u32[]{:S(2)}) %collective-permute-start.14) | collective-permute-done | bytes 458784 | tf_op jit(solution)/shard_map/ppermute | solution.py:577
  286.4 6.8 %collective-permute-done.15 = bf16[4,16,3584]{2,1,0:T(8,128)(2,1)S(1)} collective-permute-done((bf16[4,16,3584]{2,1,0:T(8,128)(2,1)}, bf16[4,16,3584]{2,1,0:T(8,128)(2,1)S(1)}, u32[]{:S(2)}, u32[]{:S(2)}) %collective-permute-start.15) | collective-permute-done | bytes 458784 | tf_op jit(solution)/shard_map/ppermute | solution.py:577
  294.4 13.4 %all_to_all.20 = bf16[4,16,7168]{2,1,0:T(8,128)(2,1)S(1)} all-to-all(bf16[4,16,7168]{2,1,0:T(8,128)(2,1)} %bitcast.120), channel_id=1, replica_groups=mesh['z'=4,'core'=2,'exp'=4] {'exp'}, dimensions={0} | all-to-all | bytes 1835008 | tf_op jit(solution)/shard_map/all_to_all | solution.py:741
  308.1 11.1 %reduce-scatter.5.cloned.1.call-done = bf16[1,16,7168]{2,1,0:T(8,128)(2,1)} async-done(((bf16[4,16,7168]{2,1,0:T(8,128)(2,1)}), bf16[1,16,7168]{2,1,0:T(8,128)(2,1)}) %reduce-scatter.5.cloned.1.call-update) | async-done | bytes 229392 | tf_op jit(solution)/shard_map/reduce_scatter | solution.py:740
  (150 shorter events, 48.1 us)
Async XLA Ops:
  14.8 55.4 %all-to-all-start = ((bf16[8,512,256]{2,1,0:T(8,128)(2,1)}), bf16[8,512,256]{2,1,0:T(8,128)(2,1)S(1)}, u32[]{:S(2)}, u32[]{:S(2)}) async-start(bf16[8,512,256]{2,1,0:T(8,128)(2,1)} %copy-done.2), calls=%async_computation | async-start | bytes 4194304 | tf_op jit(solution)/shard_map/all_to_all | solution.py:632
  21.1 82.9 %all-gather.7.cloned.1.call-start = ((), (), s32[]{:S(2)}) async-start(), calls=%async_computation.8 | async-start | bytes 1310720 | tf_op jit(solution)/shard_map/all_gather | solution.py:675
  21.2 56.0 %collective-permute-start = (bf16[7168,256]{1,0:T(8,128)(2,1)}, bf16[7168,256]{1,0:T(8,128)(2,1)}, u32[]{:S(2)}, u32[]{:S(2)}) collective-permute-start(bf16[7168,256]{1,0:T(8,128)(2,1)} %bitcast.99), channel_id=1, source_target_pairs={{0,4},{4,0},{1,5},{5,1},{2,6},{6,2},{3,7},{7,3},{8,12},{12,8},{9,1... | collective-permute-start | bytes 11010056 | tf_op jit(solution)/shard_map/ppermute | solution.py:572
  21.7 55.5 %collective-permute-start.1 = (bf16[7168,256]{1,0:T(8,128)(2,1)}, bf16[7168,256]{1,0:T(8,128)(2,1)}, u32[]{:S(2)}, u32[]{:S(2)}) collective-permute-start(bf16[7168,256]{1,0:T(8,128)(2,1)} %bitcast.102), channel_id=1, source_target_pairs={{0,4},{4,0},{1,5},{5,1},{2,6},{6,2},{3,7},{7,3},{8,12},{12,8},{9,1... | collective-permute-start | bytes 11010056 | tf_op jit(solution)/shard_map/ppermute | solution.py:572
  21.8 55.4 %collective-permute-start.2 = (bf16[256,7168]{1,0:T(8,128)(2,1)}, bf16[256,7168]{1,0:T(8,128)(2,1)}, u32[]{:S(2)}, u32[]{:S(2)}) collective-permute-start(bf16[256,7168]{1,0:T(8,128)(2,1)} %bitcast.95), channel_id=1, source_target_pairs={{0,4},{4,0},{1,5},{5,1},{2,6},{6,2},{3,7},{7,3},{8,12},{12,8},{9,1... | collective-permute-start | bytes 11010056 | tf_op jit(solution)/shard_map/ppermute | solution.py:572
  77.1 57.2 %all-gather.9.cloned.1.call-start = ((), (), s32[]{:S(2)}) async-start(), calls=%async_computation.9 | async-start | bytes 2359296 | tf_op jit(solution)/shard_map/all_gather | solution.py:681
  112.9 17.5 %all-to-all-start.1 = ((bf16[4,144,896]{2,1,0:T(8,128)(2,1)}), bf16[4,144,896]{2,1,0:T(8,128)(2,1)S(1)}, u32[]{:S(2)}, u32[]{:S(2)}) async-start(bf16[4,144,896]{2,1,0:T(8,128)(2,1)} %project.3), calls=%async_computation.1 | async-start | bytes 2064384 | tf_op jit(solution)/shard_map/all_to_all | solution.py:658
  116.5 46.8 %all-gather.11.cloned.1.call-start = ((), (), s32[]{:S(2)}) async-start(), calls=%async_computation.10 | async-start | bytes 1310720 | tf_op jit(solution)/shard_map/all_gather | solution.py:698
  140.6 24.0 %all-to-all-start.2 = ((bf16[4,128,896]{2,1,0:T(8,128)(2,1)}), bf16[4,128,896]{2,1,0:T(8,128)(2,1)S(1)}, u32[]{:S(2)}, u32[]{:S(2)}) async-start(bf16[4,128,896]{2,1,0:T(8,128)(2,1)} %project.2), calls=%async_computation.2 | async-start | bytes 1835008 | tf_op jit(solution)/shard_map/all_to_all | solution.py:658
  144.2 150.2 %reduce-scatter.3.cloned.1.call-start = ((), (), s32[]{:S(2)}) async-start(), calls=%async_computation.6 | async-start | bytes 4587520 | tf_op jit(solution)/shard_map/reduce_scatter | solution.py:723
  164.9 22.9 %collective-permute-start.6 = (bf16[4,64,1792]{2,1,0:T(8,128)(2,1)S(1)}, bf16[4,64,1792]{2,1,0:T(8,128)(2,1)S(1)}, u32[]{:S(2)}, u32[]{:S(2)}) collective-permute-start(bf16[4,64,1792]{2,1,0:T(8,128)(2,1)S(1)} %slice.101.own), channel_id=1, source_target_pairs={{0,2},{1,3},{2,0},{3,1},{4,6},{5,7},{6,4},{7,5},{8,10},{9,11},{10,... | collective-permute-start | bytes 2752520 | tf_op jit(solution)/shard_map/ppermute | solution.py:577
  166.4 22.4 %collective-permute-start.5 = (bf16[4,64,1792]{2,1,0:T(8,128)(2,1)S(1)}, bf16[4,64,1792]{2,1,0:T(8,128)(2,1)S(1)}, u32[]{:S(2)}, u32[]{:S(2)}) collective-permute-start(bf16[4,64,1792]{2,1,0:T(8,128)(2,1)S(1)} %slice.101.own), channel_id=1, source_target_pairs={{0,1},{1,0},{2,3},{3,2},{4,5},{5,4},{6,7},{7,6},{8,9},{9,8},{10,11... | collective-permute-start | bytes 2752520 | tf_op jit(solution)/shard_map/ppermute | solution.py:577
  189.9 11.9 %collective-permute-start.9 = (bf16[2,64,1792]{2,1,0:T(8,128)(2,1)S(1)}, bf16[2,64,1792]{2,1,0:T(8,128)(2,1)}, u32[]{:S(2)}, u32[]{:S(2)}) collective-permute-start(bf16[2,64,1792]{2,1,0:T(8,128)(2,1)S(1)} %slice.83), channel_id=1, source_target_pairs={{0,1},{1,0},{2,3},{3,2},{4,5},{5,4},{6,7},{7,6},{8,9},{9,8},{10,11... | collective-permute-start | bytes 1376264 | tf_op jit(solution)/shard_map/ppermute | solution.py:577
  191.3 11.6 %collective-permute-start.8 = (bf16[2,64,1792]{2,1,0:T(8,128)(2,1)S(1)}, bf16[2,64,1792]{2,1,0:T(8,128)(2,1)}, u32[]{:S(2)}, u32[]{:S(2)}) collective-permute-start(bf16[2,64,1792]{2,1,0:T(8,128)(2,1)S(1)} %slice.82), channel_id=1, source_target_pairs={{0,2},{1,3},{2,0},{3,1},{4,6},{5,7},{6,4},{7,5},{8,10},{9,11},{10,... | collective-permute-start | bytes 1376264 | tf_op jit(solution)/shard_map/ppermute | solution.py:577
  202.9 20.8 %collective-permute-start.11 = (bf16[4,64,1792]{2,1,0:T(8,128)(2,1)S(1)}, bf16[4,64,1792]{2,1,0:T(8,128)(2,1)S(1)}, u32[]{:S(2)}, u32[]{:S(2)}) collective-permute-start(bf16[4,64,1792]{2,1,0:T(8,128)(2,1)S(1)} %all_gather.27.own), channel_id=1, source_target_pairs={{0,2},{1,3},{2,0},{3,1},{4,6},{5,7},{6,4},{7,5},{8,10},{9,11},{10,... | collective-permute-start | bytes 2752520 | tf_op jit(solution)/shard_map/ppermute | solution.py:577
  203.8 20.5 %collective-permute-start.10 = (bf16[4,64,1792]{2,1,0:T(8,128)(2,1)S(1)}, bf16[4,64,1792]{2,1,0:T(8,128)(2,1)}, u32[]{:S(2)}, u32[]{:S(2)}) collective-permute-start(bf16[4,64,1792]{2,1,0:T(8,128)(2,1)S(1)} %all_gather.27.own), channel_id=1, source_target_pairs={{0,1},{1,0},{2,3},{3,2},{4,5},{5,4},{6,7},{7,6},{8,9},{9,8},{10,11... | collective-permute-start | bytes 2752520 | tf_op jit(solution)/shard_map/ppermute | solution.py:577
  224.4 94.8 %reduce-scatter.5.cloned.1.call-start = ((), (), s32[]{:S(2)}) async-start(), calls=%async_computation.7 | async-start | bytes 1146880 | tf_op jit(solution)/shard_map/reduce_scatter | solution.py:740
  225.5 10.1 %collective-permute-start.13 = (bf16[2,64,1792]{2,1,0:T(8,128)(2,1)S(1)}, bf16[2,64,1792]{2,1,0:T(8,128)(2,1)S(1)}, u32[]{:S(2)}, u32[]{:S(2)}) collective-permute-start(bf16[2,64,1792]{2,1,0:T(8,128)(2,1)S(1)} %slice.88), channel_id=1, source_target_pairs={{0,1},{1,0},{2,3},{3,2},{4,5},{5,4},{6,7},{7,6},{8,9},{9,8},{10,11... | collective-permute-start | bytes 1376264 | tf_op jit(solution)/shard_map/ppermute | solution.py:577
  253.0 13.7 %collective-permute-start.17 = (bf16[4,16,3584]{2,1,0:T(8,128)(2,1)}, bf16[4,16,3584]{2,1,0:T(8,128)(2,1)S(1)}, u32[]{:S(2)}, u32[]{:S(2)}) collective-permute-start(bf16[4,16,3584]{2,1,0:T(8,128)(2,1)} %get-tuple-element.61), channel_id=1, source_target_pairs={{0,1},{1,0},{2,3},{3,2},{4,5},{5,4},{6,7},{7,6},{8,9},{9,8},{10,11... | collective-permute-start | bytes 1376264 | tf_op jit(solution)/shard_map/ppermute | solution.py:577
  254.1 23.6 %collective-permute-start.18 = (bf16[4,16,3584]{2,1,0:T(8,128)(2,1)}, bf16[4,16,3584]{2,1,0:T(8,128)(2,1)S(1)}, u32[]{:S(2)}, u32[]{:S(2)}) collective-permute-start(bf16[4,16,3584]{2,1,0:T(8,128)(2,1)} %get-tuple-element.62), channel_id=1, source_target_pairs={{0,2},{1,3},{2,0},{3,1},{4,6},{5,7},{6,4},{7,5},{8,10},{9,11},{10,... | collective-permute-start | bytes 1376264 | tf_op jit(solution)/shard_map/ppermute | solution.py:577
  254.9 22.7 %collective-permute-start.19 = (bf16[4,16,3584]{2,1,0:T(8,128)(2,1)}, bf16[4,16,3584]{2,1,0:T(8,128)(2,1)S(1)}, u32[]{:S(2)}, u32[]{:S(2)}) collective-permute-start(bf16[4,16,3584]{2,1,0:T(8,128)(2,1)} %get-tuple-element.63), channel_id=1, source_target_pairs={{0,3},{1,2},{2,1},{3,0},{4,7},{5,6},{6,5},{7,4},{8,11},{9,10},{10,... | collective-permute-start | bytes 1376264 | tf_op jit(solution)/shard_map/ppermute | solution.py:577
  261.2 25.2 %collective-permute-start.14 = (bf16[4,16,3584]{2,1,0:T(8,128)(2,1)}, bf16[4,16,3584]{2,1,0:T(8,128)(2,1)S(1)}, u32[]{:S(2)}, u32[]{:S(2)}) collective-permute-start(bf16[4,16,3584]{2,1,0:T(8,128)(2,1)} %get-tuple-element.57), channel_id=1, source_target_pairs={{0,1},{1,0},{2,3},{3,2},{4,5},{5,4},{6,7},{7,6},{8,9},{9,8},{10,11... | collective-permute-start | bytes 1376264 | tf_op jit(solution)/shard_map/ppermute | solution.py:577
  262.4 30.8 %collective-permute-start.15 = (bf16[4,16,3584]{2,1,0:T(8,128)(2,1)}, bf16[4,16,3584]{2,1,0:T(8,128)(2,1)S(1)}, u32[]{:S(2)}, u32[]{:S(2)}) collective-permute-start(bf16[4,16,3584]{2,1,0:T(8,128)(2,1)} %get-tuple-element.58), channel_id=1, source_target_pairs={{0,2},{1,3},{2,0},{3,1},{4,6},{5,7},{6,4},{7,5},{8,10},{9,11},{10,... | collective-permute-start | bytes 1376264 | tf_op jit(solution)/shard_map/ppermute | solution.py:577
  266.7 26.5 %collective-permute-start.16 = (bf16[4,16,3584]{2,1,0:T(8,128)(2,1)}, bf16[4,16,3584]{2,1,0:T(8,128)(2,1)S(1)}, u32[]{:S(2)}, u32[]{:S(2)}) collective-permute-start(bf16[4,16,3584]{2,1,0:T(8,128)(2,1)} %get-tuple-element.59), channel_id=1, source_target_pairs={{0,3},{1,2},{2,1},{3,0},{4,7},{5,6},{6,5},{7,4},{8,11},{9,10},{10,... | collective-permute-start | bytes 1376264 | tf_op jit(solution)/shard_map/ppermute | solution.py:577
  (20 other events, 157.8 us)
Sparse Core Ops, SparseCore 0:
  77.2 26.8 all-gather.6
  105.7 28.5 all-gather.8
  135.9 27.4 all-gather.10
  224.5 66.9 reduce-scatter.2
  294.5 24.5 reduce-scatter.4

commit v10 on v9

--- a/solution.py
+++ b/solution.py
@@ -266,7 +266,7 @@
         ],
         out_specs=pl.BlockSpec((1, rows, width), lambda i: (i, 0, 0)),
         out_shape=jax.ShapeDtypeStruct((ctx_count, rows, width), jnp.bfloat16),
-        compiler_params=pltpu.CompilerParams(vmem_limit_bytes=32 * 2**20),
+        compiler_params=pltpu.CompilerParams(vmem_limit_bytes=16 * 2**20),
         name="pack",
     )(query, key, value, residual, side)
 
@@ -356,7 +356,7 @@
             pltpu.VMEM((seq_len, head_width), jnp.bfloat16),
             pltpu.VMEM((seq_len, head_width), jnp.bfloat16),
         ],
-        compiler_params=pltpu.CompilerParams(vmem_limit_bytes=48 * 2**20),
+        compiler_params=pltpu.CompilerParams(vmem_limit_bytes=24 * 2**20),
         name="attend",
     )(moved, taps, gates)
 
@@ -413,7 +413,7 @@
             scratch_shapes=[pltpu.VMEM((tokens, cols), jnp.float32)],
         ),
         out_shape=jax.ShapeDtypeStruct((exp_count, rows, cols), jnp.bfloat16),
-        compiler_params=pltpu.CompilerParams(vmem_limit_bytes=56 * 2**20),
+        compiler_params=pltpu.CompilerParams(vmem_limit_bytes=24 * 2**20),
         cost_estimate=pl.CostEstimate(
             flops=2 * tokens * depth * cols,
             bytes_accessed=2 * depth * (tokens + cols) + 2 * exp_count * rows * cols,
@@ -504,7 +504,7 @@
             ],
         ),
         out_shape=jax.ShapeDtypeStruct((2,) + lead + (half, units), jnp.bfloat16),
-        compiler_params=pltpu.CompilerParams(vmem_limit_bytes=56 * 2**20),
+        compiler_params=pltpu.CompilerParams(vmem_limit_bytes=24 * 2**20),
         cost_estimate=pl.CostEstimate(
             flops=8 * row_total * units * steps * cols,
             bytes_accessed=2 * steps * cols * (row_total + 4 * units),
@@ -558,7 +558,7 @@
             out_specs=[pl.BlockSpec(lead + (half, cols), lambda i, _: (*zeros, i))] * count,
         ),
         out_shape=[jax.ShapeDtypeStruct(shape, jnp.bfloat16)] * count,
-        compiler_params=pltpu.CompilerParams(vmem_limit_bytes=56 * 2**20),
+        compiler_params=pltpu.CompilerParams(vmem_limit_bytes=24 * 2**20),
         cost_estimate=pl.CostEstimate(
             flops=4 * rows * units * cols * (stop - start),
             bytes_accessed=2 * cols * (stop - start) * (rows + 2 * units),

time: 328 us -> 333 us (1.015)
  local copies, waits for them, and re-layouts: 15.7 us -> 36.1 us
  Pallas kernels: 57.1 us -> 42.2 us
    unnamed x39 -> x61, local copies, waits for them, and re-layouts: 8.08 us -> 26.4 us
    pallas_call x2, Pallas kernels: 21.7 us -> 16.1 us  [run_expert(): pl.pallas_call(functools.partial(expert_kernel, exp_dim), grid_spec=pltpu...]
    pallas_call x3, Pallas kernels: 16.8 us -> 11.9 us  [run_down(): pl.pallas_call(functools.partial(down_kernel, start), grid_spec=pltpu.Pre...]
    pallas_call x2, Pallas kernels: 12 us -> 7.48 us  [run_project(): pl.pallas_call(functools.partial(project_kernel, paired), grid_spec=pltpu...]
  transfers between devices with their start and end apart: 28 -> 28, of which waited for: 18 -> 19; matrix products, arithmetic and copies ran while one was open for 4% -> 3% of each run, Pallas kernels for 17% -> 13%
where the time goes in v10:
time: 333 us; the launch traced here: 332 us
  waiting for transfers between devices  169 us (51%)
  Pallas kernels  42.2 us (13%)
  local copies, waits for them, and re-layouts  36.1 us (11%)
  blocking collectives  33.8 us (10%)
  starting transfers between devices  31.1 us (9%)
  between operations  13.7 us (4%)
  other arithmetic  5.78 us (2%)
    ppermute x14, waiting for transfers between devices, plane_step(): return lax.ppermute(block, 'exp', [(i, i ^ step) for i in range(count)])  48.3 us
    all_to_all x1, waiting for transfers between devices, by_heads(): moved = lax.all_to_all(packed, ctx, split_axis=0, concat_axis=0, tiled=True)  47.8 us
    all_gather x1, waiting for transfers between devices, by_heads(): spread_first = lax.all_gather(attended[0], 'z', axis=0)  26.9 us
    unnamed x61, local copies, waits for them, and re-layouts  26.4 us
    all_gather x1, blocking collectives, by_heads(): plane_second = lax.all_gather(scaled_second, 'z', axis=0)  19.8 us
    all_gather x1, waiting for transfers between devices, by_heads(): plane_first = lax.all_gather(padded, 'z', axis=0)[:, :, :2 * cols]  17.9 us
    pallas_call x2, Pallas kernels, run_expert(): pl.pallas_call(functools.partial(expert_kernel, exp_dim), grid_spec=pltpu...  16.1 us
    ppermute x14, starting transfers between devices, plane_step(): return lax.ppermute(block, 'exp', [(i, i ^ step) for i in range(count)])  16.1 us
  transfers between devices with their start and end apart: 28, of which 19 were waited for; matrix products, arithmetic and copies ran while one was open for 3% of the time, Pallas kernels for 13%

profile of v10, /device:TPU:0, one launch (start us, length us, event | category | flops | bytes accessed | tf_op | source)
XLA Modules:
  0.0 331.5 jit_solution(4538426292670639265)
XLA Ops:
  14.7 6.3 %all-to-all-start = ((bf16[8,512,256]{2,1,0:T(8,128)(2,1)}), bf16[8,512,256]{2,1,0:T(8,128)(2,1)S(1)}, u32[]{:S(2)}, u32[]{:S(2)}) async-start(bf16[8,512,256]{2,1,0:T(8,128)(2,1)} %copy-done.10), calls=%async_computation | async-start | bytes 4194304 | tf_op jit(solution)/shard_map/all_to_all | solution.py:632
  22.4 47.8 %all-to-all-done.moved = bf16[8,512,256]{2,1,0:T(8,128)(2,1)S(1)} async-done(((bf16[8,512,256]{2,1,0:T(8,128)(2,1)}), bf16[8,512,256]{2,1,0:T(8,128)(2,1)S(1)}, u32[]{:S(2)}, u32[]{:S(2)}) %all-to-all-start) | async-done | bytes 2097184 | tf_op jit(solution)/shard_map/all_to_all | solution.py:632
  70.9 6.1 %attend.1 = (bf16[512,256]{1,0:T(8,128)(2,1)}, bf16[512,256]{1,0:T(8,128)(2,1)}) custom-call(bf16[8,512,256]{2,1,0:T(8,128)(2,1)S(1)} %all-to-all-done.moved, f32[8,1024]{1,0:T(8,128)S(1)} %tile.12.taps, f32[1024,4]{1,0:T(8,128)S(1)} %copy.85.gates), custom_call_target="tpu_custom_call" | custom-call | tf_op jit(solution)/shard_map/attend/pallas_call | solution.py:352
  77.1 26.9 %all-gather.7.cloned.1.call-done = bf16[2048,256]{1,0:T(8,128)(2,1)} async-done(((bf16[512,256]{1,0:T(8,128)(2,1)}), bf16[2048,256]{1,0:T(8,128)(2,1)}) %all-gather.7.cloned.1.call-update) | async-done | bytes 1048592 | tf_op jit(solution)/shard_map/all_gather | solution.py:675
  110.3 3.8 %project.3 = bf16[4,144,896]{2,1,0:T(8,128)(2,1)} custom-call(s32[1]{0:T(128)} %bitcast.2.spots, bf16[4,1,512,256]{3,2,1,0:T(8,128)(2,1)S(1)} %bitcast.116, bf16[4,1,512,256]{3,2,1,0:T(8,128)(2,1)S(1)} %bitcast.117, bf16[2048,896]{1,0:T(8,128)(2,1)S(1)} %copy-done.11, bf16[4,16,896]{2,1,0:T(8,128)(2,1)S(1)} %bitcast.110), custom_call_target="tpu_custom_call" | custom-call | flops 1879048192 | bytes 6799360 | tf_op jit(solution)/shard_map/project/pallas_call | solution.py:401
  114.0 3.6 %all-to-all-start.1 = ((bf16[4,144,896]{2,1,0:T(8,128)(2,1)}), bf16[4,144,896]{2,1,0:T(8,128)(2,1)S(1)}, u32[]{:S(2)}, u32[]{:S(2)}) async-start(bf16[4,144,896]{2,1,0:T(8,128)(2,1)} %project.3), calls=%async_computation.1 | async-start | bytes 2064384 | tf_op jit(solution)/shard_map/all_to_all | solution.py:658
  118.5 13.0 %all-to-all-done.1 = bf16[4,144,896]{2,1,0:T(8,128)(2,1)S(1)} async-done(((bf16[4,144,896]{2,1,0:T(8,128)(2,1)}), bf16[4,144,896]{2,1,0:T(8,128)(2,1)S(1)}, u32[]{:S(2)}, u32[]{:S(2)}) %all-to-all-start.1) | async-done | bytes 1032224 | tf_op jit(solution)/shard_map/all_to_all | solution.py:658
  137.9 3.7 %project.2 = bf16[4,128,896]{2,1,0:T(8,128)(2,1)} custom-call(s32[1]{0:T(128)} %bitcast.2.spots, bf16[4,2,512,256]{3,2,1,0:T(8,128)(2,1)S(1)} %bitcast.105, bf16[4,2,512,256]{3,2,1,0:T(8,128)(2,1)S(1)} %bitcast.106, bf16[2048,896]{1,0:T(8,128)(2,1)S(1)} %copy-done.12, bf16[4,16,896]{2,1,0:T(8,128)(2,1)S(1)} %bitcast.111), custom_call_target="tpu_custom_call" | custom-call | flops 1879048192 | bytes 6684672 | tf_op jit(solution)/shard_map/project/pallas_call | solution.py:401
  141.6 3.8 %all-to-all-start.2 = ((bf16[4,128,896]{2,1,0:T(8,128)(2,1)}), bf16[4,128,896]{2,1,0:T(8,128)(2,1)S(1)}, u32[]{:S(2)}, u32[]{:S(2)}) async-start(bf16[4,128,896]{2,1,0:T(8,128)(2,1)} %project.2), calls=%async_computation.2 | async-start | bytes 1835008 | tf_op jit(solution)/shard_map/all_to_all | solution.py:658
  145.4 17.9 %all-gather.11.cloned.1.call-done = bf16[256,2048]{1,0:T(8,128)(2,1)} async-done(((bf16[64,2048]{1,0:T(8,128)(2,1)}), bf16[256,2048]{1,0:T(8,128)(2,1)}) %all-gather.11.cloned.1.call-update) | async-done | bytes 1048592 | tf_op jit(solution)/shard_map/all_gather | solution.py:698
  168.8 19.8 %all_gather.27.own = bf16[4,64,1792]{2,1,0:T(8,128)(2,1)S(1)} all-gather(bf16[1,64,1792]{2,1,0:T(8,128)(2,1)S(1)} %fusion.1), channel_id=1, replica_groups=mesh['z'=4,'core'=2,'exp'=4] {'z'}, dimensions={0}, use_global_device_ids=true | all-gather | bytes 1146880 | tf_op jit(solution)/shard_map/all_gather | solution.py:702
  193.5 10.0 %collective-permute-done.9.far_b = bf16[2,64,1792]{2,1,0:T(8,128)(2,1)} collective-permute-done((bf16[2,64,1792]{2,1,0:T(8,128)(2,1)}, bf16[2,64,1792]{2,1,0:T(8,128)(2,1)}, u32[]{:S(2)}, u32[]{:S(2)}) %collective-permute-start.9) | collective-permute-done | bytes 458784 | tf_op jit(solution)/shard_map/ppermute | solution.py:577
  212.4 7.9 %expert.2 = bf16[2,4,4,16,256]{4,3,2,1,0:T(8,128)(2,1)S(1)} custom-call(s32[2]{0:T(128)S(1)} %pad_add_fusion.spots, bf16[4,64,1792]{2,1,0:T(8,128)(2,1)S(1)} %slice.101.own, bf16[4,64,1792]{2,1,0:T(8,128)(2,1)S(1)} %copy-done.14, bf16[4,64,1792]{2,1,0:T(8,128)(2,1)S(1)} %collective-permute-done.6.across, bf16[2,64,1792]{2,1,0:T(8,128)(2,1)} %collective-permute-done.8.far_a, ...), custom_call_target="tpu_custom_call" | custom-call | flops 3758096384 | bytes 18350080 | tf_op jit(solution)/shard_map/expert/pallas_call | solution.py:478
  220.3 5.4 %down.3 = bf16[4,4,16,7168]{3,2,1,0:T(8,128)(2,1)S(1)} custom-call(s32[2]{0:T(128)S(1)} %pad_add_fusion.spots, bf16[2,256,256]{2,1,0:T(8,128)(2,1)S(1)} %bitcast.109, bf16[256,7168]{1,0:T(8,128)(2,1)S(1)} %bitcast.95, bf16[256,7168]{1,0:T(8,128)(2,1)} %collective-permute-done.2.down_v, f32[4,16,1792]{2,1,0:T(8,128)S(1)} %pad_maximum_fusion.2.hidden), custom_call_target="tpu_custom_call" | custom-call | flops 1879048192 | bytes 11010048 | tf_op jit(solution)/shard_map/down/pallas_call | solution.py:547
  233.7 7.2 %collective-permute-done.13.far_b = bf16[2,64,1792]{2,1,0:T(8,128)(2,1)S(1)} collective-permute-done((bf16[2,64,1792]{2,1,0:T(8,128)(2,1)}, bf16[2,64,1792]{2,1,0:T(8,128)(2,1)S(1)}, u32[]{:S(2)}, u32[]{:S(2)}) %collective-permute-start.13) | collective-permute-done | bytes 458784 | tf_op jit(solution)/shard_map/ppermute | solution.py:577
  245.9 8.2 %expert.3 = bf16[2,4,4,16,256]{4,3,2,1,0:T(8,128)(2,1)S(1)} custom-call(s32[2]{0:T(128)S(1)} %pad_add_fusion.spots, bf16[4,64,1792]{2,1,0:T(8,128)(2,1)S(1)} %all_gather.27.own, bf16[4,64,1792]{2,1,0:T(8,128)(2,1)} %collective-permute-done.10.along, bf16[4,64,1792]{2,1,0:T(8,128)(2,1)} %collective-permute-done.11.across, ...), custom_call_target="tpu_custom_call" | custom-call | flops 3758096384 | bytes 18350080 | tf_op jit(solution)/shard_map/expert/pallas_call | solution.py:478
  254.1 3.3 down.5
  261.0 3.3 down.4
  266.3 4.7 %collective-permute-done.17 = bf16[4,16,3584]{2,1,0:T(8,128)(2,1)S(1)} collective-permute-done((bf16[4,16,3584]{2,1,0:T(8,128)(2,1)S(1)}, bf16[4,16,3584]{2,1,0:T(8,128)(2,1)S(1)}, u32[]{:S(2)}, u32[]{:S(2)}) %collective-permute-start.17) | collective-permute-done | bytes 458784 | tf_op jit(solution)/shard_map/ppermute | solution.py:577
  272.3 7.7 %collective-permute-done.18 = bf16[4,16,3584]{2,1,0:T(8,128)(2,1)S(1)} collective-permute-done((bf16[4,16,3584]{2,1,0:T(8,128)(2,1)S(1)}, bf16[4,16,3584]{2,1,0:T(8,128)(2,1)S(1)}, u32[]{:S(2)}, u32[]{:S(2)}) %collective-permute-start.18) | collective-permute-done | bytes 458784 | tf_op jit(solution)/shard_map/ppermute | solution.py:577
  281.8 8.8 %collective-permute-done.14 = bf16[4,16,3584]{2,1,0:T(8,128)(2,1)S(1)} collective-permute-done((bf16[4,16,3584]{2,1,0:T(8,128)(2,1)S(1)}, bf16[4,16,3584]{2,1,0:T(8,128)(2,1)S(1)}, u32[]{:S(2)}, u32[]{:S(2)}) %collective-permute-start.14) | collective-permute-done | bytes 458784 | tf_op jit(solution)/shard_map/ppermute | solution.py:577
  290.6 4.7 %collective-permute-done.15 = bf16[4,16,3584]{2,1,0:T(8,128)(2,1)S(1)} collective-permute-done((bf16[4,16,3584]{2,1,0:T(8,128)(2,1)S(1)}, bf16[4,16,3584]{2,1,0:T(8,128)(2,1)S(1)}, u32[]{:S(2)}, u32[]{:S(2)}) %collective-permute-start.15) | collective-permute-done | bytes 458784 | tf_op jit(solution)/shard_map/ppermute | solution.py:577
  297.9 14.0 %all_to_all.20 = bf16[4,16,7168]{2,1,0:T(8,128)(2,1)S(1)} all-to-all(bf16[4,16,7168]{2,1,0:T(8,128)(2,1)} %bitcast.127), channel_id=1, replica_groups=mesh['z'=4,'core'=2,'exp'=4] {'exp'}, dimensions={0} | all-to-all | bytes 1835008 | tf_op jit(solution)/shard_map/all_to_all | solution.py:741
  312.2 11.1 %reduce-scatter.5.cloned.1.call-done = bf16[1,16,7168]{2,1,0:T(8,128)(2,1)} async-done(((bf16[4,16,7168]{2,1,0:T(8,128)(2,1)}), bf16[1,16,7168]{2,1,0:T(8,128)(2,1)}) %reduce-scatter.5.cloned.1.call-update) | async-done | bytes 229392 | tf_op jit(solution)/shard_map/reduce_scatter | solution.py:740
  (172 shorter events, 69.0 us)
Async XLA Ops:
  14.7 55.4 %all-to-all-start = ((bf16[8,512,256]{2,1,0:T(8,128)(2,1)}), bf16[8,512,256]{2,1,0:T(8,128)(2,1)S(1)}, u32[]{:S(2)}, u32[]{:S(2)}) async-start(bf16[8,512,256]{2,1,0:T(8,128)(2,1)} %copy-done.10), calls=%async_computation | async-start | bytes 4194304 | tf_op jit(solution)/shard_map/all_to_all | solution.py:632
  21.1 83.0 %all-gather.7.cloned.1.call-start = ((), (), s32[]{:S(2)}) async-start(), calls=%async_computation.8 | async-start | bytes 1310720 | tf_op jit(solution)/shard_map/all_gather | solution.py:675
  21.1 56.0 %collective-permute-start = (bf16[7168,256]{1,0:T(8,128)(2,1)}, bf16[7168,256]{1,0:T(8,128)(2,1)}, u32[]{:S(2)}, u32[]{:S(2)}) collective-permute-start(bf16[7168,256]{1,0:T(8,128)(2,1)} %bitcast.98), channel_id=1, source_target_pairs={{0,4},{4,0},{1,5},{5,1},{2,6},{6,2},{3,7},{7,3},{8,12},{12,8},{9,1... | collective-permute-start | bytes 11010056 | tf_op jit(solution)/shard_map/ppermute | solution.py:572
  21.6 55.5 %collective-permute-start.1 = (bf16[7168,256]{1,0:T(8,128)(2,1)}, bf16[7168,256]{1,0:T(8,128)(2,1)}, u32[]{:S(2)}, u32[]{:S(2)}) collective-permute-start(bf16[7168,256]{1,0:T(8,128)(2,1)} %bitcast.101), channel_id=1, source_target_pairs={{0,4},{4,0},{1,5},{5,1},{2,6},{6,2},{3,7},{7,3},{8,12},{12,8},{9,1... | collective-permute-start | bytes 11010056 | tf_op jit(solution)/shard_map/ppermute | solution.py:572
  21.7 55.4 %collective-permute-start.2 = (bf16[256,7168]{1,0:T(8,128)(2,1)}, bf16[256,7168]{1,0:T(8,128)(2,1)}, u32[]{:S(2)}, u32[]{:S(2)}) collective-permute-start(bf16[256,7168]{1,0:T(8,128)(2,1)} %bitcast.94), channel_id=1, source_target_pairs={{0,4},{4,0},{1,5},{5,1},{2,6},{6,2},{3,7},{7,3},{8,12},{12,8},{9,1... | collective-permute-start | bytes 11010056 | tf_op jit(solution)/shard_map/ppermute | solution.py:572
  77.0 57.2 %all-gather.9.cloned.1.call-start = ((), (), s32[]{:S(2)}) async-start(), calls=%async_computation.9 | async-start | bytes 2359296 | tf_op jit(solution)/shard_map/all_gather | solution.py:681
  114.0 17.5 %all-to-all-start.1 = ((bf16[4,144,896]{2,1,0:T(8,128)(2,1)}), bf16[4,144,896]{2,1,0:T(8,128)(2,1)S(1)}, u32[]{:S(2)}, u32[]{:S(2)}) async-start(bf16[4,144,896]{2,1,0:T(8,128)(2,1)} %project.3), calls=%async_computation.1 | async-start | bytes 2064384 | tf_op jit(solution)/shard_map/all_to_all | solution.py:658
  117.7 45.6 %all-gather.11.cloned.1.call-start = ((), (), s32[]{:S(2)}) async-start(), calls=%async_computation.10 | async-start | bytes 1310720 | tf_op jit(solution)/shard_map/all_gather | solution.py:698
  141.6 22.9 %all-to-all-start.2 = ((bf16[4,128,896]{2,1,0:T(8,128)(2,1)}), bf16[4,128,896]{2,1,0:T(8,128)(2,1)S(1)}, u32[]{:S(2)}, u32[]{:S(2)}) async-start(bf16[4,128,896]{2,1,0:T(8,128)(2,1)} %project.2), calls=%async_computation.2 | async-start | bytes 1835008 | tf_op jit(solution)/shard_map/all_to_all | solution.py:658
  145.4 152.5 %reduce-scatter.3.cloned.1.call-start = ((), (), s32[]{:S(2)}) async-start(), calls=%async_computation.6 | async-start | bytes 4587520 | tf_op jit(solution)/shard_map/reduce_scatter | solution.py:723
  164.8 23.7 %collective-permute-start.6 = (bf16[4,64,1792]{2,1,0:T(8,128)(2,1)S(1)}, bf16[4,64,1792]{2,1,0:T(8,128)(2,1)S(1)}, u32[]{:S(2)}, u32[]{:S(2)}) collective-permute-start(bf16[4,64,1792]{2,1,0:T(8,128)(2,1)S(1)} %slice.101.own), channel_id=1, source_target_pairs={{0,2},{1,3},{2,0},{3,1},{4,6},{5,7},{6,4},{7,5},{8,10},{9,11},{10,... | collective-permute-start | bytes 2752520 | tf_op jit(solution)/shard_map/ppermute | solution.py:577
  166.4 22.4 %collective-permute-start.5 = (bf16[4,64,1792]{2,1,0:T(8,128)(2,1)S(1)}, bf16[4,64,1792]{2,1,0:T(8,128)(2,1)S(1)}, u32[]{:S(2)}, u32[]{:S(2)}) collective-permute-start(bf16[4,64,1792]{2,1,0:T(8,128)(2,1)S(1)} %slice.101.own), channel_id=1, source_target_pairs={{0,1},{1,0},{2,3},{3,2},{4,5},{5,4},{6,7},{7,6},{8,9},{9,8},{10,11... | collective-permute-start | bytes 2752520 | tf_op jit(solution)/shard_map/ppermute | solution.py:577
  191.4 12.1 %collective-permute-start.9 = (bf16[2,64,1792]{2,1,0:T(8,128)(2,1)}, bf16[2,64,1792]{2,1,0:T(8,128)(2,1)}, u32[]{:S(2)}, u32[]{:S(2)}) collective-permute-start(bf16[2,64,1792]{2,1,0:T(8,128)(2,1)} %slice.83), channel_id=1, source_target_pairs={{0,1},{1,0},{2,3},{3,2},{4,5},{5,4},{6,7},{7,6},{8,9},{9,8},{10,11... | collective-permute-start | bytes 1376264 | tf_op jit(solution)/shard_map/ppermute | solution.py:577
  192.8 11.8 %collective-permute-start.8 = (bf16[2,64,1792]{2,1,0:T(8,128)(2,1)}, bf16[2,64,1792]{2,1,0:T(8,128)(2,1)}, u32[]{:S(2)}, u32[]{:S(2)}) collective-permute-start(bf16[2,64,1792]{2,1,0:T(8,128)(2,1)} %slice.82), channel_id=1, source_target_pairs={{0,2},{1,3},{2,0},{3,1},{4,6},{5,7},{6,4},{7,5},{8,10},{9,11},{10,... | collective-permute-start | bytes 1376264 | tf_op jit(solution)/shard_map/ppermute | solution.py:577
  204.6 22.9 %collective-permute-start.11 = (bf16[4,64,1792]{2,1,0:T(8,128)(2,1)S(1)}, bf16[4,64,1792]{2,1,0:T(8,128)(2,1)}, u32[]{:S(2)}, u32[]{:S(2)}) collective-permute-start(bf16[4,64,1792]{2,1,0:T(8,128)(2,1)S(1)} %all_gather.27.own), channel_id=1, source_target_pairs={{0,2},{1,3},{2,0},{3,1},{4,6},{5,7},{6,4},{7,5},{8,10},{9,11},{10,... | collective-permute-start | bytes 2752520 | tf_op jit(solution)/shard_map/ppermute | solution.py:577
  205.2 22.3 %collective-permute-start.10 = (bf16[4,64,1792]{2,1,0:T(8,128)(2,1)S(1)}, bf16[4,64,1792]{2,1,0:T(8,128)(2,1)}, u32[]{:S(2)}, u32[]{:S(2)}) collective-permute-start(bf16[4,64,1792]{2,1,0:T(8,128)(2,1)S(1)} %all_gather.27.own), channel_id=1, source_target_pairs={{0,1},{1,0},{2,3},{3,2},{4,5},{5,4},{6,7},{7,6},{8,9},{9,8},{10,11... | collective-permute-start | bytes 2752520 | tf_op jit(solution)/shard_map/ppermute | solution.py:577
  227.6 95.7 %reduce-scatter.5.cloned.1.call-start = ((), (), s32[]{:S(2)}) async-start(), calls=%async_computation.7 | async-start | bytes 1146880 | tf_op jit(solution)/shard_map/reduce_scatter | solution.py:740
  230.6 10.3 %collective-permute-start.13 = (bf16[2,64,1792]{2,1,0:T(8,128)(2,1)}, bf16[2,64,1792]{2,1,0:T(8,128)(2,1)S(1)}, u32[]{:S(2)}, u32[]{:S(2)}) collective-permute-start(bf16[2,64,1792]{2,1,0:T(8,128)(2,1)} %slice.88), channel_id=1, source_target_pairs={{0,1},{1,0},{2,3},{3,2},{4,5},{5,4},{6,7},{7,6},{8,9},{9,8},{10,11... | collective-permute-start | bytes 1376264 | tf_op jit(solution)/shard_map/ppermute | solution.py:577
  257.4 13.5 %collective-permute-start.17 = (bf16[4,16,3584]{2,1,0:T(8,128)(2,1)S(1)}, bf16[4,16,3584]{2,1,0:T(8,128)(2,1)S(1)}, u32[]{:S(2)}, u32[]{:S(2)}) collective-permute-start(bf16[4,16,3584]{2,1,0:T(8,128)(2,1)S(1)} %get-tuple-element.61), channel_id=1, source_target_pairs={{0,1},{1,0},{2,3},{3,2},{4,5},{5,4},{6,7},{7,6},{8,9},{9,8},{10,11... | collective-permute-start | bytes 1376264 | tf_op jit(solution)/shard_map/ppermute | solution.py:577
  258.1 21.9 %collective-permute-start.18 = (bf16[4,16,3584]{2,1,0:T(8,128)(2,1)S(1)}, bf16[4,16,3584]{2,1,0:T(8,128)(2,1)S(1)}, u32[]{:S(2)}, u32[]{:S(2)}) collective-permute-start(bf16[4,16,3584]{2,1,0:T(8,128)(2,1)S(1)} %get-tuple-element.62), channel_id=1, source_target_pairs={{0,2},{1,3},{2,0},{3,1},{4,6},{5,7},{6,4},{7,5},{8,10},{9,11},{10,... | collective-permute-start | bytes 1376264 | tf_op jit(solution)/shard_map/ppermute | solution.py:577
  259.4 22.1 %collective-permute-start.19 = (bf16[4,16,3584]{2,1,0:T(8,128)(2,1)S(1)}, bf16[4,16,3584]{2,1,0:T(8,128)(2,1)S(1)}, u32[]{:S(2)}, u32[]{:S(2)}) collective-permute-start(bf16[4,16,3584]{2,1,0:T(8,128)(2,1)S(1)} %get-tuple-element.63), channel_id=1, source_target_pairs={{0,3},{1,2},{2,1},{3,0},{4,7},{5,6},{6,5},{7,4},{8,11},{9,10},{10,... | collective-permute-start | bytes 1376264 | tf_op jit(solution)/shard_map/ppermute | solution.py:577
  264.2 26.3 %collective-permute-start.14 = (bf16[4,16,3584]{2,1,0:T(8,128)(2,1)S(1)}, bf16[4,16,3584]{2,1,0:T(8,128)(2,1)S(1)}, u32[]{:S(2)}, u32[]{:S(2)}) collective-permute-start(bf16[4,16,3584]{2,1,0:T(8,128)(2,1)S(1)} %get-tuple-element.57), channel_id=1, source_target_pairs={{0,1},{1,0},{2,3},{3,2},{4,5},{5,4},{6,7},{7,6},{8,9},{9,8},{10,11... | collective-permute-start | bytes 1376264 | tf_op jit(solution)/shard_map/ppermute | solution.py:577
  264.9 30.3 %collective-permute-start.15 = (bf16[4,16,3584]{2,1,0:T(8,128)(2,1)S(1)}, bf16[4,16,3584]{2,1,0:T(8,128)(2,1)S(1)}, u32[]{:S(2)}, u32[]{:S(2)}) collective-permute-start(bf16[4,16,3584]{2,1,0:T(8,128)(2,1)S(1)} %get-tuple-element.58), channel_id=1, source_target_pairs={{0,2},{1,3},{2,0},{3,1},{4,6},{5,7},{6,4},{7,5},{8,10},{9,11},{10,... | collective-permute-start | bytes 1376264 | tf_op jit(solution)/shard_map/ppermute | solution.py:577
  270.9 25.7 %collective-permute-start.16 = (bf16[4,16,3584]{2,1,0:T(8,128)(2,1)S(1)}, bf16[4,16,3584]{2,1,0:T(8,128)(2,1)S(1)}, u32[]{:S(2)}, u32[]{:S(2)}) collective-permute-start(bf16[4,16,3584]{2,1,0:T(8,128)(2,1)S(1)} %get-tuple-element.59), channel_id=1, source_target_pairs={{0,3},{1,2},{2,1},{3,0},{4,7},{5,6},{6,5},{7,4},{8,11},{9,10},{10,... | collective-permute-start | bytes 1376264 | tf_op jit(solution)/shard_map/ppermute | solution.py:577
  (31 other events, 153.3 us)
Sparse Core Ops, SparseCore 0:
  77.2 26.8 all-gather.6
  105.6 28.5 all-gather.8
  135.8 27.4 all-gather.10
  227.7 67.8 reduce-scatter.2
  298.0 25.1 reduce-scatter.4

commit v11 on v9

--- a/solution.py
+++ b/solution.py
@@ -423,6 +423,34 @@
     )(spots, left_a, left_b, proj, table)
 
 
+def hold_kernel(count, *refs):
+    sources, targets, token, arrivals = refs[:count], refs[count : 2 * count], refs[-2], refs[-1]
+    copies = [
+        pltpu.make_async_copy(source, target, arrivals.at[spot])
+        for spot, (source, target) in enumerate(zip(sources, targets))
+    ]
+    for copy in copies:
+        copy.start()
+    token[...] = jnp.zeros_like(token)
+    for copy in copies:
+        copy.wait()
+
+
+def hold(blocks):
+    count = len(blocks)
+    *held, token = pl.pallas_call(
+        functools.partial(hold_kernel, count),
+        in_specs=[pl.BlockSpec(memory_space=pl.ANY)] * count,
+        out_specs=[pl.BlockSpec(memory_space=pltpu.VMEM)] * (count + 1),
+        out_shape=[pltpu.VMEM(block.shape, block.dtype) for block in blocks]
+        + [jax.ShapeDtypeStruct((8, 128), jnp.float32)],
+        scratch_shapes=[pltpu.SemaphoreType.DMA((count,))],
+        compiler_params=pltpu.CompilerParams(vmem_limit_bytes=4 * 2**20),
+        name="hold",
+    )(*blocks)
+    return held, token
+
+
 def expert_kernel(exp_dim, spots, own, along, across, far_a, far_b, gain, gate_w, up_w, gate_v, up_v, route, out, total, squares):
     step = pl.program_id(0)
 
@@ -433,8 +461,10 @@
 
     far = jnp.where(step < pl.num_programs(0) // 2, far_a[0], far_b[0])
     block = jnp.concatenate([own[0], along[0], across[0], far], 0)
+    first = pl.multiple_of(step * block.shape[1], block.shape[1])
     for spot, weight in enumerate((gate_w, up_w, gate_v, up_v)):
-        total[spot] += jnp.dot(block, weight[...], preferred_element_type=jnp.float32)
+        piece = weight[pl.ds(first, block.shape[1]), :]
+        total[spot] += jnp.dot(block, piece, preferred_element_type=jnp.float32)
     lane = squares.shape[1]
     collected = squares[...]
     for part in range(block.shape[1] // lane):
@@ -474,7 +504,7 @@
     lane = math.gcd(128, cols)
     lead = (exp_count, tokens // half) if exp_dim == 0 else (tokens // half, exp_count)
     by_chip = pl.BlockSpec((1, tokens, cols), lambda i, _: (i, 0, 0))
-    by_cols = pl.BlockSpec((cols, units), lambda i, _: (i, 0))
+    by_cols = pl.BlockSpec(memory_space=pltpu.VMEM)
     out = pl.pallas_call(
         functools.partial(expert_kernel, exp_dim),
         grid_spec=pltpu.PrefetchScalarGridSpec(
@@ -504,7 +534,7 @@
             ],
         ),
         out_shape=jax.ShapeDtypeStruct((2,) + lead + (half, units), jnp.bfloat16),
-        compiler_params=pltpu.CompilerParams(vmem_limit_bytes=56 * 2**20),
+        compiler_params=pltpu.CompilerParams(vmem_limit_bytes=16 * 2**20),
         cost_estimate=pl.CostEstimate(
             flops=8 * row_total * units * steps * cols,
             bytes_accessed=2 * steps * cols * (row_total + 4 * units),
@@ -517,7 +547,9 @@
 
 def down_kernel(start, spots, active, down_w, down_v, hidden, *outs):
     left = jnp.concatenate([active[0], active[1]], 1)
-    right = jnp.concatenate([down_w[...], down_v[...]], 0)
+    cols = hidden.shape[2]
+    lanes = pl.ds(pl.multiple_of((pl.program_id(0) + start) * cols, cols), cols)
+    right = jnp.concatenate([down_w[:, lanes], down_v[:, lanes]], 0)
     sums = jnp.dot(left, right, preferred_element_type=jnp.float32).astype(jnp.bfloat16)
     kept = outs[0]
     if len(outs) == 1:
@@ -541,7 +573,7 @@
     whole = stop - start == chip_count
     lead = (chip_count, exp_count) if whole else (chip_count,)
     zeros = (0,) * len(lead + (half,))
-    by_cols = pl.BlockSpec((units, cols), lambda i, _: (0, i + start))
+    by_cols = pl.BlockSpec(memory_space=pltpu.VMEM)
     count = 1 if whole else exp_count
     shape = lead + (half, (stop - start) * cols)
     return pl.pallas_call(
@@ -558,7 +590,7 @@
             out_specs=[pl.BlockSpec(lead + (half, cols), lambda i, _: (*zeros, i))] * count,
         ),
         out_shape=[jax.ShapeDtypeStruct(shape, jnp.bfloat16)] * count,
-        compiler_params=pltpu.CompilerParams(vmem_limit_bytes=56 * 2**20),
+        compiler_params=pltpu.CompilerParams(vmem_limit_bytes=16 * 2**20),
         cost_estimate=pl.CostEstimate(
             flops=4 * rows * units * cols * (stop - start),
             bytes_accessed=2 * cols * (stop - start) * (rows + 2 * units),
@@ -693,17 +725,20 @@
         core_spot, spread_second, spread_second, True, out_proj, table, exp_count, False
     )
     pieces, sums_first = lax.optimization_barrier((pieces, sums_first))
+    weights = (expert_gate[0], expert_up[0], other_gate, other_up, expert_down[0], other_down)
+    *weights, pieces = lax.optimization_barrier((*weights, pieces))
+    (*weights, down_w, down_v), token = hold(weights)
     wide = 1 << (2 * cols - 1).bit_length()
     padded = jnp.pad(scaled_first, ((0, 0), (0, wide - 2 * cols)))
     plane_first = lax.all_gather(padded, "z", axis=0)[:, :, : 2 * cols]
-    pieces, plane_first = lax.optimization_barrier((exchange(pieces), plane_first))
+    pieces, plane_first, token = lax.optimization_barrier((exchange(pieces), plane_first, token))
+    spots = spots + token[0, :2].astype(jnp.int32)
     sums_second, scaled_second = settle(pieces, 1)
     along, across = plane_step(plane_first, 1), plane_step(plane_first, 2)
     plane_second = lax.all_gather(scaled_second, "z", axis=0)
     along, across, plane_second = lax.optimization_barrier((along, across, plane_second))
     far_a, far_b = plane_step(along[:middle], 2), plane_step(across[middle:], 1)
     far_a, far_b, plane_second = lax.optimization_barrier((far_a, far_b, plane_second))
-    weights = (expert_gate[0], expert_up[0], other_gate, other_up)
 
     def run_active(blocks, group):
         route_rows = route[:, :, group].reshape(exp_count, chip_count * half, 1)
@@ -711,7 +746,7 @@
 
     def run_outs(active, sums, start, stop):
         return run_down(
-            spots, active, expert_down[0], other_down, sums, exp_count, start, stop
+            spots, active, down_w, down_v, sums, exp_count, start, stop
         )
 
     active = run_active((plane_first, along, across, far_a, far_b), 0)

time: 328 us -> 355 us (1.082)
  local copies, waits for them, and re-layouts: 15.7 us -> 53.8 us
  Pallas kernels: 57.1 us -> 44.5 us
    unnamed x39 -> x83, local copies, waits for them, and re-layouts: 8.08 us -> 44.8 us
    pallas_call x3, Pallas kernels: 16.8 us -> 7.63 us  [run_down(): pl.pallas_call(functools.partial(down_kernel, start), grid_spec=pltpu.Pre...]
    pallas_call x2, Pallas kernels: 21.7 us -> 13.4 us  [run_expert(): pl.pallas_call(functools.partial(expert_kernel, exp_dim), grid_spec=pltpu...]
    pallas_call x0 -> x1, Pallas kernels: none -> 4.8 us  [hold(): pl.pallas_call(functools.partial(hold_kernel, count), in_specs=[pl.BlockS...]
  transfers between devices with their start and end apart: 28 -> 28, of which waited for: 18 -> 18; matrix products, arithmetic and copies ran while one was open for 4% -> 3% of each run, Pallas kernels for 17% -> 12%
where the time goes in v11:
time: 355 us; the launch traced here: 354 us
  waiting for transfers between devices  172 us (48%)
  local copies, waits for them, and re-layouts  53.8 us (15%)
  Pallas kernels  44.5 us (13%)
  blocking collectives  33.2 us (9%)
  starting transfers between devices  31 us (9%)
  between operations  13.7 us (4%)
  other arithmetic  5.73 us (2%)
    ppermute x14, waiting for transfers between devices, plane_step(): return lax.ppermute(block, 'exp', [(i, i ^ step) for i in range(count)])  49.6 us
    all_to_all x1, waiting for transfers between devices, by_heads(): moved = lax.all_to_all(packed, ctx, split_axis=0, concat_axis=0, tiled=True)  47.8 us
    unnamed x83, local copies, waits for them, and re-layouts  44.8 us
    all_gather x1, waiting for transfers between devices, by_heads(): spread_first = lax.all_gather(attended[0], 'z', axis=0)  26.9 us
    all_gather x1, blocking collectives, by_heads(): plane_second = lax.all_gather(scaled_second, 'z', axis=0)  19.8 us
    all_gather x1, waiting for transfers between devices, by_heads(): plane_first = lax.all_gather(padded, 'z', axis=0)[:, :, :2 * cols]  19.1 us
    ppermute x14, starting transfers between devices, plane_step(): return lax.ppermute(block, 'exp', [(i, i ^ step) for i in range(count)])  16 us
    pallas_call x2, Pallas kernels, run_expert(): pl.pallas_call(functools.partial(expert_kernel, exp_dim), grid_spec=pltpu...  13.4 us
  transfers between devices with their start and end apart: 28, of which 18 were waited for; matrix products, arithmetic and copies ran while one was open for 3% of the time, Pallas kernels for 12%

profile of v11, /device:TPU:0, one launch (start us, length us, event | category | flops | bytes accessed | tf_op | source)
XLA Modules:
  0.0 353.8 jit_solution(10647818581672024770)
XLA Ops:
  14.8 6.3 %all-to-all-start = ((bf16[8,512,256]{2,1,0:T(8,128)(2,1)}), bf16[8,512,256]{2,1,0:T(8,128)(2,1)S(1)}, u32[]{:S(2)}, u32[]{:S(2)}) async-start(bf16[8,512,256]{2,1,0:T(8,128)(2,1)} %copy-done.21), calls=%async_computation | async-start | bytes 4194304 | tf_op jit(solution)/shard_map/all_to_all | solution.py:664
  22.4 47.8 %all-to-all-done.moved = bf16[8,512,256]{2,1,0:T(8,128)(2,1)S(1)} async-done(((bf16[8,512,256]{2,1,0:T(8,128)(2,1)}), bf16[8,512,256]{2,1,0:T(8,128)(2,1)S(1)}, u32[]{:S(2)}, u32[]{:S(2)}) %all-to-all-start) | async-done | bytes 2097184 | tf_op jit(solution)/shard_map/all_to_all | solution.py:664
  71.0 6.0 %attend.1 = (bf16[512,256]{1,0:T(8,128)(2,1)}, bf16[512,256]{1,0:T(8,128)(2,1)}) custom-call(bf16[8,512,256]{2,1,0:T(8,128)(2,1)S(1)} %all-to-all-done.moved, f32[8,1024]{1,0:T(8,128)S(1)} %tile.12.taps, f32[1024,4]{1,0:T(8,128)S(1)} %copy.85.gates), custom_call_target="tpu_custom_call" | custom-call | tf_op jit(solution)/shard_map/attend/pallas_call | solution.py:352
  77.2 26.9 %all-gather.7.cloned.1.call-done = bf16[2048,256]{1,0:T(8,128)(2,1)} async-done(((bf16[512,256]{1,0:T(8,128)(2,1)}), bf16[2048,256]{1,0:T(8,128)(2,1)}) %all-gather.7.cloned.1.call-update) | async-done | bytes 1048592 | tf_op jit(solution)/shard_map/all_gather | solution.py:707
  107.2 5.7 %project.3 = bf16[4,144,896]{2,1,0:T(8,128)(2,1)} custom-call(s32[1]{0:T(128)} %bitcast.16.spots, bf16[4,1,512,256]{3,2,1,0:T(8,128)(2,1)} %bitcast.137, bf16[4,1,512,256]{3,2,1,0:T(8,128)(2,1)} %bitcast.22.left_b, bf16[2048,896]{1,0:T(8,128)(2,1)} %proj.3, bf16[4,16,896]{2,1,0:T(8,128)(2,1)} %bitcast.124), custom_call_target="tpu_custom_call" | custom-call | flops 1879048192 | bytes 6799360 | tf_op jit(solution)/shard_map/project/pallas_call | solution.py:401
  112.9 3.8 %all-to-all-start.1 = ((bf16[4,144,896]{2,1,0:T(8,128)(2,1)}), bf16[4,144,896]{2,1,0:T(8,128)(2,1)S(1)}, u32[]{:S(2)}, u32[]{:S(2)}) async-start(bf16[4,144,896]{2,1,0:T(8,128)(2,1)} %project.3), calls=%async_computation.1 | async-start | bytes 2064384 | tf_op jit(solution)/shard_map/all_to_all | solution.py:690
  117.5 13.0 %all-to-all-done.1 = bf16[4,144,896]{2,1,0:T(8,128)(2,1)S(1)} async-done(((bf16[4,144,896]{2,1,0:T(8,128)(2,1)}), bf16[4,144,896]{2,1,0:T(8,128)(2,1)S(1)}, u32[]{:S(2)}, u32[]{:S(2)}) %all-to-all-start.1) | async-done | bytes 1032224 | tf_op jit(solution)/shard_map/all_to_all | solution.py:690
  134.3 6.2 %project.2 = bf16[4,128,896]{2,1,0:T(8,128)(2,1)} custom-call(s32[1]{0:T(128)} %bitcast.16.spots, bf16[4,2,512,256]{3,2,1,0:T(8,128)(2,1)} %bitcast.109, bf16[4,2,512,256]{3,2,1,0:T(8,128)(2,1)} %bitcast.110, bf16[2048,896]{1,0:T(8,128)(2,1)} %proj.3, bf16[4,16,896]{2,1,0:T(8,128)(2,1)} %bitcast.125), custom_call_target="tpu_custom_call" | custom-call | flops 1879048192 | bytes 6684672 | tf_op jit(solution)/shard_map/project/pallas_call | solution.py:401
  140.5 3.6 %all-to-all-start.2 = ((bf16[4,128,896]{2,1,0:T(8,128)(2,1)}), bf16[4,128,896]{2,1,0:T(8,128)(2,1)S(1)}, u32[]{:S(2)}, u32[]{:S(2)}) async-start(bf16[4,128,896]{2,1,0:T(8,128)(2,1)} %project.2), calls=%async_computation.2 | async-start | bytes 1835008 | tf_op jit(solution)/shard_map/all_to_all | solution.py:690
  144.2 19.1 %all-gather.11.cloned.1.call-done = bf16[256,2048]{1,0:T(8,128)(2,1)} async-done(((bf16[64,2048]{1,0:T(8,128)(2,1)}), bf16[256,2048]{1,0:T(8,128)(2,1)}) %all-gather.11.cloned.1.call-update) | async-done | bytes 1048592 | tf_op jit(solution)/shard_map/all_gather | solution.py:733
  170.7 4.8 %hold.1 = (bf16[7168,256]{1,0:T(8,128)(2,1)S(1)}, bf16[7168,256]{1,0:T(8,128)(2,1)S(1)}, bf16[7168,256]{1,0:T(8,128)(2,1)S(1)}, bf16[7168,256]{1,0:T(8,128)(2,1)...) custom-call(bf16[7168,256]{1,0:T(8,128)(2,1)S(1)} %bitcast.98, ...), custom_call_target="tpu_custom_call" | custom-call | tf_op jit(solution)/shard_map/hold/pallas_call | solution.py:441
  190.0 19.8 %all_gather.27.own = bf16[4,64,1792]{2,1,0:T(8,128)(2,1)S(1)} all-gather(bf16[1,64,1792]{2,1,0:T(8,128)(2,1)S(1)} %fusion.1), channel_id=1, replica_groups=mesh['z'=4,'core'=2,'exp'=4] {'z'}, dimensions={0}, use_global_device_ids=true | all-gather | bytes 1146880 | tf_op jit(solution)/shard_map/all_gather | solution.py:738
  216.3 9.1 %collective-permute-done.9.far_b = bf16[2,64,1792]{2,1,0:T(8,128)(2,1)} collective-permute-done((bf16[2,64,1792]{2,1,0:T(8,128)(2,1)}, bf16[2,64,1792]{2,1,0:T(8,128)(2,1)}, u32[]{:S(2)}, u32[]{:S(2)}) %collective-permute-start.9) | collective-permute-done | bytes 458784 | tf_op jit(solution)/shard_map/ppermute | solution.py:609
  237.5 6.9 %expert.2 = bf16[2,4,4,16,256]{4,3,2,1,0:T(8,128)(2,1)S(1)} custom-call(s32[2]{0:T(128)S(1)} %add_add_fusion.spots, bf16[4,64,1792]{2,1,0:T(8,128)(2,1)S(1)} %slice.105.own, bf16[4,64,1792]{2,1,0:T(8,128)(2,1)S(1)} %copy-done.26, bf16[4,64,1792]{2,1,0:T(8,128)(2,1)S(1)} %collective-permute-done.6.across, bf16[2,64,1792]{2,1,0:T(8,128)(2,1)} %collective-permute-done.8.far_a, ...), custom_call_target="tpu_custom_call" | custom-call | flops 3758096384 | bytes 18350080 | tf_op jit(solution)/shard_map/expert/pallas_call | solution.py:508
  244.4 3.5 down.3
  255.3 7.0 %collective-permute-done.13.far_b = bf16[2,64,1792]{2,1,0:T(8,128)(2,1)S(1)} collective-permute-done((bf16[2,64,1792]{2,1,0:T(8,128)(2,1)S(1)}, bf16[2,64,1792]{2,1,0:T(8,128)(2,1)S(1)}, u32[]{:S(2)}, u32[]{:S(2)}) %collective-permute-start.13) | collective-permute-done | bytes 458784 | tf_op jit(solution)/shard_map/ppermute | solution.py:609
  267.6 2.1 copy-done.16
  271.7 6.6 %expert.3 = bf16[2,4,4,16,256]{4,3,2,1,0:T(8,128)(2,1)S(1)} custom-call(s32[2]{0:T(128)S(1)} %add_add_fusion.spots, bf16[4,64,1792]{2,1,0:T(8,128)(2,1)S(1)} %all_gather.27.own, bf16[4,64,1792]{2,1,0:T(8,128)(2,1)} %collective-permute-done.10.along, bf16[4,64,1792]{2,1,0:T(8,128)(2,1)} %collective-permute-done.11.across, ...), custom_call_target="tpu_custom_call" | custom-call | flops 3758096384 | bytes 18350080 | tf_op jit(solution)/shard_map/expert/pallas_call | solution.py:508
  287.9 6.0 %collective-permute-done.17 = bf16[4,16,3584]{2,1,0:T(8,128)(2,1)S(1)} collective-permute-done((bf16[4,16,3584]{2,1,0:T(8,128)(2,1)S(1)}, bf16[4,16,3584]{2,1,0:T(8,128)(2,1)S(1)}, u32[]{:S(2)}, u32[]{:S(2)}) %collective-permute-start.17) | collective-permute-done | bytes 458784 | tf_op jit(solution)/shard_map/ppermute | solution.py:609
  295.2 8.7 %collective-permute-done.18 = bf16[4,16,3584]{2,1,0:T(8,128)(2,1)S(1)} collective-permute-done((bf16[4,16,3584]{2,1,0:T(8,128)(2,1)S(1)}, bf16[4,16,3584]{2,1,0:T(8,128)(2,1)S(1)}, u32[]{:S(2)}, u32[]{:S(2)}) %collective-permute-start.18) | collective-permute-done | bytes 458784 | tf_op jit(solution)/shard_map/ppermute | solution.py:609
  304.8 8.8 %collective-permute-done.14 = bf16[4,16,3584]{2,1,0:T(8,128)(2,1)S(1)} collective-permute-done((bf16[4,16,3584]{2,1,0:T(8,128)(2,1)S(1)}, bf16[4,16,3584]{2,1,0:T(8,128)(2,1)S(1)}, u32[]{:S(2)}, u32[]{:S(2)}) %collective-permute-start.14) | collective-permute-done | bytes 458784 | tf_op jit(solution)/shard_map/ppermute | solution.py:609
  313.6 6.0 %collective-permute-done.16 = bf16[4,16,3584]{2,1,0:T(8,128)(2,1)S(1)} collective-permute-done((bf16[4,16,3584]{2,1,0:T(8,128)(2,1)S(1)}, bf16[4,16,3584]{2,1,0:T(8,128)(2,1)S(1)}, u32[]{:S(2)}, u32[]{:S(2)}) %collective-permute-start.16) | collective-permute-done | bytes 458784 | tf_op jit(solution)/shard_map/ppermute | solution.py:609
  320.9 13.4 %all_to_all.20 = bf16[4,16,7168]{2,1,0:T(8,128)(2,1)S(1)} all-to-all(bf16[4,16,7168]{2,1,0:T(8,128)(2,1)} %bitcast.120), channel_id=1, replica_groups=mesh['z'=4,'core'=2,'exp'=4] {'exp'}, dimensions={0} | all-to-all | bytes 1835008 | tf_op jit(solution)/shard_map/all_to_all | solution.py:776
  334.4 11.1 %reduce-scatter.5.cloned.1.call-done = bf16[1,16,7168]{2,1,0:T(8,128)(2,1)} async-done(((bf16[4,16,7168]{2,1,0:T(8,128)(2,1)}), bf16[1,16,7168]{2,1,0:T(8,128)(2,1)}) %reduce-scatter.5.cloned.1.call-update) | async-done | bytes 229392 | tf_op jit(solution)/shard_map/reduce_scatter | solution.py:775
  (195 shorter events, 87.8 us)
Async XLA Ops:
  14.8 55.4 %all-to-all-start = ((bf16[8,512,256]{2,1,0:T(8,128)(2,1)}), bf16[8,512,256]{2,1,0:T(8,128)(2,1)S(1)}, u32[]{:S(2)}, u32[]{:S(2)}) async-start(bf16[8,512,256]{2,1,0:T(8,128)(2,1)} %copy-done.21), calls=%async_computation | async-start | bytes 4194304 | tf_op jit(solution)/shard_map/all_to_all | solution.py:664
  21.1 83.0 %all-gather.7.cloned.1.call-start = ((), (), s32[]{:S(2)}) async-start(), calls=%async_computation.8 | async-start | bytes 1310720 | tf_op jit(solution)/shard_map/all_gather | solution.py:707
  21.2 56.0 %collective-permute-start = (bf16[7168,256]{1,0:T(8,128)(2,1)}, bf16[7168,256]{1,0:T(8,128)(2,1)}, u32[]{:S(2)}, u32[]{:S(2)}) collective-permute-start(bf16[7168,256]{1,0:T(8,128)(2,1)} %bitcast.97), channel_id=1, source_target_pairs={{0,4},{4,0},{1,5},{5,1},{2,6},{6,2},{3,7},{7,3},{8,12},{12,8},{9,1... | collective-permute-start | bytes 11010056 | tf_op jit(solution)/shard_map/ppermute | solution.py:604
  21.6 55.5 %collective-permute-start.1 = (bf16[7168,256]{1,0:T(8,128)(2,1)}, bf16[7168,256]{1,0:T(8,128)(2,1)}, u32[]{:S(2)}, u32[]{:S(2)}) collective-permute-start(bf16[7168,256]{1,0:T(8,128)(2,1)} %bitcast.99), channel_id=1, source_target_pairs={{0,4},{4,0},{1,5},{5,1},{2,6},{6,2},{3,7},{7,3},{8,12},{12,8},{9,1... | collective-permute-start | bytes 11010056 | tf_op jit(solution)/shard_map/ppermute | solution.py:604
  21.7 55.4 %collective-permute-start.2 = (bf16[256,7168]{1,0:T(8,128)(2,1)}, bf16[256,7168]{1,0:T(8,128)(2,1)}, u32[]{:S(2)}, u32[]{:S(2)}) collective-permute-start(bf16[256,7168]{1,0:T(8,128)(2,1)} %bitcast.101), channel_id=1, source_target_pairs={{0,4},{4,0},{1,5},{5,1},{2,6},{6,2},{3,7},{7,3},{8,12},{12,8},{9,1... | collective-permute-start | bytes 11010056 | tf_op jit(solution)/shard_map/ppermute | solution.py:604
  77.1 57.2 %all-gather.9.cloned.1.call-start = ((), (), s32[]{:S(2)}) async-start(), calls=%async_computation.9 | async-start | bytes 2359296 | tf_op jit(solution)/shard_map/all_gather | solution.py:713
  112.9 17.7 %all-to-all-start.1 = ((bf16[4,144,896]{2,1,0:T(8,128)(2,1)}), bf16[4,144,896]{2,1,0:T(8,128)(2,1)S(1)}, u32[]{:S(2)}, u32[]{:S(2)}) async-start(bf16[4,144,896]{2,1,0:T(8,128)(2,1)} %project.3), calls=%async_computation.1 | async-start | bytes 2064384 | tf_op jit(solution)/shard_map/all_to_all | solution.py:690
  116.7 46.7 %all-gather.11.cloned.1.call-start = ((), (), s32[]{:S(2)}) async-start(), calls=%async_computation.10 | async-start | bytes 1310720 | tf_op jit(solution)/shard_map/all_gather | solution.py:733
  140.5 46.0 %all-to-all-start.2 = ((bf16[4,128,896]{2,1,0:T(8,128)(2,1)}), bf16[4,128,896]{2,1,0:T(8,128)(2,1)S(1)}, u32[]{:S(2)}, u32[]{:S(2)}) async-start(bf16[4,128,896]{2,1,0:T(8,128)(2,1)} %project.2), calls=%async_computation.2 | async-start | bytes 1835008 | tf_op jit(solution)/shard_map/all_to_all | solution.py:690
  144.2 176.6 %reduce-scatter.3.cloned.1.call-start = ((), (), s32[]{:S(2)}) async-start(), calls=%async_computation.6 | async-start | bytes 4587520 | tf_op jit(solution)/shard_map/reduce_scatter | solution.py:758
  186.8 22.9 %collective-permute-start.6 = (bf16[4,64,1792]{2,1,0:T(8,128)(2,1)S(1)}, bf16[4,64,1792]{2,1,0:T(8,128)(2,1)S(1)}, u32[]{:S(2)}, u32[]{:S(2)}) collective-permute-start(bf16[4,64,1792]{2,1,0:T(8,128)(2,1)S(1)} %slice.105.own), channel_id=1, source_target_pairs={{0,2},{1,3},{2,0},{3,1},{4,6},{5,7},{6,4},{7,5},{8,10},{9,11},{10,... | collective-permute-start | bytes 2752520 | tf_op jit(solution)/shard_map/ppermute | solution.py:609
  188.4 22.4 %collective-permute-start.5 = (bf16[4,64,1792]{2,1,0:T(8,128)(2,1)S(1)}, bf16[4,64,1792]{2,1,0:T(8,128)(2,1)S(1)}, u32[]{:S(2)}, u32[]{:S(2)}) collective-permute-start(bf16[4,64,1792]{2,1,0:T(8,128)(2,1)S(1)} %slice.105.own), channel_id=1, source_target_pairs={{0,1},{1,0},{2,3},{3,2},{4,5},{5,4},{6,7},{7,6},{8,9},{9,8},{10,11... | collective-permute-start | bytes 2752520 | tf_op jit(solution)/shard_map/ppermute | solution.py:609
  213.4 12.1 %collective-permute-start.9 = (bf16[2,64,1792]{2,1,0:T(8,128)(2,1)}, bf16[2,64,1792]{2,1,0:T(8,128)(2,1)}, u32[]{:S(2)}, u32[]{:S(2)}) collective-permute-start(bf16[2,64,1792]{2,1,0:T(8,128)(2,1)} %slice.87), channel_id=1, source_target_pairs={{0,1},{1,0},{2,3},{3,2},{4,5},{5,4},{6,7},{7,6},{8,9},{9,8},{10,11... | collective-permute-start | bytes 1376264 | tf_op jit(solution)/shard_map/ppermute | solution.py:609
  214.8 11.8 %collective-permute-start.8 = (bf16[2,64,1792]{2,1,0:T(8,128)(2,1)}, bf16[2,64,1792]{2,1,0:T(8,128)(2,1)}, u32[]{:S(2)}, u32[]{:S(2)}) collective-permute-start(bf16[2,64,1792]{2,1,0:T(8,128)(2,1)} %slice.86), channel_id=1, source_target_pairs={{0,2},{1,3},{2,0},{3,1},{4,6},{5,7},{6,4},{7,5},{8,10},{9,11},{10,... | collective-permute-start | bytes 1376264 | tf_op jit(solution)/shard_map/ppermute | solution.py:609
  226.6 23.2 %collective-permute-start.11 = (bf16[4,64,1792]{2,1,0:T(8,128)(2,1)S(1)}, bf16[4,64,1792]{2,1,0:T(8,128)(2,1)}, u32[]{:S(2)}, u32[]{:S(2)}) collective-permute-start(bf16[4,64,1792]{2,1,0:T(8,128)(2,1)S(1)} %all_gather.27.own), channel_id=1, source_target_pairs={{0,2},{1,3},{2,0},{3,1},{4,6},{5,7},{6,4},{7,5},{8,10},{9,11},{10,... | collective-permute-start | bytes 2752520 | tf_op jit(solution)/shard_map/ppermute | solution.py:609
  227.2 22.6 %collective-permute-start.10 = (bf16[4,64,1792]{2,1,0:T(8,128)(2,1)S(1)}, bf16[4,64,1792]{2,1,0:T(8,128)(2,1)}, u32[]{:S(2)}, u32[]{:S(2)}) collective-permute-start(bf16[4,64,1792]{2,1,0:T(8,128)(2,1)S(1)} %all_gather.27.own), channel_id=1, source_target_pairs={{0,1},{1,0},{2,3},{3,2},{4,5},{5,4},{6,7},{7,6},{8,9},{9,8},{10,11... | collective-permute-start | bytes 2752520 | tf_op jit(solution)/shard_map/ppermute | solution.py:609
  249.9 95.7 %reduce-scatter.5.cloned.1.call-start = ((), (), s32[]{:S(2)}) async-start(), calls=%async_computation.7 | async-start | bytes 1146880 | tf_op jit(solution)/shard_map/reduce_scatter | solution.py:775
  252.1 10.1 %collective-permute-start.13 = (bf16[2,64,1792]{2,1,0:T(8,128)(2,1)S(1)}, bf16[2,64,1792]{2,1,0:T(8,128)(2,1)S(1)}, u32[]{:S(2)}, u32[]{:S(2)}) collective-permute-start(bf16[2,64,1792]{2,1,0:T(8,128)(2,1)S(1)} %slice.92), channel_id=1, source_target_pairs={{0,1},{1,0},{2,3},{3,2},{4,5},{5,4},{6,7},{7,6},{8,9},{9,8},{10,11... | collective-permute-start | bytes 1376264 | tf_op jit(solution)/shard_map/ppermute | solution.py:609
  280.4 13.5 %collective-permute-start.17 = (bf16[4,16,3584]{2,1,0:T(8,128)(2,1)S(1)}, bf16[4,16,3584]{2,1,0:T(8,128)(2,1)S(1)}, u32[]{:S(2)}, u32[]{:S(2)}) collective-permute-start(bf16[4,16,3584]{2,1,0:T(8,128)(2,1)S(1)} %get-tuple-element.91), channel_id=1, source_target_pairs={{0,1},{1,0},{2,3},{3,2},{4,5},{5,4},{6,7},{7,6},{8,9},{9,8},{10,11... | collective-permute-start | bytes 1376264 | tf_op jit(solution)/shard_map/ppermute | solution.py:609
  281.0 23.0 %collective-permute-start.18 = (bf16[4,16,3584]{2,1,0:T(8,128)(2,1)S(1)}, bf16[4,16,3584]{2,1,0:T(8,128)(2,1)S(1)}, u32[]{:S(2)}, u32[]{:S(2)}) collective-permute-start(bf16[4,16,3584]{2,1,0:T(8,128)(2,1)S(1)} %get-tuple-element.92), channel_id=1, source_target_pairs={{0,2},{1,3},{2,0},{3,1},{4,6},{5,7},{6,4},{7,5},{8,10},{9,11},{10,... | collective-permute-start | bytes 1376264 | tf_op jit(solution)/shard_map/ppermute | solution.py:609
  282.3 22.2 %collective-permute-start.19 = (bf16[4,16,3584]{2,1,0:T(8,128)(2,1)S(1)}, bf16[4,16,3584]{2,1,0:T(8,128)(2,1)S(1)}, u32[]{:S(2)}, u32[]{:S(2)}) collective-permute-start(bf16[4,16,3584]{2,1,0:T(8,128)(2,1)S(1)} %get-tuple-element.93), channel_id=1, source_target_pairs={{0,3},{1,2},{2,1},{3,0},{4,7},{5,6},{6,5},{7,4},{8,11},{9,10},{10,... | collective-permute-start | bytes 1376264 | tf_op jit(solution)/shard_map/ppermute | solution.py:609
  286.0 27.6 %collective-permute-start.14 = (bf16[4,16,3584]{2,1,0:T(8,128)(2,1)S(1)}, bf16[4,16,3584]{2,1,0:T(8,128)(2,1)S(1)}, u32[]{:S(2)}, u32[]{:S(2)}) collective-permute-start(bf16[4,16,3584]{2,1,0:T(8,128)(2,1)S(1)} %get-tuple-element.87), channel_id=1, source_target_pairs={{0,1},{1,0},{2,3},{3,2},{4,5},{5,4},{6,7},{7,6},{8,9},{9,8},{10,11... | collective-permute-start | bytes 1376264 | tf_op jit(solution)/shard_map/ppermute | solution.py:609
  286.6 27.0 %collective-permute-start.15 = (bf16[4,16,3584]{2,1,0:T(8,128)(2,1)S(1)}, bf16[4,16,3584]{2,1,0:T(8,128)(2,1)S(1)}, u32[]{:S(2)}, u32[]{:S(2)}) collective-permute-start(bf16[4,16,3584]{2,1,0:T(8,128)(2,1)S(1)} %get-tuple-element.88), channel_id=1, source_target_pairs={{0,2},{1,3},{2,0},{3,1},{4,6},{5,7},{6,4},{7,5},{8,10},{9,11},{10,... | collective-permute-start | bytes 1376264 | tf_op jit(solution)/shard_map/ppermute | solution.py:609
  293.9 25.7 %collective-permute-start.16 = (bf16[4,16,3584]{2,1,0:T(8,128)(2,1)S(1)}, bf16[4,16,3584]{2,1,0:T(8,128)(2,1)S(1)}, u32[]{:S(2)}, u32[]{:S(2)}) collective-permute-start(bf16[4,16,3584]{2,1,0:T(8,128)(2,1)S(1)} %get-tuple-element.89), channel_id=1, source_target_pairs={{0,3},{1,2},{2,1},{3,0},{4,7},{5,6},{6,5},{7,4},{8,11},{9,10},{10,... | collective-permute-start | bytes 1376264 | tf_op jit(solution)/shard_map/ppermute | solution.py:609
  (42 other events, 256.1 us)
Sparse Core Ops, SparseCore 0:
  77.2 26.8 all-gather.6
  105.7 28.5 all-gather.8
  135.9 27.4 all-gather.10
  250.0 67.8 reduce-scatter.2
  321.0 24.5 reduce-scatter.4

commit v12 on v9

--- a/solution.py
+++ b/solution.py
@@ -266,7 +266,7 @@
         ],
         out_specs=pl.BlockSpec((1, rows, width), lambda i: (i, 0, 0)),
         out_shape=jax.ShapeDtypeStruct((ctx_count, rows, width), jnp.bfloat16),
-        compiler_params=pltpu.CompilerParams(vmem_limit_bytes=32 * 2**20),
+        compiler_params=pltpu.CompilerParams(vmem_limit_bytes=56 * 2**20),
         name="pack",
     )(query, key, value, residual, side)
 

time: 328 us -> 329 us (level)
  local copies, waits for them, and re-layouts: 15.7 us -> 10.7 us
  Pallas kernels: 57.1 us -> 62 us
    pallas_call x1, Pallas kernels: 0.61 us -> 5.65 us  [pack(): pl.pallas_call(pack_kernel, grid=(ctx_count,), in_specs=[heads, heads, he...]
    unnamed x39 -> x29, local copies, waits for them, and re-layouts: 8.08 us -> 3.15 us
where the time goes in v12:
time: 329 us; the launch traced here: 327 us
  waiting for transfers between devices  169 us (51%)
  Pallas kernels  62 us (19%)
  blocking collectives  33.2 us (10%)
  starting transfers between devices  30.7 us (9%)
  between operations  13.6 us (4%)
  local copies, waits for them, and re-layouts  10.7 us (3%)
  other arithmetic  7.78 us (2%)
    ppermute x14, waiting for transfers between devices, plane_step(): return lax.ppermute(block, 'exp', [(i, i ^ step) for i in range(count)])  47.8 us
    all_to_all x1, waiting for transfers between devices, by_heads(): moved = lax.all_to_all(packed, ctx, split_axis=0, concat_axis=0, tiled=True)  47.8 us
    all_gather x1, waiting for transfers between devices, by_heads(): spread_first = lax.all_gather(attended[0], 'z', axis=0)  26.9 us
    pallas_call x2, Pallas kernels, run_expert(): pl.pallas_call(functools.partial(expert_kernel, exp_dim), grid_spec=pltpu...  21.7 us
    all_gather x1, blocking collectives, by_heads(): plane_second = lax.all_gather(scaled_second, 'z', axis=0)  19.8 us
    all_gather x1, waiting for transfers between devices, by_heads(): plane_first = lax.all_gather(padded, 'z', axis=0)[:, :, :2 * cols]  19.2 us
    pallas_call x3, Pallas kernels, run_down(): pl.pallas_call(functools.partial(down_kernel, start), grid_spec=pltpu.Pre...  16.7 us
    ppermute x14, starting transfers between devices, plane_step(): return lax.ppermute(block, 'exp', [(i, i ^ step) for i in range(count)])  15.7 us
  transfers between devices with their start and end apart: 28, of which 18 were waited for; matrix products, arithmetic and copies ran while one was open for 4% of the time, Pallas kernels for 17%

profile of v12, /device:TPU:0, one launch (start us, length us, event | category | flops | bytes accessed | tf_op | source)
XLA Modules:
  0.0 327.5 jit_solution(10945452071387938709)
XLA Ops:
  9.2 5.7 %pack.1 = bf16[8,512,256]{2,1,0:T(8,128)(2,1)} custom-call(bf16[128,2048]{1,0:T(8,128)(2,1)} %query.1, bf16[128,2048]{1,0:T(8,128)(2,1)} %key.1, bf16[128,2048]{1,0:T(8,128)(2,1)} %value.1, bf16[32,7168]{1,0:T(8,128)(2,1)} %residual.1, bf16[8,32,128]{2,1,0:T(8,128)(2,1)} %bitcast.126), custom_call_target="tpu_custom_call" | custom-call | tf_op jit(solution)/shard_map/pack/pallas_call | solution.py:257
  14.9 6.3 %all-to-all-start = ((bf16[8,512,256]{2,1,0:T(8,128)(2,1)}), bf16[8,512,256]{2,1,0:T(8,128)(2,1)S(1)}, u32[]{:S(2)}, u32[]{:S(2)}) async-start(bf16[8,512,256]{2,1,0:T(8,128)(2,1)} %pack.1), calls=%async_computation | async-start | bytes 4194304 | tf_op jit(solution)/shard_map/all_to_all | solution.py:632
  22.5 47.8 %all-to-all-done.moved = bf16[8,512,256]{2,1,0:T(8,128)(2,1)S(1)} async-done(((bf16[8,512,256]{2,1,0:T(8,128)(2,1)}), bf16[8,512,256]{2,1,0:T(8,128)(2,1)S(1)}, u32[]{:S(2)}, u32[]{:S(2)}) %all-to-all-start) | async-done | bytes 2097184 | tf_op jit(solution)/shard_map/all_to_all | solution.py:632
  71.1 6.0 %attend.1 = (bf16[512,256]{1,0:T(8,128)(2,1)}, bf16[512,256]{1,0:T(8,128)(2,1)}) custom-call(bf16[8,512,256]{2,1,0:T(8,128)(2,1)S(1)} %all-to-all-done.moved, f32[8,1024]{1,0:T(8,128)S(1)} %tile.12.taps, f32[1024,4]{1,0:T(8,128)S(1)} %copy.85.gates), custom_call_target="tpu_custom_call" | custom-call | tf_op jit(solution)/shard_map/attend/pallas_call | solution.py:352
  77.3 26.9 %all-gather.7.cloned.1.call-done = bf16[2048,256]{1,0:T(8,128)(2,1)} async-done(((bf16[512,256]{1,0:T(8,128)(2,1)}), bf16[2048,256]{1,0:T(8,128)(2,1)}) %all-gather.7.cloned.1.call-update) | async-done | bytes 1048592 | tf_op jit(solution)/shard_map/all_gather | solution.py:675
  107.3 5.7 %project.3 = bf16[4,144,896]{2,1,0:T(8,128)(2,1)} custom-call(s32[1]{0:T(128)} %bitcast.2.spots, bf16[4,1,512,256]{3,2,1,0:T(8,128)(2,1)} %bitcast.139, bf16[4,1,512,256]{3,2,1,0:T(8,128)(2,1)} %bitcast.22.left_b, bf16[2048,896]{1,0:T(8,128)(2,1)} %proj.3, bf16[4,16,896]{2,1,0:T(8,128)(2,1)} %bitcast.123), custom_call_target="tpu_custom_call" | custom-call | flops 1879048192 | bytes 6799360 | tf_op jit(solution)/shard_map/project/pallas_call | solution.py:401
  113.0 3.6 %all-to-all-start.1 = ((bf16[4,144,896]{2,1,0:T(8,128)(2,1)}), bf16[4,144,896]{2,1,0:T(8,128)(2,1)S(1)}, u32[]{:S(2)}, u32[]{:S(2)}) async-start(bf16[4,144,896]{2,1,0:T(8,128)(2,1)} %project.3), calls=%async_computation.1 | async-start | bytes 2064384 | tf_op jit(solution)/shard_map/all_to_all | solution.py:658
  116.7 13.8 %all-to-all-done.1 = bf16[4,144,896]{2,1,0:T(8,128)(2,1)S(1)} async-done(((bf16[4,144,896]{2,1,0:T(8,128)(2,1)}), bf16[4,144,896]{2,1,0:T(8,128)(2,1)S(1)}, u32[]{:S(2)}, u32[]{:S(2)}) %all-to-all-start.1) | async-done | bytes 1032224 | tf_op jit(solution)/shard_map/all_to_all | solution.py:658
  134.4 6.2 %project.2 = bf16[4,128,896]{2,1,0:T(8,128)(2,1)} custom-call(s32[1]{0:T(128)} %bitcast.2.spots, bf16[4,2,512,256]{3,2,1,0:T(8,128)(2,1)} %bitcast.105, bf16[4,2,512,256]{3,2,1,0:T(8,128)(2,1)} %bitcast.106, bf16[2048,896]{1,0:T(8,128)(2,1)} %proj.3, bf16[4,16,896]{2,1,0:T(8,128)(2,1)} %bitcast.124), custom_call_target="tpu_custom_call" | custom-call | flops 1879048192 | bytes 6684672 | tf_op jit(solution)/shard_map/project/pallas_call | solution.py:401
  140.6 3.6 %all-to-all-start.2 = ((bf16[4,128,896]{2,1,0:T(8,128)(2,1)}), bf16[4,128,896]{2,1,0:T(8,128)(2,1)S(1)}, u32[]{:S(2)}, u32[]{:S(2)}) async-start(bf16[4,128,896]{2,1,0:T(8,128)(2,1)} %project.2), calls=%async_computation.2 | async-start | bytes 1835008 | tf_op jit(solution)/shard_map/all_to_all | solution.py:658
  144.3 19.2 %all-gather.11.cloned.1.call-done = bf16[256,2048]{1,0:T(8,128)(2,1)} async-done(((bf16[64,2048]{1,0:T(8,128)(2,1)}), bf16[256,2048]{1,0:T(8,128)(2,1)}) %all-gather.11.cloned.1.call-update) | async-done | bytes 1048592 | tf_op jit(solution)/shard_map/all_gather | solution.py:698
  168.1 19.8 %all_gather.27.own = bf16[4,64,1792]{2,1,0:T(8,128)(2,1)S(1)} all-gather(bf16[1,64,1792]{2,1,0:T(8,128)(2,1)S(1)} %fusion.1), channel_id=1, replica_groups=mesh['z'=4,'core'=2,'exp'=4] {'z'}, dimensions={0}, use_global_device_ids=true | all-gather | bytes 1146880 | tf_op jit(solution)/shard_map/all_gather | solution.py:702
  192.6 9.2 %collective-permute-done.9.far_b = bf16[2,64,1792]{2,1,0:T(8,128)(2,1)} collective-permute-done((bf16[2,64,1792]{2,1,0:T(8,128)(2,1)S(1)}, bf16[2,64,1792]{2,1,0:T(8,128)(2,1)}, u32[]{:S(2)}, u32[]{:S(2)}) %collective-permute-start.9) | collective-permute-done | bytes 458784 | tf_op jit(solution)/shard_map/ppermute | solution.py:577
  205.5 10.8 %expert.2 = bf16[2,4,4,16,256]{4,3,2,1,0:T(8,128)(2,1)} custom-call(s32[2]{0:T(128)} %pad_add_fusion.spots, bf16[4,64,1792]{2,1,0:T(8,128)(2,1)} %copy-done.2, bf16[4,64,1792]{2,1,0:T(8,128)(2,1)} %copy-done.5, bf16[4,64,1792]{2,1,0:T(8,128)(2,1)} %copy-done.4, bf16[2,64,1792]{2,1,0:T(8,128)(2,1)} %collective-permute-done.8.far_a, ...), custom_call_target="tpu_custom_call" | custom-call | flops 3758096384 | bytes 18350080 | tf_op jit(solution)/shard_map/expert/pallas_call | solution.py:478
  216.3 7.5 %down.3 = bf16[4,4,16,7168]{3,2,1,0:T(8,128)(2,1)} custom-call(s32[2]{0:T(128)} %pad_add_fusion.spots, bf16[2,256,256]{2,1,0:T(8,128)(2,1)} %bitcast.117, bf16[256,7168]{1,0:T(8,128)(2,1)} %bitcast.95, bf16[256,7168]{1,0:T(8,128)(2,1)} %collective-permute-done.2.down_v, f32[4,16,1792]{2,1,0:T(8,128)} %pad_maximum_fusion.2.hidden), custom_call_target="tpu_custom_call" | custom-call | flops 1879048192 | bytes 11010048 | tf_op jit(solution)/shard_map/down/pallas_call | solution.py:547
  229.5 6.2 %collective-permute-done.13.far_b = bf16[2,64,1792]{2,1,0:T(8,128)(2,1)S(1)} collective-permute-done((bf16[2,64,1792]{2,1,0:T(8,128)(2,1)S(1)}, bf16[2,64,1792]{2,1,0:T(8,128)(2,1)S(1)}, u32[]{:S(2)}, u32[]{:S(2)}) %collective-permute-start.13) | collective-permute-done | bytes 458784 | tf_op jit(solution)/shard_map/ppermute | solution.py:577
  237.6 10.9 %expert.3 = bf16[2,4,4,16,256]{4,3,2,1,0:T(8,128)(2,1)} custom-call(s32[2]{0:T(128)} %pad_add_fusion.spots, bf16[4,64,1792]{2,1,0:T(8,128)(2,1)} %copy-done.3, bf16[4,64,1792]{2,1,0:T(8,128)(2,1)} %collective-permute-done.10.along, bf16[4,64,1792]{2,1,0:T(8,128)(2,1)} %copy-done.6, bf16[2,64,1792]{2,1,0:T(8,128)(2,1)} %copy-done.10, ...), custom_call_target="tpu_custom_call" | custom-call | flops 3758096384 | bytes 18350080 | tf_op jit(solution)/shard_map/expert/pallas_call | solution.py:478
  248.4 4.6 %down.5 = (bf16[4,16,3584]{2,1,0:T(8,128)(2,1)}, bf16[4,16,3584]{2,1,0:T(8,128)(2,1)}, bf16[4,16,3584]{2,1,0:T(8,128)(2,1)}, bf16[4,16,3584]{2,1,0:T(8,128)(2,1)}) custom-call(s32[2]{0:T(128)} %pad_add_fusion.spots, bf16[2,256,256]{2,1,0:T(8,128)(2,1)} %bitcast.107, bf16[256,7168]{1,0:T(8,128)(2,1)} %bitcast.96, ...), custom_call_target="tpu_custom_call" | custom-call | flops 939524096 | bytes 5505024 | tf_op jit(solution)/shard_map/down/pallas_call | solution.py:547
  256.5 4.7 %down.4 = (bf16[4,16,3584]{2,1,0:T(8,128)(2,1)}, bf16[4,16,3584]{2,1,0:T(8,128)(2,1)}, bf16[4,16,3584]{2,1,0:T(8,128)(2,1)}, bf16[4,16,3584]{2,1,0:T(8,128)(2,1)}) custom-call(s32[2]{0:T(128)} %pad_add_fusion.spots, bf16[2,256,256]{2,1,0:T(8,128)(2,1)} %bitcast.108, bf16[256,7168]{1,0:T(8,128)(2,1)} %bitcast.97, ...), custom_call_target="tpu_custom_call" | custom-call | flops 939524096 | bytes 5505024 | tf_op jit(solution)/shard_map/down/pallas_call | solution.py:547
  268.1 9.6 %collective-permute-done.18 = bf16[4,16,3584]{2,1,0:T(8,128)(2,1)S(1)} collective-permute-done((bf16[4,16,3584]{2,1,0:T(8,128)(2,1)}, bf16[4,16,3584]{2,1,0:T(8,128)(2,1)S(1)}, u32[]{:S(2)}, u32[]{:S(2)}) %collective-permute-start.18) | collective-permute-done | bytes 458784 | tf_op jit(solution)/shard_map/ppermute | solution.py:577
  278.0 8.5 %collective-permute-done.14 = bf16[4,16,3584]{2,1,0:T(8,128)(2,1)S(1)} collective-permute-done((bf16[4,16,3584]{2,1,0:T(8,128)(2,1)}, bf16[4,16,3584]{2,1,0:T(8,128)(2,1)S(1)}, u32[]{:S(2)}, u32[]{:S(2)}) %collective-permute-start.14) | collective-permute-done | bytes 458784 | tf_op jit(solution)/shard_map/ppermute | solution.py:577
  286.4 6.8 %collective-permute-done.15 = bf16[4,16,3584]{2,1,0:T(8,128)(2,1)S(1)} collective-permute-done((bf16[4,16,3584]{2,1,0:T(8,128)(2,1)}, bf16[4,16,3584]{2,1,0:T(8,128)(2,1)S(1)}, u32[]{:S(2)}, u32[]{:S(2)}) %collective-permute-start.15) | collective-permute-done | bytes 458784 | tf_op jit(solution)/shard_map/ppermute | solution.py:577
  294.5 13.4 %all_to_all.20 = bf16[4,16,7168]{2,1,0:T(8,128)(2,1)S(1)} all-to-all(bf16[4,16,7168]{2,1,0:T(8,128)(2,1)} %bitcast.119), channel_id=1, replica_groups=mesh['z'=4,'core'=2,'exp'=4] {'exp'}, dimensions={0} | all-to-all | bytes 1835008 | tf_op jit(solution)/shard_map/all_to_all | solution.py:741
  308.1 11.1 %reduce-scatter.5.cloned.1.call-done = bf16[1,16,7168]{2,1,0:T(8,128)(2,1)} async-done(((bf16[4,16,7168]{2,1,0:T(8,128)(2,1)}), bf16[1,16,7168]{2,1,0:T(8,128)(2,1)}) %reduce-scatter.5.cloned.1.call-update) | async-done | bytes 229392 | tf_op jit(solution)/shard_map/reduce_scatter | solution.py:740
  (140 shorter events, 46.1 us)
Async XLA Ops:
  14.9 55.4 %all-to-all-start = ((bf16[8,512,256]{2,1,0:T(8,128)(2,1)}), bf16[8,512,256]{2,1,0:T(8,128)(2,1)S(1)}, u32[]{:S(2)}, u32[]{:S(2)}) async-start(bf16[8,512,256]{2,1,0:T(8,128)(2,1)} %pack.1), calls=%async_computation | async-start | bytes 4194304 | tf_op jit(solution)/shard_map/all_to_all | solution.py:632
  21.2 82.9 %all-gather.7.cloned.1.call-start = ((), (), s32[]{:S(2)}) async-start(), calls=%async_computation.8 | async-start | bytes 1310720 | tf_op jit(solution)/shard_map/all_gather | solution.py:675
  21.3 56.0 %collective-permute-start = (bf16[7168,256]{1,0:T(8,128)(2,1)}, bf16[7168,256]{1,0:T(8,128)(2,1)}, u32[]{:S(2)}, u32[]{:S(2)}) collective-permute-start(bf16[7168,256]{1,0:T(8,128)(2,1)} %bitcast.98), channel_id=1, source_target_pairs={{0,4},{4,0},{1,5},{5,1},{2,6},{6,2},{3,7},{7,3},{8,12},{12,8},{9,1... | collective-permute-start | bytes 11010056 | tf_op jit(solution)/shard_map/ppermute | solution.py:572
  21.7 55.5 %collective-permute-start.1 = (bf16[7168,256]{1,0:T(8,128)(2,1)}, bf16[7168,256]{1,0:T(8,128)(2,1)}, u32[]{:S(2)}, u32[]{:S(2)}) collective-permute-start(bf16[7168,256]{1,0:T(8,128)(2,1)} %bitcast.101), channel_id=1, source_target_pairs={{0,4},{4,0},{1,5},{5,1},{2,6},{6,2},{3,7},{7,3},{8,12},{12,8},{9,1... | collective-permute-start | bytes 11010056 | tf_op jit(solution)/shard_map/ppermute | solution.py:572
  21.8 55.4 %collective-permute-start.2 = (bf16[256,7168]{1,0:T(8,128)(2,1)}, bf16[256,7168]{1,0:T(8,128)(2,1)}, u32[]{:S(2)}, u32[]{:S(2)}) collective-permute-start(bf16[256,7168]{1,0:T(8,128)(2,1)} %bitcast.94), channel_id=1, source_target_pairs={{0,4},{4,0},{1,5},{5,1},{2,6},{6,2},{3,7},{7,3},{8,12},{12,8},{9,1... | collective-permute-start | bytes 11010056 | tf_op jit(solution)/shard_map/ppermute | solution.py:572
  77.2 57.2 %all-gather.9.cloned.1.call-start = ((), (), s32[]{:S(2)}) async-start(), calls=%async_computation.9 | async-start | bytes 2359296 | tf_op jit(solution)/shard_map/all_gather | solution.py:681
  113.0 17.5 %all-to-all-start.1 = ((bf16[4,144,896]{2,1,0:T(8,128)(2,1)}), bf16[4,144,896]{2,1,0:T(8,128)(2,1)S(1)}, u32[]{:S(2)}, u32[]{:S(2)}) async-start(bf16[4,144,896]{2,1,0:T(8,128)(2,1)} %project.3), calls=%async_computation.1 | async-start | bytes 2064384 | tf_op jit(solution)/shard_map/all_to_all | solution.py:658
  116.6 46.8 %all-gather.11.cloned.1.call-start = ((), (), s32[]{:S(2)}) async-start(), calls=%async_computation.10 | async-start | bytes 1310720 | tf_op jit(solution)/shard_map/all_gather | solution.py:698
  140.6 24.1 %all-to-all-start.2 = ((bf16[4,128,896]{2,1,0:T(8,128)(2,1)}), bf16[4,128,896]{2,1,0:T(8,128)(2,1)S(1)}, u32[]{:S(2)}, u32[]{:S(2)}) async-start(bf16[4,128,896]{2,1,0:T(8,128)(2,1)} %project.2), calls=%async_computation.2 | async-start | bytes 1835008 | tf_op jit(solution)/shard_map/all_to_all | solution.py:658
  144.3 150.2 %reduce-scatter.3.cloned.1.call-start = ((), (), s32[]{:S(2)}) async-start(), calls=%async_computation.6 | async-start | bytes 4587520 | tf_op jit(solution)/shard_map/reduce_scatter | solution.py:723
  165.0 22.9 %collective-permute-start.6 = (bf16[4,64,1792]{2,1,0:T(8,128)(2,1)S(1)}, bf16[4,64,1792]{2,1,0:T(8,128)(2,1)S(1)}, u32[]{:S(2)}, u32[]{:S(2)}) collective-permute-start(bf16[4,64,1792]{2,1,0:T(8,128)(2,1)S(1)} %slice.101.own), channel_id=1, source_target_pairs={{0,2},{1,3},{2,0},{3,1},{4,6},{5,7},{6,4},{7,5},{8,10},{9,11},{10,... | collective-permute-start | bytes 2752520 | tf_op jit(solution)/shard_map/ppermute | solution.py:577
  166.5 22.4 %collective-permute-start.5 = (bf16[4,64,1792]{2,1,0:T(8,128)(2,1)S(1)}, bf16[4,64,1792]{2,1,0:T(8,128)(2,1)S(1)}, u32[]{:S(2)}, u32[]{:S(2)}) collective-permute-start(bf16[4,64,1792]{2,1,0:T(8,128)(2,1)S(1)} %slice.101.own), channel_id=1, source_target_pairs={{0,1},{1,0},{2,3},{3,2},{4,5},{5,4},{6,7},{7,6},{8,9},{9,8},{10,11... | collective-permute-start | bytes 2752520 | tf_op jit(solution)/shard_map/ppermute | solution.py:577
  189.9 11.9 %collective-permute-start.9 = (bf16[2,64,1792]{2,1,0:T(8,128)(2,1)S(1)}, bf16[2,64,1792]{2,1,0:T(8,128)(2,1)}, u32[]{:S(2)}, u32[]{:S(2)}) collective-permute-start(bf16[2,64,1792]{2,1,0:T(8,128)(2,1)S(1)} %slice.83), channel_id=1, source_target_pairs={{0,1},{1,0},{2,3},{3,2},{4,5},{5,4},{6,7},{7,6},{8,9},{9,8},{10,11... | collective-permute-start | bytes 1376264 | tf_op jit(solution)/shard_map/ppermute | solution.py:577
  191.4 11.6 %collective-permute-start.8 = (bf16[2,64,1792]{2,1,0:T(8,128)(2,1)S(1)}, bf16[2,64,1792]{2,1,0:T(8,128)(2,1)}, u32[]{:S(2)}, u32[]{:S(2)}) collective-permute-start(bf16[2,64,1792]{2,1,0:T(8,128)(2,1)S(1)} %slice.82), channel_id=1, source_target_pairs={{0,2},{1,3},{2,0},{3,1},{4,6},{5,7},{6,4},{7,5},{8,10},{9,11},{10,... | collective-permute-start | bytes 1376264 | tf_op jit(solution)/shard_map/ppermute | solution.py:577
  203.0 20.8 %collective-permute-start.11 = (bf16[4,64,1792]{2,1,0:T(8,128)(2,1)S(1)}, bf16[4,64,1792]{2,1,0:T(8,128)(2,1)S(1)}, u32[]{:S(2)}, u32[]{:S(2)}) collective-permute-start(bf16[4,64,1792]{2,1,0:T(8,128)(2,1)S(1)} %all_gather.27.own), channel_id=1, source_target_pairs={{0,2},{1,3},{2,0},{3,1},{4,6},{5,7},{6,4},{7,5},{8,10},{9,11},{10,... | collective-permute-start | bytes 2752520 | tf_op jit(solution)/shard_map/ppermute | solution.py:577
  203.9 20.5 %collective-permute-start.10 = (bf16[4,64,1792]{2,1,0:T(8,128)(2,1)S(1)}, bf16[4,64,1792]{2,1,0:T(8,128)(2,1)}, u32[]{:S(2)}, u32[]{:S(2)}) collective-permute-start(bf16[4,64,1792]{2,1,0:T(8,128)(2,1)S(1)} %all_gather.27.own), channel_id=1, source_target_pairs={{0,1},{1,0},{2,3},{3,2},{4,5},{5,4},{6,7},{7,6},{8,9},{9,8},{10,11... | collective-permute-start | bytes 2752520 | tf_op jit(solution)/shard_map/ppermute | solution.py:577
  224.4 94.8 %reduce-scatter.5.cloned.1.call-start = ((), (), s32[]{:S(2)}) async-start(), calls=%async_computation.7 | async-start | bytes 1146880 | tf_op jit(solution)/shard_map/reduce_scatter | solution.py:740
  225.6 10.0 %collective-permute-start.13 = (bf16[2,64,1792]{2,1,0:T(8,128)(2,1)S(1)}, bf16[2,64,1792]{2,1,0:T(8,128)(2,1)S(1)}, u32[]{:S(2)}, u32[]{:S(2)}) collective-permute-start(bf16[2,64,1792]{2,1,0:T(8,128)(2,1)S(1)} %slice.88), channel_id=1, source_target_pairs={{0,1},{1,0},{2,3},{3,2},{4,5},{5,4},{6,7},{7,6},{8,9},{9,8},{10,11... | collective-permute-start | bytes 1376264 | tf_op jit(solution)/shard_map/ppermute | solution.py:577
  253.0 13.7 %collective-permute-start.17 = (bf16[4,16,3584]{2,1,0:T(8,128)(2,1)}, bf16[4,16,3584]{2,1,0:T(8,128)(2,1)S(1)}, u32[]{:S(2)}, u32[]{:S(2)}) collective-permute-start(bf16[4,16,3584]{2,1,0:T(8,128)(2,1)} %get-tuple-element.61), channel_id=1, source_target_pairs={{0,1},{1,0},{2,3},{3,2},{4,5},{5,4},{6,7},{7,6},{8,9},{9,8},{10,11... | collective-permute-start | bytes 1376264 | tf_op jit(solution)/shard_map/ppermute | solution.py:577
  254.2 23.6 %collective-permute-start.18 = (bf16[4,16,3584]{2,1,0:T(8,128)(2,1)}, bf16[4,16,3584]{2,1,0:T(8,128)(2,1)S(1)}, u32[]{:S(2)}, u32[]{:S(2)}) collective-permute-start(bf16[4,16,3584]{2,1,0:T(8,128)(2,1)} %get-tuple-element.62), channel_id=1, source_target_pairs={{0,2},{1,3},{2,0},{3,1},{4,6},{5,7},{6,4},{7,5},{8,10},{9,11},{10,... | collective-permute-start | bytes 1376264 | tf_op jit(solution)/shard_map/ppermute | solution.py:577
  255.0 22.7 %collective-permute-start.19 = (bf16[4,16,3584]{2,1,0:T(8,128)(2,1)}, bf16[4,16,3584]{2,1,0:T(8,128)(2,1)S(1)}, u32[]{:S(2)}, u32[]{:S(2)}) collective-permute-start(bf16[4,16,3584]{2,1,0:T(8,128)(2,1)} %get-tuple-element.63), channel_id=1, source_target_pairs={{0,3},{1,2},{2,1},{3,0},{4,7},{5,6},{6,5},{7,4},{8,11},{9,10},{10,... | collective-permute-start | bytes 1376264 | tf_op jit(solution)/shard_map/ppermute | solution.py:577
  261.2 25.2 %collective-permute-start.14 = (bf16[4,16,3584]{2,1,0:T(8,128)(2,1)}, bf16[4,16,3584]{2,1,0:T(8,128)(2,1)S(1)}, u32[]{:S(2)}, u32[]{:S(2)}) collective-permute-start(bf16[4,16,3584]{2,1,0:T(8,128)(2,1)} %get-tuple-element.57), channel_id=1, source_target_pairs={{0,1},{1,0},{2,3},{3,2},{4,5},{5,4},{6,7},{7,6},{8,9},{9,8},{10,11... | collective-permute-start | bytes 1376264 | tf_op jit(solution)/shard_map/ppermute | solution.py:577
  262.4 30.8 %collective-permute-start.15 = (bf16[4,16,3584]{2,1,0:T(8,128)(2,1)}, bf16[4,16,3584]{2,1,0:T(8,128)(2,1)S(1)}, u32[]{:S(2)}, u32[]{:S(2)}) collective-permute-start(bf16[4,16,3584]{2,1,0:T(8,128)(2,1)} %get-tuple-element.58), channel_id=1, source_target_pairs={{0,2},{1,3},{2,0},{3,1},{4,6},{5,7},{6,4},{7,5},{8,10},{9,11},{10,... | collective-permute-start | bytes 1376264 | tf_op jit(solution)/shard_map/ppermute | solution.py:577
  266.7 26.5 %collective-permute-start.16 = (bf16[4,16,3584]{2,1,0:T(8,128)(2,1)}, bf16[4,16,3584]{2,1,0:T(8,128)(2,1)S(1)}, u32[]{:S(2)}, u32[]{:S(2)}) collective-permute-start(bf16[4,16,3584]{2,1,0:T(8,128)(2,1)} %get-tuple-element.59), channel_id=1, source_target_pairs={{0,3},{1,2},{2,1},{3,0},{4,7},{5,6},{6,5},{7,4},{8,11},{9,10},{10,... | collective-permute-start | bytes 1376264 | tf_op jit(solution)/shard_map/ppermute | solution.py:577
  (15 other events, 152.2 us)
Sparse Core Ops, SparseCore 0:
  77.3 26.8 all-gather.6
  105.8 28.5 all-gather.8
  136.0 27.4 all-gather.10
  224.6 66.9 reduce-scatter.2
  294.6 24.5 reduce-scatter.4
